TPU v7x, 32 devices: a whole 2x2x4 slice. The times are simulated.
32 devices in a mesh: pair: 2 (over y), tm: 16 (over z, x, core).
Axes of the slice: x: 2, y: 2, z: 4, core: 2. Of those that a mesh axis runs over, the one named last changes fastest.
Arguments:
- fields: float32 [2, 16, 256, 256], P('pair', 'tm'), may hold values from -4 to 4
- forcing: float32 [2, 16, 256, 256], P('pair', 'tm'), may hold values from -4 to 4.3
- diffusion: float32 [256, 256], replicated, may hold values from 0.5 to 2
- reaction: float32 [256, 256], replicated, may hold values from 0.02 to 0.2
- wrap_factor: float32 [1], replicated, may hold values from 0.05 to 0.4
- mean_diffusion: float32 [1], replicated, may hold values from 0.8 to 1.25
- spectral_shift: float32 [1], replicated, may hold values from 0.05 to 1
Outputs:
- updated: float32 [2, 16, 256, 256], P('pair', 'tm')
All inputs are finite; a program needn't handle non-finite values.
Results may differ from a plain program's by a relative error of at most 0.0003.
Values sent between devices are 32-bit elements; how exact they have to be, the bound alone decides.
No kernel may reach another device: no remote copies, remote signals or barrier semaphores. Data moves between devices by JAX's collectives and lax.ppermute only.
A program may use at most 64 MiB of HBM per device.

v0:
```python
import functools

import jax
import jax.numpy as jnp
import ml_dtypes
import numpy as np
from jax import lax
from jax.experimental import pallas as pl
from jax.experimental.pallas import tpu as pltpu
from jax.sharding import PartitionSpec as P

gamma_inv = 0.5
AXES = ("pair", "tm")


def cas_table(length):
    places = np.arange(length)
    angles = (places[:, None] * places[None, :] % length) * (2.0 * np.pi / length)
    table = np.cos(angles) + np.sin(angles)
    high = table.astype(ml_dtypes.bfloat16)
    low = (table - high.astype(np.float64)).astype(ml_dtypes.bfloat16)
    return jnp.asarray(high), jnp.asarray(low)


def split(values):
    high = values.astype(jnp.bfloat16)
    return high, (values - high.astype(jnp.float32)).astype(jnp.bfloat16)


def product(left, right, left_dim, right_dim):
    dims = (((left_dim,), (right_dim,)), ((), ()))

    def one(a, b):
        return lax.dot_general(a, b, dims, preferred_element_type=jnp.float32)

    return one(left[0], right[0]) + (one(left[0], right[1]) + one(left[1], right[0]))


def roll(values, shift, axis):
    return pltpu.roll(values, shift % values.shape[axis], axis)


def first_kernel(
    mean_ref, shift_ref, alpha_ref, pair_ref,
    own_ref, partner_ref, wrap_ref, source_ref, diffusion_ref, reaction_ref, high_ref, low_ref,
    out_ref,
):
    mean, shift, alpha = mean_ref[0], shift_ref[0], alpha_ref[0]
    cells = diffusion_ref[...]
    own, partner, reaction = own_ref[...], partner_ref[...], reaction_ref[...]
    east = 0.5 * (cells + roll(cells, -1, 0)) - mean
    north = 0.5 * (cells + roll(cells, -1, 1)) - mean
    flux_x = east * (roll(own, -1, 0) - own)
    flux_y = north * (roll(own, -1, 1) - own)
    spread = flux_x - roll(flux_x, 1, 0) + flux_y - roll(flux_y, 1, 1)
    adjoint = pair_ref[0] == 1
    state_coupling = reaction * own * own * own + gamma_inv * partner
    adjoint_coupling = 3.0 * reaction * partner * partner * own - partner
    coupling = jnp.where(adjoint, adjoint_coupling, state_coupling)
    side = source_ref[...] + (spread + shift * own - coupling) - alpha * wrap_ref[...]
    out_ref[...] = product((high_ref[...], low_ref[...]), split(side), 1, 1)


def solve_steps(rows, total, scale, rate, alpha, last_ref, work_ref, keep_ref):
    power = rate
    for _ in range(total - 1):
        power = power * rate
    gain = alpha / (1.0 - alpha * power)
    for group in range(2):
        order = range(total) if group == 0 else range(total - 1, -1, -1)
        places = [slice((group * total + step) * rows, (group * total + step + 1) * rows) for step in order]
        value = jnp.zeros_like(rate)
        for place in places:
            scaled = work_ref[place, :] * scale
            work_ref[place, :] = scaled
            value = rate * (value + scaled)
        if last_ref is not None:
            value = value - last_ref[group * rows : (group + 1) * rows, :]
        value = gain * value
        for place in places:
            value = rate * (value + work_ref[place, :])
            work_ref[place, :] = value
        if keep_ref is not None:
            keep_ref[group * rows : (group + 1) * rows, :] = value


def middle_kernel(rows, total, scale, alpha_ref, in_ref, rate_ref, high_ref, low_ref, out_ref, keep_ref, work_ref):
    table = (high_ref[...], low_ref[...])
    work_ref[...] = product(split(in_ref[...]), table, 1, 0)
    solve_steps(rows, total, scale, rate_ref[...], alpha_ref[0], None, work_ref, keep_ref)
    fields = product(split(work_ref[...]), table, 1, 0)
    band = rows * total
    half = fields.shape[1] // 2
    lane = lax.broadcasted_iota(jnp.int32, (band, half), 1)
    ends = (lane == 0) | (lane == half - 1)
    for side in range(2):
        inner = slice(side * half, (side + 1) * half)
        other = slice((1 - side) * half, (2 - side) * half)
        place = slice(side * band, (side + 1) * band)
        out_ref[place, :half] = fields[:band, inner]
        out_ref[place, half : 2 * half] = fields[band:, inner]
        out_ref[place, 2 * half :] = jnp.where(ends, fields[:band, other], roll(fields[band:, other], half // 2, 1))


def second_kernel(
    mean_ref, shift_ref, pair_ref,
    in_ref, source_ref, other_source_ref, diffusion_ref, reaction_ref, high_ref, low_ref,
    out_ref,
):
    mean, shift, place = mean_ref[0], shift_ref[0], pair_ref[0]
    table = (high_ref[...], low_ref[...])
    fields = product(split(in_ref[...]), table, 0, 0)
    half = fields.shape[0] // 3
    inner = pl.ds(pl.multiple_of(place * half, half), half)
    outer = pl.ds(pl.multiple_of((1 - place) * half, half), half)
    cells, others = diffusion_ref[inner, :], diffusion_ref[outer, :]
    reaction = reaction_ref[inner, :]
    row = lax.broadcasted_iota(jnp.int32, cells.shape, 0)
    top, bottom = row == 0, row == half - 1

    def after(values, beyond):
        return jnp.where(bottom, beyond, roll(values, -1, 0))

    def before(values, beyond):
        return jnp.where(top, beyond, roll(values, 1, 0))

    east = 0.5 * (cells + after(cells, others[0:1])) - mean
    west = 0.5 * (cells + before(cells, others[half - 1 : half])) - mean
    north = 0.5 * (cells + roll(cells, -1, 1)) - mean

    def linear(values, following, preceding):
        flux_y = north * (roll(values, -1, 1) - values)
        flux_x = east * (after(values, following) - values) - west * (values - before(values, preceding))
        return flux_x + flux_y - roll(flux_y, 1, 1) + shift * values

    state, adjoint = fields[:half], fields[half : 2 * half]
    beside = fields[2 * half :]
    middle = half // 2
    own_source, other_source = source_ref[inner, :], other_source_ref[...]
    state_source = jnp.where(place == 0, own_source, other_source)
    adjoint_source = jnp.where(place == 0, other_source, own_source)
    cube = reaction * state * state
    state_side = (
        state_source + linear(state, beside[0:1], beside[half - 1 : half]) - (cube * state + gamma_inv * adjoint)
    )
    adjoint_side = (
        adjoint_source
        + linear(adjoint, beside[middle : middle + 1], beside[middle - 1 : middle])
        - (3.0 * cube * adjoint - state)
    )
    sides = jnp.concatenate([state_side, adjoint_side], 0)
    out_ref[...] = product(table, split(sides), 1, 1)


def final_kernel(rows, total, scale, alpha_ref, in_ref, rate_ref, last_ref, high_ref, low_ref, out_ref, work_ref):
    table = (high_ref[...], low_ref[...])
    band = rows * total
    half = in_ref.shape[1] // 2
    joined = [
        jnp.concatenate([in_ref[:band, part], in_ref[band:, part]], 1)
        for part in (slice(0, half), slice(half, 2 * half))
    ]
    work_ref[...] = product(split(jnp.concatenate(joined, 0)), table, 1, 0)
    solve_steps(rows, total, scale, rate_ref[...], alpha_ref[0], last_ref, work_ref, None)
    out_ref[...] = product(split(work_ref[...]), table, 1, 0)


def close_kernel(in_ref, high_ref, low_ref, out_ref):
    out_ref[...] = product(split(in_ref[...]), (high_ref[...], low_ref[...]), 0, 0)


def call(kernel, scalars, arrays, out_shapes, scratch=()):
    spec_scalar = pl.BlockSpec(memory_space=pltpu.SMEM)
    spec_array = pl.BlockSpec(memory_space=pltpu.VMEM)
    return pl.pallas_call(
        kernel,
        out_shape=[jax.ShapeDtypeStruct(shape, jnp.float32) for shape in out_shapes],
        in_specs=[spec_scalar] * len(scalars) + [spec_array] * len(arrays),
        out_specs=[spec_array] * len(out_shapes),
        scratch_shapes=[pltpu.VMEM(shape, jnp.float32) for shape in scratch],
        compiler_params=pltpu.CompilerParams(vmem_limit_bytes=16 * 1024 * 1024),
    )(*scalars, *arrays)


def on_device(fields, forcing, diffusion, reaction, wrap_factor, mean_diffusion, spectral_shift):
    total = lax.axis_size("tm")
    place = lax.axis_index("pair")
    own, source = fields[0, 0], forcing[0, 0]
    grid_x, grid_y = own.shape
    half = grid_x // 2
    rows = grid_y // (2 * total)
    scale = 1.0 / (grid_x * grid_y)
    x_table, y_table = cas_table(grid_x), cas_table(grid_y)
    pair_flag = place.astype(jnp.int32).reshape(1)

    partner = lax.ppermute(own, "pair", [(0, 1), (1, 0)])
    wrap = lax.ppermute(own, AXES, [(total - 1, 0), (total, 2 * total - 1)])
    sent_source = lax.dynamic_slice_in_dim(source, (1 - place) * half, half, 0)
    other_source = lax.ppermute(sent_source, "pair", [(0, 1), (1, 0)])

    eigen_x = jnp.asarray((4.0 * np.sin(np.arange(grid_x) * (np.pi / grid_x)) ** 2).astype(np.float32))
    eigen_y = jnp.asarray((4.0 * np.sin(np.arange(grid_y) * (np.pi / grid_y)) ** 2).astype(np.float32))
    device = place * total + lax.axis_index("tm")
    eigen_y = lax.dynamic_slice_in_dim(eigen_y, device * rows, rows, 0)
    rate = 1.0 / (1.0 + spectral_shift + mean_diffusion * (eigen_y[:, None] + eigen_x[None, :]))

    def exchange(values):
        return lax.all_to_all(values, AXES, 0, 0, tiled=True)

    (sides,) = call(
        first_kernel,
        (mean_diffusion, spectral_shift, wrap_factor, pair_flag),
        (own, partner, wrap, source, diffusion, reaction, *y_table),
        [(grid_y, grid_x)],
    )
    halves, last = call(
        functools.partial(middle_kernel, rows, total, scale),
        (wrap_factor,),
        (exchange(sides), rate, *x_table),
        [(grid_y, 3 * half), (2 * rows, grid_x)],
        [(grid_y, grid_x)],
    )
    (sides,) = call(
        second_kernel,
        (mean_diffusion, spectral_shift, pair_flag),
        (exchange(halves), source, other_source, diffusion, reaction, *y_table),
        [(grid_y, grid_x)],
    )
    (wholes,) = call(
        functools.partial(final_kernel, rows, total, scale),
        (wrap_factor,),
        (exchange(sides), rate, last, *x_table),
        [(grid_y, grid_x)],
        [(grid_y, grid_x)],
    )
    (updated,) = call(close_kernel, (), (exchange(wholes), *y_table), [(grid_x, grid_y)])
    return updated[None, None]


def solution(mesh):
    in_specs = (P("pair", "tm", None, None), P("pair", "tm", None, None), P(), P(), P(), P(), P())
    out_specs = P("pair", "tm", None, None)
    return jax.shard_map(
        on_device, mesh=mesh, in_specs=in_specs, out_specs=out_specs, check_vma=False
    )
```

profile of v0, /device:TPU:0, one launch (start us, length us, event | category | flops | bytes accessed | tf_op | source)
XLA Modules:
  0.0 79.8 jit_solution(11828571282010507009)
XLA Ops:
  0.0 3.0 %collective-permute-start = (f32[256,256]{1,0:T(8,128)}, f32[256,256]{1,0:T(8,128)S(1)}, u32[]{:S(2)}, u32[]{:S(2)}) collective-permute-start(f32[256,256]{1,0:T(8,128)} %bitcast.25), channel_id=1, source_target_pairs={{0,16},{16,0},{1,17},{17,1},{2,18},{18,2},{3,19},{19,3},{4,20},{20... | collective-permute-start | bytes 786440 | tf_op jit(solution)/shard_map/ppermute | solution.py:196
  3.0 1.3 %collective-permute-start.1 = (f32[256,256]{1,0:T(8,128)}, f32[256,256]{1,0:T(8,128)S(1)}, u32[]{:S(2)}, u32[]{:S(2)}) collective-permute-start(f32[256,256]{1,0:T(8,128)} %bitcast.26), channel_id=1, source_target_pairs={{15,0},{16,31}} | collective-permute-start | bytes 786440 | tf_op jit(solution)/shard_map/ppermute | solution.py:197
  6.2 3.3 %collective-permute-done.partner_ref = f32[256,256]{1,0:T(8,128)S(1)} collective-permute-done((f32[256,256]{1,0:T(8,128)}, f32[256,256]{1,0:T(8,128)S(1)}, u32[]{:S(2)}, u32[]{:S(2)}) %collective-permute-start) | collective-permute-done | bytes 262176 | tf_op jit(solution)/shard_map/ppermute | solution.py:196
  9.5 4.1 %collective-permute-done.1.wrap_ref = f32[256,256]{1,0:T(8,128)S(1)} collective-permute-done((f32[256,256]{1,0:T(8,128)}, f32[256,256]{1,0:T(8,128)S(1)}, u32[]{:S(2)}, u32[]{:S(2)}) %collective-permute-start.1) | collective-permute-done | bytes 262176 | tf_op jit(solution)/shard_map/ppermute | solution.py:197
  13.6 0.9 %copy-done = bf16[256,256]{1,0:T(8,128)(2,1)S(1)} copy-done((bf16[256,256]{1,0:T(8,128)(2,1)S(1)}, bf16[256,256]{1,0:T(8,128)(2,1)}, u32[]{:S(2)}) %copy-start) | copy-done | bytes 131096
  14.5 0.9 %copy-done.2 = bf16[256,256]{1,0:T(8,128)(2,1)S(1)} copy-done((bf16[256,256]{1,0:T(8,128)(2,1)S(1)}, bf16[256,256]{1,0:T(8,128)(2,1)}, u32[]{:S(2)}) %copy-start.2) | copy-done | bytes 131096
  15.4 0.9 %copy-done.4 = f32[1,1,256,256]{3,2,1,0:T(8,128)S(1)} copy-done((f32[1,1,256,256]{3,2,1,0:T(8,128)S(1)}, f32[1,1,256,256]{3,2,1,0:T(8,128)}, u32[]{:S(2)}) %copy-start.4) | copy-done | bytes 262168
  16.3 0.9 %copy-done.6 = f32[256,256]{1,0:T(8,128)S(1)} copy-done((f32[256,256]{1,0:T(8,128)S(1)}, f32[256,256]{1,0:T(8,128)}, u32[]{:S(2)}) %copy-start.6) | copy-done | bytes 262168
  17.3 0.9 %copy-done.8 = f32[256,256]{1,0:T(8,128)S(1)} copy-done((f32[256,256]{1,0:T(8,128)S(1)}, f32[256,256]{1,0:T(8,128)}, u32[]{:S(2)}) %copy-start.8) | copy-done | bytes 262168
  18.2 0.9 %copy-done.10 = f32[1,1,256,256]{3,2,1,0:T(8,128)S(1)} copy-done((f32[1,1,256,256]{3,2,1,0:T(8,128)S(1)}, f32[1,1,256,256]{3,2,1,0:T(8,128)}, u32[]{:S(2)}) %copy-start.10) | copy-done | bytes 262168
  19.2 1.4 %shard_map.127 = f32[256,256]{1,0:T(8,128)} custom-call(f32[1]{0:T(128)} %copy.15.mean_ref, f32[1]{0:T(128)S(6)} %copy.16.shift_ref, f32[1]{0:T(128)S(6)} %copy.14.alpha_ref, s32[1]{0:T(128)} %bitcast.pair_ref, f32[256,256]{1,0:T(8,128)S(1)} %bitcast.27, f32[256,256]{1,0:T(8,128)S(1)} %collective-permute-done.partner_ref, ...), custom_call_target="tpu_custom_call" | custom-call | tf_op jit(solution)/shard_map/pallas_call | solution.py:175
  20.5 4.0 %all-to-all-start = ((f32[32,8,256]{2,1,0:T(8,128)}), f32[32,8,256]{2,1,0:T(8,128)S(1)}, u32[]{:S(2)}, u32[]{:S(2)}) async-start(f32[32,8,256]{2,1,0:T(8,128)} %bitcast.3), calls=%async_computation | async-start | bytes 524288 | tf_op jit(solution)/shard_map/all_to_all | solution.py:208
  24.5 0.0 copy-start.11
  24.6 0.7 copy-done.11
  25.2 0.1 dynamic_slice.8
  25.3 0.1 add_divide_fusion.rate_ref
  25.4 9.5 %all-to-all-done = f32[32,8,256]{2,1,0:T(8,128)S(1)} async-done(((f32[32,8,256]{2,1,0:T(8,128)}), f32[32,8,256]{2,1,0:T(8,128)S(1)}, u32[]{:S(2)}, u32[]{:S(2)}) %all-to-all-start) | async-done | bytes 262176 | tf_op jit(solution)/shard_map/all_to_all | solution.py:208
  34.8 0.0 copy-done.1
  34.8 0.0 copy-done.3
  34.8 1.5 %shard_map.128 = (f32[256,384]{1,0:T(8,128)}, f32[16,256]{1,0:T(8,128)S(1)}) custom-call(f32[1]{0:T(128)S(6)} %copy.14.alpha_ref, f32[256,256]{1,0:T(8,128)S(1)} %bitcast.21, f32[8,256]{1,0:T(8,128)S(1)} %add_divide_fusion.rate_ref, bf16[256,256]{1,0:T(8,128)(2,1)S(1)} %copy-done.1, bf16[256,256]{1,0:T(8,128)(2,1)S(1)} %copy-done.3), custom_call_target="tpu_custom_call" | custom-call | tf_op jit(solution)/shard_map/pallas_call | solution.py:175
  36.4 2.7 %all-to-all-start.1 = ((f32[32,8,384]{2,1,0:T(8,128)}), f32[32,8,384]{2,1,0:T(8,128)S(1)}, u32[]{:S(2)}, u32[]{:S(2)}) async-start(f32[32,8,384]{2,1,0:T(8,128)} %bitcast.7), calls=%async_computation.1 | async-start | bytes 786432 | tf_op jit(solution)/shard_map/all_to_all | solution.py:208
  39.1 0.0 copy-start.7
  39.1 0.0 copy-done.5
  39.2 1.7 %collective-permute-start.2 = (f32[128,256]{1,0:T(8,128)S(1)}, f32[128,256]{1,0:T(8,128)S(1)}, u32[]{:S(2)}, u32[]{:S(2)}) collective-permute-start(f32[128,256]{1,0:T(8,128)S(1)} %dynamic-slice_bitcast_fusion), channel_id=1, source_target_pairs={{0,16},{16,0},{1,17},{17,1},{2,18},{18,2},{3,19},{19,3},{4,20},{20... | collective-permute-start | bytes 393224 | tf_op jit(solution)/shard_map/ppermute | solution.py:199
  40.9 6.8 %collective-permute-done.2.other_source_ref = f32[128,256]{1,0:T(8,128)S(1)} collective-permute-done((f32[128,256]{1,0:T(8,128)S(1)}, f32[128,256]{1,0:T(8,128)S(1)}, u32[]{:S(2)}, u32[]{:S(2)}) %collective-permute-start.2) | collective-permute-done | bytes 131104 | tf_op jit(solution)/shard_map/ppermute | solution.py:199
  47.6 4.6 %all-to-all-done.1 = f32[32,8,384]{2,1,0:T(8,128)S(1)} async-done(((f32[32,8,384]{2,1,0:T(8,128)}), f32[32,8,384]{2,1,0:T(8,128)S(1)}, u32[]{:S(2)}, u32[]{:S(2)}) %all-to-all-start.1) | async-done | bytes 393248 | tf_op jit(solution)/shard_map/all_to_all | solution.py:208
  52.2 0.0 copy-done.7
  52.2 0.9 %shard_map.129 = f32[256,256]{1,0:T(8,128)S(1)} custom-call(f32[1]{0:T(128)} %copy.15.mean_ref, f32[1]{0:T(128)S(6)} %copy.16.shift_ref, s32[1]{0:T(128)} %bitcast.pair_ref, f32[256,384]{1,0:T(8,128)S(1)} %bitcast.19, f32[256,256]{1,0:T(8,128)S(1)} %bitcast.18, f32[128,256]{1,0:T(8,128)S(1)} %collective-permute-done.2.other_source_ref, ...), custom_call_target="tpu_custom_call" | custom-call | tf_op jit(solution)/shard_map/pallas_call | solution.py:175
  53.1 12.3 %all_to_all.44 = f32[32,8,256]{2,1,0:T(8,128)S(1)} all-to-all(f32[32,8,256]{2,1,0:T(8,128)S(1)} %bitcast.24), channel_id=1, replica_groups=mesh['pair'=2,'tm'=16] {'pair','tm'}, dimensions={0} | all-to-all | bytes 524288 | tf_op jit(solution)/shard_map/all_to_all | solution.py:208
  65.4 0.7 shard_map.130
  66.2 12.6 %all_to_all.45 = f32[32,8,256]{2,1,0:T(8,128)S(1)} all-to-all(f32[32,8,256]{2,1,0:T(8,128)S(1)} %bitcast.23), channel_id=1, replica_groups=mesh['pair'=2,'tm'=16] {'pair','tm'}, dimensions={0} | all-to-all | bytes 524288 | tf_op jit(solution)/shard_map/all_to_all | solution.py:208
  78.8 1.0 %shard_map.131 = f32[256,256]{1,0:T(8,128)} custom-call(f32[256,256]{1,0:T(8,128)S(1)} %bitcast.20, bf16[256,256]{1,0:T(8,128)(2,1)S(1)} %copy-done.1, bf16[256,256]{1,0:T(8,128)(2,1)S(1)} %copy-done.3), custom_call_target="tpu_custom_call" | custom-call | tf_op jit(solution)/shard_map/pallas_call | solution.py:175
  (12 shorter events, 0.0 us)
Async XLA Ops:
  0.0 9.5 %collective-permute-start = (f32[256,256]{1,0:T(8,128)}, f32[256,256]{1,0:T(8,128)S(1)}, u32[]{:S(2)}, u32[]{:S(2)}) collective-permute-start(f32[256,256]{1,0:T(8,128)} %bitcast.25), channel_id=1, source_target_pairs={{0,16},{16,0},{1,17},{17,1},{2,18},{18,2},{3,19},{19,3},{4,20},{20... | collective-permute-start | bytes 786440 | tf_op jit(solution)/shard_map/ppermute | solution.py:196
  3.0 10.6 %collective-permute-start.1 = (f32[256,256]{1,0:T(8,128)}, f32[256,256]{1,0:T(8,128)S(1)}, u32[]{:S(2)}, u32[]{:S(2)}) collective-permute-start(f32[256,256]{1,0:T(8,128)} %bitcast.26), channel_id=1, source_target_pairs={{15,0},{16,31}} | collective-permute-start | bytes 786440 | tf_op jit(solution)/shard_map/ppermute | solution.py:197
  13.6 0.9 %copy-start = (bf16[256,256]{1,0:T(8,128)(2,1)S(1)}, bf16[256,256]{1,0:T(8,128)(2,1)}, u32[]{:S(2)}) copy-start(bf16[256,256]{1,0:T(8,128)(2,1)} %constant.32.clone.high_ref) | copy-start | bytes 393220
  14.5 0.9 %copy-start.2 = (bf16[256,256]{1,0:T(8,128)(2,1)S(1)}, bf16[256,256]{1,0:T(8,128)(2,1)}, u32[]{:S(2)}) copy-start(bf16[256,256]{1,0:T(8,128)(2,1)} %constant.33.clone.low_ref) | copy-start | bytes 393220
  15.4 0.9 %copy-start.4 = (f32[1,1,256,256]{3,2,1,0:T(8,128)S(1)}, f32[1,1,256,256]{3,2,1,0:T(8,128)}, u32[]{:S(2)}) copy-start(f32[1,1,256,256]{3,2,1,0:T(8,128)} %param.14) | copy-start | bytes 786436
  16.3 0.9 %copy-start.6 = (f32[256,256]{1,0:T(8,128)S(1)}, f32[256,256]{1,0:T(8,128)}, u32[]{:S(2)}) copy-start(f32[256,256]{1,0:T(8,128)} %diffusion_ref.3) | copy-start | bytes 786436
  17.3 0.9 %copy-start.8 = (f32[256,256]{1,0:T(8,128)S(1)}, f32[256,256]{1,0:T(8,128)}, u32[]{:S(2)}) copy-start(f32[256,256]{1,0:T(8,128)} %reaction_ref.3) | copy-start | bytes 786436
  18.2 0.9 %copy-start.10 = (f32[1,1,256,256]{3,2,1,0:T(8,128)S(1)}, f32[1,1,256,256]{3,2,1,0:T(8,128)}, u32[]{:S(2)}) copy-start(f32[1,1,256,256]{3,2,1,0:T(8,128)} %param.13) | copy-start | bytes 786436
  20.5 14.3 %copy-start.1 = (bf16[256,256]{1,0:T(8,128)(2,1)S(1)}, bf16[256,256]{1,0:T(8,128)(2,1)}, u32[]{:S(2)}) copy-start(bf16[256,256]{1,0:T(8,128)(2,1)} %constant.32.clone.high_ref) | copy-start | bytes 393220
  20.5 14.3 %copy-start.3 = (bf16[256,256]{1,0:T(8,128)(2,1)S(1)}, bf16[256,256]{1,0:T(8,128)(2,1)}, u32[]{:S(2)}) copy-start(bf16[256,256]{1,0:T(8,128)(2,1)} %constant.33.clone.low_ref) | copy-start | bytes 393220
  20.5 14.3 %all-to-all-start = ((f32[32,8,256]{2,1,0:T(8,128)}), f32[32,8,256]{2,1,0:T(8,128)S(1)}, u32[]{:S(2)}, u32[]{:S(2)}) async-start(f32[32,8,256]{2,1,0:T(8,128)} %bitcast.3), calls=%async_computation | async-start | bytes 524288 | tf_op jit(solution)/shard_map/all_to_all | solution.py:208
  24.5 0.7 copy-start.11
  36.4 2.8 %copy-start.5 = (f32[1,1,256,256]{3,2,1,0:T(8,128)S(1)}, f32[1,1,256,256]{3,2,1,0:T(8,128)}, u32[]{:S(2)}) copy-start(f32[1,1,256,256]{3,2,1,0:T(8,128)} %param.14) | copy-start | bytes 786436
  36.4 15.8 %copy-start.9 = (f32[256,256]{1,0:T(8,128)S(1)}, f32[256,256]{1,0:T(8,128)}, u32[]{:S(2)}) copy-start(f32[256,256]{1,0:T(8,128)} %reaction_ref.3) | copy-start | bytes 786436
  36.4 15.8 %all-to-all-start.1 = ((f32[32,8,384]{2,1,0:T(8,128)}), f32[32,8,384]{2,1,0:T(8,128)S(1)}, u32[]{:S(2)}, u32[]{:S(2)}) async-start(f32[32,8,384]{2,1,0:T(8,128)} %bitcast.7), calls=%async_computation.1 | async-start | bytes 786432 | tf_op jit(solution)/shard_map/all_to_all | solution.py:208
  39.1 13.1 %copy-start.7 = (f32[256,256]{1,0:T(8,128)S(1)}, f32[256,256]{1,0:T(8,128)}, u32[]{:S(2)}) copy-start(f32[256,256]{1,0:T(8,128)} %diffusion_ref.3) | copy-start | bytes 786436
  39.2 8.5 %collective-permute-start.2 = (f32[128,256]{1,0:T(8,128)S(1)}, f32[128,256]{1,0:T(8,128)S(1)}, u32[]{:S(2)}, u32[]{:S(2)}) collective-permute-start(f32[128,256]{1,0:T(8,128)S(1)} %dynamic-slice_bitcast_fusion), channel_id=1, source_target_pairs={{0,16},{16,0},{1,17},{17,1},{2,18},{18,2},{3,19},{19,3},{4,20},{20... | collective-permute-start | bytes 393224 | tf_op jit(solution)/shard_map/ppermute | solution.py:199
where the time goes:
time: 80.3 us; the launch traced here: 79.8 us
  waiting for transfers between devices  28.1 us (35%)
  blocking collectives  25 us (31%)
  starting transfers between devices  12.7 us (16%)
  local copies, waits for them, and re-layouts  6.39 us (8%)
  Pallas kernels  5.5 us (7%)
  between operations  2.04 us (3%)
    all_to_all x2, blocking collectives, exchange(): return lax.all_to_all(values, AXES, 0, 0, tiled=True)  25 us
    all_to_all x2, waiting for transfers between devices, exchange(): return lax.all_to_all(values, AXES, 0, 0, tiled=True)  14 us
    ppermute x1, waiting for transfers between devices, on_device(): other_source = lax.ppermute(sent_source, 'pair', [(0, 1), (1, 0)])  6.75 us
    all_to_all x2, starting transfers between devices, exchange(): return lax.all_to_all(values, AXES, 0, 0, tiled=True)  6.72 us
    unnamed x24, local copies, waits for them, and re-layouts  6.3 us
    pallas_call x5, Pallas kernels, call(): pl.pallas_call(kernel, out_shape=[jax.ShapeDtypeStruct(shape, jnp.float32...  5.5 us
    ppermute x1, waiting for transfers between devices, on_device(): wrap = lax.ppermute(own, AXES, [(total - 1, 0), (total, 2 * total - 1)])  4.07 us
    ppermute x1, waiting for transfers between devices, on_device(): partner = lax.ppermute(own, 'pair', [(0, 1), (1, 0)])  3.28 us
  transfers between devices with their start and end apart: 5, of which 5 were waited for; matrix products, arithmetic and copies ran while one was open for 0% of the time, Pallas kernels for 0%

commit v1 on v0

v1 whole, which is shorter than its diff:
```python
import functools
import math

import jax
import jax.numpy as jnp
import ml_dtypes
import numpy as np
from jax import lax
from jax.experimental import pallas as pl
from jax.experimental.pallas import tpu as pltpu
from jax.sharding import PartitionSpec as P

gamma_inv = 0.5
AXES = ("pair", "tm")


def cas_table(length):
    places = np.arange(length)
    angles = (places[:, None] * places[None, :] % length) * (2.0 * np.pi / length)
    table = np.cos(angles) + np.sin(angles)
    high = table.astype(ml_dtypes.bfloat16)
    low = (table - high.astype(np.float64)).astype(ml_dtypes.bfloat16)
    return jnp.asarray(np.stack([high, low]))


def split(values):
    high = values.astype(jnp.bfloat16)
    return high, (values - high.astype(jnp.float32)).astype(jnp.bfloat16)


def product(left, right, left_dim, right_dim):
    dims = (((left_dim,), (right_dim,)), ((), ()))

    def one(a, b):
        return lax.dot_general(a, b, dims, preferred_element_type=jnp.float32)

    return one(left[0], right[0]) + (one(left[0], right[1]) + one(left[1], right[0]))


def roll(values, shift, axis):
    return pltpu.roll(values, shift % values.shape[axis], axis)


def coefficients(mean, shift, last):
    return jnp.where(last, 0.0, mean), jnp.where(last, -1.0, shift)


def own_kernel(
    total, rows,
    mean_ref, shift_ref, pair_ref, step_ref,
    own_ref, source_ref, diffusion_ref, reaction_ref, table_ref,
    side_ref, rate_ref,
):
    adjoint = pair_ref[0] == 1
    last = step_ref[0] == jnp.where(adjoint, 0, total - 1)
    mean, shift = coefficients(mean_ref[0], shift_ref[0], last)
    cells, own = diffusion_ref[...], own_ref[...]
    east = 0.5 * (cells + roll(cells, -1, 0)) - mean
    north = 0.5 * (cells + roll(cells, -1, 1)) - mean
    flux_x = east * (roll(own, -1, 0) - own)
    flux_y = north * (roll(own, -1, 1) - own)
    spread = flux_x - roll(flux_x, 1, 0) + flux_y - roll(flux_y, 1, 1)
    cube = jnp.where(adjoint, 0.0, 1.0) * (reaction_ref[...] * own * own * own)
    side_ref[...] = source_ref[...] + (spread + shift * own - cube)
    shape = rate_ref.shape
    band = (pair_ref[0] * total + step_ref[0]) * rows
    row_ids = band + lax.broadcasted_iota(jnp.int32, shape, 0)
    col_ids = lax.broadcasted_iota(jnp.int32, shape, 1)
    sine_rows = jnp.sin(row_ids.astype(jnp.float32) * (math.pi / own.shape[1]))
    sine_cols = jnp.sin(col_ids.astype(jnp.float32) * (math.pi / own.shape[0]))
    eigen = 4.0 * sine_rows * sine_rows + 4.0 * sine_cols * sine_cols
    rate_ref[...] = 1.0 / (1.0 + shift_ref[0] + mean_ref[0] * eigen)


def first_kernel(pair_ref, side_ref, own_ref, partner_ref, reaction_ref, table_ref, out_ref):
    partner = partner_ref[...]
    adjoint_part = 3.0 * reaction_ref[...] * partner * partner * own_ref[...] - partner
    side = side_ref[...] - jnp.where(pair_ref[0] == 1, adjoint_part, gamma_inv * partner)
    out_ref[...] = product(halves_of(table_ref), split(side), 1, 1)


def halves_of(table_ref):
    return table_ref[0], table_ref[1]


def step_places(group, total, rows):
    order = range(total) if group == 0 else range(total - 1, -1, -1)
    return [slice((group * total + step) * rows, (group * total + step + 1) * rows) for step in order]


def solve_steps(rows, total, rate, alpha, work_ref):
    power = rate
    for _ in range(total - 1):
        power = power * rate
    gain = alpha / (1.0 - alpha * power)
    for group in range(2):
        places = step_places(group, total, rows)
        value = jnp.zeros_like(rate)
        for place in places:
            value = rate * (value + work_ref[place, :])
        value = gain * value
        for place in places:
            value = rate * (value + work_ref[place, :])
            work_ref[place, :] = value


def middle_kernel(rows, total, scale, alpha_ref, in_ref, rate_ref, table_ref, out_ref, side_ref, last_ref, work_ref):
    table = halves_of(table_ref)
    sides = product(split(in_ref[...]), table, 1, 0) * scale
    side_ref[...] = sides
    work_ref[...] = sides
    solve_steps(rows, total, rate_ref[...], alpha_ref[0], work_ref)
    for group in range(2):
        last_ref[group * rows : (group + 1) * rows, :] = work_ref[step_places(group, total, rows)[-1], :]
    fields = product(split(work_ref[...]), table, 1, 0)
    band = rows * total
    half = fields.shape[1] // 2
    lane = lax.broadcasted_iota(jnp.int32, (band, half), 1)
    ends = (lane == 0) | (lane == half - 1)
    for side in range(2):
        inner = slice(side * half, (side + 1) * half)
        other = slice((1 - side) * half, (2 - side) * half)
        place = slice(side * band, (side + 1) * band)
        out_ref[place, :half] = fields[:band, inner]
        out_ref[place, half : 2 * half] = fields[band:, inner]
        out_ref[place, 2 * half :] = jnp.where(ends, fields[:band, other], roll(fields[band:, other], half // 2, 1))


def second_kernel(
    total,
    mean_ref, shift_ref, pair_ref, step_ref,
    in_ref, own_ref, partner_ref, diffusion_ref, reaction_ref, table_ref,
    out_ref,
):
    place, step = pair_ref[0], step_ref[0]
    table = halves_of(table_ref)
    solved = product(split(in_ref[...]), table, 0, 0)
    half = solved.shape[0] // 3
    middle = half // 2
    inner = pl.ds(pl.multiple_of(place * half, half), half)
    outer = pl.ds(pl.multiple_of((1 - place) * half, half), half)
    cells, others = diffusion_ref[inner, :], diffusion_ref[outer, :]
    reaction = reaction_ref[inner, :]
    row = lax.broadcasted_iota(jnp.int32, cells.shape, 0)
    top, bottom = row == 0, row == half - 1

    def after(values, beyond):
        return jnp.where(bottom, beyond, roll(values, -1, 0))

    def before(values, beyond):
        return jnp.where(top, beyond, roll(values, 1, 0))

    east = 0.5 * (cells + after(cells, others[0:1]))
    west = 0.5 * (cells + before(cells, others[half - 1 : half]))
    north = 0.5 * (cells + roll(cells, -1, 1))

    def linear(values, following, preceding, last):
        mean, shift = coefficients(mean_ref[0], shift_ref[0], last)
        flux_y = (north - mean) * (roll(values, -1, 1) - values)
        flux_x = (east - mean) * (after(values, following) - values)
        flux_x = flux_x - (west - mean) * (values - before(values, preceding))
        return flux_x + flux_y - roll(flux_y, 1, 1) + shift * values

    def change(group, first_row, last_step):
        own = place == group
        former_here = jnp.where(own, own_ref[inner, :], partner_ref[inner, :])
        former_there = jnp.where(own, own_ref[outer, :], partner_ref[outer, :])
        last = step == last_step
        taken = jnp.where(last, 0.0, 1.0)
        delta = solved[group * half : (group + 1) * half] - taken * former_here
        beside = solved[2 * half :]
        following = beside[first_row : first_row + 1] - taken * former_there[0:1]
        before_row = (first_row - 1) % half
        preceding = beside[before_row : before_row + 1] - taken * former_there[half - 1 : half]
        return former_here, delta, linear(delta, following, preceding, last)

    state, state_delta, state_side = change(0, 0, total - 1)
    adjoint, adjoint_delta, adjoint_side = change(1, middle, 0)
    new_state, new_adjoint = state + state_delta, adjoint + adjoint_delta
    square, new_square = state * state, new_state * new_state
    state_side = state_side - (reaction * (new_square * new_state - square * state) + gamma_inv * adjoint_delta)
    adjoint_side = adjoint_side - (3.0 * reaction * (new_square * new_adjoint - square * adjoint) - state_delta)
    sides = jnp.concatenate([state_side, adjoint_side], 0)
    out_ref[...] = product(table, split(sides), 1, 1)


def final_kernel(rows, total, scale, alpha_ref, in_ref, rate_ref, side_ref, last_ref, table_ref, out_ref, work_ref):
    table = halves_of(table_ref)
    band = rows * total
    half = in_ref.shape[1] // 2
    joined = [
        jnp.concatenate([in_ref[:band, part], in_ref[band:, part]], 1)
        for part in (slice(0, half), slice(half, 2 * half))
    ]
    work_ref[...] = product(split(jnp.concatenate(joined, 0)), table, 1, 0) * scale + side_ref[...]
    solve_steps(rows, total, rate_ref[...], alpha_ref[0], work_ref)
    for group in range(2):
        place = step_places(group, total, rows)[-1]
        work_ref[place, :] = work_ref[place, :] + last_ref[group * rows : (group + 1) * rows, :]
    out_ref[...] = product(split(work_ref[...]), table, 1, 0)


def close_kernel(total, pair_ref, step_ref, in_ref, own_ref, table_ref, out_ref):
    last = step_ref[0] == jnp.where(pair_ref[0] == 1, 0, total - 1)
    kept = jnp.where(last, 1.0, 0.0) * own_ref[...]
    out_ref[...] = kept + product(split(in_ref[...]), halves_of(table_ref), 0, 0)


def call(kernel, scalars, arrays, out_shapes, scratch=()):
    spec_scalar = pl.BlockSpec(memory_space=pltpu.SMEM)
    spec_array = pl.BlockSpec(memory_space=pltpu.VMEM)
    return pl.pallas_call(
        kernel,
        out_shape=[jax.ShapeDtypeStruct(shape, jnp.float32) for shape in out_shapes],
        in_specs=[spec_scalar] * len(scalars) + [spec_array] * len(arrays),
        out_specs=[spec_array] * len(out_shapes),
        scratch_shapes=[pltpu.VMEM(shape, jnp.float32) for shape in scratch],
        compiler_params=pltpu.CompilerParams(vmem_limit_bytes=16 * 1024 * 1024),
    )(*scalars, *arrays)


def on_device(fields, forcing, diffusion, reaction, wrap_factor, mean_diffusion, spectral_shift):
    total = lax.axis_size("tm")
    own, source = fields[0, 0], forcing[0, 0]
    grid_x, grid_y = own.shape
    half = grid_x // 2
    rows = grid_y // (2 * total)
    scale = 1.0 / (grid_x * grid_y)
    x_table, y_table = cas_table(grid_x), cas_table(grid_y)
    pair = lax.axis_index("pair").astype(jnp.int32).reshape(1)
    step = lax.axis_index("tm").astype(jnp.int32).reshape(1)
    grid, band = (grid_x, grid_y), (grid_y, grid_x)

    def exchange(values):
        return lax.all_to_all(values, AXES, 0, 0, tiled=True)

    partner = lax.ppermute(own, "pair", [(0, 1), (1, 0)])
    side, rate = call(
        functools.partial(own_kernel, total, rows),
        (mean_diffusion, spectral_shift, pair, step),
        (own, source, diffusion, reaction, y_table),
        [grid, (rows, grid_x)],
    )
    (sides,) = call(first_kernel, (pair,), (side, own, partner, reaction, y_table), [band])
    halves, kept_side, last = call(
        functools.partial(middle_kernel, rows, total, scale),
        (wrap_factor,),
        (exchange(sides), rate, x_table),
        [(grid_y, 3 * half), band, (2 * rows, grid_x)],
        [band],
    )
    (sides,) = call(
        functools.partial(second_kernel, total),
        (mean_diffusion, spectral_shift, pair, step),
        (exchange(halves), own, partner, diffusion, reaction, y_table),
        [band],
    )
    (wholes,) = call(
        functools.partial(final_kernel, rows, total, scale),
        (wrap_factor,),
        (exchange(sides), rate, kept_side, last, x_table),
        [band],
        [band],
    )
    (updated,) = call(
        functools.partial(close_kernel, total), (pair, step), (exchange(wholes), own, y_table), [grid]
    )
    return updated[None, None]


def solution(mesh):
    in_specs = (P("pair", "tm", None, None), P("pair", "tm", None, None), P(), P(), P(), P(), P())
    out_specs = P("pair", "tm", None, None)
    return jax.shard_map(
        on_device, mesh=mesh, in_specs=in_specs, out_specs=out_specs, check_vma=False
    )
```

time: 80.3 us -> 71.4 us (0.89)
  waiting for transfers between devices: 28.1 us -> 9.68 us
  blocking collectives: 25 us -> 40.5 us
  starting transfers between devices: 12.7 us -> 8.41 us
  local copies, waits for them, and re-layouts: 6.39 us -> 5.4 us
    all_to_all x2 -> x3, blocking collectives: 25 us -> 40.5 us  [exchange(): return lax.all_to_all(values, AXES, 0, 0, tiled=True)]
    ppermute x2 -> x0, waiting for transfers between devices: 10.8 us -> none  [the longest x1 6.75 us: on_device(): other_source = lax.ppermute(sent_source, 'pair', [(0, 1), (1, 0)])]
    all_to_all x2 -> x1, waiting for transfers between devices: 14 us -> 9.65 us  [exchange(): return lax.all_to_all(values, AXES, 0, 0, tiled=True)]
    ppermute x1, waiting for transfers between devices: 3.28 us -> 0.03 us  [on_device(): partner = lax.ppermute(own, 'pair', [(0, 1), (1, 0)])]
    ppermute x2 -> x0, starting transfers between devices: 3 us -> none  [the longest x1 1.72 us: on_device(): other_source = lax.ppermute(sent_source, 'pair', [(0, 1), (1, 0)])]
    all_to_all x2 -> x1, starting transfers between devices: 6.72 us -> 5.44 us  [exchange(): return lax.all_to_all(values, AXES, 0, 0, tiled=True)]
    unnamed x24 -> x18, local copies, waits for them, and re-layouts: 6.3 us -> 5.4 us
    pallas_call x5 -> x6, Pallas kernels: 5.5 us -> 4.95 us  [call(): pl.pallas_call(kernel, out_shape=[jax.ShapeDtypeStruct(shape, jnp.float32...]
  transfers between devices with their start and end apart: 5 -> 2, of which waited for: 5 -> 1; matrix products, arithmetic and copies ran while one was open for 0% -> 0% of each run, Pallas kernels for 0% -> 1%
where the time goes in v1:
time: 71.4 us; the launch traced here: 70.9 us
  blocking collectives  40.5 us (57%)
  waiting for transfers between devices  9.68 us (14%)
  starting transfers between devices  8.41 us (12%)
  local copies, waits for them, and re-layouts  5.4 us (8%)
  Pallas kernels  4.95 us (7%)
  between operations  2.01 us (3%)
    all_to_all x3, blocking collectives, exchange(): return lax.all_to_all(values, AXES, 0, 0, tiled=True)  40.5 us
    all_to_all x1, waiting for transfers between devices, exchange(): return lax.all_to_all(values, AXES, 0, 0, tiled=True)  9.65 us
    all_to_all x1, starting transfers between devices, exchange(): return lax.all_to_all(values, AXES, 0, 0, tiled=True)  5.44 us
    unnamed x18, local copies, waits for them, and re-layouts  5.4 us
    pallas_call x6, Pallas kernels, call(): pl.pallas_call(kernel, out_shape=[jax.ShapeDtypeStruct(shape, jnp.float32...  4.95 us
    ppermute x1, starting transfers between devices, on_device(): partner = lax.ppermute(own, 'pair', [(0, 1), (1, 0)])  2.97 us
  transfers between devices with their start and end apart: 2, of which 1 were waited for; matrix products, arithmetic and copies ran while one was open for 0% of the time, Pallas kernels for 1%

profile of v1, /device:TPU:0, one launch (start us, length us, event | category | flops | bytes accessed | tf_op | source)
XLA Modules:
  0.0 70.9 jit_solution(8625718399556767000)
XLA Ops:
  0.0 3.0 %collective-permute-start = (f32[256,256]{1,0:T(8,128)}, f32[256,256]{1,0:T(8,128)S(1)}, u32[]{:S(2)}, u32[]{:S(2)}) collective-permute-start(f32[256,256]{1,0:T(8,128)} %bitcast.13), channel_id=1, source_target_pairs={{0,16},{16,0},{1,17},{17,1},{2,18},{18,2},{3,19},{19,3},{4,20},{20... | collective-permute-start | bytes 786440 | tf_op jit(solution)/shard_map/ppermute | solution.py:237
  4.3 0.0 copy-start
  4.3 0.9 %copy-done = bf16[2,256,256]{2,1,0:T(8,128)(2,1)S(1)} copy-done((bf16[2,256,256]{2,1,0:T(8,128)(2,1)S(1)}, bf16[2,256,256]{2,1,0:T(8,128)(2,1)}, u32[]{:S(2)}) %copy-start) | copy-done | bytes 262168
  5.2 0.0 copy-start.2
  5.2 0.9 %copy-done.2 = f32[1,1,256,256]{3,2,1,0:T(8,128)S(1)} copy-done((f32[1,1,256,256]{3,2,1,0:T(8,128)S(1)}, f32[1,1,256,256]{3,2,1,0:T(8,128)}, u32[]{:S(2)}) %copy-start.2) | copy-done | bytes 262168
  6.2 0.0 copy-start.4
  6.2 0.9 %copy-done.4 = f32[256,256]{1,0:T(8,128)S(1)} copy-done((f32[256,256]{1,0:T(8,128)S(1)}, f32[256,256]{1,0:T(8,128)}, u32[]{:S(2)}) %copy-start.4) | copy-done | bytes 262168
  7.1 0.0 copy-start.6
  7.1 0.9 %copy-done.6 = f32[256,256]{1,0:T(8,128)S(1)} copy-done((f32[256,256]{1,0:T(8,128)S(1)}, f32[256,256]{1,0:T(8,128)}, u32[]{:S(2)}) %copy-start.6) | copy-done | bytes 262168
  8.1 0.0 copy-start.8
  8.1 0.9 %copy-done.8 = f32[1,1,256,256]{3,2,1,0:T(8,128)S(1)} copy-done((f32[1,1,256,256]{3,2,1,0:T(8,128)S(1)}, f32[1,1,256,256]{3,2,1,0:T(8,128)}, u32[]{:S(2)}) %copy-start.8) | copy-done | bytes 262168
  9.0 0.0 copy-start.1
  9.0 0.0 copy-start.3
  9.0 0.0 copy-start.5
  9.0 0.4 shard_map.91
  9.4 0.0 collective-permute-done.partner_ref
  9.5 0.5 copy-done.1
  10.0 0.1 copy-done.3
  10.1 0.1 copy-done.5
  10.1 1.0 %shard_map.92 = f32[256,256]{1,0:T(8,128)} custom-call(s32[1]{0:T(128)} %bitcast.pair_ref, f32[256,256]{1,0:T(8,128)S(1)} %get-tuple-element.10.side_ref, f32[256,256]{1,0:T(8,128)S(1)} %bitcast.15, f32[256,256]{1,0:T(8,128)S(1)} %collective-permute-done.partner_ref, f32[256,256]{1,0:T(8,128)S(1)} %copy-done.5, bf16[2,256,256]{2,1,0:T(8,128)(2,1)S(1)} %copy-done.1), custom_call_target="tpu_custom_call" | custom-call | tf_op jit(solution)/shard_map/pallas_call | solution.py:212
  11.2 5.4 %all-to-all-start = ((f32[32,8,256]{2,1,0:T(8,128)}), f32[32,8,256]{2,1,0:T(8,128)S(1)}, u32[]{:S(2)}, u32[]{:S(2)}) async-start(f32[32,8,256]{2,1,0:T(8,128)} %bitcast.4), calls=%async_computation | async-start | bytes 524288 | tf_op jit(solution)/shard_map/all_to_all | solution.py:235
  17.3 9.6 %all-to-all-done = f32[32,8,256]{2,1,0:T(8,128)S(1)} async-done(((f32[32,8,256]{2,1,0:T(8,128)}), f32[32,8,256]{2,1,0:T(8,128)S(1)}, u32[]{:S(2)}, u32[]{:S(2)}) %all-to-all-start) | async-done | bytes 262176 | tf_op jit(solution)/shard_map/all_to_all | solution.py:235
  26.9 0.8 %shard_map.93 = (f32[256,384]{1,0:T(8,128)S(1)}, f32[256,256]{1,0:T(8,128)S(1)}, f32[16,256]{1,0:T(8,128)S(1)}) custom-call(f32[1]{0:T(128)S(6)} %copy.10.alpha_ref, f32[256,256]{1,0:T(8,128)S(1)} %bitcast.21, f32[8,256]{1,0:T(8,128)S(1)} %get-tuple-element.11.rate_ref, bf16[2,256,256]{2,1,0:T(8,128)(2,1)S(1)} %copy-done.1), custom_call_target="tpu_custom_call" | custom-call | tf_op jit(solution)/shard_map/pallas_call | solution.py:212
  27.7 0.0 copy-start.7
  27.7 15.4 %all_to_all.44 = f32[32,8,384]{2,1,0:T(8,128)S(1)} all-to-all(f32[32,8,384]{2,1,0:T(8,128)S(1)} %bitcast.24), channel_id=1, replica_groups=mesh['pair'=2,'tm'=16] {'pair','tm'}, dimensions={0} | all-to-all | bytes 786432 | tf_op jit(solution)/shard_map/all_to_all | solution.py:235
  43.1 0.0 copy-done.7
  43.1 1.0 %shard_map.94 = f32[256,256]{1,0:T(8,128)S(1)} custom-call(f32[1]{0:T(128)S(6)} %copy.11.mean_ref, f32[1]{0:T(128)S(6)} %copy.12.shift_ref, s32[1]{0:T(128)} %bitcast.pair_ref, s32[1]{0:T(128)} %bitcast.1.step_ref, f32[256,384]{1,0:T(8,128)S(1)} %bitcast.18, f32[256,256]{1,0:T(8,128)S(1)} %bitcast.16, f32[256,256]{1,0:T(8,128)S(1)} %collective-permute-done.partner_ref, ...), custom_call_target="tpu_custom_call" | custom-call | tf_op jit(solution)/shard_map/pallas_call | solution.py:212
  44.1 12.4 %all_to_all.45 = f32[32,8,256]{2,1,0:T(8,128)S(1)} all-to-all(f32[32,8,256]{2,1,0:T(8,128)S(1)} %bitcast.19), channel_id=1, replica_groups=mesh['pair'=2,'tm'=16] {'pair','tm'}, dimensions={0} | all-to-all | bytes 524288 | tf_op jit(solution)/shard_map/all_to_all | solution.py:235
  56.6 0.7 shard_map.95
  57.3 12.6 %all_to_all.46 = f32[32,8,256]{2,1,0:T(8,128)S(1)} all-to-all(f32[32,8,256]{2,1,0:T(8,128)S(1)} %bitcast.23), channel_id=1, replica_groups=mesh['pair'=2,'tm'=16] {'pair','tm'}, dimensions={0} | all-to-all | bytes 524288 | tf_op jit(solution)/shard_map/all_to_all | solution.py:235
  69.9 1.0 %shard_map.96 = f32[256,256]{1,0:T(8,128)} custom-call(s32[1]{0:T(128)} %bitcast.pair_ref, s32[1]{0:T(128)} %bitcast.1.step_ref, f32[256,256]{1,0:T(8,128)S(1)} %bitcast.20, f32[256,256]{1,0:T(8,128)S(1)} %bitcast.17, bf16[2,256,256]{2,1,0:T(8,128)(2,1)S(1)} %copy-done.1), custom_call_target="tpu_custom_call" | custom-call | tf_op jit(solution)/shard_map/pallas_call | solution.py:212
Async XLA Ops:
  0.0 9.5 %collective-permute-start = (f32[256,256]{1,0:T(8,128)}, f32[256,256]{1,0:T(8,128)S(1)}, u32[]{:S(2)}, u32[]{:S(2)}) collective-permute-start(f32[256,256]{1,0:T(8,128)} %bitcast.13), channel_id=1, source_target_pairs={{0,16},{16,0},{1,17},{17,1},{2,18},{18,2},{3,19},{19,3},{4,20},{20... | collective-permute-start | bytes 786440 | tf_op jit(solution)/shard_map/ppermute | solution.py:237
  4.3 1.0 %copy-start = (bf16[2,256,256]{2,1,0:T(8,128)(2,1)S(1)}, bf16[2,256,256]{2,1,0:T(8,128)(2,1)}, u32[]{:S(2)}) copy-start(bf16[2,256,256]{2,1,0:T(8,128)(2,1)} %constant.11.clone.table_ref) | copy-start | bytes 786436
  5.2 0.9 %copy-start.2 = (f32[1,1,256,256]{3,2,1,0:T(8,128)S(1)}, f32[1,1,256,256]{3,2,1,0:T(8,128)}, u32[]{:S(2)}) copy-start(f32[1,1,256,256]{3,2,1,0:T(8,128)} %param.9) | copy-start | bytes 786436
  6.2 0.9 %copy-start.4 = (f32[256,256]{1,0:T(8,128)S(1)}, f32[256,256]{1,0:T(8,128)}, u32[]{:S(2)}) copy-start(f32[256,256]{1,0:T(8,128)} %reaction_ref.5) | copy-start | bytes 786436
  7.1 0.9 %copy-start.6 = (f32[256,256]{1,0:T(8,128)S(1)}, f32[256,256]{1,0:T(8,128)}, u32[]{:S(2)}) copy-start(f32[256,256]{1,0:T(8,128)} %diffusion_ref.3) | copy-start | bytes 786436
  8.1 0.9 %copy-start.8 = (f32[1,1,256,256]{3,2,1,0:T(8,128)S(1)}, f32[1,1,256,256]{3,2,1,0:T(8,128)}, u32[]{:S(2)}) copy-start(f32[1,1,256,256]{3,2,1,0:T(8,128)} %param.10) | copy-start | bytes 786436
  9.0 0.9 %copy-start.1 = (bf16[2,256,256]{2,1,0:T(8,128)(2,1)S(1)}, bf16[2,256,256]{2,1,0:T(8,128)(2,1)}, u32[]{:S(2)}) copy-start(bf16[2,256,256]{2,1,0:T(8,128)(2,1)} %constant.11.clone.table_ref) | copy-start | bytes 786436
  9.0 1.0 %copy-start.3 = (f32[1,1,256,256]{3,2,1,0:T(8,128)S(1)}, f32[1,1,256,256]{3,2,1,0:T(8,128)}, u32[]{:S(2)}) copy-start(f32[1,1,256,256]{3,2,1,0:T(8,128)} %param.9) | copy-start | bytes 786436
  9.0 1.1 %copy-start.5 = (f32[256,256]{1,0:T(8,128)S(1)}, f32[256,256]{1,0:T(8,128)}, u32[]{:S(2)}) copy-start(f32[256,256]{1,0:T(8,128)} %reaction_ref.5) | copy-start | bytes 786436
  11.2 15.7 %all-to-all-start = ((f32[32,8,256]{2,1,0:T(8,128)}), f32[32,8,256]{2,1,0:T(8,128)S(1)}, u32[]{:S(2)}, u32[]{:S(2)}) async-start(f32[32,8,256]{2,1,0:T(8,128)} %bitcast.4), calls=%async_computation | async-start | bytes 524288 | tf_op jit(solution)/shard_map/all_to_all | solution.py:235
  27.7 15.5 %copy-start.7 = (f32[256,256]{1,0:T(8,128)S(1)}, f32[256,256]{1,0:T(8,128)}, u32[]{:S(2)}) copy-start(f32[256,256]{1,0:T(8,128)} %diffusion_ref.3) | copy-start | bytes 786436

commit v2 on v1

--- a/solution.py
+++ b/solution.py
@@ -47,9 +47,9 @@
 
 def own_kernel(
     total, rows,
-    mean_ref, shift_ref, pair_ref, step_ref,
+    mean_ref, shift_ref, alpha_ref, pair_ref, step_ref,
     own_ref, source_ref, diffusion_ref, reaction_ref, table_ref,
-    side_ref, rate_ref,
+    side_ref, rate_ref, wrap_ref,
 ):
     adjoint = pair_ref[0] == 1
     last = step_ref[0] == jnp.where(adjoint, 0, total - 1)
@@ -69,7 +69,15 @@
     sine_rows = jnp.sin(row_ids.astype(jnp.float32) * (math.pi / own.shape[1]))
     sine_cols = jnp.sin(col_ids.astype(jnp.float32) * (math.pi / own.shape[0]))
     eigen = 4.0 * sine_rows * sine_rows + 4.0 * sine_cols * sine_cols
-    rate_ref[...] = 1.0 / (1.0 + shift_ref[0] + mean_ref[0] * eigen)
+    rate = 1.0 / (1.0 + shift_ref[0] + mean_ref[0] * eigen)
+    rate_ref[...] = rate
+    power = rate
+    for _ in range(total - 1):
+        power = power * rate
+    wrap = alpha_ref[0] / (1.0 - alpha_ref[0] * power)
+    for step in range(total):
+        wrap = wrap * rate
+        wrap_ref[step * rows : (step + 1) * rows, :] = wrap
 
 
 def first_kernel(pair_ref, side_ref, own_ref, partner_ref, reaction_ref, table_ref, out_ref):
@@ -88,28 +96,29 @@
     return [slice((group * total + step) * rows, (group * total + step + 1) * rows) for step in order]
 
 
-def solve_steps(rows, total, rate, alpha, work_ref):
-    power = rate
-    for _ in range(total - 1):
-        power = power * rate
-    gain = alpha / (1.0 - alpha * power)
-    for group in range(2):
-        places = step_places(group, total, rows)
-        value = jnp.zeros_like(rate)
-        for place in places:
-            value = rate * (value + work_ref[place, :])
-        value = gain * value
-        for place in places:
-            value = rate * (value + work_ref[place, :])
-            work_ref[place, :] = value
-
-
-def middle_kernel(rows, total, scale, alpha_ref, in_ref, rate_ref, table_ref, out_ref, side_ref, last_ref, work_ref):
+def solve_steps(rows, total, rate, wrap_ref, work_ref):
+    places = [step_places(group, total, rows) for group in range(2)]
+    values = [jnp.zeros_like(rate)] * 2
+    for step in range(total):
+        for group in range(2):
+            place = places[group][step]
+            values[group] = rate * (values[group] + work_ref[place, :])
+            work_ref[place, :] = values[group]
+    for step in range(total):
+        wrap = wrap_ref[step * rows : (step + 1) * rows, :]
+        for group in range(2):
+            place = places[group][step]
+            work_ref[place, :] = work_ref[place, :] + wrap * values[group]
+
+
+def middle_kernel(
+    rows, total, scale, in_ref, rate_ref, wrap_ref, table_ref, out_ref, side_ref, last_ref, work_ref
+):
     table = halves_of(table_ref)
     sides = product(split(in_ref[...]), table, 1, 0) * scale
     side_ref[...] = sides
     work_ref[...] = sides
-    solve_steps(rows, total, rate_ref[...], alpha_ref[0], work_ref)
+    solve_steps(rows, total, rate_ref[...], wrap_ref, work_ref)
     for group in range(2):
         last_ref[group * rows : (group + 1) * rows, :] = work_ref[step_places(group, total, rows)[-1], :]
     fields = product(split(work_ref[...]), table, 1, 0)
@@ -184,7 +193,9 @@
     out_ref[...] = product(table, split(sides), 1, 1)
 
 
-def final_kernel(rows, total, scale, alpha_ref, in_ref, rate_ref, side_ref, last_ref, table_ref, out_ref, work_ref):
+def final_kernel(
+    rows, total, scale, in_ref, rate_ref, wrap_ref, side_ref, last_ref, table_ref, out_ref, work_ref
+):
     table = halves_of(table_ref)
     band = rows * total
     half = in_ref.shape[1] // 2
@@ -193,7 +204,7 @@
         for part in (slice(0, half), slice(half, 2 * half))
     ]
     work_ref[...] = product(split(jnp.concatenate(joined, 0)), table, 1, 0) * scale + side_ref[...]
-    solve_steps(rows, total, rate_ref[...], alpha_ref[0], work_ref)
+    solve_steps(rows, total, rate_ref[...], wrap_ref, work_ref)
     for group in range(2):
         place = step_places(group, total, rows)[-1]
         work_ref[place, :] = work_ref[place, :] + last_ref[group * rows : (group + 1) * rows, :]
@@ -235,17 +246,17 @@
         return lax.all_to_all(values, AXES, 0, 0, tiled=True)
 
     partner = lax.ppermute(own, "pair", [(0, 1), (1, 0)])
-    side, rate = call(
+    side, rate, wrap = call(
         functools.partial(own_kernel, total, rows),
-        (mean_diffusion, spectral_shift, pair, step),
+        (mean_diffusion, spectral_shift, wrap_factor, pair, step),
         (own, source, diffusion, reaction, y_table),
-        [grid, (rows, grid_x)],
+        [grid, (rows, grid_x), (total * rows, grid_x)],
     )
     (sides,) = call(first_kernel, (pair,), (side, own, partner, reaction, y_table), [band])
     halves, kept_side, last = call(
         functools.partial(middle_kernel, rows, total, scale),
-        (wrap_factor,),
-        (exchange(sides), rate, x_table),
+        (),
+        (exchange(sides), rate, wrap, x_table),
         [(grid_y, 3 * half), band, (2 * rows, grid_x)],
         [band],
     )
@@ -257,8 +268,8 @@
     )
     (wholes,) = call(
         functools.partial(final_kernel, rows, total, scale),
-        (wrap_factor,),
-        (exchange(sides), rate, kept_side, last, x_table),
+        (),
+        (exchange(sides), rate, wrap, kept_side, last, x_table),
         [band],
         [band],
     )

time: 71.4 us -> 70.5 us (0.987)
  blocking collectives: 40.5 us -> 55.5 us
  waiting for transfers between devices: 9.68 us -> 0.01 us
  starting transfers between devices: 8.41 us -> 2.97 us
  Pallas kernels: 4.95 us -> 4.2 us
    all_to_all x3 -> x4, blocking collectives: 40.5 us -> 55.5 us  [exchange(): return lax.all_to_all(values, AXES, 0, 0, tiled=True)]
    all_to_all x1 -> x0, waiting for transfers between devices: 9.65 us -> none  [exchange(): return lax.all_to_all(values, AXES, 0, 0, tiled=True)]
    all_to_all x1 -> x0, starting transfers between devices: 5.44 us -> none  [exchange(): return lax.all_to_all(values, AXES, 0, 0, tiled=True)]
    pallas_call x6, Pallas kernels: 4.95 us -> 4.2 us  [call(): pl.pallas_call(kernel, out_shape=[jax.ShapeDtypeStruct(shape, jnp.float32...]
  transfers between devices with their start and end apart: 2 -> 1, of which waited for: 1 -> 0; matrix products, arithmetic and copies ran while one was open for 0% -> 0% of each run, Pallas kernels for 1% -> 1%
where the time goes in v2:
time: 70.5 us; the launch traced here: 70.1 us
  blocking collectives  55.5 us (79%)
  local copies, waits for them, and re-layouts  5.42 us (8%)
  Pallas kernels  4.2 us (6%)
  starting transfers between devices  2.97 us (4%)
  between operations  2.01 us (3%)
    all_to_all x4, blocking collectives, exchange(): return lax.all_to_all(values, AXES, 0, 0, tiled=True)  55.5 us
    unnamed x18, local copies, waits for them, and re-layouts  5.42 us
    pallas_call x6, Pallas kernels, call(): pl.pallas_call(kernel, out_shape=[jax.ShapeDtypeStruct(shape, jnp.float32...  4.2 us
    ppermute x1, starting transfers between devices, on_device(): partner = lax.ppermute(own, 'pair', [(0, 1), (1, 0)])  2.97 us
  transfers between devices with their start and end apart: 1, of which 0 were waited for; matrix products, arithmetic and copies ran while one was open for 0% of the time, Pallas kernels for 1%

profile of v2, /device:TPU:0, one launch (start us, length us, event | category | flops | bytes accessed | tf_op | source)
XLA Modules:
  0.0 70.1 jit_solution(12921710002756612516)
XLA Ops:
  0.0 3.0 %collective-permute-start = (f32[256,256]{1,0:T(8,128)}, f32[256,256]{1,0:T(8,128)S(1)}, u32[]{:S(2)}, u32[]{:S(2)}) collective-permute-start(f32[256,256]{1,0:T(8,128)} %bitcast.13), channel_id=1, source_target_pairs={{0,16},{16,0},{1,17},{17,1},{2,18},{18,2},{3,19},{19,3},{4,20},{20... | collective-permute-start | bytes 786440 | tf_op jit(solution)/shard_map/ppermute | solution.py:248
  4.9 0.0 copy-start
  4.9 0.9 %copy-done = bf16[2,256,256]{2,1,0:T(8,128)(2,1)S(1)} copy-done((bf16[2,256,256]{2,1,0:T(8,128)(2,1)S(1)}, bf16[2,256,256]{2,1,0:T(8,128)(2,1)}, u32[]{:S(2)}) %copy-start) | copy-done | bytes 262168
  5.9 0.0 copy-start.2
  5.9 0.9 %copy-done.2 = f32[1,1,256,256]{3,2,1,0:T(8,128)S(1)} copy-done((f32[1,1,256,256]{3,2,1,0:T(8,128)S(1)}, f32[1,1,256,256]{3,2,1,0:T(8,128)}, u32[]{:S(2)}) %copy-start.2) | copy-done | bytes 262168
  6.8 0.0 copy-start.4
  6.8 0.9 %copy-done.4 = f32[256,256]{1,0:T(8,128)S(1)} copy-done((f32[256,256]{1,0:T(8,128)S(1)}, f32[256,256]{1,0:T(8,128)}, u32[]{:S(2)}) %copy-start.4) | copy-done | bytes 262168
  7.8 0.0 copy-start.6
  7.8 0.9 %copy-done.6 = f32[256,256]{1,0:T(8,128)S(1)} copy-done((f32[256,256]{1,0:T(8,128)S(1)}, f32[256,256]{1,0:T(8,128)}, u32[]{:S(2)}) %copy-start.6) | copy-done | bytes 262168
  8.7 0.0 copy-start.8
  8.7 0.9 %copy-done.8 = f32[1,1,256,256]{3,2,1,0:T(8,128)S(1)} copy-done((f32[1,1,256,256]{3,2,1,0:T(8,128)S(1)}, f32[1,1,256,256]{3,2,1,0:T(8,128)}, u32[]{:S(2)}) %copy-start.8) | copy-done | bytes 262168
  9.7 0.0 copy-start.1
  9.7 0.0 copy-start.3
  9.7 0.0 copy-start.5
  9.7 0.4 shard_map.91
  10.1 0.0 collective-permute-done.partner_ref
  10.1 0.5 copy-done.1
  10.6 0.1 copy-done.3
  10.7 0.1 copy-done.5
  10.8 0.3 shard_map.92
  11.1 15.0 %all_to_all.44 = f32[32,8,256]{2,1,0:T(8,128)S(1)} all-to-all(f32[32,8,256]{2,1,0:T(8,128)S(1)} %bitcast.24), channel_id=1, replica_groups=mesh['pair'=2,'tm'=16] {'pair','tm'}, dimensions={0} | all-to-all | bytes 524288 | tf_op jit(solution)/shard_map/all_to_all | solution.py:246
  26.1 0.7 %shard_map.93 = (f32[256,384]{1,0:T(8,128)S(1)}, f32[256,256]{1,0:T(8,128)S(1)}, f32[16,256]{1,0:T(8,128)S(1)}) custom-call(f32[256,256]{1,0:T(8,128)S(1)} %bitcast.22, f32[8,256]{1,0:T(8,128)S(1)} %get-tuple-element.12.rate_ref, f32[128,256]{1,0:T(8,128)S(1)} %get-tuple-element.13.wrap_ref, bf16[2,256,256]{2,1,0:T(8,128)(2,1)S(1)} %copy-done.1), custom_call_target="tpu_custom_call" | custom-call | tf_op jit(solution)/shard_map/pallas_call | solution.py:223
  26.9 0.0 copy-start.7
  26.9 15.4 %all_to_all.45 = f32[32,8,384]{2,1,0:T(8,128)S(1)} all-to-all(f32[32,8,384]{2,1,0:T(8,128)S(1)} %bitcast.25), channel_id=1, replica_groups=mesh['pair'=2,'tm'=16] {'pair','tm'}, dimensions={0} | all-to-all | bytes 786432 | tf_op jit(solution)/shard_map/all_to_all | solution.py:246
  42.3 0.0 copy-done.7
  42.3 1.0 %shard_map.94 = f32[256,256]{1,0:T(8,128)S(1)} custom-call(f32[1]{0:T(128)S(6)} %copy.11.mean_ref, f32[1]{0:T(128)S(6)} %copy.12.shift_ref, s32[1]{0:T(128)} %bitcast.pair_ref, s32[1]{0:T(128)} %bitcast.1.step_ref, f32[256,384]{1,0:T(8,128)S(1)} %bitcast.18, f32[256,256]{1,0:T(8,128)S(1)} %bitcast.16, f32[256,256]{1,0:T(8,128)S(1)} %collective-permute-done.partner_ref, ...), custom_call_target="tpu_custom_call" | custom-call | tf_op jit(solution)/shard_map/pallas_call | solution.py:223
  43.3 12.4 %all_to_all.46 = f32[32,8,256]{2,1,0:T(8,128)S(1)} all-to-all(f32[32,8,256]{2,1,0:T(8,128)S(1)} %bitcast.19), channel_id=1, replica_groups=mesh['pair'=2,'tm'=16] {'pair','tm'}, dimensions={0} | all-to-all | bytes 524288 | tf_op jit(solution)/shard_map/all_to_all | solution.py:246
  55.8 0.7 shard_map.95
  56.4 12.6 %all_to_all.47 = f32[32,8,256]{2,1,0:T(8,128)S(1)} all-to-all(f32[32,8,256]{2,1,0:T(8,128)S(1)} %bitcast.23), channel_id=1, replica_groups=mesh['pair'=2,'tm'=16] {'pair','tm'}, dimensions={0} | all-to-all | bytes 524288 | tf_op jit(solution)/shard_map/all_to_all | solution.py:246
  69.1 1.0 %shard_map.96 = f32[256,256]{1,0:T(8,128)} custom-call(s32[1]{0:T(128)} %bitcast.pair_ref, s32[1]{0:T(128)} %bitcast.1.step_ref, f32[256,256]{1,0:T(8,128)S(1)} %bitcast.20, f32[256,256]{1,0:T(8,128)S(1)} %bitcast.17, bf16[2,256,256]{2,1,0:T(8,128)(2,1)S(1)} %copy-done.1), custom_call_target="tpu_custom_call" | custom-call | tf_op jit(solution)/shard_map/pallas_call | solution.py:223
Async XLA Ops:
  0.0 10.1 %collective-permute-start = (f32[256,256]{1,0:T(8,128)}, f32[256,256]{1,0:T(8,128)S(1)}, u32[]{:S(2)}, u32[]{:S(2)}) collective-permute-start(f32[256,256]{1,0:T(8,128)} %bitcast.13), channel_id=1, source_target_pairs={{0,16},{16,0},{1,17},{17,1},{2,18},{18,2},{3,19},{19,3},{4,20},{20... | collective-permute-start | bytes 786440 | tf_op jit(solution)/shard_map/ppermute | solution.py:248
  4.9 1.0 %copy-start = (bf16[2,256,256]{2,1,0:T(8,128)(2,1)S(1)}, bf16[2,256,256]{2,1,0:T(8,128)(2,1)}, u32[]{:S(2)}) copy-start(bf16[2,256,256]{2,1,0:T(8,128)(2,1)} %constant.11.clone.table_ref) | copy-start | bytes 786436
  5.9 0.9 %copy-start.2 = (f32[1,1,256,256]{3,2,1,0:T(8,128)S(1)}, f32[1,1,256,256]{3,2,1,0:T(8,128)}, u32[]{:S(2)}) copy-start(f32[1,1,256,256]{3,2,1,0:T(8,128)} %param.9) | copy-start | bytes 786436
  6.8 0.9 %copy-start.4 = (f32[256,256]{1,0:T(8,128)S(1)}, f32[256,256]{1,0:T(8,128)}, u32[]{:S(2)}) copy-start(f32[256,256]{1,0:T(8,128)} %reaction_ref.5) | copy-start | bytes 786436
  7.8 0.9 %copy-start.6 = (f32[256,256]{1,0:T(8,128)S(1)}, f32[256,256]{1,0:T(8,128)}, u32[]{:S(2)}) copy-start(f32[256,256]{1,0:T(8,128)} %diffusion_ref.3) | copy-start | bytes 786436
  8.7 0.9 %copy-start.8 = (f32[1,1,256,256]{3,2,1,0:T(8,128)S(1)}, f32[1,1,256,256]{3,2,1,0:T(8,128)}, u32[]{:S(2)}) copy-start(f32[1,1,256,256]{3,2,1,0:T(8,128)} %param.10) | copy-start | bytes 786436
  9.7 0.9 %copy-start.1 = (bf16[2,256,256]{2,1,0:T(8,128)(2,1)S(1)}, bf16[2,256,256]{2,1,0:T(8,128)(2,1)}, u32[]{:S(2)}) copy-start(bf16[2,256,256]{2,1,0:T(8,128)(2,1)} %constant.11.clone.table_ref) | copy-start | bytes 786436
  9.7 1.0 %copy-start.3 = (f32[1,1,256,256]{3,2,1,0:T(8,128)S(1)}, f32[1,1,256,256]{3,2,1,0:T(8,128)}, u32[]{:S(2)}) copy-start(f32[1,1,256,256]{3,2,1,0:T(8,128)} %param.9) | copy-start | bytes 786436
  9.7 1.1 %copy-start.5 = (f32[256,256]{1,0:T(8,128)S(1)}, f32[256,256]{1,0:T(8,128)}, u32[]{:S(2)}) copy-start(f32[256,256]{1,0:T(8,128)} %reaction_ref.5) | copy-start | bytes 786436
  26.9 15.5 %copy-start.7 = (f32[256,256]{1,0:T(8,128)S(1)}, f32[256,256]{1,0:T(8,128)}, u32[]{:S(2)}) copy-start(f32[256,256]{1,0:T(8,128)} %diffusion_ref.3) | copy-start | bytes 786436

commit v3 on v2

--- a/solution.py
+++ b/solution.py
@@ -124,28 +124,47 @@
     fields = product(split(work_ref[...]), table, 1, 0)
     band = rows * total
     half = fields.shape[1] // 2
+    block = 2 * rows + 1
+    row = lax.broadcasted_iota(jnp.int32, (band, half), 0)
     lane = lax.broadcasted_iota(jnp.int32, (band, half), 1)
-    ends = (lane == 0) | (lane == half - 1)
     for side in range(2):
-        inner = slice(side * half, (side + 1) * half)
-        other = slice((1 - side) * half, (2 - side) * half)
-        place = slice(side * band, (side + 1) * band)
-        out_ref[place, :half] = fields[:band, inner]
-        out_ref[place, half : 2 * half] = fields[band:, inner]
-        out_ref[place, 2 * half :] = jnp.where(ends, fields[:band, other], roll(fields[band:, other], half // 2, 1))
+        inner, outer = side * half, (1 - side) * half
+        packed = jnp.zeros((band, half), jnp.float32)
+        for group in range(2):
+            for number, column in enumerate((outer, outer + half - 1)):
+                values = fields[group * band : (group + 1) * band, column : column + 1]
+                packed = jnp.where(lane == (2 * group + number) * rows + row % rows, values, packed)
+        packed = packed.reshape(total, rows, half).sum(1)
+        for step in range(total):
+            start = (side * total + step) * block
+            for group in range(2):
+                place = slice((group * total + step) * rows, (group * total + step + 1) * rows)
+                out_ref[start + group * rows : start + (group + 1) * rows, :] = fields[place, inner : inner + half]
+            out_ref[start + 2 * rows : start + block, :] = packed[step : step + 1]
 
 
 def second_kernel(
     total,
     mean_ref, shift_ref, pair_ref, step_ref,
     in_ref, own_ref, partner_ref, diffusion_ref, reaction_ref, table_ref,
-    out_ref,
+    out_ref, work_ref,
 ):
     place, step = pair_ref[0], step_ref[0]
     table = halves_of(table_ref)
-    solved = product(split(in_ref[...]), table, 0, 0)
-    half = solved.shape[0] // 3
-    middle = half // 2
+    grid_x, grid_y = own_ref.shape
+    half = grid_x // 2
+    rows = grid_y // (2 * total)
+    block = 2 * rows + 1
+    row = lax.broadcasted_iota(jnp.int32, (rows, half), 0)
+    lane = lax.broadcasted_iota(jnp.int32, (rows, half), 1)
+    diagonal = (lane % rows == row) & (lane < 4 * rows)
+    for source in range(2 * total):
+        start, band = source * block, slice(source * rows, (source + 1) * rows)
+        for group in range(2):
+            work_ref[band, group * half : (group + 1) * half] = in_ref[start + group * rows : start + (group + 1) * rows, :]
+        work_ref[band, 2 * half :] = jnp.where(diagonal, in_ref[start + 2 * rows : start + block, :], 0.0)
+    solved = product(split(work_ref[...]), table, 0, 0)
+    beside = solved[2 * half : 2 * half + 4 * rows].reshape(4, rows, grid_y).sum(1)
     inner = pl.ds(pl.multiple_of(place * half, half), half)
     outer = pl.ds(pl.multiple_of((1 - place) * half, half), half)
     cells, others = diffusion_ref[inner, :], diffusion_ref[outer, :]
@@ -170,21 +189,19 @@
         flux_x = flux_x - (west - mean) * (values - before(values, preceding))
         return flux_x + flux_y - roll(flux_y, 1, 1) + shift * values
 
-    def change(group, first_row, last_step):
+    def change(group, last_step):
         own = place == group
         former_here = jnp.where(own, own_ref[inner, :], partner_ref[inner, :])
         former_there = jnp.where(own, own_ref[outer, :], partner_ref[outer, :])
         last = step == last_step
         taken = jnp.where(last, 0.0, 1.0)
         delta = solved[group * half : (group + 1) * half] - taken * former_here
-        beside = solved[2 * half :]
-        following = beside[first_row : first_row + 1] - taken * former_there[0:1]
-        before_row = (first_row - 1) % half
-        preceding = beside[before_row : before_row + 1] - taken * former_there[half - 1 : half]
+        following = beside[2 * group : 2 * group + 1] - taken * former_there[0:1]
+        preceding = beside[2 * group + 1 : 2 * group + 2] - taken * former_there[half - 1 : half]
         return former_here, delta, linear(delta, following, preceding, last)
 
-    state, state_delta, state_side = change(0, 0, total - 1)
-    adjoint, adjoint_delta, adjoint_side = change(1, middle, 0)
+    state, state_delta, state_side = change(0, total - 1)
+    adjoint, adjoint_delta, adjoint_side = change(1, 0)
     new_state, new_adjoint = state + state_delta, adjoint + adjoint_delta
     square, new_square = state * state, new_state * new_state
     state_side = state_side - (reaction * (new_square * new_state - square * state) + gamma_inv * adjoint_delta)
@@ -245,6 +262,10 @@
     def exchange(values):
         return lax.all_to_all(values, AXES, 0, 0, tiled=True)
 
+    def exchange_blocks(values):
+        blocks = values.reshape(2 * total, -1, 1, values.shape[1])
+        return lax.all_to_all(blocks, AXES, 0, 0, tiled=True).reshape(values.shape)
+
     partner = lax.ppermute(own, "pair", [(0, 1), (1, 0)])
     side, rate, wrap = call(
         functools.partial(own_kernel, total, rows),
@@ -257,14 +278,15 @@
         functools.partial(middle_kernel, rows, total, scale),
         (),
         (exchange(sides), rate, wrap, x_table),
-        [(grid_y, 3 * half), band, (2 * rows, grid_x)],
+        [(2 * total * (2 * rows + 1), half), band, (2 * rows, grid_x)],
         [band],
     )
     (sides,) = call(
         functools.partial(second_kernel, total),
         (mean_diffusion, spectral_shift, pair, step),
-        (exchange(halves), own, partner, diffusion, reaction, y_table),
+        (exchange_blocks(halves), own, partner, diffusion, reaction, y_table),
         [band],
+        [(grid_y, 3 * half)],
     )
     (wholes,) = call(
         functools.partial(final_kernel, rows, total, scale),

time: 70.5 us -> 68.3 us (0.969)
  blocking collectives: 55.5 us -> 53.2 us
    all_to_all x4 -> x3, blocking collectives: 55.5 us -> 40.2 us  [exchange(): return lax.all_to_all(values, AXES, 0, 0, tiled=True)]
    all_to_all x0 -> x1, blocking collectives: none -> 13 us  [exchange_blocks(): return lax.all_to_all(blocks, AXES, 0, 0, tiled=True).reshape(values.shape)]
where the time goes in v3:
time: 68.3 us; the launch traced here: 67.9 us
  blocking collectives  53.2 us (78%)
  local copies, waits for them, and re-layouts  5.42 us (8%)
  Pallas kernels  4.3 us (6%)
  starting transfers between devices  2.97 us (4%)
  between operations  2.01 us (3%)
    all_to_all x3, blocking collectives, exchange(): return lax.all_to_all(values, AXES, 0, 0, tiled=True)  40.2 us
    all_to_all x1, blocking collectives, exchange_blocks(): return lax.all_to_all(blocks, AXES, 0, 0, tiled=True).reshape(values.shape)  13 us
    unnamed x18, local copies, waits for them, and re-layouts  5.42 us
    pallas_call x6, Pallas kernels, call(): pl.pallas_call(kernel, out_shape=[jax.ShapeDtypeStruct(shape, jnp.float32...  4.3 us
    ppermute x1, starting transfers between devices, on_device(): partner = lax.ppermute(own, 'pair', [(0, 1), (1, 0)])  2.97 us
  transfers between devices with their start and end apart: 1, of which 0 were waited for; matrix products, arithmetic and copies ran while one was open for 0% of the time, Pallas kernels for 1%

profile of v3, /device:TPU:0, one launch (start us, length us, event | category | flops | bytes accessed | tf_op | source)
XLA Modules:
  0.0 67.9 jit_solution(11667639694255199083)
XLA Ops:
  0.0 3.0 %collective-permute-start = (f32[256,256]{1,0:T(8,128)}, f32[256,256]{1,0:T(8,128)S(1)}, u32[]{:S(2)}, u32[]{:S(2)}) collective-permute-start(f32[256,256]{1,0:T(8,128)} %bitcast.13), channel_id=1, source_target_pairs={{0,16},{16,0},{1,17},{17,1},{2,18},{18,2},{3,19},{19,3},{4,20},{20... | collective-permute-start | bytes 786440 | tf_op jit(solution)/shard_map/ppermute | solution.py:269
  4.9 0.0 copy-start
  4.9 0.9 %copy-done = bf16[2,256,256]{2,1,0:T(8,128)(2,1)S(1)} copy-done((bf16[2,256,256]{2,1,0:T(8,128)(2,1)S(1)}, bf16[2,256,256]{2,1,0:T(8,128)(2,1)}, u32[]{:S(2)}) %copy-start) | copy-done | bytes 262168
  5.9 0.0 copy-start.2
  5.9 0.9 %copy-done.2 = f32[1,1,256,256]{3,2,1,0:T(8,128)S(1)} copy-done((f32[1,1,256,256]{3,2,1,0:T(8,128)S(1)}, f32[1,1,256,256]{3,2,1,0:T(8,128)}, u32[]{:S(2)}) %copy-start.2) | copy-done | bytes 262168
  6.8 0.0 copy-start.4
  6.8 0.9 %copy-done.4 = f32[256,256]{1,0:T(8,128)S(1)} copy-done((f32[256,256]{1,0:T(8,128)S(1)}, f32[256,256]{1,0:T(8,128)}, u32[]{:S(2)}) %copy-start.4) | copy-done | bytes 262168
  7.8 0.0 copy-start.6
  7.8 0.9 %copy-done.6 = f32[256,256]{1,0:T(8,128)S(1)} copy-done((f32[256,256]{1,0:T(8,128)S(1)}, f32[256,256]{1,0:T(8,128)}, u32[]{:S(2)}) %copy-start.6) | copy-done | bytes 262168
  8.7 0.0 copy-start.8
  8.7 0.9 %copy-done.8 = f32[1,1,256,256]{3,2,1,0:T(8,128)S(1)} copy-done((f32[1,1,256,256]{3,2,1,0:T(8,128)S(1)}, f32[1,1,256,256]{3,2,1,0:T(8,128)}, u32[]{:S(2)}) %copy-start.8) | copy-done | bytes 262168
  9.7 0.0 copy-start.1
  9.7 0.0 copy-start.3
  9.7 0.0 copy-start.5
  9.7 0.4 shard_map.91
  10.1 0.0 collective-permute-done.partner_ref
  10.1 0.5 copy-done.1
  10.6 0.1 copy-done.3
  10.7 0.1 copy-done.5
  10.8 0.3 shard_map.92
  11.1 15.0 %all_to_all.38 = f32[32,8,256]{2,1,0:T(8,128)S(1)} all-to-all(f32[32,8,256]{2,1,0:T(8,128)S(1)} %bitcast.24), channel_id=1, replica_groups=mesh['pair'=2,'tm'=16] {'pair','tm'}, dimensions={0} | all-to-all | bytes 524288 | tf_op jit(solution)/shard_map/all_to_all | solution.py:263
  26.1 0.8 %shard_map.93 = (f32[544,128]{1,0:T(8,128)S(1)}, f32[256,256]{1,0:T(8,128)S(1)}, f32[16,256]{1,0:T(8,128)S(1)}) custom-call(f32[256,256]{1,0:T(8,128)S(1)} %bitcast.21, f32[8,256]{1,0:T(8,128)S(1)} %get-tuple-element.12.rate_ref, f32[128,256]{1,0:T(8,128)S(1)} %get-tuple-element.13.wrap_ref, bf16[2,256,256]{2,1,0:T(8,128)(2,1)S(1)} %copy-done.1), custom_call_target="tpu_custom_call" | custom-call | tf_op jit(solution)/shard_map/pallas_call | solution.py:240
  27.0 0.0 copy-start.7
  27.0 13.0 %all_to_all.39 = f32[32,17,1,128]{3,2,1,0:T(1,128)S(1)} all-to-all(f32[32,17,1,128]{3,2,1,0:T(1,128)S(1)} %bitcast.25), channel_id=1, replica_groups=mesh['pair'=2,'tm'=16] {'pair','tm'}, dimensions={0} | all-to-all | bytes 557056 | tf_op jit(solution)/shard_map/all_to_all | solution.py:267
  40.0 0.0 copy-done.7
  40.0 1.0 %shard_map.94 = f32[256,256]{1,0:T(8,128)S(1)} custom-call(f32[1]{0:T(128)S(6)} %copy.12.mean_ref, f32[1]{0:T(128)S(6)} %copy.13.shift_ref, s32[1]{0:T(128)} %bitcast.pair_ref, s32[1]{0:T(128)} %bitcast.1.step_ref, f32[544,128]{1,0:T(8,128)S(1)} %bitcast.18, f32[256,256]{1,0:T(8,128)S(1)} %bitcast.16, f32[256,256]{1,0:T(8,128)S(1)} %collective-permute-done.partner_ref, ...), custom_call_target="tpu_custom_call" | custom-call | tf_op jit(solution)/shard_map/pallas_call | solution.py:240
  41.0 12.6 %all_to_all.40 = f32[32,8,256]{2,1,0:T(8,128)S(1)} all-to-all(f32[32,8,256]{2,1,0:T(8,128)S(1)} %bitcast.23), channel_id=1, replica_groups=mesh['pair'=2,'tm'=16] {'pair','tm'}, dimensions={0} | all-to-all | bytes 524288 | tf_op jit(solution)/shard_map/all_to_all | solution.py:263
  53.6 0.7 shard_map.95
  54.3 12.6 %all_to_all.41 = f32[32,8,256]{2,1,0:T(8,128)S(1)} all-to-all(f32[32,8,256]{2,1,0:T(8,128)S(1)} %bitcast.22), channel_id=1, replica_groups=mesh['pair'=2,'tm'=16] {'pair','tm'}, dimensions={0} | all-to-all | bytes 524288 | tf_op jit(solution)/shard_map/all_to_all | solution.py:263
  66.9 1.0 %shard_map.96 = f32[256,256]{1,0:T(8,128)} custom-call(s32[1]{0:T(128)} %bitcast.pair_ref, s32[1]{0:T(128)} %bitcast.1.step_ref, f32[256,256]{1,0:T(8,128)S(1)} %bitcast.19, f32[256,256]{1,0:T(8,128)S(1)} %bitcast.17, bf16[2,256,256]{2,1,0:T(8,128)(2,1)S(1)} %copy-done.1), custom_call_target="tpu_custom_call" | custom-call | tf_op jit(solution)/shard_map/pallas_call | solution.py:240
Async XLA Ops:
  0.0 10.1 %collective-permute-start = (f32[256,256]{1,0:T(8,128)}, f32[256,256]{1,0:T(8,128)S(1)}, u32[]{:S(2)}, u32[]{:S(2)}) collective-permute-start(f32[256,256]{1,0:T(8,128)} %bitcast.13), channel_id=1, source_target_pairs={{0,16},{16,0},{1,17},{17,1},{2,18},{18,2},{3,19},{19,3},{4,20},{20... | collective-permute-start | bytes 786440 | tf_op jit(solution)/shard_map/ppermute | solution.py:269
  4.9 1.0 %copy-start = (bf16[2,256,256]{2,1,0:T(8,128)(2,1)S(1)}, bf16[2,256,256]{2,1,0:T(8,128)(2,1)}, u32[]{:S(2)}) copy-start(bf16[2,256,256]{2,1,0:T(8,128)(2,1)} %constant.11.clone.table_ref) | copy-start | bytes 786436
  5.9 0.9 %copy-start.2 = (f32[1,1,256,256]{3,2,1,0:T(8,128)S(1)}, f32[1,1,256,256]{3,2,1,0:T(8,128)}, u32[]{:S(2)}) copy-start(f32[1,1,256,256]{3,2,1,0:T(8,128)} %param.9) | copy-start | bytes 786436
  6.8 0.9 %copy-start.4 = (f32[256,256]{1,0:T(8,128)S(1)}, f32[256,256]{1,0:T(8,128)}, u32[]{:S(2)}) copy-start(f32[256,256]{1,0:T(8,128)} %reaction_ref.5) | copy-start | bytes 786436
  7.8 0.9 %copy-start.6 = (f32[256,256]{1,0:T(8,128)S(1)}, f32[256,256]{1,0:T(8,128)}, u32[]{:S(2)}) copy-start(f32[256,256]{1,0:T(8,128)} %diffusion_ref.3) | copy-start | bytes 786436
  8.7 0.9 %copy-start.8 = (f32[1,1,256,256]{3,2,1,0:T(8,128)S(1)}, f32[1,1,256,256]{3,2,1,0:T(8,128)}, u32[]{:S(2)}) copy-start(f32[1,1,256,256]{3,2,1,0:T(8,128)} %param.10) | copy-start | bytes 786436
  9.7 0.9 %copy-start.1 = (bf16[2,256,256]{2,1,0:T(8,128)(2,1)S(1)}, bf16[2,256,256]{2,1,0:T(8,128)(2,1)}, u32[]{:S(2)}) copy-start(bf16[2,256,256]{2,1,0:T(8,128)(2,1)} %constant.11.clone.table_ref) | copy-start | bytes 786436
  9.7 1.0 %copy-start.3 = (f32[1,1,256,256]{3,2,1,0:T(8,128)S(1)}, f32[1,1,256,256]{3,2,1,0:T(8,128)}, u32[]{:S(2)}) copy-start(f32[1,1,256,256]{3,2,1,0:T(8,128)} %param.9) | copy-start | bytes 786436
  9.7 1.1 %copy-start.5 = (f32[256,256]{1,0:T(8,128)S(1)}, f32[256,256]{1,0:T(8,128)}, u32[]{:S(2)}) copy-start(f32[256,256]{1,0:T(8,128)} %reaction_ref.5) | copy-start | bytes 786436
  27.0 13.0 %copy-start.7 = (f32[256,256]{1,0:T(8,128)S(1)}, f32[256,256]{1,0:T(8,128)}, u32[]{:S(2)}) copy-start(f32[256,256]{1,0:T(8,128)} %diffusion_ref.3) | copy-start | bytes 786436

commit v4 on v0

v4 whole, which is shorter than its diff:
```python
import functools
import math

import jax
import jax.numpy as jnp
import ml_dtypes
import numpy as np
from jax import lax
from jax.experimental import pallas as pl
from jax.experimental.pallas import tpu as pltpu
from jax.sharding import PartitionSpec as P

ITERS = 2

gamma_inv = 0.5


def cas_table(length):
    places = np.arange(length)
    angles = (places[:, None] * places[None, :] % length) * (2.0 * np.pi / length)
    table = np.cos(angles) + np.sin(angles)
    high = table.astype(ml_dtypes.bfloat16)
    low = (table - high.astype(np.float64)).astype(ml_dtypes.bfloat16)
    return jnp.asarray(np.stack([high, low]))


def eigenvalues(length):
    return jnp.asarray((4.0 * np.sin(np.arange(length) * (np.pi / length)) ** 2).astype(np.float32))


def split(values):
    high = values.astype(jnp.bfloat16)
    return high, (values - high.astype(jnp.float32)).astype(jnp.bfloat16)


def parts(table_ref):
    return table_ref[0], table_ref[1]


def product(left, right):
    def one(a, b):
        return jnp.dot(a, b, preferred_element_type=jnp.float32)

    return one(left[0], right[0]) + (one(left[0], right[1]) + one(left[1], right[0]))


def roll(values, shift, axis):
    return pltpu.roll(values, shift % values.shape[axis], axis)


def own_kernel(mean_ref, shift_ref, adjoint_ref, last_ref, own_ref, source_ref, diffusion_ref, reaction_ref, out_ref):
    last = last_ref[0] == 1
    mean = jnp.where(last, 0.0, mean_ref[0])
    shift = jnp.where(last, -1.0, shift_ref[0])
    cells, own = diffusion_ref[...], own_ref[...]
    east = 0.5 * (cells + roll(cells, -1, 0)) - mean
    north = 0.5 * (cells + roll(cells, -1, 1)) - mean
    flux_x = east * (roll(own, -1, 0) - own)
    flux_y = north * (roll(own, -1, 1) - own)
    spread = flux_x - roll(flux_x, 1, 0) + flux_y - roll(flux_y, 1, 1)
    cube = jnp.where(adjoint_ref[0] == 1, 0.0, 1.0) * (reaction_ref[...] * own * own * own)
    out_ref[...] = source_ref[...] + (spread + shift * own - cube)


def forward_kernel(
    scale, adjoint_ref, core_ref, side_ref, own_ref, partner_ref, reaction_ref, x_ref, y_ref, keep_ref, send_ref, work_ref
):
    partner = partner_ref[...]
    adjoint_part = 3.0 * reaction_ref[...] * partner * partner * own_ref[...] - partner
    side = side_ref[...] - jnp.where(adjoint_ref[0] == 1, adjoint_part, gamma_inv * partner)
    rows = product(parts(x_ref), split(side))
    work_ref[...] = product(split(rows), parts(y_ref)) * scale
    half = keep_ref.shape[0]
    core = core_ref[0]
    keep_ref[...] = work_ref[pl.ds(pl.multiple_of(core * half, half), half), :]
    send_ref[...] = work_ref[pl.ds(pl.multiple_of((1 - core) * half, half), half), :]


def inverse_kernel(core_ref, last_ref, keep_ref, came_ref, own_ref, x_ref, y_ref, out_ref, work_ref):
    half = keep_ref.shape[0]
    core = core_ref[0]
    work_ref[pl.ds(pl.multiple_of(core * half, half), half), :] = keep_ref[...]
    work_ref[pl.ds(pl.multiple_of((1 - core) * half, half), half), :] = came_ref[...]
    rows = product(split(work_ref[...]), parts(y_ref))
    former = jnp.where(last_ref[0] == 1, 1.0, 0.0) * own_ref[...]
    out_ref[...] = former + product(parts(x_ref), split(rows))


def call(kernel, scalars, arrays, out_shapes, scratch=(), flops=0):
    spec_scalar = pl.BlockSpec(memory_space=pltpu.SMEM)
    spec_array = pl.BlockSpec(memory_space=pltpu.VMEM)
    return pl.pallas_call(
        kernel,
        out_shape=[jax.ShapeDtypeStruct(shape, jnp.float32) for shape in out_shapes],
        in_specs=[spec_scalar] * len(scalars) + [spec_array] * len(arrays),
        out_specs=[spec_array] * len(out_shapes),
        scratch_shapes=[pltpu.VMEM(shape, jnp.float32) for shape in scratch],
        compiler_params=pltpu.CompilerParams(vmem_limit_bytes=16 * 1024 * 1024),
    )(*scalars, *arrays)


def swap(values, axis, mask):
    return lax.ppermute(values, axis, [(i, i ^ mask) for i in range(lax.axis_size(axis))])


def power(base, exponent):
    result = None
    while exponent:
        if exponent & 1:
            result = base if result is None else result * base
        base, exponent = base * base, exponent >> 1
    return result


def solve_steps(kept, came, rate, alpha, place, total):
    odd = (place & 1) == 1
    first, second = jnp.where(odd, came, kept), jnp.where(odd, kept, came)
    carry = rate * (rate * first + second)
    levels = []
    bit, steps = 1, 2
    while steps < total:
        count = 4 if steps * 4 <= total else 2
        factor = power(rate, steps)
        powers = [jnp.ones_like(rate)]
        for _ in range(count - 1):
            powers.append(powers[-1] * factor)
        mine = (place >> bit) & (count - 1)
        alone = count == 2 and bit > 1
        masks = [number << bit for number in range(1, count)]
        if alone:
            masks = [(1 << bit) | (1 << (bit - 1))]
        pieces = [carry] + [swap(carry, "tm", mask) for mask in masks]
        whole, before = jnp.zeros_like(rate), jnp.zeros_like(rate)
        for number, piece in enumerate(pieces):
            index = mine ^ number
            weight, ahead = powers[count - 1], jnp.zeros_like(rate)
            for choice in range(1, count):
                weight = jnp.where(index == choice, powers[count - 1 - choice], weight)
            for gap in range(1, count):
                ahead = jnp.where(mine - index == gap, powers[gap - 1], ahead)
            whole = whole + weight * piece
            before = before + ahead * piece
        reach = powers[0]
        for choice in range(1, count):
            reach = jnp.where(mine == choice, powers[choice], reach)
        levels.append((reach, before))
        carry, bit, steps = whole, bit + count.bit_length() - 1, steps * count
    entering = alpha * carry / (1.0 - alpha * power(rate, total))
    for reach, before in reversed(levels):
        entering = reach * entering + before
    first = rate * (entering + first)
    second = rate * (first + second)
    return jnp.where(odd, second, first), jnp.where(odd, first, second)


def on_device(fields, forcing, diffusion, reaction, wrap_factor, mean_diffusion, spectral_shift):
    total = lax.axis_size("tm")
    own, source = fields[0, 0], forcing[0, 0]
    grid_x, grid_y = own.shape
    half = grid_x // 2
    scale = 1.0 / (grid_x * grid_y)
    x_table, y_table = cas_table(grid_x), cas_table(grid_y)
    group, step = lax.axis_index("pair"), lax.axis_index("tm")
    place = jnp.where(group == 1, total - 1 - step, step)
    core = step & 1

    def scalar(value):
        return value.astype(jnp.int32).reshape(1)

    adjoint, last, side_of = scalar(group), scalar(place == total - 1), scalar(core)
    eigen_x = lax.dynamic_slice_in_dim(eigenvalues(grid_x), core * half, half, 0)
    rate = 1.0 / (1.0 + spectral_shift + mean_diffusion * (eigen_x[:, None] + eigenvalues(grid_y)[None, :]))

    for _ in range(ITERS):
        partner = swap(own, "pair", 1)
        (side,) = call(
            own_kernel,
            (mean_diffusion, spectral_shift, adjoint, last),
            (own, source, diffusion, reaction),
            [own.shape],
        )
        keep, send = call(
            functools.partial(forward_kernel, scale),
            (adjoint, side_of),
            (side, own, partner, reaction, x_table, y_table),
            [(half, grid_y)] * 2,
            [own.shape],
        )
        keep, send = solve_steps(keep, swap(send, "tm", 1), rate, wrap_factor, place, total)
        (own,) = call(
            inverse_kernel,
            (side_of, last),
            (keep, swap(send, "tm", 1), own, x_table, y_table),
            [own.shape],
            [own.shape],
        )
    return own[None, None]


def solution(mesh):
    in_specs = (P("pair", "tm", None, None), P("pair", "tm", None, None), P(), P(), P(), P(), P())
    out_specs = P("pair", "tm", None, None)
    return jax.shard_map(
        on_device, mesh=mesh, in_specs=in_specs, out_specs=out_specs, check_vma=False
    )
```

time: 80.3 us -> 63.1 us (0.79)
  blocking collectives: 25 us -> 0 us
  starting transfers between devices: 12.7 us -> 19.4 us
  waiting for transfers between devices: 28.1 us -> 30.9 us
  local copies, waits for them, and re-layouts: 6.39 us -> 4.57 us
  other arithmetic: 0.08 us -> 1.6 us
  Pallas kernels: 5.5 us -> 4.19 us
    all_to_all x2 -> x0, blocking collectives: 25 us -> none  [exchange(): return lax.all_to_all(values, AXES, 0, 0, tiled=True)]
    ppermute x3 -> x14, waiting for transfers between devices: 14.1 us -> 30.9 us  [swap(): lax.ppermute(values, axis, [(i, i ^ mask) for i in range(lax.axis_size(ax...]
    all_to_all x2 -> x0, waiting for transfers between devices: 14 us -> none  [exchange(): return lax.all_to_all(values, AXES, 0, 0, tiled=True)]
    ppermute x3 -> x14, starting transfers between devices: 5.97 us -> 19.4 us  [swap(): lax.ppermute(values, axis, [(i, i ^ mask) for i in range(lax.axis_size(ax...]
    all_to_all x2 -> x0, starting transfers between devices: 6.72 us -> none  [exchange(): return lax.all_to_all(values, AXES, 0, 0, tiled=True)]
    unnamed x24 -> x20, local copies, waits for them, and re-layouts: 6.3 us -> 4.49 us
    pallas_call x5 -> x6, Pallas kernels: 5.5 us -> 4.19 us  [call(): pl.pallas_call(kernel, out_shape=[jax.ShapeDtypeStruct(shape, jnp.float32...]
    select_n x0 -> x4, other arithmetic: none -> 1.02 us  [solve_steps(): return (jnp.where(odd, second, first), jnp.where(odd, first, second))]
  transfers between devices with their start and end apart: 5 -> 14, of which waited for: 5 -> 13; matrix products, arithmetic and copies ran while one was open for 0% -> 0% of each run, Pallas kernels for 0% -> 1%
where the time goes in v4:
time: 63.1 us; the launch traced here: 62.8 us
  waiting for transfers between devices  30.9 us (49%)
  starting transfers between devices  19.4 us (31%)
  local copies, waits for them, and re-layouts  4.57 us (7%)
  Pallas kernels  4.19 us (7%)
  between operations  2.13 us (3%)
  other arithmetic  1.6 us (3%)
    ppermute x14, waiting for transfers between devices, swap(): lax.ppermute(values, axis, [(i, i ^ mask) for i in range(lax.axis_size(ax...  30.9 us
    ppermute x14, starting transfers between devices, swap(): lax.ppermute(values, axis, [(i, i ^ mask) for i in range(lax.axis_size(ax...  19.4 us
    unnamed x20, local copies, waits for them, and re-layouts  4.49 us
    pallas_call x6, Pallas kernels, call(): pl.pallas_call(kernel, out_shape=[jax.ShapeDtypeStruct(shape, jnp.float32...  4.19 us
  transfers between devices with their start and end apart: 14, of which 13 were waited for; matrix products, arithmetic and copies ran while one was open for 0% of the time, Pallas kernels for 1%

profile of v4, /device:TPU:0, one launch (start us, length us, event | category | flops | bytes accessed | tf_op | source)
XLA Modules:
  0.0 62.8 jit_solution(7747209108376905775)
XLA Ops:
  0.0 3.0 %collective-permute-start = (f32[256,256]{1,0:T(8,128)}, f32[256,256]{1,0:T(8,128)S(1)}, u32[]{:S(2)}, u32[]{:S(2)}) collective-permute-start(f32[256,256]{1,0:T(8,128)} %bitcast.19), channel_id=1, source_target_pairs={{0,16},{16,0},{1,17},{17,1},{2,18},{18,2},{3,19},{19,3},{4,20},{20... | collective-permute-start | bytes 786440 | tf_op jit(solution)/shard_map/ppermute | solution.py:103
  4.3 0.9 %copy-done.1 = f32[256,256]{1,0:T(8,128)S(1)} copy-done((f32[256,256]{1,0:T(8,128)S(1)}, f32[256,256]{1,0:T(8,128)}, u32[]{:S(2)}) %copy-start.1) | copy-done | bytes 262168
  5.2 0.9 %copy-done.3 = f32[1,1,256,256]{3,2,1,0:T(8,128)S(1)} copy-done((f32[1,1,256,256]{3,2,1,0:T(8,128)S(1)}, f32[1,1,256,256]{3,2,1,0:T(8,128)}, u32[]{:S(2)}) %copy-start.3) | copy-done | bytes 262168
  6.2 0.9 %copy-done.5 = f32[1,1,256,256]{3,2,1,0:T(8,128)S(1)} copy-done((f32[1,1,256,256]{3,2,1,0:T(8,128)S(1)}, f32[1,1,256,256]{3,2,1,0:T(8,128)}, u32[]{:S(2)}) %copy-start.5) | copy-done | bytes 262168
  7.1 0.9 %copy-done.7 = f32[256,256]{1,0:T(8,128)S(1)} copy-done((f32[256,256]{1,0:T(8,128)S(1)}, f32[256,256]{1,0:T(8,128)}, u32[]{:S(2)}) %copy-start.7) | copy-done | bytes 262168
  8.5 1.0 %collective-permute-done.partner_ref = f32[256,256]{1,0:T(8,128)S(1)} collective-permute-done((f32[256,256]{1,0:T(8,128)}, f32[256,256]{1,0:T(8,128)S(1)}, u32[]{:S(2)}, u32[]{:S(2)}) %collective-permute-start) | collective-permute-done | bytes 262176 | tf_op jit(solution)/shard_map/ppermute | solution.py:103
  9.5 0.7 %shard_map.110 = (f32[128,256]{1,0:T(8,128)S(1)}, f32[128,256]{1,0:T(8,128)S(1)}) custom-call(s32[1]{0:T(128)} %bitcast.5.adjoint_ref, s32[1]{0:T(128)} %bitcast.core_ref, f32[256,256]{1,0:T(8,128)S(1)} %shard_map.109.side_ref, f32[256,256]{1,0:T(8,128)S(1)} %bitcast.21, f32[256,256]{1,0:T(8,128)S(1)} %collective-permute-done.partner_ref, ...), custom_call_target="tpu_custom_call" | custom-call | tf_op jit(solution)/shard_map/pallas_call | solution.py:92
  10.3 0.7 %copy-done.9 = f32[256]{0:T(256)S(1)} copy-done((f32[256]{0:T(256)S(1)}, f32[256]{0:T(256)}, u32[]{:S(2)}) %copy-start.9) | copy-done | bytes 1048
  11.0 0.6 collective-permute-done.1
  11.7 2.8 %collective-permute-start.4 = (f32[128,256]{1,0:T(8,128)S(1)}, f32[128,256]{1,0:T(8,128)S(1)}, u32[]{:S(2)}, u32[]{:S(2)}) collective-permute-start(f32[128,256]{1,0:T(8,128)S(1)} %add_multiply_fusion.5), channel_id=1, source_target_pairs={{0,6},{1,7},{2,4},{3,5},{4,2},{5,3},{6,0},{7,1},{8,14},{9,15},{10,... | collective-permute-start | bytes 393224 | tf_op jit(solution)/shard_map/ppermute | solution.py:103
  14.5 0.5 collective-permute-start.3
  15.3 3.7 %collective-permute-done.4 = f32[128,256]{1,0:T(8,128)S(1)} collective-permute-done((f32[128,256]{1,0:T(8,128)S(1)}, f32[128,256]{1,0:T(8,128)S(1)}, u32[]{:S(2)}, u32[]{:S(2)}) %collective-permute-start.4) | collective-permute-done | bytes 131104 | tf_op jit(solution)/shard_map/ppermute | solution.py:103
  19.0 2.3 %collective-permute-done.3 = f32[128,256]{1,0:T(8,128)S(1)} collective-permute-done((f32[128,256]{1,0:T(8,128)S(1)}, f32[128,256]{1,0:T(8,128)S(1)}, u32[]{:S(2)}, u32[]{:S(2)}) %collective-permute-start.3) | collective-permute-done | bytes 131104 | tf_op jit(solution)/shard_map/ppermute | solution.py:103
  21.5 3.7 %collective-permute-start.5 = (f32[128,256]{1,0:T(8,128)S(1)}, f32[128,256]{1,0:T(8,128)S(1)}, u32[]{:S(2)}, u32[]{:S(2)}) collective-permute-start(f32[128,256]{1,0:T(8,128)S(1)} %multiply_add_fusion.1), channel_id=1, source_target_pairs={{0,12},{1,13},{2,14},{3,15},{4,8},{5,9},{6,10},{7,11},{8,4},{9,5},... | collective-permute-start | bytes 393224 | tf_op jit(solution)/shard_map/ppermute | solution.py:103
  25.8 2.7 %collective-permute-done.5 = f32[128,256]{1,0:T(8,128)S(1)} collective-permute-done((f32[128,256]{1,0:T(8,128)S(1)}, f32[128,256]{1,0:T(8,128)S(1)}, u32[]{:S(2)}, u32[]{:S(2)}) %collective-permute-start.5) | collective-permute-done | bytes 131104 | tf_op jit(solution)/shard_map/ppermute | solution.py:103
  28.5 0.4 fusion.2
  29.1 1.2 %collective-permute-done.6.came_ref = f32[128,256]{1,0:T(8,128)S(1)} collective-permute-done((f32[128,256]{1,0:T(8,128)S(1)}, f32[128,256]{1,0:T(8,128)S(1)}, u32[]{:S(2)}, u32[]{:S(2)}) %collective-permute-start.6) | collective-permute-done | bytes 131104 | tf_op jit(solution)/shard_map/ppermute | solution.py:103
  30.3 0.7 %shard_map.111.own_ref = f32[256,256]{1,0:T(8,128)S(1)} custom-call(s32[1]{0:T(128)} %bitcast.core_ref, s32[1]{0:T(128)} %bitcast.1.last_ref, f32[128,256]{1,0:T(8,128)S(1)} %fusion.3.keep_ref, f32[128,256]{1,0:T(8,128)S(1)} %collective-permute-done.6.came_ref, f32[256,256]{1,0:T(8,128)S(1)} %bitcast.22, bf16[2,256,256]{2,1,0:T(8,128)(2,1)S(1)} %copy-done, ...), custom_call_target="tpu_custom_call" | custom-call | tf_op jit(solution)/shard_map/pallas_call | solution.py:92
  31.0 1.6 %collective-permute-start.7 = (f32[256,256]{1,0:T(8,128)S(1)}, f32[256,256]{1,0:T(8,128)S(1)}, u32[]{:S(2)}, u32[]{:S(2)}) collective-permute-start(f32[256,256]{1,0:T(8,128)S(1)} %shard_map.111.own_ref), channel_id=1, source_target_pairs={{0,16},{16,0},{1,17},{17,1},{2,18},{18,2},{3,19},{19,3},{4,20},{20... | collective-permute-start | bytes 786440 | tf_op jit(solution)/shard_map/ppermute | solution.py:103
  33.0 6.4 %collective-permute-done.7.partner_ref = f32[256,256]{1,0:T(8,128)S(1)} collective-permute-done((f32[256,256]{1,0:T(8,128)S(1)}, f32[256,256]{1,0:T(8,128)S(1)}, u32[]{:S(2)}, u32[]{:S(2)}) %collective-permute-start.7) | collective-permute-done | bytes 262176 | tf_op jit(solution)/shard_map/ppermute | solution.py:103
  39.4 0.7 %shard_map.113 = (f32[128,256]{1,0:T(8,128)S(1)}, f32[128,256]{1,0:T(8,128)S(1)}) custom-call(s32[1]{0:T(128)} %bitcast.5.adjoint_ref, s32[1]{0:T(128)} %bitcast.core_ref, f32[256,256]{1,0:T(8,128)S(1)} %shard_map.112.side_ref, f32[256,256]{1,0:T(8,128)S(1)} %shard_map.111.own_ref, f32[256,256]{1,0:T(8,128)S(1)} %collective-permute-done.7.partner_ref, ...), custom_call_target="tpu_custom_call" | custom-call | tf_op jit(solution)/shard_map/pallas_call | solution.py:92
  40.2 1.3 %collective-permute-done.8 = f32[128,256]{1,0:T(8,128)S(1)} collective-permute-done((f32[128,256]{1,0:T(8,128)S(1)}, f32[128,256]{1,0:T(8,128)S(1)}, u32[]{:S(2)}, u32[]{:S(2)}) %collective-permute-start.8) | collective-permute-done | bytes 131104 | tf_op jit(solution)/shard_map/ppermute | solution.py:103
  41.6 3.8 %collective-permute-start.11 = (f32[128,256]{1,0:T(8,128)S(1)}, f32[128,256]{1,0:T(8,128)S(1)}, u32[]{:S(2)}, u32[]{:S(2)}) collective-permute-start(f32[128,256]{1,0:T(8,128)S(1)} %add_multiply_fusion.2), channel_id=1, source_target_pairs={{0,6},{1,7},{2,4},{3,5},{4,2},{5,3},{6,0},{7,1},{8,14},{9,15},{10,... | collective-permute-start | bytes 393224 | tf_op jit(solution)/shard_map/ppermute | solution.py:103
  45.4 0.6 %collective-permute-start.9 = (f32[128,256]{1,0:T(8,128)S(1)}, f32[128,256]{1,0:T(8,128)S(1)}, u32[]{:S(2)}, u32[]{:S(2)}) collective-permute-start(f32[128,256]{1,0:T(8,128)S(1)} %add_multiply_fusion.2), channel_id=1, source_target_pairs={{0,2},{1,3},{2,0},{3,1},{4,6},{5,7},{6,4},{7,5},{8,10},{9,11},{10,... | collective-permute-start | bytes 393224 | tf_op jit(solution)/shard_map/ppermute | solution.py:103
  46.1 3.6 %collective-permute-done.11 = f32[128,256]{1,0:T(8,128)S(1)} collective-permute-done((f32[128,256]{1,0:T(8,128)S(1)}, f32[128,256]{1,0:T(8,128)S(1)}, u32[]{:S(2)}, u32[]{:S(2)}) %collective-permute-start.11) | collective-permute-done | bytes 131104 | tf_op jit(solution)/shard_map/ppermute | solution.py:103
  49.7 1.7 %collective-permute-done.10 = f32[128,256]{1,0:T(8,128)S(1)} collective-permute-done((f32[128,256]{1,0:T(8,128)S(1)}, f32[128,256]{1,0:T(8,128)S(1)}, u32[]{:S(2)}, u32[]{:S(2)}) %collective-permute-start.10) | collective-permute-done | bytes 131104 | tf_op jit(solution)/shard_map/ppermute | solution.py:103
  51.4 0.7 %collective-permute-done.9 = f32[128,256]{1,0:T(8,128)S(1)} collective-permute-done((f32[128,256]{1,0:T(8,128)S(1)}, f32[128,256]{1,0:T(8,128)S(1)}, u32[]{:S(2)}, u32[]{:S(2)}) %collective-permute-start.9) | collective-permute-done | bytes 131104 | tf_op jit(solution)/shard_map/ppermute | solution.py:103
  52.2 3.0 %collective-permute-start.12 = (f32[128,256]{1,0:T(8,128)S(1)}, f32[128,256]{1,0:T(8,128)S(1)}, u32[]{:S(2)}, u32[]{:S(2)}) collective-permute-start(f32[128,256]{1,0:T(8,128)S(1)} %multiply_add_fusion), channel_id=1, source_target_pairs={{0,12},{1,13},{2,14},{3,15},{4,8},{5,9},{6,10},{7,11},{8,4},{9,5},... | collective-permute-start | bytes 393224 | tf_op jit(solution)/shard_map/ppermute | solution.py:103
  55.2 4.4 %collective-permute-done.12 = f32[128,256]{1,0:T(8,128)S(1)} collective-permute-done((f32[128,256]{1,0:T(8,128)S(1)}, f32[128,256]{1,0:T(8,128)S(1)}, u32[]{:S(2)}, u32[]{:S(2)}) %collective-permute-start.12) | collective-permute-done | bytes 131104 | tf_op jit(solution)/shard_map/ppermute | solution.py:103
  59.6 0.4 fusion.4
  60.2 1.2 %collective-permute-done.13.came_ref = f32[128,256]{1,0:T(8,128)S(1)} collective-permute-done((f32[128,256]{1,0:T(8,128)S(1)}, f32[128,256]{1,0:T(8,128)S(1)}, u32[]{:S(2)}, u32[]{:S(2)}) %collective-permute-start.13) | collective-permute-done | bytes 131104 | tf_op jit(solution)/shard_map/ppermute | solution.py:103
  61.4 1.4 %shard_map.114 = f32[256,256]{1,0:T(8,128)} custom-call(s32[1]{0:T(128)} %bitcast.core_ref, s32[1]{0:T(128)} %bitcast.1.last_ref, f32[128,256]{1,0:T(8,128)S(1)} %fusion.5.keep_ref, f32[128,256]{1,0:T(8,128)S(1)} %collective-permute-done.13.came_ref, f32[256,256]{1,0:T(8,128)S(1)} %shard_map.111.own_ref, bf16[2,256,256]{2,1,0:T(8,128)(2,1)S(1)} %copy-done, ...), custom_call_target="tpu_custom_call" | custom-call | tf_op jit(solution)/shard_map/pallas_call | solution.py:92
  (31 shorter events, 2.3 us)
Async XLA Ops:
  0.0 9.5 %collective-permute-start = (f32[256,256]{1,0:T(8,128)}, f32[256,256]{1,0:T(8,128)S(1)}, u32[]{:S(2)}, u32[]{:S(2)}) collective-permute-start(f32[256,256]{1,0:T(8,128)} %bitcast.19), channel_id=1, source_target_pairs={{0,16},{16,0},{1,17},{17,1},{2,18},{18,2},{3,19},{19,3},{4,20},{20... | collective-permute-start | bytes 786440 | tf_op jit(solution)/shard_map/ppermute | solution.py:103
  4.3 1.0 %copy-start.1 = (f32[256,256]{1,0:T(8,128)S(1)}, f32[256,256]{1,0:T(8,128)}, u32[]{:S(2)}) copy-start(f32[256,256]{1,0:T(8,128)} %reaction_ref.7) | copy-start | bytes 786436
  5.2 0.9 %copy-start.3 = (f32[1,1,256,256]{3,2,1,0:T(8,128)S(1)}, f32[1,1,256,256]{3,2,1,0:T(8,128)}, u32[]{:S(2)}) copy-start(f32[1,1,256,256]{3,2,1,0:T(8,128)} %param.11) | copy-start | bytes 786436
  6.2 0.9 %copy-start.5 = (f32[1,1,256,256]{3,2,1,0:T(8,128)S(1)}, f32[1,1,256,256]{3,2,1,0:T(8,128)}, u32[]{:S(2)}) copy-start(f32[1,1,256,256]{3,2,1,0:T(8,128)} %param.12) | copy-start | bytes 786436
  7.1 0.9 %copy-start.7 = (f32[256,256]{1,0:T(8,128)S(1)}, f32[256,256]{1,0:T(8,128)}, u32[]{:S(2)}) copy-start(f32[256,256]{1,0:T(8,128)} %diffusion_ref.3) | copy-start | bytes 786436
  8.1 1.4 %copy-start = (bf16[2,256,256]{2,1,0:T(8,128)(2,1)S(1)}, bf16[2,256,256]{2,1,0:T(8,128)(2,1)}, u32[]{:S(2)}) copy-start(bf16[2,256,256]{2,1,0:T(8,128)(2,1)} %constant.34.clone.x_ref.y_ref) | copy-start | bytes 786436
  8.1 1.4 %copy-start.2 = (f32[256,256]{1,0:T(8,128)S(1)}, f32[256,256]{1,0:T(8,128)}, u32[]{:S(2)}) copy-start(f32[256,256]{1,0:T(8,128)} %reaction_ref.7) | copy-start | bytes 786436
  10.2 1.4 %collective-permute-start.1 = (f32[128,256]{1,0:T(8,128)S(1)}, f32[128,256]{1,0:T(8,128)S(1)}, u32[]{:S(2)}, u32[]{:S(2)}) collective-permute-start(f32[128,256]{1,0:T(8,128)S(1)} %get-tuple-element.9), channel_id=1, source_target_pairs={{0,1},{1,0},{2,3},{3,2},{4,5},{5,4},{6,7},{7,6},{8,9},{9,8},{10,11... | collective-permute-start | bytes 393224 | tf_op jit(solution)/shard_map/ppermute | solution.py:103
  10.3 0.7 %copy-start.9 = (f32[256]{0:T(256)S(1)}, f32[256]{0:T(256)}, u32[]{:S(2)}) copy-start(f32[256]{0:T(256)} %constant.35.clone) | copy-start | bytes 3076
  11.7 7.3 %collective-permute-start.4 = (f32[128,256]{1,0:T(8,128)S(1)}, f32[128,256]{1,0:T(8,128)S(1)}, u32[]{:S(2)}, u32[]{:S(2)}) collective-permute-start(f32[128,256]{1,0:T(8,128)S(1)} %add_multiply_fusion.5), channel_id=1, source_target_pairs={{0,6},{1,7},{2,4},{3,5},{4,2},{5,3},{6,0},{7,1},{8,14},{9,15},{10,... | collective-permute-start | bytes 393224 | tf_op jit(solution)/shard_map/ppermute | solution.py:103
  14.5 6.8 %collective-permute-start.3 = (f32[128,256]{1,0:T(8,128)S(1)}, f32[128,256]{1,0:T(8,128)S(1)}, u32[]{:S(2)}, u32[]{:S(2)}) collective-permute-start(f32[128,256]{1,0:T(8,128)S(1)} %add_multiply_fusion.5), channel_id=1, source_target_pairs={{0,4},{1,5},{2,6},{3,7},{4,0},{5,1},{6,2},{7,3},{8,12},{9,13},{10,... | collective-permute-start | bytes 393224 | tf_op jit(solution)/shard_map/ppermute | solution.py:103
  14.9 6.3 %collective-permute-start.2 = (f32[128,256]{1,0:T(8,128)S(1)}, f32[128,256]{1,0:T(8,128)S(1)}, u32[]{:S(2)}, u32[]{:S(2)}) collective-permute-start(f32[128,256]{1,0:T(8,128)S(1)} %add_multiply_fusion.5), channel_id=1, source_target_pairs={{0,2},{1,3},{2,0},{3,1},{4,6},{5,7},{6,4},{7,5},{8,10},{9,11},{10,... | collective-permute-start | bytes 393224 | tf_op jit(solution)/shard_map/ppermute | solution.py:103
  21.5 7.0 %collective-permute-start.5 = (f32[128,256]{1,0:T(8,128)S(1)}, f32[128,256]{1,0:T(8,128)S(1)}, u32[]{:S(2)}, u32[]{:S(2)}) collective-permute-start(f32[128,256]{1,0:T(8,128)S(1)} %multiply_add_fusion.1), channel_id=1, source_target_pairs={{0,12},{1,13},{2,14},{3,15},{4,8},{5,9},{6,10},{7,11},{8,4},{9,5},... | collective-permute-start | bytes 393224 | tf_op jit(solution)/shard_map/ppermute | solution.py:103
  28.9 1.4 %collective-permute-start.6 = (f32[128,256]{1,0:T(8,128)S(1)}, f32[128,256]{1,0:T(8,128)S(1)}, u32[]{:S(2)}, u32[]{:S(2)}) collective-permute-start(f32[128,256]{1,0:T(8,128)S(1)} %get-tuple-element.15), channel_id=1, source_target_pairs={{0,1},{1,0},{2,3},{3,2},{4,5},{5,4},{6,7},{7,6},{8,9},{9,8},{10,11... | collective-permute-start | bytes 393224 | tf_op jit(solution)/shard_map/ppermute | solution.py:103
  29.0 1.3 %copy-start.4 = (f32[1,1,256,256]{3,2,1,0:T(8,128)S(1)}, f32[1,1,256,256]{3,2,1,0:T(8,128)}, u32[]{:S(2)}) copy-start(f32[1,1,256,256]{3,2,1,0:T(8,128)} %param.11) | copy-start | bytes 786436
  29.1 3.5 %copy-start.6 = (f32[1,1,256,256]{3,2,1,0:T(8,128)S(1)}, f32[1,1,256,256]{3,2,1,0:T(8,128)}, u32[]{:S(2)}) copy-start(f32[1,1,256,256]{3,2,1,0:T(8,128)} %param.12) | copy-start | bytes 786436
  29.1 3.5 %copy-start.8 = (f32[256,256]{1,0:T(8,128)S(1)}, f32[256,256]{1,0:T(8,128)}, u32[]{:S(2)}) copy-start(f32[256,256]{1,0:T(8,128)} %diffusion_ref.3) | copy-start | bytes 786436
  31.0 8.4 %collective-permute-start.7 = (f32[256,256]{1,0:T(8,128)S(1)}, f32[256,256]{1,0:T(8,128)S(1)}, u32[]{:S(2)}, u32[]{:S(2)}) collective-permute-start(f32[256,256]{1,0:T(8,128)S(1)} %shard_map.111.own_ref), channel_id=1, source_target_pairs={{0,16},{16,0},{1,17},{17,1},{2,18},{18,2},{3,19},{19,3},{4,20},{20... | collective-permute-start | bytes 786440 | tf_op jit(solution)/shard_map/ppermute | solution.py:103
  40.1 1.4 %collective-permute-start.8 = (f32[128,256]{1,0:T(8,128)S(1)}, f32[128,256]{1,0:T(8,128)S(1)}, u32[]{:S(2)}, u32[]{:S(2)}) collective-permute-start(f32[128,256]{1,0:T(8,128)S(1)} %get-tuple-element.11), channel_id=1, source_target_pairs={{0,1},{1,0},{2,3},{3,2},{4,5},{5,4},{6,7},{7,6},{8,9},{9,8},{10,11... | collective-permute-start | bytes 393224 | tf_op jit(solution)/shard_map/ppermute | solution.py:103
  41.6 8.1 %collective-permute-start.11 = (f32[128,256]{1,0:T(8,128)S(1)}, f32[128,256]{1,0:T(8,128)S(1)}, u32[]{:S(2)}, u32[]{:S(2)}) collective-permute-start(f32[128,256]{1,0:T(8,128)S(1)} %add_multiply_fusion.2), channel_id=1, source_target_pairs={{0,6},{1,7},{2,4},{3,5},{4,2},{5,3},{6,0},{7,1},{8,14},{9,15},{10,... | collective-permute-start | bytes 393224 | tf_op jit(solution)/shard_map/ppermute | solution.py:103
  45.4 5.9 %collective-permute-start.10 = (f32[128,256]{1,0:T(8,128)S(1)}, f32[128,256]{1,0:T(8,128)S(1)}, u32[]{:S(2)}, u32[]{:S(2)}) collective-permute-start(f32[128,256]{1,0:T(8,128)S(1)} %add_multiply_fusion.2), channel_id=1, source_target_pairs={{0,4},{1,5},{2,6},{3,7},{4,0},{5,1},{6,2},{7,3},{8,12},{9,13},{10,... | collective-permute-start | bytes 393224 | tf_op jit(solution)/shard_map/ppermute | solution.py:103
  45.4 6.6 %collective-permute-start.9 = (f32[128,256]{1,0:T(8,128)S(1)}, f32[128,256]{1,0:T(8,128)S(1)}, u32[]{:S(2)}, u32[]{:S(2)}) collective-permute-start(f32[128,256]{1,0:T(8,128)S(1)} %add_multiply_fusion.2), channel_id=1, source_target_pairs={{0,2},{1,3},{2,0},{3,1},{4,6},{5,7},{6,4},{7,5},{8,10},{9,11},{10,... | collective-permute-start | bytes 393224 | tf_op jit(solution)/shard_map/ppermute | solution.py:103
  52.2 7.4 %collective-permute-start.12 = (f32[128,256]{1,0:T(8,128)S(1)}, f32[128,256]{1,0:T(8,128)S(1)}, u32[]{:S(2)}, u32[]{:S(2)}) collective-permute-start(f32[128,256]{1,0:T(8,128)S(1)} %multiply_add_fusion), channel_id=1, source_target_pairs={{0,12},{1,13},{2,14},{3,15},{4,8},{5,9},{6,10},{7,11},{8,4},{9,5},... | collective-permute-start | bytes 393224 | tf_op jit(solution)/shard_map/ppermute | solution.py:103
  60.0 1.4 %collective-permute-start.13 = (f32[128,256]{1,0:T(8,128)S(1)}, f32[128,256]{1,0:T(8,128)S(1)}, u32[]{:S(2)}, u32[]{:S(2)}) collective-permute-start(f32[128,256]{1,0:T(8,128)S(1)} %get-tuple-element.13), channel_id=1, source_target_pairs={{0,1},{1,0},{2,3},{3,2},{4,5},{5,4},{6,7},{7,6},{8,9},{9,8},{10,11... | collective-permute-start | bytes 393224 | tf_op jit(solution)/shard_map/ppermute | solution.py:103

commit v5 on v4

v5 whole, which is shorter than its diff:
```python
import functools
import math

import jax
import jax.numpy as jnp
import ml_dtypes
import numpy as np
from jax import lax
from jax.experimental import pallas as pl
from jax.experimental.pallas import tpu as pltpu
from jax.sharding import PartitionSpec as P

ITERS = 2

gamma_inv = 0.5


def cas_table(length):
    places = np.arange(length)
    angles = (places[:, None] * places[None, :] % length) * (2.0 * np.pi / length)
    table = np.cos(angles) + np.sin(angles)
    high = table.astype(ml_dtypes.bfloat16)
    low = (table - high.astype(np.float64)).astype(ml_dtypes.bfloat16)
    return jnp.asarray(np.stack([high, low]))


def eigenvalues(length):
    return jnp.asarray((4.0 * np.sin(np.arange(length) * (np.pi / length)) ** 2).astype(np.float32))


def split(values):
    high = values.astype(jnp.bfloat16)
    return high, (values - high.astype(jnp.float32)).astype(jnp.bfloat16)


def parts(table_ref):
    return table_ref[0], table_ref[1]


def product(left, right):
    def one(a, b):
        return jnp.dot(a, b, preferred_element_type=jnp.float32)

    return one(left[0], right[0]) + (one(left[0], right[1]) + one(left[1], right[0]))


def roll(values, shift, axis):
    return pltpu.roll(values, shift % values.shape[axis], axis)


def own_kernel(mean_ref, shift_ref, adjoint_ref, last_ref, own_ref, source_ref, diffusion_ref, reaction_ref, out_ref):
    last = last_ref[0] == 1
    mean = jnp.where(last, 0.0, mean_ref[0])
    shift = jnp.where(last, -1.0, shift_ref[0])
    cells, own = diffusion_ref[...], own_ref[...]
    east = 0.5 * (cells + roll(cells, -1, 0)) - mean
    north = 0.5 * (cells + roll(cells, -1, 1)) - mean
    flux_x = east * (roll(own, -1, 0) - own)
    flux_y = north * (roll(own, -1, 1) - own)
    spread = flux_x - roll(flux_x, 1, 0) + flux_y - roll(flux_y, 1, 1)
    cube = jnp.where(adjoint_ref[0] == 1, 0.0, 1.0) * (reaction_ref[...] * own * own * own)
    out_ref[...] = source_ref[...] + (spread + shift * own - cube)


def gather_halves(core, work_ref, kept_ref, came_ref):
    half = kept_ref.shape[0]
    work_ref[pl.ds(pl.multiple_of(core * half, half), half), :] = kept_ref[...]
    work_ref[pl.ds(pl.multiple_of((1 - core) * half, half), half), :] = came_ref[...]
    return split(work_ref[...])


def forward(scale, adjoint, core, side, own, partner, reaction, x_table, y_table, keep_ref, send_ref, work_ref):
    adjoint_part = 3.0 * reaction * partner * partner * own - partner
    side = side - jnp.where(adjoint, adjoint_part, gamma_inv * partner)
    rows = product(x_table, split(side))
    work_ref[...] = product(split(rows), y_table) * scale
    half = keep_ref.shape[0]
    keep_ref[...] = work_ref[pl.ds(pl.multiple_of(core * half, half), half), :]
    send_ref[...] = work_ref[pl.ds(pl.multiple_of((1 - core) * half, half), half), :]


def first_kernel(
    scale, adjoint_ref, core_ref, side_ref, own_ref, partner_ref, reaction_ref, x_ref, y_ref, keep_ref, send_ref, work_ref
):
    forward(
        scale, adjoint_ref[0] == 1, core_ref[0], side_ref[...], own_ref[...], partner_ref[...], reaction_ref[...],
        parts(x_ref), parts(y_ref), keep_ref, send_ref, work_ref,
    )


def later_kernel(
    scale, adjoint_ref, core_ref, partner_last_ref,
    side_ref, own_ref, kept_ref, came_ref, former_ref, reaction_ref, x_ref, y_ref,
    keep_ref, send_ref, *refs,
):
    x_table, y_table = parts(x_ref), parts(y_ref)
    work_ref = refs[-1]
    rows = product(gather_halves(core_ref[0], work_ref, kept_ref, came_ref), y_table)
    former = jnp.where(partner_last_ref[0] == 1, 1.0, 0.0) * former_ref[...]
    partner = former + product(x_table, split(rows))
    if len(refs) > 1:
        refs[0][...] = partner
    forward(
        scale, adjoint_ref[0] == 1, core_ref[0], side_ref[...], own_ref[...], partner, reaction_ref[...],
        x_table, y_table, keep_ref, send_ref, work_ref,
    )


def inverse_kernel(core_ref, last_ref, kept_ref, came_ref, own_ref, x_ref, y_ref, out_ref, work_ref):
    rows = product(gather_halves(core_ref[0], work_ref, kept_ref, came_ref), parts(y_ref))
    former = jnp.where(last_ref[0] == 1, 1.0, 0.0) * own_ref[...]
    out_ref[...] = former + product(parts(x_ref), split(rows))


def steps_kernel(odd_ref, entering_ref, kept_ref, came_ref, rate_ref, new_ref, sent_ref):
    odd = odd_ref[0] == 1
    kept, came, rate = kept_ref[...], came_ref[...], rate_ref[...]
    first = rate * (entering_ref[...] + jnp.where(odd, came, kept))
    second = rate * (first + jnp.where(odd, kept, came))
    new_ref[...] = jnp.where(odd, second, first)
    sent_ref[...] = jnp.where(odd, first, second)


def call(kernel, scalars, arrays, out_shapes, scratch=(), flops=0):
    spec_scalar = pl.BlockSpec(memory_space=pltpu.SMEM)
    spec_array = pl.BlockSpec(memory_space=pltpu.VMEM)
    return pl.pallas_call(
        kernel,
        out_shape=[jax.ShapeDtypeStruct(shape, jnp.float32) for shape in out_shapes],
        in_specs=[spec_scalar] * len(scalars) + [spec_array] * len(arrays),
        out_specs=[spec_array] * len(out_shapes),
        scratch_shapes=[pltpu.VMEM(shape, jnp.float32) for shape in scratch],
        compiler_params=pltpu.CompilerParams(vmem_limit_bytes=16 * 1024 * 1024),
    )(*scalars, *arrays)


def swap(values, axis, mask):
    return lax.ppermute(values, axis, [(i, i ^ mask) for i in range(lax.axis_size(axis))])


def power(base, exponent):
    result = None
    while exponent:
        if exponent & 1:
            result = base if result is None else result * base
        base, exponent = base * base, exponent >> 1
    return result


def pick(options, index):
    result = options[0]
    for number in range(1, len(options)):
        result = jnp.where(index == number, options[number], result)
    return result


def scan_factors(rate, alpha, place, total):
    none = jnp.zeros_like(rate)
    pair = (pick([rate * rate, rate], place & 1), pick([rate, rate * rate], place & 1))
    all_masks, levels, reach = [], [], None
    bit, steps = 1, 2
    while steps < total:
        count = 4 if steps * 4 <= total else 2
        masks = [number << bit for number in range(1, count)]
        if count == 2 and bit > 1:
            masks = [(1 << bit) | (1 << (bit - 1))]
        factor = power(rate, steps)
        powers = [jnp.ones_like(rate)]
        for _ in range(count - 1):
            powers.append(powers[-1] * factor)
        mine = (place >> bit) & (count - 1)
        join = [pick(powers[::-1], mine ^ number) for number in range(count)]
        enter = [pick([none] + powers, jnp.maximum(mine - (mine ^ number), 0)) for number in range(count)]
        through = pick(powers, mine)
        bit, steps = bit + count.bit_length() - 1, steps * count
        if steps == total:
            round_trip = alpha / (1.0 - alpha * power(rate, total)) * through
            enter = [round_trip * one + two for one, two in zip(join, enter)]
        if reach is not None:
            enter = [reach * one for one in enter]
        reach = through if reach is None else reach * through
        all_masks.append(masks)
        levels.append((join, enter))
    pair, levels = lax.optimization_barrier((pair, levels))
    return pair, [(masks, *level) for masks, level in zip(all_masks, levels)]


def carry_in(kept, came, pair, levels, share):
    others = [swap(kept, "pair", 1), swap(came, "pair", 1)] if share else [None, None]
    carry = pair[0] * kept + pair[1] * came
    entering = jnp.zeros_like(carry)
    for masks, join, enter in levels[:-1]:
        pieces = [carry] + [swap(carry, "tm", mask) for mask in masks]
        carry = sum(one * piece for one, piece in zip(join, pieces))
        entering = entering + sum(one * piece for one, piece in zip(enter, pieces))
    carry, others[0] = lax.optimization_barrier((carry, others[0]))
    masks, _, enter = levels[-1]
    entering = lax.optimization_barrier(entering + enter[0] * carry)
    entering = entering + sum(one * swap(carry, "tm", mask) for one, mask in zip(enter[1:], masks))
    return lax.optimization_barrier((entering, others))


def on_device(fields, forcing, diffusion, reaction, wrap_factor, mean_diffusion, spectral_shift):
    total = lax.axis_size("tm")
    own, source = fields[0, 0], forcing[0, 0]
    grid_x, grid_y = own.shape
    half = grid_x // 2
    scale = 1.0 / (grid_x * grid_y)
    tables = cas_table(grid_x), cas_table(grid_y)
    group, step = lax.axis_index("pair"), lax.axis_index("tm")
    place = jnp.where(group == 1, total - 1 - step, step)
    other_place = total - 1 - place
    core = step & 1

    def scalar(value):
        return value.astype(jnp.int32).reshape(1)

    adjoint, side_of = scalar(group), scalar(core)
    odd, other_odd = scalar(place & 1), scalar(other_place & 1)
    last, other_last = scalar(place == total - 1), scalar(other_place == total - 1)
    eigen_x = lax.dynamic_slice_in_dim(eigenvalues(grid_x), core * half, half, 0)
    rate = 1.0 / (1.0 + spectral_shift + mean_diffusion * (eigen_x[:, None] + eigenvalues(grid_y)[None, :]))
    pair, levels = scan_factors(rate, wrap_factor, place, total)

    def own_side(own):
        (side,) = call(
            own_kernel,
            (mean_diffusion, spectral_shift, adjoint, last),
            (own, source, diffusion, reaction),
            [own.shape],
        )
        return side

    def both_steps(odd, entering, kept, came):
        return call(steps_kernel, (odd,), (entering, kept, came, rate), [kept.shape] * 2)

    partner = [swap(own, "pair", 1)]
    side = own_side(own)
    for iteration in range(ITERS):
        more = iteration + 1 < ITERS
        if iteration == 0:
            kept, sent = call(
                functools.partial(first_kernel, scale),
                (adjoint, side_of),
                (side, own, *partner, reaction, *tables),
                [(half, grid_y)] * 2,
                [own.shape],
            )
        else:
            kept, sent, *partner = call(
                functools.partial(later_kernel, scale),
                (adjoint, side_of, other_last),
                (side, own, other_kept, other_came, *partner, reaction, *tables),
                [(half, grid_y)] * 2 + [own.shape] * more,
                [own.shape],
            )
        came = swap(sent, "tm", 1)
        entering, other_sides = carry_in(kept, came, pair, levels, more)
        new, sent = both_steps(odd, entering, kept, came)
        if more:
            other_entering = swap(entering, "pair", 1)
        (own,) = call(
            inverse_kernel,
            (side_of, last),
            (new, swap(sent, "tm", 1), own, *tables),
            [own.shape],
            [own.shape],
        )
        if more:
            side = own_side(own)
            other_entering, side = lax.optimization_barrier((other_entering, side))
            other_kept, other_sent = both_steps(other_odd, other_entering, *other_sides)
            other_came = swap(other_sent, "tm", 1)
    return own[None, None]


def solution(mesh):
    in_specs = (P("pair", "tm", None, None), P("pair", "tm", None, None), P(), P(), P(), P(), P())
    out_specs = P("pair", "tm", None, None)
    return jax.shard_map(
        on_device, mesh=mesh, in_specs=in_specs, out_specs=out_specs, check_vma=False
    )
```

time: 63.1 us -> 59.6 us (0.945)
  waiting for transfers between devices: 30.9 us -> 27.1 us
  starting transfers between devices: 19.4 us -> 21.7 us
  local copies, waits for them, and re-layouts: 4.57 us -> 2.37 us
  Pallas kernels: 4.19 us -> 4.92 us
    ppermute x14 -> x17, waiting for transfers between devices: 30.9 us -> 27.1 us  [swap(): lax.ppermute(values, axis, [(i, i ^ mask) for i in range(lax.axis_size(ax...]
    ppermute x14 -> x17, starting transfers between devices: 19.4 us -> 21.7 us  [swap(): lax.ppermute(values, axis, [(i, i ^ mask) for i in range(lax.axis_size(ax...]
    unnamed x20 -> x24, local copies, waits for them, and re-layouts: 4.49 us -> 2.29 us
    select_n x4 -> x1, other arithmetic: 1.02 us -> 0.13 us  [pick(): result = jnp.where(index == number, options[number], result)]
    pallas_call x6 -> x9, Pallas kernels: 4.19 us -> 4.92 us  [call(): pl.pallas_call(kernel, out_shape=[jax.ShapeDtypeStruct(shape, jnp.float32...]
  transfers between devices with their start and end apart: 14 -> 17, of which waited for: 13 -> 14; matrix products, arithmetic and copies ran while one was open for 0% -> 2% of each run, Pallas kernels for 1% -> 2%
where the time goes in v5:
time: 59.6 us; the launch traced here: 59.4 us
  waiting for transfers between devices  27.1 us (45%)
  starting transfers between devices  21.7 us (36%)
  Pallas kernels  4.92 us (8%)
  local copies, waits for them, and re-layouts  2.37 us (4%)
  between operations  2.31 us (4%)
  other arithmetic  1 us (2%)
    ppermute x17, waiting for transfers between devices, swap(): lax.ppermute(values, axis, [(i, i ^ mask) for i in range(lax.axis_size(ax...  27.1 us
    ppermute x17, starting transfers between devices, swap(): lax.ppermute(values, axis, [(i, i ^ mask) for i in range(lax.axis_size(ax...  21.7 us
    pallas_call x9, Pallas kernels, call(): pl.pallas_call(kernel, out_shape=[jax.ShapeDtypeStruct(shape, jnp.float32...  4.92 us
    unnamed x24, local copies, waits for them, and re-layouts  2.29 us
  transfers between devices with their start and end apart: 17, of which 14 were waited for; matrix products, arithmetic and copies ran while one was open for 2% of the time, Pallas kernels for 2%

profile of v5, /device:TPU:0, one launch (start us, length us, event | category | flops | bytes accessed | tf_op | source)
XLA Modules:
  0.0 59.4 jit_solution(1726071193454158247)
XLA Ops:
  0.0 3.0 %collective-permute-start = (f32[256,256]{1,0:T(8,128)}, f32[256,256]{1,0:T(8,128)S(1)}, u32[]{:S(2)}, u32[]{:S(2)}) collective-permute-start(f32[256,256]{1,0:T(8,128)} %bitcast.17), channel_id=1, source_target_pairs={{0,16},{16,0},{1,17},{17,1},{2,18},{18,2},{3,19},{19,3},{4,20},{20... | collective-permute-start | bytes 786440 | tf_op jit(solution)/shard_map/ppermute | solution.py:138
  5.4 0.9 %copy-done.3 = f32[1,1,256,256]{3,2,1,0:T(8,128)S(1)} copy-done((f32[1,1,256,256]{3,2,1,0:T(8,128)S(1)}, f32[1,1,256,256]{3,2,1,0:T(8,128)}, u32[]{:S(2)}) %copy-start.3) | copy-done | bytes 262168
  6.3 0.9 %copy-done.5 = f32[256,256]{1,0:T(8,128)S(1)} copy-done((f32[256,256]{1,0:T(8,128)S(1)}, f32[256,256]{1,0:T(8,128)}, u32[]{:S(2)}) %copy-start.5) | copy-done | bytes 262168
  7.3 0.4 shard_map.109.side_ref
  7.9 1.6 %collective-permute-done.partner_ref.former_ref = f32[256,256]{1,0:T(8,128)S(1)} collective-permute-done((f32[256,256]{1,0:T(8,128)}, f32[256,256]{1,0:T(8,128)S(1)}, u32[]{:S(2)}, u32[]{:S(2)}) %collective-permute-start) | collective-permute-done | bytes 262176 | tf_op jit(solution)/shard_map/ppermute | solution.py:138
  9.5 0.7 %shard_map.110 = (f32[128,256]{1,0:T(8,128)S(1)}, f32[128,256]{1,0:T(8,128)S(1)}) custom-call(s32[1]{0:T(128)} %bitcast.6.adjoint_ref, s32[1]{0:T(128)} %bitcast.core_ref, f32[256,256]{1,0:T(8,128)S(1)} %shard_map.109.side_ref, f32[256,256]{1,0:T(8,128)S(1)} %bitcast.19, f32[256,256]{1,0:T(8,128)S(1)} %collective-permute-done.partner_ref.former_ref, ...), custom_call_target="tpu_custom_call" | custom-call | tf_op jit(solution)/shard_map/pallas_call | solution.py:127
  10.4 1.2 %collective-permute-done.1.came_ref = f32[128,256]{1,0:T(8,128)S(1)} collective-permute-done((f32[128,256]{1,0:T(8,128)S(1)}, f32[128,256]{1,0:T(8,128)S(1)}, u32[]{:S(2)}, u32[]{:S(2)}) %collective-permute-start.1) | collective-permute-done | bytes 131104 | tf_op jit(solution)/shard_map/ppermute | solution.py:138
  11.6 2.8 %collective-permute-start.4 = (f32[128,256]{1,0:T(8,128)S(1)}, f32[128,256]{1,0:T(8,128)S(1)}, u32[]{:S(2)}, u32[]{:S(2)}) collective-permute-start(f32[128,256]{1,0:T(8,128)S(1)} %multiply_add_fusion.7), channel_id=1, source_target_pairs={{0,6},{1,7},{2,4},{3,5},{4,2},{5,3},{6,0},{7,1},{8,14},{9,15},{10,... | collective-permute-start | bytes 393224 | tf_op jit(solution)/shard_map/ppermute | solution.py:138
  14.4 0.4 collective-permute-start.3
  14.9 0.3 collective-permute-start.2
  15.2 1.7 %collective-permute-start.5 = (f32[128,256]{1,0:T(8,128)S(1)}, f32[128,256]{1,0:T(8,128)S(1)}, u32[]{:S(2)}, u32[]{:S(2)}) collective-permute-start(f32[128,256]{1,0:T(8,128)S(1)} %get-tuple-element.36.kept_ref), channel_id=1, source_target_pairs={{0,16},{16,0},{1,17},{17,1},{2,18},{18,2},{3,19},{19,3},{4,20},{20... | collective-permute-start | bytes 393224 | tf_op jit(solution)/shard_map/ppermute | solution.py:138
  16.9 0.3 collective-permute-start.7
  17.2 1.7 %collective-permute-done.4 = f32[128,256]{1,0:T(8,128)S(1)} collective-permute-done((f32[128,256]{1,0:T(8,128)S(1)}, f32[128,256]{1,0:T(8,128)S(1)}, u32[]{:S(2)}, u32[]{:S(2)}) %collective-permute-start.4) | collective-permute-done | bytes 131104 | tf_op jit(solution)/shard_map/ppermute | solution.py:138
  18.9 2.3 %collective-permute-done.3 = f32[128,256]{1,0:T(8,128)S(1)} collective-permute-done((f32[128,256]{1,0:T(8,128)S(1)}, f32[128,256]{1,0:T(8,128)S(1)}, u32[]{:S(2)}, u32[]{:S(2)}) %collective-permute-start.3) | collective-permute-done | bytes 131104 | tf_op jit(solution)/shard_map/ppermute | solution.py:138
  21.5 3.7 %collective-permute-start.6 = (f32[128,256]{1,0:T(8,128)S(1)}, f32[128,256]{1,0:T(8,128)S(1)}, u32[]{:S(2)}, u32[]{:S(2)}) collective-permute-start(f32[128,256]{1,0:T(8,128)S(1)} %multiply_add_fusion.6), channel_id=1, source_target_pairs={{0,12},{1,13},{2,14},{3,15},{4,8},{5,9},{6,10},{7,11},{8,4},{9,5},... | collective-permute-start | bytes 393224 | tf_op jit(solution)/shard_map/ppermute | solution.py:138
  25.3 3.1 %collective-permute-done.6 = f32[128,256]{1,0:T(8,128)S(1)} collective-permute-done((f32[128,256]{1,0:T(8,128)S(1)}, f32[128,256]{1,0:T(8,128)S(1)}, u32[]{:S(2)}, u32[]{:S(2)}) %collective-permute-start.6) | collective-permute-done | bytes 131104 | tf_op jit(solution)/shard_map/ppermute | solution.py:138
  28.5 1.6 %collective-permute-start.8 = (f32[128,256]{1,0:T(8,128)S(1)}, f32[128,256]{1,0:T(8,128)S(1)}, u32[]{:S(2)}, u32[]{:S(2)}) collective-permute-start(f32[128,256]{1,0:T(8,128)S(1)} %multiply_add_fusion.4.entering_ref), channel_id=1, source_target_pairs={{0,16},{16,0},{1,17},{17,1},{2,18},{18,2},{3,19},{19,3},{4,20},{20... | collective-permute-start | bytes 393224 | tf_op jit(solution)/shard_map/ppermute | solution.py:138
  30.1 0.7 %shard_map.112.own_ref = f32[256,256]{1,0:T(8,128)S(1)} custom-call(s32[1]{0:T(128)} %bitcast.core_ref, s32[1]{0:T(128)} %bitcast.1.last_ref, f32[128,256]{1,0:T(8,128)S(1)} %get-tuple-element.51.kept_ref, f32[128,256]{1,0:T(8,128)S(1)} %collective-permute-done.9.came_ref, f32[256,256]{1,0:T(8,128)S(1)} %bitcast.20, bf16[2,256,256]{2,1,0:T(8,128)(2,1)S(1)} %copy-done, ...), custom_call_target="tpu_custom_call" | custom-call | tf_op jit(solution)/shard_map/pallas_call | solution.py:127
  31.1 0.4 shard_map.113.side_ref
  31.5 2.9 %collective-permute-done.8.entering_ref = f32[128,256]{1,0:T(8,128)S(1)} collective-permute-done((f32[128,256]{1,0:T(8,128)S(1)}, f32[128,256]{1,0:T(8,128)S(1)}, u32[]{:S(2)}, u32[]{:S(2)}) %collective-permute-start.8) | collective-permute-done | bytes 131104 | tf_op jit(solution)/shard_map/ppermute | solution.py:138
  34.5 1.3 %collective-permute-done.10.came_ref = f32[128,256]{1,0:T(8,128)S(1)} collective-permute-done((f32[128,256]{1,0:T(8,128)S(1)}, f32[128,256]{1,0:T(8,128)S(1)}, u32[]{:S(2)}, u32[]{:S(2)}) %collective-permute-start.10) | collective-permute-done | bytes 131104 | tf_op jit(solution)/shard_map/ppermute | solution.py:138
  35.9 1.3 %shard_map.115 = (f32[128,256]{1,0:T(8,128)S(1)}, f32[128,256]{1,0:T(8,128)S(1)}) custom-call(s32[1]{0:T(128)} %bitcast.6.adjoint_ref, s32[1]{0:T(128)} %bitcast.core_ref, s32[1]{0:T(128)} %bitcast.7.partner_last_ref, f32[256,256]{1,0:T(8,128)S(1)} %shard_map.113.side_ref, f32[256,256]{1,0:T(8,128)S(1)} %shard_map.112.own_ref, ...), custom_call_target="tpu_custom_call" | custom-call | tf_op jit(solution)/shard_map/pallas_call | solution.py:127
  37.4 1.2 %collective-permute-done.11.came_ref = f32[128,256]{1,0:T(8,128)S(1)} collective-permute-done((f32[128,256]{1,0:T(8,128)S(1)}, f32[128,256]{1,0:T(8,128)S(1)}, u32[]{:S(2)}, u32[]{:S(2)}) %collective-permute-start.11) | collective-permute-done | bytes 131104 | tf_op jit(solution)/shard_map/ppermute | solution.py:138
  38.7 3.8 %collective-permute-start.14 = (f32[128,256]{1,0:T(8,128)S(1)}, f32[128,256]{1,0:T(8,128)S(1)}, u32[]{:S(2)}, u32[]{:S(2)}) collective-permute-start(f32[128,256]{1,0:T(8,128)S(1)} %multiply_add_fusion.3), channel_id=1, source_target_pairs={{0,6},{1,7},{2,4},{3,5},{4,2},{5,3},{6,0},{7,1},{8,14},{9,15},{10,... | collective-permute-start | bytes 393224 | tf_op jit(solution)/shard_map/ppermute | solution.py:138
  42.5 0.6 %collective-permute-start.12 = (f32[128,256]{1,0:T(8,128)S(1)}, f32[128,256]{1,0:T(8,128)S(1)}, u32[]{:S(2)}, u32[]{:S(2)}) collective-permute-start(f32[128,256]{1,0:T(8,128)S(1)} %multiply_add_fusion.3), channel_id=1, source_target_pairs={{0,2},{1,3},{2,0},{3,1},{4,6},{5,7},{6,4},{7,5},{8,10},{9,11},{10,... | collective-permute-start | bytes 393224 | tf_op jit(solution)/shard_map/ppermute | solution.py:138
  43.1 3.6 %collective-permute-done.14 = f32[128,256]{1,0:T(8,128)S(1)} collective-permute-done((f32[128,256]{1,0:T(8,128)S(1)}, f32[128,256]{1,0:T(8,128)S(1)}, u32[]{:S(2)}, u32[]{:S(2)}) %collective-permute-start.14) | collective-permute-done | bytes 131104 | tf_op jit(solution)/shard_map/ppermute | solution.py:138
  46.7 1.7 %collective-permute-done.13 = f32[128,256]{1,0:T(8,128)S(1)} collective-permute-done((f32[128,256]{1,0:T(8,128)S(1)}, f32[128,256]{1,0:T(8,128)S(1)}, u32[]{:S(2)}, u32[]{:S(2)}) %collective-permute-start.13) | collective-permute-done | bytes 131104 | tf_op jit(solution)/shard_map/ppermute | solution.py:138
  48.4 0.7 %collective-permute-done.12 = f32[128,256]{1,0:T(8,128)S(1)} collective-permute-done((f32[128,256]{1,0:T(8,128)S(1)}, f32[128,256]{1,0:T(8,128)S(1)}, u32[]{:S(2)}, u32[]{:S(2)}) %collective-permute-start.12) | collective-permute-done | bytes 131104 | tf_op jit(solution)/shard_map/ppermute | solution.py:138
  49.1 3.0 %collective-permute-start.15 = (f32[128,256]{1,0:T(8,128)S(1)}, f32[128,256]{1,0:T(8,128)S(1)}, u32[]{:S(2)}, u32[]{:S(2)}) collective-permute-start(f32[128,256]{1,0:T(8,128)S(1)} %multiply_add_fusion.2), channel_id=1, source_target_pairs={{0,12},{1,13},{2,14},{3,15},{4,8},{5,9},{6,10},{7,11},{8,4},{9,5},... | collective-permute-start | bytes 393224 | tf_op jit(solution)/shard_map/ppermute | solution.py:138
  52.2 4.3 %collective-permute-done.15 = f32[128,256]{1,0:T(8,128)S(1)} collective-permute-done((f32[128,256]{1,0:T(8,128)S(1)}, f32[128,256]{1,0:T(8,128)S(1)}, u32[]{:S(2)}, u32[]{:S(2)}) %collective-permute-start.15) | collective-permute-done | bytes 131104 | tf_op jit(solution)/shard_map/ppermute | solution.py:138
  56.7 1.3 %collective-permute-done.16.came_ref = f32[128,256]{1,0:T(8,128)S(1)} collective-permute-done((f32[128,256]{1,0:T(8,128)S(1)}, f32[128,256]{1,0:T(8,128)S(1)}, u32[]{:S(2)}, u32[]{:S(2)}) %collective-permute-start.16) | collective-permute-done | bytes 131104 | tf_op jit(solution)/shard_map/ppermute | solution.py:138
  58.0 1.4 %shard_map.117 = f32[256,256]{1,0:T(8,128)} custom-call(s32[1]{0:T(128)} %bitcast.core_ref, s32[1]{0:T(128)} %bitcast.1.last_ref, f32[128,256]{1,0:T(8,128)S(1)} %get-tuple-element.61.kept_ref, f32[128,256]{1,0:T(8,128)S(1)} %collective-permute-done.16.came_ref, f32[256,256]{1,0:T(8,128)S(1)} %shard_map.112.own_ref, bf16[2,256,256]{2,1,0:T(8,128)(2,1)S(1)} %copy-done, ...), custom_call_target="tpu_custom_call" | custom-call | tf_op jit(solution)/shard_map/pallas_call | solution.py:127
  (48 shorter events, 2.3 us)
Async XLA Ops:
  0.0 9.5 %collective-permute-start = (f32[256,256]{1,0:T(8,128)}, f32[256,256]{1,0:T(8,128)S(1)}, u32[]{:S(2)}, u32[]{:S(2)}) collective-permute-start(f32[256,256]{1,0:T(8,128)} %bitcast.17), channel_id=1, source_target_pairs={{0,16},{16,0},{1,17},{17,1},{2,18},{18,2},{3,19},{19,3},{4,20},{20... | collective-permute-start | bytes 786440 | tf_op jit(solution)/shard_map/ppermute | solution.py:138
  3.0 2.0 %copy-start.11 = (f32[256]{0:T(256)S(1)}, f32[256]{0:T(256)}, u32[]{:S(2)}) copy-start(f32[256]{0:T(256)} %constant.37.clone) | copy-start | bytes 3076
  3.0 2.4 %copy-start.2 = (f32[1,1,256,256]{3,2,1,0:T(8,128)S(1)}, f32[1,1,256,256]{3,2,1,0:T(8,128)}, u32[]{:S(2)}) copy-start(f32[1,1,256,256]{3,2,1,0:T(8,128)} %param.11) | copy-start | bytes 786436
  3.0 2.4 %copy-start.1 = (f32[256,256]{1,0:T(8,128)S(1)}, f32[256,256]{1,0:T(8,128)}, u32[]{:S(2)}) copy-start(f32[256,256]{1,0:T(8,128)} %reaction_ref.7) | copy-start | bytes 786436
  5.3 1.0 %copy-start.3 = (f32[1,1,256,256]{3,2,1,0:T(8,128)S(1)}, f32[1,1,256,256]{3,2,1,0:T(8,128)}, u32[]{:S(2)}) copy-start(f32[1,1,256,256]{3,2,1,0:T(8,128)} %param.12) | copy-start | bytes 786436
  6.3 0.9 %copy-start.5 = (f32[256,256]{1,0:T(8,128)S(1)}, f32[256,256]{1,0:T(8,128)}, u32[]{:S(2)}) copy-start(f32[256,256]{1,0:T(8,128)} %diffusion_ref.3) | copy-start | bytes 786436
  7.6 1.8 %copy-start = (bf16[2,256,256]{2,1,0:T(8,128)(2,1)S(1)}, bf16[2,256,256]{2,1,0:T(8,128)(2,1)}, u32[]{:S(2)}) copy-start(bf16[2,256,256]{2,1,0:T(8,128)(2,1)} %constant.36.clone.x_ref.y_ref) | copy-start | bytes 786436
  7.9 17.3 %copy-start.7 = (f32[128,256]{1,0:T(8,128)}, f32[128,256]{1,0:T(8,128)S(1)}, u32[]{:S(2)}) copy-start(f32[128,256]{1,0:T(8,128)S(1)} %get-tuple-element.41) | copy-start | bytes 393220
  7.9 17.3 %copy-start.9 = (f32[128,256]{1,0:T(8,128)}, f32[128,256]{1,0:T(8,128)S(1)}, u32[]{:S(2)}) copy-start(f32[128,256]{1,0:T(8,128)S(1)} %get-tuple-element.40) | copy-start | bytes 393220
  10.2 1.4 %collective-permute-start.1 = (f32[128,256]{1,0:T(8,128)S(1)}, f32[128,256]{1,0:T(8,128)S(1)}, u32[]{:S(2)}, u32[]{:S(2)}) collective-permute-start(f32[128,256]{1,0:T(8,128)S(1)} %get-tuple-element.38), channel_id=1, source_target_pairs={{0,1},{1,0},{2,3},{3,2},{4,5},{5,4},{6,7},{7,6},{8,9},{9,8},{10,11... | collective-permute-start | bytes 393224 | tf_op jit(solution)/shard_map/ppermute | solution.py:138
  11.6 7.3 %collective-permute-start.4 = (f32[128,256]{1,0:T(8,128)S(1)}, f32[128,256]{1,0:T(8,128)S(1)}, u32[]{:S(2)}, u32[]{:S(2)}) collective-permute-start(f32[128,256]{1,0:T(8,128)S(1)} %multiply_add_fusion.7), channel_id=1, source_target_pairs={{0,6},{1,7},{2,4},{3,5},{4,2},{5,3},{6,0},{7,1},{8,14},{9,15},{10,... | collective-permute-start | bytes 393224 | tf_op jit(solution)/shard_map/ppermute | solution.py:138
  14.4 6.8 %collective-permute-start.3 = (f32[128,256]{1,0:T(8,128)S(1)}, f32[128,256]{1,0:T(8,128)S(1)}, u32[]{:S(2)}, u32[]{:S(2)}) collective-permute-start(f32[128,256]{1,0:T(8,128)S(1)} %multiply_add_fusion.7), channel_id=1, source_target_pairs={{0,4},{1,5},{2,6},{3,7},{4,0},{5,1},{6,2},{7,3},{8,12},{9,13},{10,... | collective-permute-start | bytes 393224 | tf_op jit(solution)/shard_map/ppermute | solution.py:138
  14.9 6.3 %collective-permute-start.2 = (f32[128,256]{1,0:T(8,128)S(1)}, f32[128,256]{1,0:T(8,128)S(1)}, u32[]{:S(2)}, u32[]{:S(2)}) collective-permute-start(f32[128,256]{1,0:T(8,128)S(1)} %multiply_add_fusion.7), channel_id=1, source_target_pairs={{0,2},{1,3},{2,0},{3,1},{4,6},{5,7},{6,4},{7,5},{8,10},{9,11},{10,... | collective-permute-start | bytes 393224 | tf_op jit(solution)/shard_map/ppermute | solution.py:138
  15.2 6.3 %collective-permute-start.5 = (f32[128,256]{1,0:T(8,128)S(1)}, f32[128,256]{1,0:T(8,128)S(1)}, u32[]{:S(2)}, u32[]{:S(2)}) collective-permute-start(f32[128,256]{1,0:T(8,128)S(1)} %get-tuple-element.36.kept_ref), channel_id=1, source_target_pairs={{0,16},{16,0},{1,17},{17,1},{2,18},{18,2},{3,19},{19,3},{4,20},{20... | collective-permute-start | bytes 393224 | tf_op jit(solution)/shard_map/ppermute | solution.py:138
  16.9 11.4 %collective-permute-start.7 = (f32[128,256]{1,0:T(8,128)S(1)}, f32[128,256]{1,0:T(8,128)S(1)}, u32[]{:S(2)}, u32[]{:S(2)}) collective-permute-start(f32[128,256]{1,0:T(8,128)S(1)} %collective-permute-done.1.came_ref), channel_id=1, source_target_pairs={{0,16},{16,0},{1,17},{17,1},{2,18},{18,2},{3,19},{19,3},{4,20},{20... | collective-permute-start | bytes 393224 | tf_op jit(solution)/shard_map/ppermute | solution.py:138
  21.5 6.9 %collective-permute-start.6 = (f32[128,256]{1,0:T(8,128)S(1)}, f32[128,256]{1,0:T(8,128)S(1)}, u32[]{:S(2)}, u32[]{:S(2)}) collective-permute-start(f32[128,256]{1,0:T(8,128)S(1)} %multiply_add_fusion.6), channel_id=1, source_target_pairs={{0,12},{1,13},{2,14},{3,15},{4,8},{5,9},{6,10},{7,11},{8,4},{9,5},... | collective-permute-start | bytes 393224 | tf_op jit(solution)/shard_map/ppermute | solution.py:138
  28.4 1.7 %collective-permute-start.9 = (f32[128,256]{1,0:T(8,128)S(1)}, f32[128,256]{1,0:T(8,128)S(1)}, u32[]{:S(2)}, u32[]{:S(2)}) collective-permute-start(f32[128,256]{1,0:T(8,128)S(1)} %get-tuple-element.52), channel_id=1, source_target_pairs={{0,1},{1,0},{2,3},{3,2},{4,5},{5,4},{6,7},{7,6},{8,9},{9,8},{10,11... | collective-permute-start | bytes 393224 | tf_op jit(solution)/shard_map/ppermute | solution.py:138
  28.5 5.9 %collective-permute-start.8 = (f32[128,256]{1,0:T(8,128)S(1)}, f32[128,256]{1,0:T(8,128)S(1)}, u32[]{:S(2)}, u32[]{:S(2)}) collective-permute-start(f32[128,256]{1,0:T(8,128)S(1)} %multiply_add_fusion.4.entering_ref), channel_id=1, source_target_pairs={{0,16},{16,0},{1,17},{17,1},{2,18},{18,2},{3,19},{19,3},{4,20},{20... | collective-permute-start | bytes 393224 | tf_op jit(solution)/shard_map/ppermute | solution.py:138
  30.1 1.0 %copy-start.4 = (f32[1,1,256,256]{3,2,1,0:T(8,128)S(1)}, f32[1,1,256,256]{3,2,1,0:T(8,128)}, u32[]{:S(2)}) copy-start(f32[1,1,256,256]{3,2,1,0:T(8,128)} %param.12) | copy-start | bytes 786436
  30.1 1.0 %copy-start.6 = (f32[256,256]{1,0:T(8,128)S(1)}, f32[256,256]{1,0:T(8,128)}, u32[]{:S(2)}) copy-start(f32[256,256]{1,0:T(8,128)} %diffusion_ref.3) | copy-start | bytes 786436
  34.5 1.4 %collective-permute-start.10 = (f32[128,256]{1,0:T(8,128)S(1)}, f32[128,256]{1,0:T(8,128)S(1)}, u32[]{:S(2)}, u32[]{:S(2)}) collective-permute-start(f32[128,256]{1,0:T(8,128)S(1)} %get-tuple-element.58), channel_id=1, source_target_pairs={{0,1},{1,0},{2,3},{3,2},{4,5},{5,4},{6,7},{7,6},{8,9},{9,8},{10,11... | collective-permute-start | bytes 393224 | tf_op jit(solution)/shard_map/ppermute | solution.py:138
  37.2 1.4 %collective-permute-start.11 = (f32[128,256]{1,0:T(8,128)S(1)}, f32[128,256]{1,0:T(8,128)S(1)}, u32[]{:S(2)}, u32[]{:S(2)}) collective-permute-start(f32[128,256]{1,0:T(8,128)S(1)} %get-tuple-element.60), channel_id=1, source_target_pairs={{0,1},{1,0},{2,3},{3,2},{4,5},{5,4},{6,7},{7,6},{8,9},{9,8},{10,11... | collective-permute-start | bytes 393224 | tf_op jit(solution)/shard_map/ppermute | solution.py:138
  38.6 13.5 %copy-start.8 = (f32[128,256]{1,0:T(8,128)S(1)}, f32[128,256]{1,0:T(8,128)}, u32[]{:S(2)}) copy-start(f32[128,256]{1,0:T(8,128)} %copy-done.7) | copy-start | bytes 393220
  38.6 13.5 %copy-start.10 = (f32[128,256]{1,0:T(8,128)S(1)}, f32[128,256]{1,0:T(8,128)}, u32[]{:S(2)}) copy-start(f32[128,256]{1,0:T(8,128)} %copy-done.9) | copy-start | bytes 393220
  38.7 8.1 %collective-permute-start.14 = (f32[128,256]{1,0:T(8,128)S(1)}, f32[128,256]{1,0:T(8,128)S(1)}, u32[]{:S(2)}, u32[]{:S(2)}) collective-permute-start(f32[128,256]{1,0:T(8,128)S(1)} %multiply_add_fusion.3), channel_id=1, source_target_pairs={{0,6},{1,7},{2,4},{3,5},{4,2},{5,3},{6,0},{7,1},{8,14},{9,15},{10,... | collective-permute-start | bytes 393224 | tf_op jit(solution)/shard_map/ppermute | solution.py:138
  42.4 5.9 %collective-permute-start.13 = (f32[128,256]{1,0:T(8,128)S(1)}, f32[128,256]{1,0:T(8,128)S(1)}, u32[]{:S(2)}, u32[]{:S(2)}) collective-permute-start(f32[128,256]{1,0:T(8,128)S(1)} %multiply_add_fusion.3), channel_id=1, source_target_pairs={{0,4},{1,5},{2,6},{3,7},{4,0},{5,1},{6,2},{7,3},{8,12},{9,13},{10,... | collective-permute-start | bytes 393224 | tf_op jit(solution)/shard_map/ppermute | solution.py:138
  42.5 6.6 %collective-permute-start.12 = (f32[128,256]{1,0:T(8,128)S(1)}, f32[128,256]{1,0:T(8,128)S(1)}, u32[]{:S(2)}, u32[]{:S(2)}) collective-permute-start(f32[128,256]{1,0:T(8,128)S(1)} %multiply_add_fusion.3), channel_id=1, source_target_pairs={{0,2},{1,3},{2,0},{3,1},{4,6},{5,7},{6,4},{7,5},{8,10},{9,11},{10,... | collective-permute-start | bytes 393224 | tf_op jit(solution)/shard_map/ppermute | solution.py:138
  49.1 7.4 %collective-permute-start.15 = (f32[128,256]{1,0:T(8,128)S(1)}, f32[128,256]{1,0:T(8,128)S(1)}, u32[]{:S(2)}, u32[]{:S(2)}) collective-permute-start(f32[128,256]{1,0:T(8,128)S(1)} %multiply_add_fusion.2), channel_id=1, source_target_pairs={{0,12},{1,13},{2,14},{3,15},{4,8},{5,9},{6,10},{7,11},{8,4},{9,5},... | collective-permute-start | bytes 393224 | tf_op jit(solution)/shard_map/ppermute | solution.py:138
  56.6 1.4 %collective-permute-start.16 = (f32[128,256]{1,0:T(8,128)S(1)}, f32[128,256]{1,0:T(8,128)S(1)}, u32[]{:S(2)}, u32[]{:S(2)}) collective-permute-start(f32[128,256]{1,0:T(8,128)S(1)} %get-tuple-element.62), channel_id=1, source_target_pairs={{0,1},{1,0},{2,3},{3,2},{4,5},{5,4},{6,7},{7,6},{8,9},{9,8},{10,11... | collective-permute-start | bytes 393224 | tf_op jit(solution)/shard_map/ppermute | solution.py:138

commit v6 on v5

--- a/solution.py
+++ b/solution.py
@@ -69,11 +69,19 @@
     return split(work_ref[...])
 
 
-def forward(scale, adjoint, core, side, own, partner, reaction, x_table, y_table, keep_ref, send_ref, work_ref):
+def row_halves(count):
+    return slice(0, count // 2), slice(count // 2, count)
+
+
+def both_sides(x_ref, middle, y_table, place):
+    return product(split(product((x_ref[0, place], x_ref[1, place]), middle)), y_table)
+
+
+def forward(scale, adjoint, core, side, own, partner, reaction, x_ref, y_ref, keep_ref, send_ref, work_ref):
     adjoint_part = 3.0 * reaction * partner * partner * own - partner
-    side = side - jnp.where(adjoint, adjoint_part, gamma_inv * partner)
-    rows = product(x_table, split(side))
-    work_ref[...] = product(split(rows), y_table) * scale
+    side = split(side - jnp.where(adjoint, adjoint_part, gamma_inv * partner))
+    for place in row_halves(work_ref.shape[0]):
+        work_ref[place, :] = both_sides(x_ref, side, parts(y_ref), place) * scale
     half = keep_ref.shape[0]
     keep_ref[...] = work_ref[pl.ds(pl.multiple_of(core * half, half), half), :]
     send_ref[...] = work_ref[pl.ds(pl.multiple_of((1 - core) * half, half), half), :]
@@ -84,7 +92,7 @@
 ):
     forward(
         scale, adjoint_ref[0] == 1, core_ref[0], side_ref[...], own_ref[...], partner_ref[...], reaction_ref[...],
-        parts(x_ref), parts(y_ref), keep_ref, send_ref, work_ref,
+        x_ref, y_ref, keep_ref, send_ref, work_ref,
     )
 
 
@@ -93,23 +101,23 @@
     side_ref, own_ref, kept_ref, came_ref, former_ref, reaction_ref, x_ref, y_ref,
     keep_ref, send_ref, *refs,
 ):
-    x_table, y_table = parts(x_ref), parts(y_ref)
     work_ref = refs[-1]
-    rows = product(gather_halves(core_ref[0], work_ref, kept_ref, came_ref), y_table)
+    modes = gather_halves(core_ref[0], work_ref, kept_ref, came_ref)
     former = jnp.where(partner_last_ref[0] == 1, 1.0, 0.0) * former_ref[...]
-    partner = former + product(x_table, split(rows))
+    partner = former + both_sides(x_ref, modes, parts(y_ref), slice(None))
     if len(refs) > 1:
         refs[0][...] = partner
     forward(
         scale, adjoint_ref[0] == 1, core_ref[0], side_ref[...], own_ref[...], partner, reaction_ref[...],
-        x_table, y_table, keep_ref, send_ref, work_ref,
+        x_ref, y_ref, keep_ref, send_ref, work_ref,
     )
 
 
 def inverse_kernel(core_ref, last_ref, kept_ref, came_ref, own_ref, x_ref, y_ref, out_ref, work_ref):
-    rows = product(gather_halves(core_ref[0], work_ref, kept_ref, came_ref), parts(y_ref))
-    former = jnp.where(last_ref[0] == 1, 1.0, 0.0) * own_ref[...]
-    out_ref[...] = former + product(parts(x_ref), split(rows))
+    modes = gather_halves(core_ref[0], work_ref, kept_ref, came_ref)
+    former = jnp.where(last_ref[0] == 1, 1.0, 0.0)
+    for place in row_halves(work_ref.shape[0]):
+        out_ref[place, :] = former * own_ref[place, :] + both_sides(x_ref, modes, parts(y_ref), place)
 
 
 def steps_kernel(odd_ref, entering_ref, kept_ref, came_ref, rate_ref, new_ref, sent_ref):
@@ -161,7 +169,8 @@
     bit, steps = 1, 2
     while steps < total:
         count = 4 if steps * 4 <= total else 2
-        masks = [number << bit for number in range(1, count)]
+        numbers = [2, 3, 1] if count == 4 else [1]
+        masks = [number << bit for number in numbers]
         if count == 2 and bit > 1:
             masks = [(1 << bit) | (1 << (bit - 1))]
         factor = power(rate, steps)
@@ -169,8 +178,8 @@
         for _ in range(count - 1):
             powers.append(powers[-1] * factor)
         mine = (place >> bit) & (count - 1)
-        join = [pick(powers[::-1], mine ^ number) for number in range(count)]
-        enter = [pick([none] + powers, jnp.maximum(mine - (mine ^ number), 0)) for number in range(count)]
+        join = [pick(powers[::-1], mine ^ number) for number in [0] + numbers]
+        enter = [pick([none] + powers, jnp.maximum(mine - (mine ^ number), 0)) for number in [0] + numbers]
         through = pick(powers, mine)
         bit, steps = bit + count.bit_length() - 1, steps * count
         if steps == total:

time: 59.6 us -> 58.5 us (0.982)
  waiting for transfers between devices: 27.1 us -> 26.3 us
    ppermute x17, waiting for transfers between devices: 27.1 us -> 26.3 us  [swap(): lax.ppermute(values, axis, [(i, i ^ mask) for i in range(lax.axis_size(ax...]
where the time goes in v6:
time: 58.5 us; the launch traced here: 58.3 us
  waiting for transfers between devices  26.3 us (45%)
  starting transfers between devices  21.6 us (37%)
  Pallas kernels  4.53 us (8%)
  local copies, waits for them, and re-layouts  2.48 us (4%)
  between operations  2.32 us (4%)
  other arithmetic  1 us (2%)
    ppermute x17, waiting for transfers between devices, swap(): lax.ppermute(values, axis, [(i, i ^ mask) for i in range(lax.axis_size(ax...  26.3 us
    ppermute x17, starting transfers between devices, swap(): lax.ppermute(values, axis, [(i, i ^ mask) for i in range(lax.axis_size(ax...  21.6 us
    pallas_call x9, Pallas kernels, call(): pl.pallas_call(kernel, out_shape=[jax.ShapeDtypeStruct(shape, jnp.float32...  4.53 us
    unnamed x24, local copies, waits for them, and re-layouts  2.39 us
  transfers between devices with their start and end apart: 17, of which 14 were waited for; matrix products, arithmetic and copies ran while one was open for 2% of the time, Pallas kernels for 2%

profile of v6, /device:TPU:0, one launch (start us, length us, event | category | flops | bytes accessed | tf_op | source)
XLA Modules:
  0.0 58.3 jit_solution(16482259353500680999)
XLA Ops:
  0.0 3.0 %collective-permute-start = (f32[256,256]{1,0:T(8,128)}, f32[256,256]{1,0:T(8,128)S(1)}, u32[]{:S(2)}, u32[]{:S(2)}) collective-permute-start(f32[256,256]{1,0:T(8,128)} %bitcast.17), channel_id=1, source_target_pairs={{0,16},{16,0},{1,17},{17,1},{2,18},{18,2},{3,19},{19,3},{4,20},{20... | collective-permute-start | bytes 786440 | tf_op jit(solution)/shard_map/ppermute | solution.py:146
  5.4 0.9 %copy-done.3 = f32[1,1,256,256]{3,2,1,0:T(8,128)S(1)} copy-done((f32[1,1,256,256]{3,2,1,0:T(8,128)S(1)}, f32[1,1,256,256]{3,2,1,0:T(8,128)}, u32[]{:S(2)}) %copy-start.3) | copy-done | bytes 262168
  6.3 0.9 %copy-done.5 = f32[256,256]{1,0:T(8,128)S(1)} copy-done((f32[256,256]{1,0:T(8,128)S(1)}, f32[256,256]{1,0:T(8,128)}, u32[]{:S(2)}) %copy-start.5) | copy-done | bytes 262168
  7.3 0.4 shard_map.109.side_ref
  7.9 1.6 %collective-permute-done.partner_ref.former_ref = f32[256,256]{1,0:T(8,128)S(1)} collective-permute-done((f32[256,256]{1,0:T(8,128)}, f32[256,256]{1,0:T(8,128)S(1)}, u32[]{:S(2)}, u32[]{:S(2)}) %collective-permute-start) | collective-permute-done | bytes 262176 | tf_op jit(solution)/shard_map/ppermute | solution.py:146
  9.5 0.6 %shard_map.110 = (f32[128,256]{1,0:T(8,128)S(1)}, f32[128,256]{1,0:T(8,128)S(1)}) custom-call(s32[1]{0:T(128)} %bitcast.6.adjoint_ref, s32[1]{0:T(128)} %bitcast.core_ref, f32[256,256]{1,0:T(8,128)S(1)} %shard_map.109.side_ref, f32[256,256]{1,0:T(8,128)S(1)} %bitcast.19, f32[256,256]{1,0:T(8,128)S(1)} %collective-permute-done.partner_ref.former_ref, ...), custom_call_target="tpu_custom_call" | custom-call | tf_op jit(solution)/shard_map/pallas_call | solution.py:135
  10.3 1.2 %collective-permute-done.1.came_ref = f32[128,256]{1,0:T(8,128)S(1)} collective-permute-done((f32[128,256]{1,0:T(8,128)S(1)}, f32[128,256]{1,0:T(8,128)S(1)}, u32[]{:S(2)}, u32[]{:S(2)}) %collective-permute-start.1) | collective-permute-done | bytes 131104 | tf_op jit(solution)/shard_map/ppermute | solution.py:146
  11.6 1.8 %collective-permute-start.4 = (f32[128,256]{1,0:T(8,128)S(1)}, f32[128,256]{1,0:T(8,128)S(1)}, u32[]{:S(2)}, u32[]{:S(2)}) collective-permute-start(f32[128,256]{1,0:T(8,128)S(1)} %multiply_add_fusion.7), channel_id=1, source_target_pairs={{0,2},{1,3},{2,0},{3,1},{4,6},{5,7},{6,4},{7,5},{8,10},{9,11},{10,... | collective-permute-start | bytes 393224 | tf_op jit(solution)/shard_map/ppermute | solution.py:146
  13.3 1.5 %collective-permute-start.3 = (f32[128,256]{1,0:T(8,128)S(1)}, f32[128,256]{1,0:T(8,128)S(1)}, u32[]{:S(2)}, u32[]{:S(2)}) collective-permute-start(f32[128,256]{1,0:T(8,128)S(1)} %multiply_add_fusion.7), channel_id=1, source_target_pairs={{0,6},{1,7},{2,4},{3,5},{4,2},{5,3},{6,0},{7,1},{8,14},{9,15},{10,... | collective-permute-start | bytes 393224 | tf_op jit(solution)/shard_map/ppermute | solution.py:146
  15.1 1.7 %collective-permute-start.5 = (f32[128,256]{1,0:T(8,128)S(1)}, f32[128,256]{1,0:T(8,128)S(1)}, u32[]{:S(2)}, u32[]{:S(2)}) collective-permute-start(f32[128,256]{1,0:T(8,128)S(1)} %get-tuple-element.36.kept_ref), channel_id=1, source_target_pairs={{0,16},{16,0},{1,17},{17,1},{2,18},{18,2},{3,19},{19,3},{4,20},{20... | collective-permute-start | bytes 393224 | tf_op jit(solution)/shard_map/ppermute | solution.py:146
  17.1 2.2 %collective-permute-done.4 = f32[128,256]{1,0:T(8,128)S(1)} collective-permute-done((f32[128,256]{1,0:T(8,128)S(1)}, f32[128,256]{1,0:T(8,128)S(1)}, u32[]{:S(2)}, u32[]{:S(2)}) %collective-permute-start.4) | collective-permute-done | bytes 131104 | tf_op jit(solution)/shard_map/ppermute | solution.py:146
  19.3 1.3 %collective-permute-done.3 = f32[128,256]{1,0:T(8,128)S(1)} collective-permute-done((f32[128,256]{1,0:T(8,128)S(1)}, f32[128,256]{1,0:T(8,128)S(1)}, u32[]{:S(2)}, u32[]{:S(2)}) %collective-permute-start.3) | collective-permute-done | bytes 131104 | tf_op jit(solution)/shard_map/ppermute | solution.py:146
  20.6 0.7 %collective-permute-done.2 = f32[128,256]{1,0:T(8,128)S(1)} collective-permute-done((f32[128,256]{1,0:T(8,128)S(1)}, f32[128,256]{1,0:T(8,128)S(1)}, u32[]{:S(2)}, u32[]{:S(2)}) %collective-permute-start.2) | collective-permute-done | bytes 131104 | tf_op jit(solution)/shard_map/ppermute | solution.py:146
  21.4 3.8 %collective-permute-start.6 = (f32[128,256]{1,0:T(8,128)S(1)}, f32[128,256]{1,0:T(8,128)S(1)}, u32[]{:S(2)}, u32[]{:S(2)}) collective-permute-start(f32[128,256]{1,0:T(8,128)S(1)} %multiply_add_fusion.6), channel_id=1, source_target_pairs={{0,12},{1,13},{2,14},{3,15},{4,8},{5,9},{6,10},{7,11},{8,4},{9,5},... | collective-permute-start | bytes 393224 | tf_op jit(solution)/shard_map/ppermute | solution.py:146
  25.3 3.0 %collective-permute-done.6 = f32[128,256]{1,0:T(8,128)S(1)} collective-permute-done((f32[128,256]{1,0:T(8,128)S(1)}, f32[128,256]{1,0:T(8,128)S(1)}, u32[]{:S(2)}, u32[]{:S(2)}) %collective-permute-start.6) | collective-permute-done | bytes 131104 | tf_op jit(solution)/shard_map/ppermute | solution.py:146
  28.4 1.7 %collective-permute-start.8 = (f32[128,256]{1,0:T(8,128)S(1)}, f32[128,256]{1,0:T(8,128)S(1)}, u32[]{:S(2)}, u32[]{:S(2)}) collective-permute-start(f32[128,256]{1,0:T(8,128)S(1)} %multiply_add_fusion.4.entering_ref), channel_id=1, source_target_pairs={{0,16},{16,0},{1,17},{17,1},{2,18},{18,2},{3,19},{19,3},{4,20},{20... | collective-permute-start | bytes 393224 | tf_op jit(solution)/shard_map/ppermute | solution.py:146
  30.2 0.6 shard_map.112.own_ref
  30.7 0.4 copy-done.4
  31.2 0.4 shard_map.113.side_ref
  31.6 2.8 %collective-permute-done.8.entering_ref = f32[128,256]{1,0:T(8,128)S(1)} collective-permute-done((f32[128,256]{1,0:T(8,128)S(1)}, f32[128,256]{1,0:T(8,128)S(1)}, u32[]{:S(2)}, u32[]{:S(2)}) %collective-permute-start.8) | collective-permute-done | bytes 131104 | tf_op jit(solution)/shard_map/ppermute | solution.py:146
  34.5 1.3 %collective-permute-done.10.came_ref = f32[128,256]{1,0:T(8,128)S(1)} collective-permute-done((f32[128,256]{1,0:T(8,128)S(1)}, f32[128,256]{1,0:T(8,128)S(1)}, u32[]{:S(2)}, u32[]{:S(2)}) %collective-permute-start.10) | collective-permute-done | bytes 131104 | tf_op jit(solution)/shard_map/ppermute | solution.py:146
  35.8 1.2 %shard_map.115 = (f32[128,256]{1,0:T(8,128)S(1)}, f32[128,256]{1,0:T(8,128)S(1)}) custom-call(s32[1]{0:T(128)} %bitcast.6.adjoint_ref, s32[1]{0:T(128)} %bitcast.core_ref, s32[1]{0:T(128)} %bitcast.7.partner_last_ref, f32[256,256]{1,0:T(8,128)S(1)} %shard_map.113.side_ref, f32[256,256]{1,0:T(8,128)S(1)} %shard_map.112.own_ref, ...), custom_call_target="tpu_custom_call" | custom-call | tf_op jit(solution)/shard_map/pallas_call | solution.py:135
  37.2 1.2 %collective-permute-done.11.came_ref = f32[128,256]{1,0:T(8,128)S(1)} collective-permute-done((f32[128,256]{1,0:T(8,128)S(1)}, f32[128,256]{1,0:T(8,128)S(1)}, u32[]{:S(2)}, u32[]{:S(2)}) %collective-permute-start.11) | collective-permute-done | bytes 131104 | tf_op jit(solution)/shard_map/ppermute | solution.py:146
  38.5 1.7 %collective-permute-start.14 = (f32[128,256]{1,0:T(8,128)S(1)}, f32[128,256]{1,0:T(8,128)S(1)}, u32[]{:S(2)}, u32[]{:S(2)}) collective-permute-start(f32[128,256]{1,0:T(8,128)S(1)} %multiply_add_fusion.3), channel_id=1, source_target_pairs={{0,2},{1,3},{2,0},{3,1},{4,6},{5,7},{6,4},{7,5},{8,10},{9,11},{10,... | collective-permute-start | bytes 393224 | tf_op jit(solution)/shard_map/ppermute | solution.py:146
  40.2 2.0 %collective-permute-start.13 = (f32[128,256]{1,0:T(8,128)S(1)}, f32[128,256]{1,0:T(8,128)S(1)}, u32[]{:S(2)}, u32[]{:S(2)}) collective-permute-start(f32[128,256]{1,0:T(8,128)S(1)} %multiply_add_fusion.3), channel_id=1, source_target_pairs={{0,6},{1,7},{2,4},{3,5},{4,2},{5,3},{6,0},{7,1},{8,14},{9,15},{10,... | collective-permute-start | bytes 393224 | tf_op jit(solution)/shard_map/ppermute | solution.py:146
  42.2 4.2 %collective-permute-done.14 = f32[128,256]{1,0:T(8,128)S(1)} collective-permute-done((f32[128,256]{1,0:T(8,128)S(1)}, f32[128,256]{1,0:T(8,128)S(1)}, u32[]{:S(2)}, u32[]{:S(2)}) %collective-permute-start.14) | collective-permute-done | bytes 131104 | tf_op jit(solution)/shard_map/ppermute | solution.py:146
  46.4 1.1 %collective-permute-done.13 = f32[128,256]{1,0:T(8,128)S(1)} collective-permute-done((f32[128,256]{1,0:T(8,128)S(1)}, f32[128,256]{1,0:T(8,128)S(1)}, u32[]{:S(2)}, u32[]{:S(2)}) %collective-permute-start.13) | collective-permute-done | bytes 131104 | tf_op jit(solution)/shard_map/ppermute | solution.py:146
  47.5 1.1 %collective-permute-done.12 = f32[128,256]{1,0:T(8,128)S(1)} collective-permute-done((f32[128,256]{1,0:T(8,128)S(1)}, f32[128,256]{1,0:T(8,128)S(1)}, u32[]{:S(2)}, u32[]{:S(2)}) %collective-permute-start.12) | collective-permute-done | bytes 131104 | tf_op jit(solution)/shard_map/ppermute | solution.py:146
  48.6 3.4 %collective-permute-start.15 = (f32[128,256]{1,0:T(8,128)S(1)}, f32[128,256]{1,0:T(8,128)S(1)}, u32[]{:S(2)}, u32[]{:S(2)}) collective-permute-start(f32[128,256]{1,0:T(8,128)S(1)} %multiply_add_fusion.2), channel_id=1, source_target_pairs={{0,12},{1,13},{2,14},{3,15},{4,8},{5,9},{6,10},{7,11},{8,4},{9,5},... | collective-permute-start | bytes 393224 | tf_op jit(solution)/shard_map/ppermute | solution.py:146
  52.1 3.4 %collective-permute-done.15 = f32[128,256]{1,0:T(8,128)S(1)} collective-permute-done((f32[128,256]{1,0:T(8,128)S(1)}, f32[128,256]{1,0:T(8,128)S(1)}, u32[]{:S(2)}, u32[]{:S(2)}) %collective-permute-start.15) | collective-permute-done | bytes 131104 | tf_op jit(solution)/shard_map/ppermute | solution.py:146
  55.7 1.3 %collective-permute-done.16.came_ref = f32[128,256]{1,0:T(8,128)S(1)} collective-permute-done((f32[128,256]{1,0:T(8,128)S(1)}, f32[128,256]{1,0:T(8,128)S(1)}, u32[]{:S(2)}, u32[]{:S(2)}) %collective-permute-start.16) | collective-permute-done | bytes 131104 | tf_op jit(solution)/shard_map/ppermute | solution.py:146
  57.0 1.3 %shard_map.117 = f32[256,256]{1,0:T(8,128)} custom-call(s32[1]{0:T(128)} %bitcast.core_ref, s32[1]{0:T(128)} %bitcast.1.last_ref, f32[128,256]{1,0:T(8,128)S(1)} %get-tuple-element.61.kept_ref, f32[128,256]{1,0:T(8,128)S(1)} %collective-permute-done.16.came_ref, f32[256,256]{1,0:T(8,128)S(1)} %shard_map.112.own_ref, bf16[2,256,256]{2,1,0:T(8,128)(2,1)S(1)} %copy-done, ...), custom_call_target="tpu_custom_call" | custom-call | tf_op jit(solution)/shard_map/pallas_call | solution.py:135
  (48 shorter events, 2.4 us)
Async XLA Ops:
  0.0 9.5 %collective-permute-start = (f32[256,256]{1,0:T(8,128)}, f32[256,256]{1,0:T(8,128)S(1)}, u32[]{:S(2)}, u32[]{:S(2)}) collective-permute-start(f32[256,256]{1,0:T(8,128)} %bitcast.17), channel_id=1, source_target_pairs={{0,16},{16,0},{1,17},{17,1},{2,18},{18,2},{3,19},{19,3},{4,20},{20... | collective-permute-start | bytes 786440 | tf_op jit(solution)/shard_map/ppermute | solution.py:146
  3.0 2.0 %copy-start.11 = (f32[256]{0:T(256)S(1)}, f32[256]{0:T(256)}, u32[]{:S(2)}) copy-start(f32[256]{0:T(256)} %constant.37.clone) | copy-start | bytes 3076
  3.0 2.4 %copy-start.2 = (f32[1,1,256,256]{3,2,1,0:T(8,128)S(1)}, f32[1,1,256,256]{3,2,1,0:T(8,128)}, u32[]{:S(2)}) copy-start(f32[1,1,256,256]{3,2,1,0:T(8,128)} %param.11) | copy-start | bytes 786436
  3.0 2.4 %copy-start.1 = (f32[256,256]{1,0:T(8,128)S(1)}, f32[256,256]{1,0:T(8,128)}, u32[]{:S(2)}) copy-start(f32[256,256]{1,0:T(8,128)} %reaction_ref.7) | copy-start | bytes 786436
  5.3 1.0 %copy-start.3 = (f32[1,1,256,256]{3,2,1,0:T(8,128)S(1)}, f32[1,1,256,256]{3,2,1,0:T(8,128)}, u32[]{:S(2)}) copy-start(f32[1,1,256,256]{3,2,1,0:T(8,128)} %param.12) | copy-start | bytes 786436
  6.3 0.9 %copy-start.5 = (f32[256,256]{1,0:T(8,128)S(1)}, f32[256,256]{1,0:T(8,128)}, u32[]{:S(2)}) copy-start(f32[256,256]{1,0:T(8,128)} %diffusion_ref.3) | copy-start | bytes 786436
  7.6 1.8 %copy-start = (bf16[2,256,256]{2,1,0:T(8,128)(2,1)S(1)}, bf16[2,256,256]{2,1,0:T(8,128)(2,1)}, u32[]{:S(2)}) copy-start(bf16[2,256,256]{2,1,0:T(8,128)(2,1)} %constant.36.clone.x_ref.y_ref) | copy-start | bytes 786436
  7.9 17.3 %copy-start.7 = (f32[128,256]{1,0:T(8,128)}, f32[128,256]{1,0:T(8,128)S(1)}, u32[]{:S(2)}) copy-start(f32[128,256]{1,0:T(8,128)S(1)} %get-tuple-element.41) | copy-start | bytes 393220
  7.9 17.3 %copy-start.9 = (f32[128,256]{1,0:T(8,128)}, f32[128,256]{1,0:T(8,128)S(1)}, u32[]{:S(2)}) copy-start(f32[128,256]{1,0:T(8,128)S(1)} %get-tuple-element.40) | copy-start | bytes 393220
  10.1 1.4 %collective-permute-start.1 = (f32[128,256]{1,0:T(8,128)S(1)}, f32[128,256]{1,0:T(8,128)S(1)}, u32[]{:S(2)}, u32[]{:S(2)}) collective-permute-start(f32[128,256]{1,0:T(8,128)S(1)} %get-tuple-element.38), channel_id=1, source_target_pairs={{0,1},{1,0},{2,3},{3,2},{4,5},{5,4},{6,7},{7,6},{8,9},{9,8},{10,11... | collective-permute-start | bytes 393224 | tf_op jit(solution)/shard_map/ppermute | solution.py:146
  11.6 7.8 %collective-permute-start.4 = (f32[128,256]{1,0:T(8,128)S(1)}, f32[128,256]{1,0:T(8,128)S(1)}, u32[]{:S(2)}, u32[]{:S(2)}) collective-permute-start(f32[128,256]{1,0:T(8,128)S(1)} %multiply_add_fusion.7), channel_id=1, source_target_pairs={{0,2},{1,3},{2,0},{3,1},{4,6},{5,7},{6,4},{7,5},{8,10},{9,11},{10,... | collective-permute-start | bytes 393224 | tf_op jit(solution)/shard_map/ppermute | solution.py:146
  13.3 7.3 %collective-permute-start.3 = (f32[128,256]{1,0:T(8,128)S(1)}, f32[128,256]{1,0:T(8,128)S(1)}, u32[]{:S(2)}, u32[]{:S(2)}) collective-permute-start(f32[128,256]{1,0:T(8,128)S(1)} %multiply_add_fusion.7), channel_id=1, source_target_pairs={{0,6},{1,7},{2,4},{3,5},{4,2},{5,3},{6,0},{7,1},{8,14},{9,15},{10,... | collective-permute-start | bytes 393224 | tf_op jit(solution)/shard_map/ppermute | solution.py:146
  14.9 6.4 %collective-permute-start.2 = (f32[128,256]{1,0:T(8,128)S(1)}, f32[128,256]{1,0:T(8,128)S(1)}, u32[]{:S(2)}, u32[]{:S(2)}) collective-permute-start(f32[128,256]{1,0:T(8,128)S(1)} %multiply_add_fusion.7), channel_id=1, source_target_pairs={{0,4},{1,5},{2,6},{3,7},{4,0},{5,1},{6,2},{7,3},{8,12},{9,13},{10,... | collective-permute-start | bytes 393224 | tf_op jit(solution)/shard_map/ppermute | solution.py:146
  15.1 6.3 %collective-permute-start.5 = (f32[128,256]{1,0:T(8,128)S(1)}, f32[128,256]{1,0:T(8,128)S(1)}, u32[]{:S(2)}, u32[]{:S(2)}) collective-permute-start(f32[128,256]{1,0:T(8,128)S(1)} %get-tuple-element.36.kept_ref), channel_id=1, source_target_pairs={{0,16},{16,0},{1,17},{17,1},{2,18},{18,2},{3,19},{19,3},{4,20},{20... | collective-permute-start | bytes 393224 | tf_op jit(solution)/shard_map/ppermute | solution.py:146
  16.9 11.4 %collective-permute-start.7 = (f32[128,256]{1,0:T(8,128)S(1)}, f32[128,256]{1,0:T(8,128)S(1)}, u32[]{:S(2)}, u32[]{:S(2)}) collective-permute-start(f32[128,256]{1,0:T(8,128)S(1)} %collective-permute-done.1.came_ref), channel_id=1, source_target_pairs={{0,16},{16,0},{1,17},{17,1},{2,18},{18,2},{3,19},{19,3},{4,20},{20... | collective-permute-start | bytes 393224 | tf_op jit(solution)/shard_map/ppermute | solution.py:146
  21.4 6.9 %collective-permute-start.6 = (f32[128,256]{1,0:T(8,128)S(1)}, f32[128,256]{1,0:T(8,128)S(1)}, u32[]{:S(2)}, u32[]{:S(2)}) collective-permute-start(f32[128,256]{1,0:T(8,128)S(1)} %multiply_add_fusion.6), channel_id=1, source_target_pairs={{0,12},{1,13},{2,14},{3,15},{4,8},{5,9},{6,10},{7,11},{8,4},{9,5},... | collective-permute-start | bytes 393224 | tf_op jit(solution)/shard_map/ppermute | solution.py:146
  28.4 1.8 %collective-permute-start.9 = (f32[128,256]{1,0:T(8,128)S(1)}, f32[128,256]{1,0:T(8,128)S(1)}, u32[]{:S(2)}, u32[]{:S(2)}) collective-permute-start(f32[128,256]{1,0:T(8,128)S(1)} %get-tuple-element.52), channel_id=1, source_target_pairs={{0,1},{1,0},{2,3},{3,2},{4,5},{5,4},{6,7},{7,6},{8,9},{9,8},{10,11... | collective-permute-start | bytes 393224 | tf_op jit(solution)/shard_map/ppermute | solution.py:146
  28.4 5.9 %collective-permute-start.8 = (f32[128,256]{1,0:T(8,128)S(1)}, f32[128,256]{1,0:T(8,128)S(1)}, u32[]{:S(2)}, u32[]{:S(2)}) collective-permute-start(f32[128,256]{1,0:T(8,128)S(1)} %multiply_add_fusion.4.entering_ref), channel_id=1, source_target_pairs={{0,16},{16,0},{1,17},{17,1},{2,18},{18,2},{3,19},{19,3},{4,20},{20... | collective-permute-start | bytes 393224 | tf_op jit(solution)/shard_map/ppermute | solution.py:146
  30.2 1.0 %copy-start.4 = (f32[1,1,256,256]{3,2,1,0:T(8,128)S(1)}, f32[1,1,256,256]{3,2,1,0:T(8,128)}, u32[]{:S(2)}) copy-start(f32[1,1,256,256]{3,2,1,0:T(8,128)} %param.12) | copy-start | bytes 786436
  30.2 1.0 %copy-start.6 = (f32[256,256]{1,0:T(8,128)S(1)}, f32[256,256]{1,0:T(8,128)}, u32[]{:S(2)}) copy-start(f32[256,256]{1,0:T(8,128)} %diffusion_ref.3) | copy-start | bytes 786436
  34.4 1.4 %collective-permute-start.10 = (f32[128,256]{1,0:T(8,128)S(1)}, f32[128,256]{1,0:T(8,128)S(1)}, u32[]{:S(2)}, u32[]{:S(2)}) collective-permute-start(f32[128,256]{1,0:T(8,128)S(1)} %get-tuple-element.58), channel_id=1, source_target_pairs={{0,1},{1,0},{2,3},{3,2},{4,5},{5,4},{6,7},{7,6},{8,9},{9,8},{10,11... | collective-permute-start | bytes 393224 | tf_op jit(solution)/shard_map/ppermute | solution.py:146
  37.0 1.4 %collective-permute-start.11 = (f32[128,256]{1,0:T(8,128)S(1)}, f32[128,256]{1,0:T(8,128)S(1)}, u32[]{:S(2)}, u32[]{:S(2)}) collective-permute-start(f32[128,256]{1,0:T(8,128)S(1)} %get-tuple-element.60), channel_id=1, source_target_pairs={{0,1},{1,0},{2,3},{3,2},{4,5},{5,4},{6,7},{7,6},{8,9},{9,8},{10,11... | collective-permute-start | bytes 393224 | tf_op jit(solution)/shard_map/ppermute | solution.py:146
  38.5 13.5 %copy-start.8 = (f32[128,256]{1,0:T(8,128)S(1)}, f32[128,256]{1,0:T(8,128)}, u32[]{:S(2)}) copy-start(f32[128,256]{1,0:T(8,128)} %copy-done.7) | copy-start | bytes 393220
  38.5 13.5 %copy-start.10 = (f32[128,256]{1,0:T(8,128)S(1)}, f32[128,256]{1,0:T(8,128)}, u32[]{:S(2)}) copy-start(f32[128,256]{1,0:T(8,128)} %copy-done.9) | copy-start | bytes 393220
  38.5 7.9 %collective-permute-start.14 = (f32[128,256]{1,0:T(8,128)S(1)}, f32[128,256]{1,0:T(8,128)S(1)}, u32[]{:S(2)}, u32[]{:S(2)}) collective-permute-start(f32[128,256]{1,0:T(8,128)S(1)} %multiply_add_fusion.3), channel_id=1, source_target_pairs={{0,2},{1,3},{2,0},{3,1},{4,6},{5,7},{6,4},{7,5},{8,10},{9,11},{10,... | collective-permute-start | bytes 393224 | tf_op jit(solution)/shard_map/ppermute | solution.py:146
  40.2 7.3 %collective-permute-start.13 = (f32[128,256]{1,0:T(8,128)S(1)}, f32[128,256]{1,0:T(8,128)S(1)}, u32[]{:S(2)}, u32[]{:S(2)}) collective-permute-start(f32[128,256]{1,0:T(8,128)S(1)} %multiply_add_fusion.3), channel_id=1, source_target_pairs={{0,6},{1,7},{2,4},{3,5},{4,2},{5,3},{6,0},{7,1},{8,14},{9,15},{10,... | collective-permute-start | bytes 393224 | tf_op jit(solution)/shard_map/ppermute | solution.py:146
  42.2 6.4 %collective-permute-start.12 = (f32[128,256]{1,0:T(8,128)S(1)}, f32[128,256]{1,0:T(8,128)S(1)}, u32[]{:S(2)}, u32[]{:S(2)}) collective-permute-start(f32[128,256]{1,0:T(8,128)S(1)} %multiply_add_fusion.3), channel_id=1, source_target_pairs={{0,4},{1,5},{2,6},{3,7},{4,0},{5,1},{6,2},{7,3},{8,12},{9,13},{10,... | collective-permute-start | bytes 393224 | tf_op jit(solution)/shard_map/ppermute | solution.py:146
  48.6 6.9 %collective-permute-start.15 = (f32[128,256]{1,0:T(8,128)S(1)}, f32[128,256]{1,0:T(8,128)S(1)}, u32[]{:S(2)}, u32[]{:S(2)}) collective-permute-start(f32[128,256]{1,0:T(8,128)S(1)} %multiply_add_fusion.2), channel_id=1, source_target_pairs={{0,12},{1,13},{2,14},{3,15},{4,8},{5,9},{6,10},{7,11},{8,4},{9,5},... | collective-permute-start | bytes 393224 | tf_op jit(solution)/shard_map/ppermute | solution.py:146
  55.6 1.4 %collective-permute-start.16 = (f32[128,256]{1,0:T(8,128)S(1)}, f32[128,256]{1,0:T(8,128)S(1)}, u32[]{:S(2)}, u32[]{:S(2)}) collective-permute-start(f32[128,256]{1,0:T(8,128)S(1)} %get-tuple-element.62), channel_id=1, source_target_pairs={{0,1},{1,0},{2,3},{3,2},{4,5},{5,4},{6,7},{7,6},{8,9},{9,8},{10,11... | collective-permute-start | bytes 393224 | tf_op jit(solution)/shard_map/ppermute | solution.py:146

commit v7 on v6

--- a/solution.py
+++ b/solution.py
@@ -77,39 +77,45 @@
     return product(split(product((x_ref[0, place], x_ref[1, place]), middle)), y_table)
 
 
-def forward(scale, adjoint, core, side, own, partner, reaction, x_ref, y_ref, keep_ref, send_ref, work_ref):
+def half_rows(core, half):
+    return pl.ds(pl.multiple_of(core * half, half), half)
+
+
+def send_half(scale, adjoint, core, side, own, partner, reaction, x_ref, y_ref, side_ref, send_ref):
     adjoint_part = 3.0 * reaction * partner * partner * own - partner
-    side = split(side - jnp.where(adjoint, adjoint_part, gamma_inv * partner))
-    for place in row_halves(work_ref.shape[0]):
-        work_ref[place, :] = both_sides(x_ref, side, parts(y_ref), place) * scale
-    half = keep_ref.shape[0]
-    keep_ref[...] = work_ref[pl.ds(pl.multiple_of(core * half, half), half), :]
-    send_ref[...] = work_ref[pl.ds(pl.multiple_of((1 - core) * half, half), half), :]
+    side = side - jnp.where(adjoint, adjoint_part, gamma_inv * partner)
+    place = half_rows(1 - core, send_ref.shape[0])
+    send_ref[...] = both_sides(x_ref, split(side), parts(y_ref), place) * scale
+    side_ref[...] = side
+
+
+def keep_kernel(scale, core_ref, side_ref, x_ref, y_ref, keep_ref):
+    place = half_rows(core_ref[0], keep_ref.shape[0])
+    keep_ref[...] = both_sides(x_ref, split(side_ref[...]), parts(y_ref), place) * scale
 
 
 def first_kernel(
-    scale, adjoint_ref, core_ref, side_ref, own_ref, partner_ref, reaction_ref, x_ref, y_ref, keep_ref, send_ref, work_ref
+    scale, adjoint_ref, core_ref, own_side_ref, own_ref, partner_ref, reaction_ref, x_ref, y_ref, side_ref, send_ref
 ):
-    forward(
-        scale, adjoint_ref[0] == 1, core_ref[0], side_ref[...], own_ref[...], partner_ref[...], reaction_ref[...],
-        x_ref, y_ref, keep_ref, send_ref, work_ref,
+    send_half(
+        scale, adjoint_ref[0] == 1, core_ref[0], own_side_ref[...], own_ref[...], partner_ref[...], reaction_ref[...],
+        x_ref, y_ref, side_ref, send_ref,
     )
 
 
 def later_kernel(
     scale, adjoint_ref, core_ref, partner_last_ref,
-    side_ref, own_ref, kept_ref, came_ref, former_ref, reaction_ref, x_ref, y_ref,
-    keep_ref, send_ref, *refs,
+    own_side_ref, own_ref, kept_ref, came_ref, former_ref, reaction_ref, x_ref, y_ref,
+    side_ref, send_ref, *refs,
 ):
-    work_ref = refs[-1]
-    modes = gather_halves(core_ref[0], work_ref, kept_ref, came_ref)
+    modes = gather_halves(core_ref[0], refs[-1], kept_ref, came_ref)
     former = jnp.where(partner_last_ref[0] == 1, 1.0, 0.0) * former_ref[...]
     partner = former + both_sides(x_ref, modes, parts(y_ref), slice(None))
     if len(refs) > 1:
         refs[0][...] = partner
-    forward(
-        scale, adjoint_ref[0] == 1, core_ref[0], side_ref[...], own_ref[...], partner, reaction_ref[...],
-        x_ref, y_ref, keep_ref, send_ref, work_ref,
+    send_half(
+        scale, adjoint_ref[0] == 1, core_ref[0], own_side_ref[...], own_ref[...], partner, reaction_ref[...],
+        x_ref, y_ref, side_ref, send_ref,
     )
 
 
@@ -248,22 +254,22 @@
     for iteration in range(ITERS):
         more = iteration + 1 < ITERS
         if iteration == 0:
-            kept, sent = call(
+            side, sent = call(
                 functools.partial(first_kernel, scale),
                 (adjoint, side_of),
                 (side, own, *partner, reaction, *tables),
-                [(half, grid_y)] * 2,
-                [own.shape],
+                [own.shape, (half, grid_y)],
             )
         else:
-            kept, sent, *partner = call(
+            side, sent, *partner = call(
                 functools.partial(later_kernel, scale),
                 (adjoint, side_of, other_last),
                 (side, own, other_kept, other_came, *partner, reaction, *tables),
-                [(half, grid_y)] * 2 + [own.shape] * more,
+                [own.shape, (half, grid_y)] + [own.shape] * more,
                 [own.shape],
             )
         came = swap(sent, "tm", 1)
+        (kept,) = call(functools.partial(keep_kernel, scale), (side_of,), (side, *tables), [(half, grid_y)])
         entering, other_sides = carry_in(kept, came, pair, levels, more)
         new, sent = both_steps(odd, entering, kept, came)
         if more:

time: 58.5 us -> 58.3 us (level)
  waiting for transfers between devices: 26.3 us -> 25.4 us
  Pallas kernels: 4.53 us -> 5.18 us
    ppermute x17, waiting for transfers between devices: 26.3 us -> 25.4 us  [swap(): lax.ppermute(values, axis, [(i, i ^ mask) for i in range(lax.axis_size(ax...]
    pallas_call x9 -> x11, Pallas kernels: 4.53 us -> 5.18 us  [call(): pl.pallas_call(kernel, out_shape=[jax.ShapeDtypeStruct(shape, jnp.float32...]
    unnamed x24 -> x28, local copies, waits for them, and re-layouts: 2.39 us -> 2.4 us
  transfers between devices with their start and end apart: 17 -> 17, of which waited for: 14 -> 14; matrix products, arithmetic and copies ran while one was open for 2% -> 2% of each run, Pallas kernels for 2% -> 4%
where the time goes in v7:
time: 58.3 us; the launch traced here: 58.1 us
  waiting for transfers between devices  25.4 us (44%)
  starting transfers between devices  21.6 us (37%)
  Pallas kernels  5.18 us (9%)
  local copies, waits for them, and re-layouts  2.49 us (4%)
  between operations  2.36 us (4%)
  other arithmetic  0.99 us (2%)
    ppermute x17, waiting for transfers between devices, swap(): lax.ppermute(values, axis, [(i, i ^ mask) for i in range(lax.axis_size(ax...  25.4 us
    ppermute x17, starting transfers between devices, swap(): lax.ppermute(values, axis, [(i, i ^ mask) for i in range(lax.axis_size(ax...  21.6 us
    pallas_call x11, Pallas kernels, call(): pl.pallas_call(kernel, out_shape=[jax.ShapeDtypeStruct(shape, jnp.float32...  5.18 us
    unnamed x28, local copies, waits for them, and re-layouts  2.4 us
  transfers between devices with their start and end apart: 17, of which 14 were waited for; matrix products, arithmetic and copies ran while one was open for 2% of the time, Pallas kernels for 4%

profile of v7, /device:TPU:0, one launch (start us, length us, event | category | flops | bytes accessed | tf_op | source)
XLA Modules:
  0.0 58.1 jit_solution(11545750182320483118)
XLA Ops:
  0.0 3.0 %collective-permute-start = (f32[256,256]{1,0:T(8,128)}, f32[256,256]{1,0:T(8,128)S(1)}, u32[]{:S(2)}, u32[]{:S(2)}) collective-permute-start(f32[256,256]{1,0:T(8,128)} %bitcast.17), channel_id=1, source_target_pairs={{0,16},{16,0},{1,17},{17,1},{2,18},{18,2},{3,19},{19,3},{4,20},{20... | collective-permute-start | bytes 786440 | tf_op jit(solution)/shard_map/ppermute | solution.py:152
  5.4 0.9 %copy-done.3 = f32[1,1,256,256]{3,2,1,0:T(8,128)S(1)} copy-done((f32[1,1,256,256]{3,2,1,0:T(8,128)S(1)}, f32[1,1,256,256]{3,2,1,0:T(8,128)}, u32[]{:S(2)}) %copy-start.3) | copy-done | bytes 262168
  6.3 0.9 %copy-done.5 = f32[256,256]{1,0:T(8,128)S(1)} copy-done((f32[256,256]{1,0:T(8,128)S(1)}, f32[256,256]{1,0:T(8,128)}, u32[]{:S(2)}) %copy-start.5) | copy-done | bytes 262168
  7.9 1.6 %collective-permute-done.partner_ref.former_ref = f32[256,256]{1,0:T(8,128)S(1)} collective-permute-done((f32[256,256]{1,0:T(8,128)}, f32[256,256]{1,0:T(8,128)S(1)}, u32[]{:S(2)}, u32[]{:S(2)}) %collective-permute-start) | collective-permute-done | bytes 262176 | tf_op jit(solution)/shard_map/ppermute | solution.py:152
  9.5 0.5 shard_map.110
  10.2 0.4 shard_map.111.kept_ref
  10.7 0.7 %collective-permute-done.1.came_ref = f32[128,256]{1,0:T(8,128)S(1)} collective-permute-done((f32[128,256]{1,0:T(8,128)S(1)}, f32[128,256]{1,0:T(8,128)S(1)}, u32[]{:S(2)}, u32[]{:S(2)}) %collective-permute-start.1) | collective-permute-done | bytes 131104 | tf_op jit(solution)/shard_map/ppermute | solution.py:152
  11.4 1.8 %collective-permute-start.4 = (f32[128,256]{1,0:T(8,128)S(1)}, f32[128,256]{1,0:T(8,128)S(1)}, u32[]{:S(2)}, u32[]{:S(2)}) collective-permute-start(f32[128,256]{1,0:T(8,128)S(1)} %multiply_add_fusion.7), channel_id=1, source_target_pairs={{0,2},{1,3},{2,0},{3,1},{4,6},{5,7},{6,4},{7,5},{8,10},{9,11},{10,... | collective-permute-start | bytes 393224 | tf_op jit(solution)/shard_map/ppermute | solution.py:152
  13.2 1.5 %collective-permute-start.3 = (f32[128,256]{1,0:T(8,128)S(1)}, f32[128,256]{1,0:T(8,128)S(1)}, u32[]{:S(2)}, u32[]{:S(2)}) collective-permute-start(f32[128,256]{1,0:T(8,128)S(1)} %multiply_add_fusion.7), channel_id=1, source_target_pairs={{0,6},{1,7},{2,4},{3,5},{4,2},{5,3},{6,0},{7,1},{8,14},{9,15},{10,... | collective-permute-start | bytes 393224 | tf_op jit(solution)/shard_map/ppermute | solution.py:152
  15.0 1.7 %collective-permute-start.5 = (f32[128,256]{1,0:T(8,128)S(1)}, f32[128,256]{1,0:T(8,128)S(1)}, u32[]{:S(2)}, u32[]{:S(2)}) collective-permute-start(f32[128,256]{1,0:T(8,128)S(1)} %shard_map.111.kept_ref), channel_id=1, source_target_pairs={{0,16},{16,0},{1,17},{17,1},{2,18},{18,2},{3,19},{19,3},{4,20},{20... | collective-permute-start | bytes 393224 | tf_op jit(solution)/shard_map/ppermute | solution.py:152
  17.0 2.2 %collective-permute-done.4 = f32[128,256]{1,0:T(8,128)S(1)} collective-permute-done((f32[128,256]{1,0:T(8,128)S(1)}, f32[128,256]{1,0:T(8,128)S(1)}, u32[]{:S(2)}, u32[]{:S(2)}) %collective-permute-start.4) | collective-permute-done | bytes 131104 | tf_op jit(solution)/shard_map/ppermute | solution.py:152
  19.2 1.3 %collective-permute-done.3 = f32[128,256]{1,0:T(8,128)S(1)} collective-permute-done((f32[128,256]{1,0:T(8,128)S(1)}, f32[128,256]{1,0:T(8,128)S(1)}, u32[]{:S(2)}, u32[]{:S(2)}) %collective-permute-start.3) | collective-permute-done | bytes 131104 | tf_op jit(solution)/shard_map/ppermute | solution.py:152
  20.5 0.7 %collective-permute-done.2 = f32[128,256]{1,0:T(8,128)S(1)} collective-permute-done((f32[128,256]{1,0:T(8,128)S(1)}, f32[128,256]{1,0:T(8,128)S(1)}, u32[]{:S(2)}, u32[]{:S(2)}) %collective-permute-start.2) | collective-permute-done | bytes 131104 | tf_op jit(solution)/shard_map/ppermute | solution.py:152
  21.3 3.8 %collective-permute-start.6 = (f32[128,256]{1,0:T(8,128)S(1)}, f32[128,256]{1,0:T(8,128)S(1)}, u32[]{:S(2)}, u32[]{:S(2)}) collective-permute-start(f32[128,256]{1,0:T(8,128)S(1)} %multiply_add_fusion.6), channel_id=1, source_target_pairs={{0,12},{1,13},{2,14},{3,15},{4,8},{5,9},{6,10},{7,11},{8,4},{9,5},... | collective-permute-start | bytes 393224 | tf_op jit(solution)/shard_map/ppermute | solution.py:152
  25.2 2.9 %collective-permute-done.6 = f32[128,256]{1,0:T(8,128)S(1)} collective-permute-done((f32[128,256]{1,0:T(8,128)S(1)}, f32[128,256]{1,0:T(8,128)S(1)}, u32[]{:S(2)}, u32[]{:S(2)}) %collective-permute-start.6) | collective-permute-done | bytes 131104 | tf_op jit(solution)/shard_map/ppermute | solution.py:152
  28.3 1.7 %collective-permute-start.8 = (f32[128,256]{1,0:T(8,128)S(1)}, f32[128,256]{1,0:T(8,128)S(1)}, u32[]{:S(2)}, u32[]{:S(2)}) collective-permute-start(f32[128,256]{1,0:T(8,128)S(1)} %multiply_add_fusion.4.entering_ref), channel_id=1, source_target_pairs={{0,16},{16,0},{1,17},{17,1},{2,18},{18,2},{3,19},{19,3},{4,20},{20... | collective-permute-start | bytes 393224 | tf_op jit(solution)/shard_map/ppermute | solution.py:152
  30.1 0.6 shard_map.113.own_ref
  31.1 0.4 shard_map.114.own_side_ref
  31.5 2.8 %collective-permute-done.8.entering_ref = f32[128,256]{1,0:T(8,128)S(1)} collective-permute-done((f32[128,256]{1,0:T(8,128)S(1)}, f32[128,256]{1,0:T(8,128)S(1)}, u32[]{:S(2)}, u32[]{:S(2)}) %collective-permute-start.8) | collective-permute-done | bytes 131104 | tf_op jit(solution)/shard_map/ppermute | solution.py:152
  34.4 1.3 %collective-permute-done.10.came_ref = f32[128,256]{1,0:T(8,128)S(1)} collective-permute-done((f32[128,256]{1,0:T(8,128)S(1)}, f32[128,256]{1,0:T(8,128)S(1)}, u32[]{:S(2)}, u32[]{:S(2)}) %collective-permute-start.10) | collective-permute-done | bytes 131104 | tf_op jit(solution)/shard_map/ppermute | solution.py:152
  35.7 1.1 %shard_map.116 = (f32[256,256]{1,0:T(8,128)S(1)}, f32[128,256]{1,0:T(8,128)S(1)}) custom-call(s32[1]{0:T(128)} %bitcast.6.adjoint_ref, s32[1]{0:T(128)} %bitcast.core_ref, s32[1]{0:T(128)} %bitcast.7.partner_last_ref, f32[256,256]{1,0:T(8,128)S(1)} %shard_map.114.own_side_ref, f32[256,256]{1,0:T(8,128)S(1)} %shard_map.113.own_ref, ...), custom_call_target="tpu_custom_call" | custom-call | tf_op jit(solution)/shard_map/pallas_call | solution.py:141
  37.0 0.4 shard_map.117.kept_ref
  37.4 0.8 %collective-permute-done.11.came_ref = f32[128,256]{1,0:T(8,128)S(1)} collective-permute-done((f32[128,256]{1,0:T(8,128)S(1)}, f32[128,256]{1,0:T(8,128)S(1)}, u32[]{:S(2)}, u32[]{:S(2)}) %collective-permute-start.11) | collective-permute-done | bytes 131104 | tf_op jit(solution)/shard_map/ppermute | solution.py:152
  38.3 1.7 %collective-permute-start.14 = (f32[128,256]{1,0:T(8,128)S(1)}, f32[128,256]{1,0:T(8,128)S(1)}, u32[]{:S(2)}, u32[]{:S(2)}) collective-permute-start(f32[128,256]{1,0:T(8,128)S(1)} %multiply_add_fusion.3), channel_id=1, source_target_pairs={{0,2},{1,3},{2,0},{3,1},{4,6},{5,7},{6,4},{7,5},{8,10},{9,11},{10,... | collective-permute-start | bytes 393224 | tf_op jit(solution)/shard_map/ppermute | solution.py:152
  40.0 2.0 %collective-permute-start.13 = (f32[128,256]{1,0:T(8,128)S(1)}, f32[128,256]{1,0:T(8,128)S(1)}, u32[]{:S(2)}, u32[]{:S(2)}) collective-permute-start(f32[128,256]{1,0:T(8,128)S(1)} %multiply_add_fusion.3), channel_id=1, source_target_pairs={{0,6},{1,7},{2,4},{3,5},{4,2},{5,3},{6,0},{7,1},{8,14},{9,15},{10,... | collective-permute-start | bytes 393224 | tf_op jit(solution)/shard_map/ppermute | solution.py:152
  42.0 4.2 %collective-permute-done.14 = f32[128,256]{1,0:T(8,128)S(1)} collective-permute-done((f32[128,256]{1,0:T(8,128)S(1)}, f32[128,256]{1,0:T(8,128)S(1)}, u32[]{:S(2)}, u32[]{:S(2)}) %collective-permute-start.14) | collective-permute-done | bytes 131104 | tf_op jit(solution)/shard_map/ppermute | solution.py:152
  46.1 1.1 %collective-permute-done.13 = f32[128,256]{1,0:T(8,128)S(1)} collective-permute-done((f32[128,256]{1,0:T(8,128)S(1)}, f32[128,256]{1,0:T(8,128)S(1)}, u32[]{:S(2)}, u32[]{:S(2)}) %collective-permute-start.13) | collective-permute-done | bytes 131104 | tf_op jit(solution)/shard_map/ppermute | solution.py:152
  47.2 1.1 %collective-permute-done.12 = f32[128,256]{1,0:T(8,128)S(1)} collective-permute-done((f32[128,256]{1,0:T(8,128)S(1)}, f32[128,256]{1,0:T(8,128)S(1)}, u32[]{:S(2)}, u32[]{:S(2)}) %collective-permute-start.12) | collective-permute-done | bytes 131104 | tf_op jit(solution)/shard_map/ppermute | solution.py:152
  48.4 3.4 %collective-permute-start.15 = (f32[128,256]{1,0:T(8,128)S(1)}, f32[128,256]{1,0:T(8,128)S(1)}, u32[]{:S(2)}, u32[]{:S(2)}) collective-permute-start(f32[128,256]{1,0:T(8,128)S(1)} %multiply_add_fusion.2), channel_id=1, source_target_pairs={{0,12},{1,13},{2,14},{3,15},{4,8},{5,9},{6,10},{7,11},{8,4},{9,5},... | collective-permute-start | bytes 393224 | tf_op jit(solution)/shard_map/ppermute | solution.py:152
  51.9 3.4 %collective-permute-done.15 = f32[128,256]{1,0:T(8,128)S(1)} collective-permute-done((f32[128,256]{1,0:T(8,128)S(1)}, f32[128,256]{1,0:T(8,128)S(1)}, u32[]{:S(2)}, u32[]{:S(2)}) %collective-permute-start.15) | collective-permute-done | bytes 131104 | tf_op jit(solution)/shard_map/ppermute | solution.py:152
  55.5 1.3 %collective-permute-done.16.came_ref = f32[128,256]{1,0:T(8,128)S(1)} collective-permute-done((f32[128,256]{1,0:T(8,128)S(1)}, f32[128,256]{1,0:T(8,128)S(1)}, u32[]{:S(2)}, u32[]{:S(2)}) %collective-permute-start.16) | collective-permute-done | bytes 131104 | tf_op jit(solution)/shard_map/ppermute | solution.py:152
  56.8 1.3 %shard_map.119 = f32[256,256]{1,0:T(8,128)} custom-call(s32[1]{0:T(128)} %bitcast.core_ref, s32[1]{0:T(128)} %bitcast.1.last_ref, f32[128,256]{1,0:T(8,128)S(1)} %get-tuple-element.61.kept_ref, f32[128,256]{1,0:T(8,128)S(1)} %collective-permute-done.16.came_ref, f32[256,256]{1,0:T(8,128)S(1)} %shard_map.113.own_ref, bf16[2,256,256]{2,1,0:T(8,128)(2,1)S(1)} %copy-done, ...), custom_call_target="tpu_custom_call" | custom-call | tf_op jit(solution)/shard_map/pallas_call | solution.py:141
  (54 shorter events, 3.2 us)
Async XLA Ops:
  0.0 9.5 %collective-permute-start = (f32[256,256]{1,0:T(8,128)}, f32[256,256]{1,0:T(8,128)S(1)}, u32[]{:S(2)}, u32[]{:S(2)}) collective-permute-start(f32[256,256]{1,0:T(8,128)} %bitcast.17), channel_id=1, source_target_pairs={{0,16},{16,0},{1,17},{17,1},{2,18},{18,2},{3,19},{19,3},{4,20},{20... | collective-permute-start | bytes 786440 | tf_op jit(solution)/shard_map/ppermute | solution.py:152
  3.0 2.0 %copy-start.13 = (f32[256]{0:T(256)S(1)}, f32[256]{0:T(256)}, u32[]{:S(2)}) copy-start(f32[256]{0:T(256)} %constant.37.clone) | copy-start | bytes 3076
  3.0 2.4 %copy-start.2 = (f32[1,1,256,256]{3,2,1,0:T(8,128)S(1)}, f32[1,1,256,256]{3,2,1,0:T(8,128)}, u32[]{:S(2)}) copy-start(f32[1,1,256,256]{3,2,1,0:T(8,128)} %param.11) | copy-start | bytes 786436
  3.0 2.4 %copy-start.1 = (f32[256,256]{1,0:T(8,128)S(1)}, f32[256,256]{1,0:T(8,128)}, u32[]{:S(2)}) copy-start(f32[256,256]{1,0:T(8,128)} %reaction_ref.7) | copy-start | bytes 786436
  5.3 1.0 %copy-start.3 = (f32[1,1,256,256]{3,2,1,0:T(8,128)S(1)}, f32[1,1,256,256]{3,2,1,0:T(8,128)}, u32[]{:S(2)}) copy-start(f32[1,1,256,256]{3,2,1,0:T(8,128)} %param.12) | copy-start | bytes 786436
  6.3 0.9 %copy-start.5 = (f32[256,256]{1,0:T(8,128)S(1)}, f32[256,256]{1,0:T(8,128)}, u32[]{:S(2)}) copy-start(f32[256,256]{1,0:T(8,128)} %diffusion_ref.3) | copy-start | bytes 786436
  7.6 1.8 %copy-start = (bf16[2,256,256]{2,1,0:T(8,128)(2,1)S(1)}, bf16[2,256,256]{2,1,0:T(8,128)(2,1)}, u32[]{:S(2)}) copy-start(bf16[2,256,256]{2,1,0:T(8,128)(2,1)} %constant.36.clone.x_ref.y_ref) | copy-start | bytes 786436
  7.9 17.2 %copy-start.7 = (f32[128,256]{1,0:T(8,128)}, f32[128,256]{1,0:T(8,128)S(1)}, u32[]{:S(2)}) copy-start(f32[128,256]{1,0:T(8,128)S(1)} %get-tuple-element.42) | copy-start | bytes 393220
  7.9 17.2 %copy-start.9 = (f32[128,256]{1,0:T(8,128)}, f32[128,256]{1,0:T(8,128)S(1)}, u32[]{:S(2)}) copy-start(f32[128,256]{1,0:T(8,128)S(1)} %get-tuple-element.41) | copy-start | bytes 393220
  7.9 17.2 %copy-start.11 = (f32[128,256]{1,0:T(8,128)}, f32[128,256]{1,0:T(8,128)S(1)}, u32[]{:S(2)}) copy-start(f32[128,256]{1,0:T(8,128)S(1)} %get-tuple-element.40) | copy-start | bytes 393220
  10.0 1.4 %collective-permute-start.1 = (f32[128,256]{1,0:T(8,128)S(1)}, f32[128,256]{1,0:T(8,128)S(1)}, u32[]{:S(2)}, u32[]{:S(2)}) collective-permute-start(f32[128,256]{1,0:T(8,128)S(1)} %get-tuple-element.38), channel_id=1, source_target_pairs={{0,1},{1,0},{2,3},{3,2},{4,5},{5,4},{6,7},{7,6},{8,9},{9,8},{10,11... | collective-permute-start | bytes 393224 | tf_op jit(solution)/shard_map/ppermute | solution.py:152
  11.4 7.8 %collective-permute-start.4 = (f32[128,256]{1,0:T(8,128)S(1)}, f32[128,256]{1,0:T(8,128)S(1)}, u32[]{:S(2)}, u32[]{:S(2)}) collective-permute-start(f32[128,256]{1,0:T(8,128)S(1)} %multiply_add_fusion.7), channel_id=1, source_target_pairs={{0,2},{1,3},{2,0},{3,1},{4,6},{5,7},{6,4},{7,5},{8,10},{9,11},{10,... | collective-permute-start | bytes 393224 | tf_op jit(solution)/shard_map/ppermute | solution.py:152
  13.2 7.3 %collective-permute-start.3 = (f32[128,256]{1,0:T(8,128)S(1)}, f32[128,256]{1,0:T(8,128)S(1)}, u32[]{:S(2)}, u32[]{:S(2)}) collective-permute-start(f32[128,256]{1,0:T(8,128)S(1)} %multiply_add_fusion.7), channel_id=1, source_target_pairs={{0,6},{1,7},{2,4},{3,5},{4,2},{5,3},{6,0},{7,1},{8,14},{9,15},{10,... | collective-permute-start | bytes 393224 | tf_op jit(solution)/shard_map/ppermute | solution.py:152
  14.8 6.4 %collective-permute-start.2 = (f32[128,256]{1,0:T(8,128)S(1)}, f32[128,256]{1,0:T(8,128)S(1)}, u32[]{:S(2)}, u32[]{:S(2)}) collective-permute-start(f32[128,256]{1,0:T(8,128)S(1)} %multiply_add_fusion.7), channel_id=1, source_target_pairs={{0,4},{1,5},{2,6},{3,7},{4,0},{5,1},{6,2},{7,3},{8,12},{9,13},{10,... | collective-permute-start | bytes 393224 | tf_op jit(solution)/shard_map/ppermute | solution.py:152
  15.0 6.3 %collective-permute-start.5 = (f32[128,256]{1,0:T(8,128)S(1)}, f32[128,256]{1,0:T(8,128)S(1)}, u32[]{:S(2)}, u32[]{:S(2)}) collective-permute-start(f32[128,256]{1,0:T(8,128)S(1)} %shard_map.111.kept_ref), channel_id=1, source_target_pairs={{0,16},{16,0},{1,17},{17,1},{2,18},{18,2},{3,19},{19,3},{4,20},{20... | collective-permute-start | bytes 393224 | tf_op jit(solution)/shard_map/ppermute | solution.py:152
  16.7 11.5 %collective-permute-start.7 = (f32[128,256]{1,0:T(8,128)S(1)}, f32[128,256]{1,0:T(8,128)S(1)}, u32[]{:S(2)}, u32[]{:S(2)}) collective-permute-start(f32[128,256]{1,0:T(8,128)S(1)} %collective-permute-done.1.came_ref), channel_id=1, source_target_pairs={{0,16},{16,0},{1,17},{17,1},{2,18},{18,2},{3,19},{19,3},{4,20},{20... | collective-permute-start | bytes 393224 | tf_op jit(solution)/shard_map/ppermute | solution.py:152
  21.3 6.9 %collective-permute-start.6 = (f32[128,256]{1,0:T(8,128)S(1)}, f32[128,256]{1,0:T(8,128)S(1)}, u32[]{:S(2)}, u32[]{:S(2)}) collective-permute-start(f32[128,256]{1,0:T(8,128)S(1)} %multiply_add_fusion.6), channel_id=1, source_target_pairs={{0,12},{1,13},{2,14},{3,15},{4,8},{5,9},{6,10},{7,11},{8,4},{9,5},... | collective-permute-start | bytes 393224 | tf_op jit(solution)/shard_map/ppermute | solution.py:152
  28.2 1.8 %collective-permute-start.9 = (f32[128,256]{1,0:T(8,128)S(1)}, f32[128,256]{1,0:T(8,128)S(1)}, u32[]{:S(2)}, u32[]{:S(2)}) collective-permute-start(f32[128,256]{1,0:T(8,128)S(1)} %get-tuple-element.52), channel_id=1, source_target_pairs={{0,1},{1,0},{2,3},{3,2},{4,5},{5,4},{6,7},{7,6},{8,9},{9,8},{10,11... | collective-permute-start | bytes 393224 | tf_op jit(solution)/shard_map/ppermute | solution.py:152
  28.3 5.9 %collective-permute-start.8 = (f32[128,256]{1,0:T(8,128)S(1)}, f32[128,256]{1,0:T(8,128)S(1)}, u32[]{:S(2)}, u32[]{:S(2)}) collective-permute-start(f32[128,256]{1,0:T(8,128)S(1)} %multiply_add_fusion.4.entering_ref), channel_id=1, source_target_pairs={{0,16},{16,0},{1,17},{17,1},{2,18},{18,2},{3,19},{19,3},{4,20},{20... | collective-permute-start | bytes 393224 | tf_op jit(solution)/shard_map/ppermute | solution.py:152
  30.0 1.0 %copy-start.4 = (f32[1,1,256,256]{3,2,1,0:T(8,128)S(1)}, f32[1,1,256,256]{3,2,1,0:T(8,128)}, u32[]{:S(2)}) copy-start(f32[1,1,256,256]{3,2,1,0:T(8,128)} %param.12) | copy-start | bytes 786436
  30.1 1.0 %copy-start.6 = (f32[256,256]{1,0:T(8,128)S(1)}, f32[256,256]{1,0:T(8,128)}, u32[]{:S(2)}) copy-start(f32[256,256]{1,0:T(8,128)} %diffusion_ref.3) | copy-start | bytes 786436
  34.3 1.4 %collective-permute-start.10 = (f32[128,256]{1,0:T(8,128)S(1)}, f32[128,256]{1,0:T(8,128)S(1)}, u32[]{:S(2)}, u32[]{:S(2)}) collective-permute-start(f32[128,256]{1,0:T(8,128)S(1)} %get-tuple-element.58), channel_id=1, source_target_pairs={{0,1},{1,0},{2,3},{3,2},{4,5},{5,4},{6,7},{7,6},{8,9},{9,8},{10,11... | collective-permute-start | bytes 393224 | tf_op jit(solution)/shard_map/ppermute | solution.py:152
  36.8 1.4 %collective-permute-start.11 = (f32[128,256]{1,0:T(8,128)S(1)}, f32[128,256]{1,0:T(8,128)S(1)}, u32[]{:S(2)}, u32[]{:S(2)}) collective-permute-start(f32[128,256]{1,0:T(8,128)S(1)} %get-tuple-element.60), channel_id=1, source_target_pairs={{0,1},{1,0},{2,3},{3,2},{4,5},{5,4},{6,7},{7,6},{8,9},{9,8},{10,11... | collective-permute-start | bytes 393224 | tf_op jit(solution)/shard_map/ppermute | solution.py:152
  38.2 13.6 %copy-start.8 = (f32[128,256]{1,0:T(8,128)S(1)}, f32[128,256]{1,0:T(8,128)}, u32[]{:S(2)}) copy-start(f32[128,256]{1,0:T(8,128)} %copy-done.7) | copy-start | bytes 393220
  38.2 13.5 %copy-start.10 = (f32[128,256]{1,0:T(8,128)S(1)}, f32[128,256]{1,0:T(8,128)}, u32[]{:S(2)}) copy-start(f32[128,256]{1,0:T(8,128)} %copy-done.9) | copy-start | bytes 393220
  38.3 13.5 %copy-start.12 = (f32[128,256]{1,0:T(8,128)S(1)}, f32[128,256]{1,0:T(8,128)}, u32[]{:S(2)}) copy-start(f32[128,256]{1,0:T(8,128)} %copy-done.11) | copy-start | bytes 393220
  38.3 7.9 %collective-permute-start.14 = (f32[128,256]{1,0:T(8,128)S(1)}, f32[128,256]{1,0:T(8,128)S(1)}, u32[]{:S(2)}, u32[]{:S(2)}) collective-permute-start(f32[128,256]{1,0:T(8,128)S(1)} %multiply_add_fusion.3), channel_id=1, source_target_pairs={{0,2},{1,3},{2,0},{3,1},{4,6},{5,7},{6,4},{7,5},{8,10},{9,11},{10,... | collective-permute-start | bytes 393224 | tf_op jit(solution)/shard_map/ppermute | solution.py:152
  40.0 7.3 %collective-permute-start.13 = (f32[128,256]{1,0:T(8,128)S(1)}, f32[128,256]{1,0:T(8,128)S(1)}, u32[]{:S(2)}, u32[]{:S(2)}) collective-permute-start(f32[128,256]{1,0:T(8,128)S(1)} %multiply_add_fusion.3), channel_id=1, source_target_pairs={{0,6},{1,7},{2,4},{3,5},{4,2},{5,3},{6,0},{7,1},{8,14},{9,15},{10,... | collective-permute-start | bytes 393224 | tf_op jit(solution)/shard_map/ppermute | solution.py:152
  41.9 6.4 %collective-permute-start.12 = (f32[128,256]{1,0:T(8,128)S(1)}, f32[128,256]{1,0:T(8,128)S(1)}, u32[]{:S(2)}, u32[]{:S(2)}) collective-permute-start(f32[128,256]{1,0:T(8,128)S(1)} %multiply_add_fusion.3), channel_id=1, source_target_pairs={{0,4},{1,5},{2,6},{3,7},{4,0},{5,1},{6,2},{7,3},{8,12},{9,13},{10,... | collective-permute-start | bytes 393224 | tf_op jit(solution)/shard_map/ppermute | solution.py:152
  48.4 6.9 %collective-permute-start.15 = (f32[128,256]{1,0:T(8,128)S(1)}, f32[128,256]{1,0:T(8,128)S(1)}, u32[]{:S(2)}, u32[]{:S(2)}) collective-permute-start(f32[128,256]{1,0:T(8,128)S(1)} %multiply_add_fusion.2), channel_id=1, source_target_pairs={{0,12},{1,13},{2,14},{3,15},{4,8},{5,9},{6,10},{7,11},{8,4},{9,5},... | collective-permute-start | bytes 393224 | tf_op jit(solution)/shard_map/ppermute | solution.py:152
  55.4 1.4 %collective-permute-start.16 = (f32[128,256]{1,0:T(8,128)S(1)}, f32[128,256]{1,0:T(8,128)S(1)}, u32[]{:S(2)}, u32[]{:S(2)}) collective-permute-start(f32[128,256]{1,0:T(8,128)S(1)} %get-tuple-element.62), channel_id=1, source_target_pairs={{0,1},{1,0},{2,3},{3,2},{4,5},{5,4},{6,7},{7,6},{8,9},{9,8},{10,11... | collective-permute-start | bytes 393224 | tf_op jit(solution)/shard_map/ppermute | solution.py:152

commit v8 on v7

--- a/solution.py
+++ b/solution.py
@@ -149,7 +149,8 @@
 
 
 def swap(values, axis, mask):
-    return lax.ppermute(values, axis, [(i, i ^ mask) for i in range(lax.axis_size(axis))])
+    masks = mask if isinstance(mask, tuple) else (mask, mask)
+    return lax.ppermute(values, axis, [(i, i ^ masks[i & 1]) for i in range(lax.axis_size(axis))])
 
 
 def power(base, exponent):
@@ -168,24 +169,25 @@
     return result
 
 
-def scan_factors(rate, alpha, place, total):
+def scan_factors(rate, alpha, place, core, total):
     none = jnp.zeros_like(rate)
     pair = (pick([rate * rate, rate], place & 1), pick([rate, rate * rate], place & 1))
     all_masks, levels, reach = [], [], None
     bit, steps = 1, 2
     while steps < total:
         count = 4 if steps * 4 <= total else 2
-        numbers = [2, 3, 1] if count == 4 else [1]
-        masks = [number << bit for number in numbers]
+        numbers = [(3, 3), (2, 1), (1, 2)] if count == 4 else [(1, 1)]
+        masks = [(even << bit, odd << bit) for even, odd in numbers]
         if count == 2 and bit > 1:
-            masks = [(1 << bit) | (1 << (bit - 1))]
+            masks = [((1 << bit) | (1 << (bit - 1)),) * 2]
         factor = power(rate, steps)
         powers = [jnp.ones_like(rate)]
         for _ in range(count - 1):
             powers.append(powers[-1] * factor)
         mine = (place >> bit) & (count - 1)
-        join = [pick(powers[::-1], mine ^ number) for number in [0] + numbers]
-        enter = [pick([none] + powers, jnp.maximum(mine - (mine ^ number), 0)) for number in [0] + numbers]
+        others = [mine ^ jnp.where(core == 1, odd, even) for even, odd in [(0, 0)] + numbers]
+        join = [pick(powers[::-1], other) for other in others]
+        enter = [pick([none] + powers, jnp.maximum(mine - other, 0)) for other in others]
         through = pick(powers, mine)
         bit, steps = bit + count.bit_length() - 1, steps * count
         if steps == total:
@@ -235,7 +237,7 @@
     last, other_last = scalar(place == total - 1), scalar(other_place == total - 1)
     eigen_x = lax.dynamic_slice_in_dim(eigenvalues(grid_x), core * half, half, 0)
     rate = 1.0 / (1.0 + spectral_shift + mean_diffusion * (eigen_x[:, None] + eigenvalues(grid_y)[None, :]))
-    pair, levels = scan_factors(rate, wrap_factor, place, total)
+    pair, levels = scan_factors(rate, wrap_factor, place, core, total)
 
     def own_side(own):
         (side,) = call(

time: 58.3 us -> 57.6 us (0.988)
  transfers between devices with their start and end apart: 17 -> 17, of which waited for: 14 -> 15; matrix products, arithmetic and copies ran while one was open for 2% -> 2% of each run, Pallas kernels for 4% -> 4%
where the time goes in v8:
time: 57.6 us; the launch traced here: 57.4 us
  waiting for transfers between devices  24.9 us (43%)
  starting transfers between devices  21.5 us (37%)
  Pallas kernels  5.18 us (9%)
  local copies, waits for them, and re-layouts  2.49 us (4%)
  between operations  2.36 us (4%)
  other arithmetic  0.99 us (2%)
    ppermute x17, waiting for transfers between devices, swap(): lax.ppermute(values, axis, [(i, i ^ masks[i & 1]) for i in range(lax.axis...  24.9 us
    ppermute x17, starting transfers between devices, swap(): lax.ppermute(values, axis, [(i, i ^ masks[i & 1]) for i in range(lax.axis...  21.5 us
    pallas_call x11, Pallas kernels, call(): pl.pallas_call(kernel, out_shape=[jax.ShapeDtypeStruct(shape, jnp.float32...  5.18 us
    unnamed x28, local copies, waits for them, and re-layouts  2.4 us
  transfers between devices with their start and end apart: 17, of which 15 were waited for; matrix products, arithmetic and copies ran while one was open for 2% of the time, Pallas kernels for 4%

profile of v8, /device:TPU:0, one launch (start us, length us, event | category | flops | bytes accessed | tf_op | source)
XLA Modules:
  0.0 57.4 jit_solution(15827216391698427088)
XLA Ops:
  0.0 3.0 %collective-permute-start = (f32[256,256]{1,0:T(8,128)}, f32[256,256]{1,0:T(8,128)S(1)}, u32[]{:S(2)}, u32[]{:S(2)}) collective-permute-start(f32[256,256]{1,0:T(8,128)} %bitcast.17), channel_id=1, source_target_pairs={{0,16},{16,0},{1,17},{17,1},{2,18},{18,2},{3,19},{19,3},{4,20},{20... | collective-permute-start | bytes 786440 | tf_op jit(solution)/shard_map/ppermute | solution.py:153
  5.4 0.9 %copy-done.3 = f32[1,1,256,256]{3,2,1,0:T(8,128)S(1)} copy-done((f32[1,1,256,256]{3,2,1,0:T(8,128)S(1)}, f32[1,1,256,256]{3,2,1,0:T(8,128)}, u32[]{:S(2)}) %copy-start.3) | copy-done | bytes 262168
  6.3 0.9 %copy-done.5 = f32[256,256]{1,0:T(8,128)S(1)} copy-done((f32[256,256]{1,0:T(8,128)S(1)}, f32[256,256]{1,0:T(8,128)}, u32[]{:S(2)}) %copy-start.5) | copy-done | bytes 262168
  7.9 1.6 %collective-permute-done.partner_ref.former_ref = f32[256,256]{1,0:T(8,128)S(1)} collective-permute-done((f32[256,256]{1,0:T(8,128)}, f32[256,256]{1,0:T(8,128)S(1)}, u32[]{:S(2)}, u32[]{:S(2)}) %collective-permute-start) | collective-permute-done | bytes 262176 | tf_op jit(solution)/shard_map/ppermute | solution.py:153
  9.5 0.5 shard_map.110
  10.2 0.4 shard_map.111.kept_ref
  10.7 0.7 %collective-permute-done.1.came_ref = f32[128,256]{1,0:T(8,128)S(1)} collective-permute-done((f32[128,256]{1,0:T(8,128)S(1)}, f32[128,256]{1,0:T(8,128)S(1)}, u32[]{:S(2)}, u32[]{:S(2)}) %collective-permute-start.1) | collective-permute-done | bytes 131104 | tf_op jit(solution)/shard_map/ppermute | solution.py:153
  11.4 1.8 %collective-permute-start.4 = (f32[128,256]{1,0:T(8,128)S(1)}, f32[128,256]{1,0:T(8,128)S(1)}, u32[]{:S(2)}, u32[]{:S(2)}) collective-permute-start(f32[128,256]{1,0:T(8,128)S(1)} %multiply_add_fusion.7), channel_id=1, source_target_pairs={{0,2},{1,5},{2,0},{3,7},{4,6},{5,1},{6,4},{7,3},{8,10},{9,13},{10,... | collective-permute-start | bytes 393224 | tf_op jit(solution)/shard_map/ppermute | solution.py:153
  13.2 1.6 %collective-permute-start.3 = (f32[128,256]{1,0:T(8,128)S(1)}, f32[128,256]{1,0:T(8,128)S(1)}, u32[]{:S(2)}, u32[]{:S(2)}) collective-permute-start(f32[128,256]{1,0:T(8,128)S(1)} %multiply_add_fusion.7), channel_id=1, source_target_pairs={{0,4},{1,3},{2,6},{3,1},{4,0},{5,7},{6,2},{7,5},{8,12},{9,11},{10,... | collective-permute-start | bytes 393224 | tf_op jit(solution)/shard_map/ppermute | solution.py:153
  15.0 1.7 %collective-permute-start.5 = (f32[128,256]{1,0:T(8,128)S(1)}, f32[128,256]{1,0:T(8,128)S(1)}, u32[]{:S(2)}, u32[]{:S(2)}) collective-permute-start(f32[128,256]{1,0:T(8,128)S(1)} %shard_map.111.kept_ref), channel_id=1, source_target_pairs={{0,16},{16,0},{1,17},{17,1},{2,18},{18,2},{3,19},{19,3},{4,20},{20... | collective-permute-start | bytes 393224 | tf_op jit(solution)/shard_map/ppermute | solution.py:153
  17.2 2.2 %collective-permute-done.3 = f32[128,256]{1,0:T(8,128)S(1)} collective-permute-done((f32[128,256]{1,0:T(8,128)S(1)}, f32[128,256]{1,0:T(8,128)S(1)}, u32[]{:S(2)}, u32[]{:S(2)}) %collective-permute-start.3) | collective-permute-done | bytes 131104 | tf_op jit(solution)/shard_map/ppermute | solution.py:153
  19.4 1.6 %collective-permute-done.2 = f32[128,256]{1,0:T(8,128)S(1)} collective-permute-done((f32[128,256]{1,0:T(8,128)S(1)}, f32[128,256]{1,0:T(8,128)S(1)}, u32[]{:S(2)}, u32[]{:S(2)}) %collective-permute-start.2) | collective-permute-done | bytes 131104 | tf_op jit(solution)/shard_map/ppermute | solution.py:153
  21.2 3.7 %collective-permute-start.6 = (f32[128,256]{1,0:T(8,128)S(1)}, f32[128,256]{1,0:T(8,128)S(1)}, u32[]{:S(2)}, u32[]{:S(2)}) collective-permute-start(f32[128,256]{1,0:T(8,128)S(1)} %multiply_add_fusion.6), channel_id=1, source_target_pairs={{0,12},{1,13},{2,14},{3,15},{4,8},{5,9},{6,10},{7,11},{8,4},{9,5},... | collective-permute-start | bytes 393224 | tf_op jit(solution)/shard_map/ppermute | solution.py:153
  25.1 3.0 %collective-permute-done.6 = f32[128,256]{1,0:T(8,128)S(1)} collective-permute-done((f32[128,256]{1,0:T(8,128)S(1)}, f32[128,256]{1,0:T(8,128)S(1)}, u32[]{:S(2)}, u32[]{:S(2)}) %collective-permute-start.6) | collective-permute-done | bytes 131104 | tf_op jit(solution)/shard_map/ppermute | solution.py:153
  28.3 1.7 %collective-permute-start.8 = (f32[128,256]{1,0:T(8,128)S(1)}, f32[128,256]{1,0:T(8,128)S(1)}, u32[]{:S(2)}, u32[]{:S(2)}) collective-permute-start(f32[128,256]{1,0:T(8,128)S(1)} %multiply_add_fusion.4.entering_ref), channel_id=1, source_target_pairs={{0,16},{16,0},{1,17},{17,1},{2,18},{18,2},{3,19},{19,3},{4,20},{20... | collective-permute-start | bytes 393224 | tf_op jit(solution)/shard_map/ppermute | solution.py:153
  30.0 0.6 shard_map.113.own_ref
  31.0 0.4 shard_map.114.own_side_ref
  31.4 2.8 %collective-permute-done.8.entering_ref = f32[128,256]{1,0:T(8,128)S(1)} collective-permute-done((f32[128,256]{1,0:T(8,128)S(1)}, f32[128,256]{1,0:T(8,128)S(1)}, u32[]{:S(2)}, u32[]{:S(2)}) %collective-permute-start.8) | collective-permute-done | bytes 131104 | tf_op jit(solution)/shard_map/ppermute | solution.py:153
  34.3 1.3 %collective-permute-done.10.came_ref = f32[128,256]{1,0:T(8,128)S(1)} collective-permute-done((f32[128,256]{1,0:T(8,128)S(1)}, f32[128,256]{1,0:T(8,128)S(1)}, u32[]{:S(2)}, u32[]{:S(2)}) %collective-permute-start.10) | collective-permute-done | bytes 131104 | tf_op jit(solution)/shard_map/ppermute | solution.py:153
  35.7 1.1 %shard_map.116 = (f32[256,256]{1,0:T(8,128)S(1)}, f32[128,256]{1,0:T(8,128)S(1)}) custom-call(s32[1]{0:T(128)} %bitcast.6.adjoint_ref, s32[1]{0:T(128)} %bitcast.core_ref, s32[1]{0:T(128)} %bitcast.7.partner_last_ref, f32[256,256]{1,0:T(8,128)S(1)} %shard_map.114.own_side_ref, f32[256,256]{1,0:T(8,128)S(1)} %shard_map.113.own_ref, ...), custom_call_target="tpu_custom_call" | custom-call | tf_op jit(solution)/shard_map/pallas_call | solution.py:141
  37.0 0.4 shard_map.117.kept_ref
  37.4 0.8 %collective-permute-done.11.came_ref = f32[128,256]{1,0:T(8,128)S(1)} collective-permute-done((f32[128,256]{1,0:T(8,128)S(1)}, f32[128,256]{1,0:T(8,128)S(1)}, u32[]{:S(2)}, u32[]{:S(2)}) %collective-permute-start.11) | collective-permute-done | bytes 131104 | tf_op jit(solution)/shard_map/ppermute | solution.py:153
  38.2 1.6 %collective-permute-start.14 = (f32[128,256]{1,0:T(8,128)S(1)}, f32[128,256]{1,0:T(8,128)S(1)}, u32[]{:S(2)}, u32[]{:S(2)}) collective-permute-start(f32[128,256]{1,0:T(8,128)S(1)} %multiply_add_fusion.3), channel_id=1, source_target_pairs={{0,2},{1,5},{2,0},{3,7},{4,6},{5,1},{6,4},{7,3},{8,10},{9,13},{10,... | collective-permute-start | bytes 393224 | tf_op jit(solution)/shard_map/ppermute | solution.py:153
  39.9 1.4 %collective-permute-start.13 = (f32[128,256]{1,0:T(8,128)S(1)}, f32[128,256]{1,0:T(8,128)S(1)}, u32[]{:S(2)}, u32[]{:S(2)}) collective-permute-start(f32[128,256]{1,0:T(8,128)S(1)} %multiply_add_fusion.3), channel_id=1, source_target_pairs={{0,4},{1,3},{2,6},{3,1},{4,0},{5,7},{6,2},{7,5},{8,12},{9,11},{10,... | collective-permute-start | bytes 393224 | tf_op jit(solution)/shard_map/ppermute | solution.py:153
  41.3 0.5 collective-permute-start.12
  41.8 2.4 %collective-permute-done.14 = f32[128,256]{1,0:T(8,128)S(1)} collective-permute-done((f32[128,256]{1,0:T(8,128)S(1)}, f32[128,256]{1,0:T(8,128)S(1)}, u32[]{:S(2)}, u32[]{:S(2)}) %collective-permute-start.14) | collective-permute-done | bytes 131104 | tf_op jit(solution)/shard_map/ppermute | solution.py:153
  44.2 1.9 %collective-permute-done.13 = f32[128,256]{1,0:T(8,128)S(1)} collective-permute-done((f32[128,256]{1,0:T(8,128)S(1)}, f32[128,256]{1,0:T(8,128)S(1)}, u32[]{:S(2)}, u32[]{:S(2)}) %collective-permute-start.13) | collective-permute-done | bytes 131104 | tf_op jit(solution)/shard_map/ppermute | solution.py:153
  46.1 1.6 %collective-permute-done.12 = f32[128,256]{1,0:T(8,128)S(1)} collective-permute-done((f32[128,256]{1,0:T(8,128)S(1)}, f32[128,256]{1,0:T(8,128)S(1)}, u32[]{:S(2)}, u32[]{:S(2)}) %collective-permute-start.12) | collective-permute-done | bytes 131104 | tf_op jit(solution)/shard_map/ppermute | solution.py:153
  47.7 3.6 %collective-permute-start.15 = (f32[128,256]{1,0:T(8,128)S(1)}, f32[128,256]{1,0:T(8,128)S(1)}, u32[]{:S(2)}, u32[]{:S(2)}) collective-permute-start(f32[128,256]{1,0:T(8,128)S(1)} %multiply_add_fusion.2), channel_id=1, source_target_pairs={{0,12},{1,13},{2,14},{3,15},{4,8},{5,9},{6,10},{7,11},{8,4},{9,5},... | collective-permute-start | bytes 393224 | tf_op jit(solution)/shard_map/ppermute | solution.py:153
  51.4 3.2 %collective-permute-done.15 = f32[128,256]{1,0:T(8,128)S(1)} collective-permute-done((f32[128,256]{1,0:T(8,128)S(1)}, f32[128,256]{1,0:T(8,128)S(1)}, u32[]{:S(2)}, u32[]{:S(2)}) %collective-permute-start.15) | collective-permute-done | bytes 131104 | tf_op jit(solution)/shard_map/ppermute | solution.py:153
  54.8 1.3 %collective-permute-done.16.came_ref = f32[128,256]{1,0:T(8,128)S(1)} collective-permute-done((f32[128,256]{1,0:T(8,128)S(1)}, f32[128,256]{1,0:T(8,128)S(1)}, u32[]{:S(2)}, u32[]{:S(2)}) %collective-permute-start.16) | collective-permute-done | bytes 131104 | tf_op jit(solution)/shard_map/ppermute | solution.py:153
  56.1 1.3 %shard_map.119 = f32[256,256]{1,0:T(8,128)} custom-call(s32[1]{0:T(128)} %bitcast.core_ref, s32[1]{0:T(128)} %bitcast.1.last_ref, f32[128,256]{1,0:T(8,128)S(1)} %get-tuple-element.61.kept_ref, f32[128,256]{1,0:T(8,128)S(1)} %collective-permute-done.16.came_ref, f32[256,256]{1,0:T(8,128)S(1)} %shard_map.113.own_ref, bf16[2,256,256]{2,1,0:T(8,128)(2,1)S(1)} %copy-done, ...), custom_call_target="tpu_custom_call" | custom-call | tf_op jit(solution)/shard_map/pallas_call | solution.py:141
  (54 shorter events, 3.4 us)
Async XLA Ops:
  0.0 9.5 %collective-permute-start = (f32[256,256]{1,0:T(8,128)}, f32[256,256]{1,0:T(8,128)S(1)}, u32[]{:S(2)}, u32[]{:S(2)}) collective-permute-start(f32[256,256]{1,0:T(8,128)} %bitcast.17), channel_id=1, source_target_pairs={{0,16},{16,0},{1,17},{17,1},{2,18},{18,2},{3,19},{19,3},{4,20},{20... | collective-permute-start | bytes 786440 | tf_op jit(solution)/shard_map/ppermute | solution.py:153
  3.0 2.0 %copy-start.13 = (f32[256]{0:T(256)S(1)}, f32[256]{0:T(256)}, u32[]{:S(2)}) copy-start(f32[256]{0:T(256)} %constant.48.clone) | copy-start | bytes 3076
  3.0 2.4 %copy-start.1 = (f32[256,256]{1,0:T(8,128)S(1)}, f32[256,256]{1,0:T(8,128)}, u32[]{:S(2)}) copy-start(f32[256,256]{1,0:T(8,128)} %reaction_ref.7) | copy-start | bytes 786436
  3.0 2.4 %copy-start.2 = (f32[1,1,256,256]{3,2,1,0:T(8,128)S(1)}, f32[1,1,256,256]{3,2,1,0:T(8,128)}, u32[]{:S(2)}) copy-start(f32[1,1,256,256]{3,2,1,0:T(8,128)} %param.11) | copy-start | bytes 786436
  5.4 1.0 %copy-start.3 = (f32[1,1,256,256]{3,2,1,0:T(8,128)S(1)}, f32[1,1,256,256]{3,2,1,0:T(8,128)}, u32[]{:S(2)}) copy-start(f32[1,1,256,256]{3,2,1,0:T(8,128)} %param.12) | copy-start | bytes 786436
  6.3 0.9 %copy-start.5 = (f32[256,256]{1,0:T(8,128)S(1)}, f32[256,256]{1,0:T(8,128)}, u32[]{:S(2)}) copy-start(f32[256,256]{1,0:T(8,128)} %diffusion_ref.3) | copy-start | bytes 786436
  7.6 1.8 %copy-start = (bf16[2,256,256]{2,1,0:T(8,128)(2,1)S(1)}, bf16[2,256,256]{2,1,0:T(8,128)(2,1)}, u32[]{:S(2)}) copy-start(bf16[2,256,256]{2,1,0:T(8,128)(2,1)} %constant.47.clone.x_ref.y_ref) | copy-start | bytes 786436
  7.9 17.1 %copy-start.7 = (f32[128,256]{1,0:T(8,128)}, f32[128,256]{1,0:T(8,128)S(1)}, u32[]{:S(2)}) copy-start(f32[128,256]{1,0:T(8,128)S(1)} %get-tuple-element.42) | copy-start | bytes 393220
  7.9 17.1 %copy-start.9 = (f32[128,256]{1,0:T(8,128)}, f32[128,256]{1,0:T(8,128)S(1)}, u32[]{:S(2)}) copy-start(f32[128,256]{1,0:T(8,128)S(1)} %get-tuple-element.41) | copy-start | bytes 393220
  7.9 17.1 %copy-start.11 = (f32[128,256]{1,0:T(8,128)}, f32[128,256]{1,0:T(8,128)S(1)}, u32[]{:S(2)}) copy-start(f32[128,256]{1,0:T(8,128)S(1)} %get-tuple-element.40) | copy-start | bytes 393220
  10.0 1.4 %collective-permute-start.1 = (f32[128,256]{1,0:T(8,128)S(1)}, f32[128,256]{1,0:T(8,128)S(1)}, u32[]{:S(2)}, u32[]{:S(2)}) collective-permute-start(f32[128,256]{1,0:T(8,128)S(1)} %get-tuple-element.38), channel_id=1, source_target_pairs={{0,1},{1,0},{2,3},{3,2},{4,5},{5,4},{6,7},{7,6},{8,9},{9,8},{10,11... | collective-permute-start | bytes 393224 | tf_op jit(solution)/shard_map/ppermute | solution.py:153
  11.4 5.8 %collective-permute-start.4 = (f32[128,256]{1,0:T(8,128)S(1)}, f32[128,256]{1,0:T(8,128)S(1)}, u32[]{:S(2)}, u32[]{:S(2)}) collective-permute-start(f32[128,256]{1,0:T(8,128)S(1)} %multiply_add_fusion.7), channel_id=1, source_target_pairs={{0,2},{1,5},{2,0},{3,7},{4,6},{5,1},{6,4},{7,3},{8,10},{9,13},{10,... | collective-permute-start | bytes 393224 | tf_op jit(solution)/shard_map/ppermute | solution.py:153
  13.2 6.2 %collective-permute-start.3 = (f32[128,256]{1,0:T(8,128)S(1)}, f32[128,256]{1,0:T(8,128)S(1)}, u32[]{:S(2)}, u32[]{:S(2)}) collective-permute-start(f32[128,256]{1,0:T(8,128)S(1)} %multiply_add_fusion.7), channel_id=1, source_target_pairs={{0,4},{1,3},{2,6},{3,1},{4,0},{5,7},{6,2},{7,5},{8,12},{9,11},{10,... | collective-permute-start | bytes 393224 | tf_op jit(solution)/shard_map/ppermute | solution.py:153
  14.8 6.2 %collective-permute-start.2 = (f32[128,256]{1,0:T(8,128)S(1)}, f32[128,256]{1,0:T(8,128)S(1)}, u32[]{:S(2)}, u32[]{:S(2)}) collective-permute-start(f32[128,256]{1,0:T(8,128)S(1)} %multiply_add_fusion.7), channel_id=1, source_target_pairs={{0,6},{1,7},{2,4},{3,5},{4,2},{5,3},{6,0},{7,1},{8,14},{9,15},{10,... | collective-permute-start | bytes 393224 | tf_op jit(solution)/shard_map/ppermute | solution.py:153
  15.0 6.2 %collective-permute-start.5 = (f32[128,256]{1,0:T(8,128)S(1)}, f32[128,256]{1,0:T(8,128)S(1)}, u32[]{:S(2)}, u32[]{:S(2)}) collective-permute-start(f32[128,256]{1,0:T(8,128)S(1)} %shard_map.111.kept_ref), channel_id=1, source_target_pairs={{0,16},{16,0},{1,17},{17,1},{2,18},{18,2},{3,19},{19,3},{4,20},{20... | collective-permute-start | bytes 393224 | tf_op jit(solution)/shard_map/ppermute | solution.py:153
  16.7 11.4 %collective-permute-start.7 = (f32[128,256]{1,0:T(8,128)S(1)}, f32[128,256]{1,0:T(8,128)S(1)}, u32[]{:S(2)}, u32[]{:S(2)}) collective-permute-start(f32[128,256]{1,0:T(8,128)S(1)} %collective-permute-done.1.came_ref), channel_id=1, source_target_pairs={{0,16},{16,0},{1,17},{17,1},{2,18},{18,2},{3,19},{19,3},{4,20},{20... | collective-permute-start | bytes 393224 | tf_op jit(solution)/shard_map/ppermute | solution.py:153
  21.2 6.9 %collective-permute-start.6 = (f32[128,256]{1,0:T(8,128)S(1)}, f32[128,256]{1,0:T(8,128)S(1)}, u32[]{:S(2)}, u32[]{:S(2)}) collective-permute-start(f32[128,256]{1,0:T(8,128)S(1)} %multiply_add_fusion.6), channel_id=1, source_target_pairs={{0,12},{1,13},{2,14},{3,15},{4,8},{5,9},{6,10},{7,11},{8,4},{9,5},... | collective-permute-start | bytes 393224 | tf_op jit(solution)/shard_map/ppermute | solution.py:153
  28.2 1.8 %collective-permute-start.9 = (f32[128,256]{1,0:T(8,128)S(1)}, f32[128,256]{1,0:T(8,128)S(1)}, u32[]{:S(2)}, u32[]{:S(2)}) collective-permute-start(f32[128,256]{1,0:T(8,128)S(1)} %get-tuple-element.52), channel_id=1, source_target_pairs={{0,1},{1,0},{2,3},{3,2},{4,5},{5,4},{6,7},{7,6},{8,9},{9,8},{10,11... | collective-permute-start | bytes 393224 | tf_op jit(solution)/shard_map/ppermute | solution.py:153
  28.3 5.9 %collective-permute-start.8 = (f32[128,256]{1,0:T(8,128)S(1)}, f32[128,256]{1,0:T(8,128)S(1)}, u32[]{:S(2)}, u32[]{:S(2)}) collective-permute-start(f32[128,256]{1,0:T(8,128)S(1)} %multiply_add_fusion.4.entering_ref), channel_id=1, source_target_pairs={{0,16},{16,0},{1,17},{17,1},{2,18},{18,2},{3,19},{19,3},{4,20},{20... | collective-permute-start | bytes 393224 | tf_op jit(solution)/shard_map/ppermute | solution.py:153
  30.0 1.0 %copy-start.4 = (f32[1,1,256,256]{3,2,1,0:T(8,128)S(1)}, f32[1,1,256,256]{3,2,1,0:T(8,128)}, u32[]{:S(2)}) copy-start(f32[1,1,256,256]{3,2,1,0:T(8,128)} %param.12) | copy-start | bytes 786436
  30.0 1.0 %copy-start.6 = (f32[256,256]{1,0:T(8,128)S(1)}, f32[256,256]{1,0:T(8,128)}, u32[]{:S(2)}) copy-start(f32[256,256]{1,0:T(8,128)} %diffusion_ref.3) | copy-start | bytes 786436
  34.3 1.4 %collective-permute-start.10 = (f32[128,256]{1,0:T(8,128)S(1)}, f32[128,256]{1,0:T(8,128)S(1)}, u32[]{:S(2)}, u32[]{:S(2)}) collective-permute-start(f32[128,256]{1,0:T(8,128)S(1)} %get-tuple-element.58), channel_id=1, source_target_pairs={{0,1},{1,0},{2,3},{3,2},{4,5},{5,4},{6,7},{7,6},{8,9},{9,8},{10,11... | collective-permute-start | bytes 393224 | tf_op jit(solution)/shard_map/ppermute | solution.py:153
  36.7 1.4 %collective-permute-start.11 = (f32[128,256]{1,0:T(8,128)S(1)}, f32[128,256]{1,0:T(8,128)S(1)}, u32[]{:S(2)}, u32[]{:S(2)}) collective-permute-start(f32[128,256]{1,0:T(8,128)S(1)} %get-tuple-element.60), channel_id=1, source_target_pairs={{0,1},{1,0},{2,3},{3,2},{4,5},{5,4},{6,7},{7,6},{8,9},{9,8},{10,11... | collective-permute-start | bytes 393224 | tf_op jit(solution)/shard_map/ppermute | solution.py:153
  38.2 13.1 %copy-start.8 = (f32[128,256]{1,0:T(8,128)S(1)}, f32[128,256]{1,0:T(8,128)}, u32[]{:S(2)}) copy-start(f32[128,256]{1,0:T(8,128)} %copy-done.7) | copy-start | bytes 393220
  38.2 13.1 %copy-start.10 = (f32[128,256]{1,0:T(8,128)S(1)}, f32[128,256]{1,0:T(8,128)}, u32[]{:S(2)}) copy-start(f32[128,256]{1,0:T(8,128)} %copy-done.9) | copy-start | bytes 393220
  38.2 13.1 %copy-start.12 = (f32[128,256]{1,0:T(8,128)S(1)}, f32[128,256]{1,0:T(8,128)}, u32[]{:S(2)}) copy-start(f32[128,256]{1,0:T(8,128)} %copy-done.11) | copy-start | bytes 393220
  38.2 5.9 %collective-permute-start.14 = (f32[128,256]{1,0:T(8,128)S(1)}, f32[128,256]{1,0:T(8,128)S(1)}, u32[]{:S(2)}, u32[]{:S(2)}) collective-permute-start(f32[128,256]{1,0:T(8,128)S(1)} %multiply_add_fusion.3), channel_id=1, source_target_pairs={{0,2},{1,5},{2,0},{3,7},{4,6},{5,1},{6,4},{7,3},{8,10},{9,13},{10,... | collective-permute-start | bytes 393224 | tf_op jit(solution)/shard_map/ppermute | solution.py:153
  39.9 6.2 %collective-permute-start.13 = (f32[128,256]{1,0:T(8,128)S(1)}, f32[128,256]{1,0:T(8,128)S(1)}, u32[]{:S(2)}, u32[]{:S(2)}) collective-permute-start(f32[128,256]{1,0:T(8,128)S(1)} %multiply_add_fusion.3), channel_id=1, source_target_pairs={{0,4},{1,3},{2,6},{3,1},{4,0},{5,7},{6,2},{7,5},{8,12},{9,11},{10,... | collective-permute-start | bytes 393224 | tf_op jit(solution)/shard_map/ppermute | solution.py:153
  41.3 6.4 %collective-permute-start.12 = (f32[128,256]{1,0:T(8,128)S(1)}, f32[128,256]{1,0:T(8,128)S(1)}, u32[]{:S(2)}, u32[]{:S(2)}) collective-permute-start(f32[128,256]{1,0:T(8,128)S(1)} %multiply_add_fusion.3), channel_id=1, source_target_pairs={{0,6},{1,7},{2,4},{3,5},{4,2},{5,3},{6,0},{7,1},{8,14},{9,15},{10,... | collective-permute-start | bytes 393224 | tf_op jit(solution)/shard_map/ppermute | solution.py:153
  47.7 6.9 %collective-permute-start.15 = (f32[128,256]{1,0:T(8,128)S(1)}, f32[128,256]{1,0:T(8,128)S(1)}, u32[]{:S(2)}, u32[]{:S(2)}) collective-permute-start(f32[128,256]{1,0:T(8,128)S(1)} %multiply_add_fusion.2), channel_id=1, source_target_pairs={{0,12},{1,13},{2,14},{3,15},{4,8},{5,9},{6,10},{7,11},{8,4},{9,5},... | collective-permute-start | bytes 393224 | tf_op jit(solution)/shard_map/ppermute | solution.py:153
  54.7 1.4 %collective-permute-start.16 = (f32[128,256]{1,0:T(8,128)S(1)}, f32[128,256]{1,0:T(8,128)S(1)}, u32[]{:S(2)}, u32[]{:S(2)}) collective-permute-start(f32[128,256]{1,0:T(8,128)S(1)} %get-tuple-element.62), channel_id=1, source_target_pairs={{0,1},{1,0},{2,3},{3,2},{4,5},{5,4},{6,7},{7,6},{8,9},{9,8},{10,11... | collective-permute-start | bytes 393224 | tf_op jit(solution)/shard_map/ppermute | solution.py:153

commit v9 on v8

--- a/solution.py
+++ b/solution.py
@@ -210,9 +210,9 @@
         pieces = [carry] + [swap(carry, "tm", mask) for mask in masks]
         carry = sum(one * piece for one, piece in zip(join, pieces))
         entering = entering + sum(one * piece for one, piece in zip(enter, pieces))
-    carry, others[0] = lax.optimization_barrier((carry, others[0]))
+    carry = lax.optimization_barrier(carry)
     masks, _, enter = levels[-1]
-    entering = lax.optimization_barrier(entering + enter[0] * carry)
+    entering, others = lax.optimization_barrier((entering + enter[0] * carry, others))
     entering = entering + sum(one * swap(carry, "tm", mask) for one, mask in zip(enter[1:], masks))
     return lax.optimization_barrier((entering, others))
 

time: 57.6 us -> 57.4 us (level)
  transfers between devices with their start and end apart: 17 -> 17, of which waited for: 15 -> 14; matrix products, arithmetic and copies ran while one was open for 2% -> 2% of each run, Pallas kernels for 4% -> 4%
where the time goes in v9:
time: 57.4 us; the launch traced here: 57.2 us
  waiting for transfers between devices  24.7 us (43%)
  starting transfers between devices  21.5 us (37%)
  Pallas kernels  5.18 us (9%)
  local copies, waits for them, and re-layouts  2.49 us (4%)
  between operations  2.37 us (4%)
  other arithmetic  0.99 us (2%)
    ppermute x17, waiting for transfers between devices, swap(): lax.ppermute(values, axis, [(i, i ^ masks[i & 1]) for i in range(lax.axis...  24.7 us
    ppermute x17, starting transfers between devices, swap(): lax.ppermute(values, axis, [(i, i ^ masks[i & 1]) for i in range(lax.axis...  21.5 us
    pallas_call x11, Pallas kernels, call(): pl.pallas_call(kernel, out_shape=[jax.ShapeDtypeStruct(shape, jnp.float32...  5.18 us
    unnamed x28, local copies, waits for them, and re-layouts  2.4 us
  transfers between devices with their start and end apart: 17, of which 14 were waited for; matrix products, arithmetic and copies ran while one was open for 2% of the time, Pallas kernels for 4%

profile of v9, /device:TPU:0, one launch (start us, length us, event | category | flops | bytes accessed | tf_op | source)
XLA Modules:
  0.0 57.2 jit_solution(17589807321131579640)
XLA Ops:
  0.0 3.0 %collective-permute-start = (f32[256,256]{1,0:T(8,128)}, f32[256,256]{1,0:T(8,128)S(1)}, u32[]{:S(2)}, u32[]{:S(2)}) collective-permute-start(f32[256,256]{1,0:T(8,128)} %bitcast.17), channel_id=1, source_target_pairs={{0,16},{16,0},{1,17},{17,1},{2,18},{18,2},{3,19},{19,3},{4,20},{20... | collective-permute-start | bytes 786440 | tf_op jit(solution)/shard_map/ppermute | solution.py:153
  5.4 0.9 %copy-done.3 = f32[1,1,256,256]{3,2,1,0:T(8,128)S(1)} copy-done((f32[1,1,256,256]{3,2,1,0:T(8,128)S(1)}, f32[1,1,256,256]{3,2,1,0:T(8,128)}, u32[]{:S(2)}) %copy-start.3) | copy-done | bytes 262168
  6.3 0.9 %copy-done.5 = f32[256,256]{1,0:T(8,128)S(1)} copy-done((f32[256,256]{1,0:T(8,128)S(1)}, f32[256,256]{1,0:T(8,128)}, u32[]{:S(2)}) %copy-start.5) | copy-done | bytes 262168
  7.9 1.6 %collective-permute-done.partner_ref.former_ref = f32[256,256]{1,0:T(8,128)S(1)} collective-permute-done((f32[256,256]{1,0:T(8,128)}, f32[256,256]{1,0:T(8,128)S(1)}, u32[]{:S(2)}, u32[]{:S(2)}) %collective-permute-start) | collective-permute-done | bytes 262176 | tf_op jit(solution)/shard_map/ppermute | solution.py:153
  9.5 0.5 shard_map.110
  10.2 0.4 shard_map.111.kept_ref
  10.7 0.7 %collective-permute-done.1.came_ref = f32[128,256]{1,0:T(8,128)S(1)} collective-permute-done((f32[128,256]{1,0:T(8,128)S(1)}, f32[128,256]{1,0:T(8,128)S(1)}, u32[]{:S(2)}, u32[]{:S(2)}) %collective-permute-start.1) | collective-permute-done | bytes 131104 | tf_op jit(solution)/shard_map/ppermute | solution.py:153
  11.4 1.8 %collective-permute-start.4 = (f32[128,256]{1,0:T(8,128)S(1)}, f32[128,256]{1,0:T(8,128)S(1)}, u32[]{:S(2)}, u32[]{:S(2)}) collective-permute-start(f32[128,256]{1,0:T(8,128)S(1)} %multiply_add_fusion.7), channel_id=1, source_target_pairs={{0,2},{1,5},{2,0},{3,7},{4,6},{5,1},{6,4},{7,3},{8,10},{9,13},{10,... | collective-permute-start | bytes 393224 | tf_op jit(solution)/shard_map/ppermute | solution.py:153
  13.2 1.6 %collective-permute-start.3 = (f32[128,256]{1,0:T(8,128)S(1)}, f32[128,256]{1,0:T(8,128)S(1)}, u32[]{:S(2)}, u32[]{:S(2)}) collective-permute-start(f32[128,256]{1,0:T(8,128)S(1)} %multiply_add_fusion.7), channel_id=1, source_target_pairs={{0,4},{1,3},{2,6},{3,1},{4,0},{5,7},{6,2},{7,5},{8,12},{9,11},{10,... | collective-permute-start | bytes 393224 | tf_op jit(solution)/shard_map/ppermute | solution.py:153
  15.0 1.7 %collective-permute-start.5 = (f32[128,256]{1,0:T(8,128)S(1)}, f32[128,256]{1,0:T(8,128)S(1)}, u32[]{:S(2)}, u32[]{:S(2)}) collective-permute-start(f32[128,256]{1,0:T(8,128)S(1)} %shard_map.111.kept_ref), channel_id=1, source_target_pairs={{0,16},{16,0},{1,17},{17,1},{2,18},{18,2},{3,19},{19,3},{4,20},{20... | collective-permute-start | bytes 393224 | tf_op jit(solution)/shard_map/ppermute | solution.py:153
  17.2 2.2 %collective-permute-done.3 = f32[128,256]{1,0:T(8,128)S(1)} collective-permute-done((f32[128,256]{1,0:T(8,128)S(1)}, f32[128,256]{1,0:T(8,128)S(1)}, u32[]{:S(2)}, u32[]{:S(2)}) %collective-permute-start.3) | collective-permute-done | bytes 131104 | tf_op jit(solution)/shard_map/ppermute | solution.py:153
  19.4 1.6 %collective-permute-done.2 = f32[128,256]{1,0:T(8,128)S(1)} collective-permute-done((f32[128,256]{1,0:T(8,128)S(1)}, f32[128,256]{1,0:T(8,128)S(1)}, u32[]{:S(2)}, u32[]{:S(2)}) %collective-permute-start.2) | collective-permute-done | bytes 131104 | tf_op jit(solution)/shard_map/ppermute | solution.py:153
  21.1 3.7 %collective-permute-start.7 = (f32[128,256]{1,0:T(8,128)S(1)}, f32[128,256]{1,0:T(8,128)S(1)}, u32[]{:S(2)}, u32[]{:S(2)}) collective-permute-start(f32[128,256]{1,0:T(8,128)S(1)} %multiply_add_fusion.6), channel_id=1, source_target_pairs={{0,12},{1,13},{2,14},{3,15},{4,8},{5,9},{6,10},{7,11},{8,4},{9,5},... | collective-permute-start | bytes 393224 | tf_op jit(solution)/shard_map/ppermute | solution.py:153
  24.9 3.1 %collective-permute-done.7 = f32[128,256]{1,0:T(8,128)S(1)} collective-permute-done((f32[128,256]{1,0:T(8,128)S(1)}, f32[128,256]{1,0:T(8,128)S(1)}, u32[]{:S(2)}, u32[]{:S(2)}) %collective-permute-start.7) | collective-permute-done | bytes 131104 | tf_op jit(solution)/shard_map/ppermute | solution.py:153
  28.2 1.6 %collective-permute-start.8 = (f32[128,256]{1,0:T(8,128)S(1)}, f32[128,256]{1,0:T(8,128)S(1)}, u32[]{:S(2)}, u32[]{:S(2)}) collective-permute-start(f32[128,256]{1,0:T(8,128)S(1)} %multiply_add_fusion.4.entering_ref), channel_id=1, source_target_pairs={{0,16},{16,0},{1,17},{17,1},{2,18},{18,2},{3,19},{19,3},{4,20},{20... | collective-permute-start | bytes 393224 | tf_op jit(solution)/shard_map/ppermute | solution.py:153
  29.8 0.6 shard_map.113.own_ref
  30.8 0.4 shard_map.114.own_side_ref
  31.2 2.9 %collective-permute-done.8.entering_ref = f32[128,256]{1,0:T(8,128)S(1)} collective-permute-done((f32[128,256]{1,0:T(8,128)S(1)}, f32[128,256]{1,0:T(8,128)S(1)}, u32[]{:S(2)}, u32[]{:S(2)}) %collective-permute-start.8) | collective-permute-done | bytes 131104 | tf_op jit(solution)/shard_map/ppermute | solution.py:153
  34.2 1.3 %collective-permute-done.10.came_ref = f32[128,256]{1,0:T(8,128)S(1)} collective-permute-done((f32[128,256]{1,0:T(8,128)S(1)}, f32[128,256]{1,0:T(8,128)S(1)}, u32[]{:S(2)}, u32[]{:S(2)}) %collective-permute-start.10) | collective-permute-done | bytes 131104 | tf_op jit(solution)/shard_map/ppermute | solution.py:153
  35.6 1.1 %shard_map.116 = (f32[256,256]{1,0:T(8,128)S(1)}, f32[128,256]{1,0:T(8,128)S(1)}) custom-call(s32[1]{0:T(128)} %bitcast.6.adjoint_ref, s32[1]{0:T(128)} %bitcast.core_ref, s32[1]{0:T(128)} %bitcast.7.partner_last_ref, f32[256,256]{1,0:T(8,128)S(1)} %shard_map.114.own_side_ref, f32[256,256]{1,0:T(8,128)S(1)} %shard_map.113.own_ref, ...), custom_call_target="tpu_custom_call" | custom-call | tf_op jit(solution)/shard_map/pallas_call | solution.py:141
  36.9 0.4 shard_map.117.kept_ref
  37.3 0.8 %collective-permute-done.11.came_ref = f32[128,256]{1,0:T(8,128)S(1)} collective-permute-done((f32[128,256]{1,0:T(8,128)S(1)}, f32[128,256]{1,0:T(8,128)S(1)}, u32[]{:S(2)}, u32[]{:S(2)}) %collective-permute-start.11) | collective-permute-done | bytes 131104 | tf_op jit(solution)/shard_map/ppermute | solution.py:153
  38.1 1.5 %collective-permute-start.14 = (f32[128,256]{1,0:T(8,128)S(1)}, f32[128,256]{1,0:T(8,128)S(1)}, u32[]{:S(2)}, u32[]{:S(2)}) collective-permute-start(f32[128,256]{1,0:T(8,128)S(1)} %multiply_add_fusion.3), channel_id=1, source_target_pairs={{0,2},{1,5},{2,0},{3,7},{4,6},{5,1},{6,4},{7,3},{8,10},{9,13},{10,... | collective-permute-start | bytes 393224 | tf_op jit(solution)/shard_map/ppermute | solution.py:153
  39.6 1.6 %collective-permute-start.13 = (f32[128,256]{1,0:T(8,128)S(1)}, f32[128,256]{1,0:T(8,128)S(1)}, u32[]{:S(2)}, u32[]{:S(2)}) collective-permute-start(f32[128,256]{1,0:T(8,128)S(1)} %multiply_add_fusion.3), channel_id=1, source_target_pairs={{0,4},{1,3},{2,6},{3,1},{4,0},{5,7},{6,2},{7,5},{8,12},{9,11},{10,... | collective-permute-start | bytes 393224 | tf_op jit(solution)/shard_map/ppermute | solution.py:153
  41.3 0.4 collective-permute-start.12
  41.7 2.3 %collective-permute-done.14 = f32[128,256]{1,0:T(8,128)S(1)} collective-permute-done((f32[128,256]{1,0:T(8,128)S(1)}, f32[128,256]{1,0:T(8,128)S(1)}, u32[]{:S(2)}, u32[]{:S(2)}) %collective-permute-start.14) | collective-permute-done | bytes 131104 | tf_op jit(solution)/shard_map/ppermute | solution.py:153
  44.0 1.7 %collective-permute-done.13 = f32[128,256]{1,0:T(8,128)S(1)} collective-permute-done((f32[128,256]{1,0:T(8,128)S(1)}, f32[128,256]{1,0:T(8,128)S(1)}, u32[]{:S(2)}, u32[]{:S(2)}) %collective-permute-start.13) | collective-permute-done | bytes 131104 | tf_op jit(solution)/shard_map/ppermute | solution.py:153
  45.7 1.7 %collective-permute-done.12 = f32[128,256]{1,0:T(8,128)S(1)} collective-permute-done((f32[128,256]{1,0:T(8,128)S(1)}, f32[128,256]{1,0:T(8,128)S(1)}, u32[]{:S(2)}, u32[]{:S(2)}) %collective-permute-start.12) | collective-permute-done | bytes 131104 | tf_op jit(solution)/shard_map/ppermute | solution.py:153
  47.5 3.7 %collective-permute-start.15 = (f32[128,256]{1,0:T(8,128)S(1)}, f32[128,256]{1,0:T(8,128)S(1)}, u32[]{:S(2)}, u32[]{:S(2)}) collective-permute-start(f32[128,256]{1,0:T(8,128)S(1)} %multiply_add_fusion.2), channel_id=1, source_target_pairs={{0,12},{1,13},{2,14},{3,15},{4,8},{5,9},{6,10},{7,11},{8,4},{9,5},... | collective-permute-start | bytes 393224 | tf_op jit(solution)/shard_map/ppermute | solution.py:153
  51.3 3.2 %collective-permute-done.15 = f32[128,256]{1,0:T(8,128)S(1)} collective-permute-done((f32[128,256]{1,0:T(8,128)S(1)}, f32[128,256]{1,0:T(8,128)S(1)}, u32[]{:S(2)}, u32[]{:S(2)}) %collective-permute-start.15) | collective-permute-done | bytes 131104 | tf_op jit(solution)/shard_map/ppermute | solution.py:153
  54.6 1.3 %collective-permute-done.16.came_ref = f32[128,256]{1,0:T(8,128)S(1)} collective-permute-done((f32[128,256]{1,0:T(8,128)S(1)}, f32[128,256]{1,0:T(8,128)S(1)}, u32[]{:S(2)}, u32[]{:S(2)}) %collective-permute-start.16) | collective-permute-done | bytes 131104 | tf_op jit(solution)/shard_map/ppermute | solution.py:153
  55.9 1.3 %shard_map.119 = f32[256,256]{1,0:T(8,128)} custom-call(s32[1]{0:T(128)} %bitcast.core_ref, s32[1]{0:T(128)} %bitcast.1.last_ref, f32[128,256]{1,0:T(8,128)S(1)} %get-tuple-element.63.kept_ref, f32[128,256]{1,0:T(8,128)S(1)} %collective-permute-done.16.came_ref, f32[256,256]{1,0:T(8,128)S(1)} %shard_map.113.own_ref, bf16[2,256,256]{2,1,0:T(8,128)(2,1)S(1)} %copy-done, ...), custom_call_target="tpu_custom_call" | custom-call | tf_op jit(solution)/shard_map/pallas_call | solution.py:141
  (54 shorter events, 3.3 us)
Async XLA Ops:
  0.0 9.5 %collective-permute-start = (f32[256,256]{1,0:T(8,128)}, f32[256,256]{1,0:T(8,128)S(1)}, u32[]{:S(2)}, u32[]{:S(2)}) collective-permute-start(f32[256,256]{1,0:T(8,128)} %bitcast.17), channel_id=1, source_target_pairs={{0,16},{16,0},{1,17},{17,1},{2,18},{18,2},{3,19},{19,3},{4,20},{20... | collective-permute-start | bytes 786440 | tf_op jit(solution)/shard_map/ppermute | solution.py:153
  3.0 2.0 %copy-start.13 = (f32[256]{0:T(256)S(1)}, f32[256]{0:T(256)}, u32[]{:S(2)}) copy-start(f32[256]{0:T(256)} %constant.48.clone) | copy-start | bytes 3076
  3.0 2.4 %copy-start.1 = (f32[256,256]{1,0:T(8,128)S(1)}, f32[256,256]{1,0:T(8,128)}, u32[]{:S(2)}) copy-start(f32[256,256]{1,0:T(8,128)} %reaction_ref.7) | copy-start | bytes 786436
  3.0 2.4 %copy-start.2 = (f32[1,1,256,256]{3,2,1,0:T(8,128)S(1)}, f32[1,1,256,256]{3,2,1,0:T(8,128)}, u32[]{:S(2)}) copy-start(f32[1,1,256,256]{3,2,1,0:T(8,128)} %param.11) | copy-start | bytes 786436
  5.4 1.0 %copy-start.3 = (f32[1,1,256,256]{3,2,1,0:T(8,128)S(1)}, f32[1,1,256,256]{3,2,1,0:T(8,128)}, u32[]{:S(2)}) copy-start(f32[1,1,256,256]{3,2,1,0:T(8,128)} %param.12) | copy-start | bytes 786436
  6.3 0.9 %copy-start.5 = (f32[256,256]{1,0:T(8,128)S(1)}, f32[256,256]{1,0:T(8,128)}, u32[]{:S(2)}) copy-start(f32[256,256]{1,0:T(8,128)} %diffusion_ref.3) | copy-start | bytes 786436
  7.6 1.8 %copy-start = (bf16[2,256,256]{2,1,0:T(8,128)(2,1)S(1)}, bf16[2,256,256]{2,1,0:T(8,128)(2,1)}, u32[]{:S(2)}) copy-start(bf16[2,256,256]{2,1,0:T(8,128)(2,1)} %constant.47.clone.x_ref.y_ref) | copy-start | bytes 786436
  7.9 16.9 %copy-start.7 = (f32[128,256]{1,0:T(8,128)}, f32[128,256]{1,0:T(8,128)S(1)}, u32[]{:S(2)}) copy-start(f32[128,256]{1,0:T(8,128)S(1)} %get-tuple-element.43) | copy-start | bytes 393220
  7.9 16.9 %copy-start.9 = (f32[128,256]{1,0:T(8,128)}, f32[128,256]{1,0:T(8,128)S(1)}, u32[]{:S(2)}) copy-start(f32[128,256]{1,0:T(8,128)S(1)} %get-tuple-element.42) | copy-start | bytes 393220
  7.9 16.9 %copy-start.11 = (f32[128,256]{1,0:T(8,128)}, f32[128,256]{1,0:T(8,128)S(1)}, u32[]{:S(2)}) copy-start(f32[128,256]{1,0:T(8,128)S(1)} %get-tuple-element.41) | copy-start | bytes 393220
  10.0 1.4 %collective-permute-start.1 = (f32[128,256]{1,0:T(8,128)S(1)}, f32[128,256]{1,0:T(8,128)S(1)}, u32[]{:S(2)}, u32[]{:S(2)}) collective-permute-start(f32[128,256]{1,0:T(8,128)S(1)} %get-tuple-element.39), channel_id=1, source_target_pairs={{0,1},{1,0},{2,3},{3,2},{4,5},{5,4},{6,7},{7,6},{8,9},{9,8},{10,11... | collective-permute-start | bytes 393224 | tf_op jit(solution)/shard_map/ppermute | solution.py:153
  11.4 5.8 %collective-permute-start.4 = (f32[128,256]{1,0:T(8,128)S(1)}, f32[128,256]{1,0:T(8,128)S(1)}, u32[]{:S(2)}, u32[]{:S(2)}) collective-permute-start(f32[128,256]{1,0:T(8,128)S(1)} %multiply_add_fusion.7), channel_id=1, source_target_pairs={{0,2},{1,5},{2,0},{3,7},{4,6},{5,1},{6,4},{7,3},{8,10},{9,13},{10,... | collective-permute-start | bytes 393224 | tf_op jit(solution)/shard_map/ppermute | solution.py:153
  13.2 6.2 %collective-permute-start.3 = (f32[128,256]{1,0:T(8,128)S(1)}, f32[128,256]{1,0:T(8,128)S(1)}, u32[]{:S(2)}, u32[]{:S(2)}) collective-permute-start(f32[128,256]{1,0:T(8,128)S(1)} %multiply_add_fusion.7), channel_id=1, source_target_pairs={{0,4},{1,3},{2,6},{3,1},{4,0},{5,7},{6,2},{7,5},{8,12},{9,11},{10,... | collective-permute-start | bytes 393224 | tf_op jit(solution)/shard_map/ppermute | solution.py:153
  14.8 6.2 %collective-permute-start.2 = (f32[128,256]{1,0:T(8,128)S(1)}, f32[128,256]{1,0:T(8,128)S(1)}, u32[]{:S(2)}, u32[]{:S(2)}) collective-permute-start(f32[128,256]{1,0:T(8,128)S(1)} %multiply_add_fusion.7), channel_id=1, source_target_pairs={{0,6},{1,7},{2,4},{3,5},{4,2},{5,3},{6,0},{7,1},{8,14},{9,15},{10,... | collective-permute-start | bytes 393224 | tf_op jit(solution)/shard_map/ppermute | solution.py:153
  15.0 9.9 %collective-permute-start.5 = (f32[128,256]{1,0:T(8,128)S(1)}, f32[128,256]{1,0:T(8,128)S(1)}, u32[]{:S(2)}, u32[]{:S(2)}) collective-permute-start(f32[128,256]{1,0:T(8,128)S(1)} %shard_map.111.kept_ref), channel_id=1, source_target_pairs={{0,16},{16,0},{1,17},{17,1},{2,18},{18,2},{3,19},{19,3},{4,20},{20... | collective-permute-start | bytes 393224 | tf_op jit(solution)/shard_map/ppermute | solution.py:153
  16.7 8.2 %collective-permute-start.6 = (f32[128,256]{1,0:T(8,128)S(1)}, f32[128,256]{1,0:T(8,128)S(1)}, u32[]{:S(2)}, u32[]{:S(2)}) collective-permute-start(f32[128,256]{1,0:T(8,128)S(1)} %collective-permute-done.1.came_ref), channel_id=1, source_target_pairs={{0,16},{16,0},{1,17},{17,1},{2,18},{18,2},{3,19},{19,3},{4,20},{20... | collective-permute-start | bytes 393224 | tf_op jit(solution)/shard_map/ppermute | solution.py:153
  21.1 6.9 %collective-permute-start.7 = (f32[128,256]{1,0:T(8,128)S(1)}, f32[128,256]{1,0:T(8,128)S(1)}, u32[]{:S(2)}, u32[]{:S(2)}) collective-permute-start(f32[128,256]{1,0:T(8,128)S(1)} %multiply_add_fusion.6), channel_id=1, source_target_pairs={{0,12},{1,13},{2,14},{3,15},{4,8},{5,9},{6,10},{7,11},{8,4},{9,5},... | collective-permute-start | bytes 393224 | tf_op jit(solution)/shard_map/ppermute | solution.py:153
  28.1 1.7 %collective-permute-start.9 = (f32[128,256]{1,0:T(8,128)S(1)}, f32[128,256]{1,0:T(8,128)S(1)}, u32[]{:S(2)}, u32[]{:S(2)}) collective-permute-start(f32[128,256]{1,0:T(8,128)S(1)} %get-tuple-element.54), channel_id=1, source_target_pairs={{0,1},{1,0},{2,3},{3,2},{4,5},{5,4},{6,7},{7,6},{8,9},{9,8},{10,11... | collective-permute-start | bytes 393224 | tf_op jit(solution)/shard_map/ppermute | solution.py:153
  28.2 5.9 %collective-permute-start.8 = (f32[128,256]{1,0:T(8,128)S(1)}, f32[128,256]{1,0:T(8,128)S(1)}, u32[]{:S(2)}, u32[]{:S(2)}) collective-permute-start(f32[128,256]{1,0:T(8,128)S(1)} %multiply_add_fusion.4.entering_ref), channel_id=1, source_target_pairs={{0,16},{16,0},{1,17},{17,1},{2,18},{18,2},{3,19},{19,3},{4,20},{20... | collective-permute-start | bytes 393224 | tf_op jit(solution)/shard_map/ppermute | solution.py:153
  29.8 1.0 %copy-start.4 = (f32[1,1,256,256]{3,2,1,0:T(8,128)S(1)}, f32[1,1,256,256]{3,2,1,0:T(8,128)}, u32[]{:S(2)}) copy-start(f32[1,1,256,256]{3,2,1,0:T(8,128)} %param.12) | copy-start | bytes 786436
  29.8 1.0 %copy-start.6 = (f32[256,256]{1,0:T(8,128)S(1)}, f32[256,256]{1,0:T(8,128)}, u32[]{:S(2)}) copy-start(f32[256,256]{1,0:T(8,128)} %diffusion_ref.3) | copy-start | bytes 786436
  34.2 1.4 %collective-permute-start.10 = (f32[128,256]{1,0:T(8,128)S(1)}, f32[128,256]{1,0:T(8,128)S(1)}, u32[]{:S(2)}, u32[]{:S(2)}) collective-permute-start(f32[128,256]{1,0:T(8,128)S(1)} %get-tuple-element.60), channel_id=1, source_target_pairs={{0,1},{1,0},{2,3},{3,2},{4,5},{5,4},{6,7},{7,6},{8,9},{9,8},{10,11... | collective-permute-start | bytes 393224 | tf_op jit(solution)/shard_map/ppermute | solution.py:153
  36.6 1.4 %collective-permute-start.11 = (f32[128,256]{1,0:T(8,128)S(1)}, f32[128,256]{1,0:T(8,128)S(1)}, u32[]{:S(2)}, u32[]{:S(2)}) collective-permute-start(f32[128,256]{1,0:T(8,128)S(1)} %get-tuple-element.62), channel_id=1, source_target_pairs={{0,1},{1,0},{2,3},{3,2},{4,5},{5,4},{6,7},{7,6},{8,9},{9,8},{10,11... | collective-permute-start | bytes 393224 | tf_op jit(solution)/shard_map/ppermute | solution.py:153
  38.1 13.1 %copy-start.8 = (f32[128,256]{1,0:T(8,128)S(1)}, f32[128,256]{1,0:T(8,128)}, u32[]{:S(2)}) copy-start(f32[128,256]{1,0:T(8,128)} %copy-done.7) | copy-start | bytes 393220
  38.1 13.1 %copy-start.10 = (f32[128,256]{1,0:T(8,128)S(1)}, f32[128,256]{1,0:T(8,128)}, u32[]{:S(2)}) copy-start(f32[128,256]{1,0:T(8,128)} %copy-done.9) | copy-start | bytes 393220
  38.1 13.1 %copy-start.12 = (f32[128,256]{1,0:T(8,128)S(1)}, f32[128,256]{1,0:T(8,128)}, u32[]{:S(2)}) copy-start(f32[128,256]{1,0:T(8,128)} %copy-done.11) | copy-start | bytes 393220
  38.1 5.8 %collective-permute-start.14 = (f32[128,256]{1,0:T(8,128)S(1)}, f32[128,256]{1,0:T(8,128)S(1)}, u32[]{:S(2)}, u32[]{:S(2)}) collective-permute-start(f32[128,256]{1,0:T(8,128)S(1)} %multiply_add_fusion.3), channel_id=1, source_target_pairs={{0,2},{1,5},{2,0},{3,7},{4,6},{5,1},{6,4},{7,3},{8,10},{9,13},{10,... | collective-permute-start | bytes 393224 | tf_op jit(solution)/shard_map/ppermute | solution.py:153
  39.6 6.1 %collective-permute-start.13 = (f32[128,256]{1,0:T(8,128)S(1)}, f32[128,256]{1,0:T(8,128)S(1)}, u32[]{:S(2)}, u32[]{:S(2)}) collective-permute-start(f32[128,256]{1,0:T(8,128)S(1)} %multiply_add_fusion.3), channel_id=1, source_target_pairs={{0,4},{1,3},{2,6},{3,1},{4,0},{5,7},{6,2},{7,5},{8,12},{9,11},{10,... | collective-permute-start | bytes 393224 | tf_op jit(solution)/shard_map/ppermute | solution.py:153
  41.3 6.2 %collective-permute-start.12 = (f32[128,256]{1,0:T(8,128)S(1)}, f32[128,256]{1,0:T(8,128)S(1)}, u32[]{:S(2)}, u32[]{:S(2)}) collective-permute-start(f32[128,256]{1,0:T(8,128)S(1)} %multiply_add_fusion.3), channel_id=1, source_target_pairs={{0,6},{1,7},{2,4},{3,5},{4,2},{5,3},{6,0},{7,1},{8,14},{9,15},{10,... | collective-permute-start | bytes 393224 | tf_op jit(solution)/shard_map/ppermute | solution.py:153
  47.5 6.9 %collective-permute-start.15 = (f32[128,256]{1,0:T(8,128)S(1)}, f32[128,256]{1,0:T(8,128)S(1)}, u32[]{:S(2)}, u32[]{:S(2)}) collective-permute-start(f32[128,256]{1,0:T(8,128)S(1)} %multiply_add_fusion.2), channel_id=1, source_target_pairs={{0,12},{1,13},{2,14},{3,15},{4,8},{5,9},{6,10},{7,11},{8,4},{9,5},... | collective-permute-start | bytes 393224 | tf_op jit(solution)/shard_map/ppermute | solution.py:153
  54.5 1.4 %collective-permute-start.16 = (f32[128,256]{1,0:T(8,128)S(1)}, f32[128,256]{1,0:T(8,128)S(1)}, u32[]{:S(2)}, u32[]{:S(2)}) collective-permute-start(f32[128,256]{1,0:T(8,128)S(1)} %get-tuple-element.64), channel_id=1, source_target_pairs={{0,1},{1,0},{2,3},{3,2},{4,5},{5,4},{6,7},{7,6},{8,9},{9,8},{10,11... | collective-permute-start | bytes 393224 | tf_op jit(solution)/shard_map/ppermute | solution.py:153

commit v10 on v9

--- a/solution.py
+++ b/solution.py
@@ -81,12 +81,14 @@
     return pl.ds(pl.multiple_of(core * half, half), half)
 
 
-def send_half(scale, adjoint, core, side, own, partner, reaction, x_ref, y_ref, side_ref, send_ref):
+def coupled(adjoint, side, own, partner, reaction):
     adjoint_part = 3.0 * reaction * partner * partner * own - partner
-    side = side - jnp.where(adjoint, adjoint_part, gamma_inv * partner)
+    return side - jnp.where(adjoint, adjoint_part, gamma_inv * partner)
+
+
+def send_half(scale, core, side, x_ref, y_ref, send_ref):
     place = half_rows(1 - core, send_ref.shape[0])
     send_ref[...] = both_sides(x_ref, split(side), parts(y_ref), place) * scale
-    side_ref[...] = side
 
 
 def keep_kernel(scale, core_ref, side_ref, x_ref, y_ref, keep_ref):
@@ -97,10 +99,9 @@
 def first_kernel(
     scale, adjoint_ref, core_ref, own_side_ref, own_ref, partner_ref, reaction_ref, x_ref, y_ref, side_ref, send_ref
 ):
-    send_half(
-        scale, adjoint_ref[0] == 1, core_ref[0], own_side_ref[...], own_ref[...], partner_ref[...], reaction_ref[...],
-        x_ref, y_ref, side_ref, send_ref,
-    )
+    side = coupled(adjoint_ref[0] == 1, own_side_ref[...], own_ref[...], partner_ref[...], reaction_ref[...])
+    side_ref[...] = side
+    send_half(scale, core_ref[0], side, x_ref, y_ref, send_ref)
 
 
 def later_kernel(
@@ -109,14 +110,17 @@
     side_ref, send_ref, *refs,
 ):
     modes = gather_halves(core_ref[0], refs[-1], kept_ref, came_ref)
-    former = jnp.where(partner_last_ref[0] == 1, 1.0, 0.0) * former_ref[...]
-    partner = former + both_sides(x_ref, modes, parts(y_ref), slice(None))
-    if len(refs) > 1:
-        refs[0][...] = partner
-    send_half(
-        scale, adjoint_ref[0] == 1, core_ref[0], own_side_ref[...], own_ref[...], partner, reaction_ref[...],
-        x_ref, y_ref, side_ref, send_ref,
-    )
+    former = jnp.where(partner_last_ref[0] == 1, 1.0, 0.0)
+    sides = []
+    for place in row_halves(own_ref.shape[0]):
+        partner = former * former_ref[place, :] + both_sides(x_ref, modes, parts(y_ref), place)
+        if len(refs) > 1:
+            refs[0][place, :] = partner
+        sides.append(
+            coupled(adjoint_ref[0] == 1, own_side_ref[place, :], own_ref[place, :], partner, reaction_ref[place, :])
+        )
+        side_ref[place, :] = sides[-1]
+    send_half(scale, core_ref[0], jnp.concatenate(sides, 0), x_ref, y_ref, send_ref)
 
 
 def inverse_kernel(core_ref, last_ref, kept_ref, came_ref, own_ref, x_ref, y_ref, out_ref, work_ref):

time: 57.4 us -> 57.4 us (level)
  no operation moved by 1% of the time
where the time goes in v10:
time: 57.4 us; the launch traced here: 57.1 us
  waiting for transfers between devices  24.7 us (43%)
  starting transfers between devices  21.5 us (37%)
  Pallas kernels  5.1 us (9%)
  local copies, waits for them, and re-layouts  2.49 us (4%)
  between operations  2.37 us (4%)
  other arithmetic  0.99 us (2%)
    ppermute x17, waiting for transfers between devices, swap(): lax.ppermute(values, axis, [(i, i ^ masks[i & 1]) for i in range(lax.axis...  24.7 us
    ppermute x17, starting transfers between devices, swap(): lax.ppermute(values, axis, [(i, i ^ masks[i & 1]) for i in range(lax.axis...  21.5 us
    pallas_call x11, Pallas kernels, call(): pl.pallas_call(kernel, out_shape=[jax.ShapeDtypeStruct(shape, jnp.float32...  5.1 us
    unnamed x28, local copies, waits for them, and re-layouts  2.4 us
  transfers between devices with their start and end apart: 17, of which 14 were waited for; matrix products, arithmetic and copies ran while one was open for 2% of the time, Pallas kernels for 4%

profile of v10, /device:TPU:0, one launch (start us, length us, event | category | flops | bytes accessed | tf_op | source)
XLA Modules:
  0.0 57.1 jit_solution(972941300470396500)
XLA Ops:
  0.0 3.0 %collective-permute-start = (f32[256,256]{1,0:T(8,128)}, f32[256,256]{1,0:T(8,128)S(1)}, u32[]{:S(2)}, u32[]{:S(2)}) collective-permute-start(f32[256,256]{1,0:T(8,128)} %bitcast.17), channel_id=1, source_target_pairs={{0,16},{16,0},{1,17},{17,1},{2,18},{18,2},{3,19},{19,3},{4,20},{20... | collective-permute-start | bytes 786440 | tf_op jit(solution)/shard_map/ppermute | solution.py:157
  5.4 0.9 %copy-done.3 = f32[1,1,256,256]{3,2,1,0:T(8,128)S(1)} copy-done((f32[1,1,256,256]{3,2,1,0:T(8,128)S(1)}, f32[1,1,256,256]{3,2,1,0:T(8,128)}, u32[]{:S(2)}) %copy-start.3) | copy-done | bytes 262168
  6.3 0.9 %copy-done.5 = f32[256,256]{1,0:T(8,128)S(1)} copy-done((f32[256,256]{1,0:T(8,128)S(1)}, f32[256,256]{1,0:T(8,128)}, u32[]{:S(2)}) %copy-start.5) | copy-done | bytes 262168
  7.9 1.6 %collective-permute-done.partner_ref.former_ref = f32[256,256]{1,0:T(8,128)S(1)} collective-permute-done((f32[256,256]{1,0:T(8,128)}, f32[256,256]{1,0:T(8,128)S(1)}, u32[]{:S(2)}, u32[]{:S(2)}) %collective-permute-start) | collective-permute-done | bytes 262176 | tf_op jit(solution)/shard_map/ppermute | solution.py:157
  9.5 0.5 shard_map.110
  10.2 0.4 shard_map.111.kept_ref
  10.7 0.7 %collective-permute-done.1.came_ref = f32[128,256]{1,0:T(8,128)S(1)} collective-permute-done((f32[128,256]{1,0:T(8,128)S(1)}, f32[128,256]{1,0:T(8,128)S(1)}, u32[]{:S(2)}, u32[]{:S(2)}) %collective-permute-start.1) | collective-permute-done | bytes 131104 | tf_op jit(solution)/shard_map/ppermute | solution.py:157
  11.4 1.8 %collective-permute-start.4 = (f32[128,256]{1,0:T(8,128)S(1)}, f32[128,256]{1,0:T(8,128)S(1)}, u32[]{:S(2)}, u32[]{:S(2)}) collective-permute-start(f32[128,256]{1,0:T(8,128)S(1)} %multiply_add_fusion.7), channel_id=1, source_target_pairs={{0,2},{1,5},{2,0},{3,7},{4,6},{5,1},{6,4},{7,3},{8,10},{9,13},{10,... | collective-permute-start | bytes 393224 | tf_op jit(solution)/shard_map/ppermute | solution.py:157
  13.2 1.6 %collective-permute-start.3 = (f32[128,256]{1,0:T(8,128)S(1)}, f32[128,256]{1,0:T(8,128)S(1)}, u32[]{:S(2)}, u32[]{:S(2)}) collective-permute-start(f32[128,256]{1,0:T(8,128)S(1)} %multiply_add_fusion.7), channel_id=1, source_target_pairs={{0,4},{1,3},{2,6},{3,1},{4,0},{5,7},{6,2},{7,5},{8,12},{9,11},{10,... | collective-permute-start | bytes 393224 | tf_op jit(solution)/shard_map/ppermute | solution.py:157
  15.0 1.7 %collective-permute-start.5 = (f32[128,256]{1,0:T(8,128)S(1)}, f32[128,256]{1,0:T(8,128)S(1)}, u32[]{:S(2)}, u32[]{:S(2)}) collective-permute-start(f32[128,256]{1,0:T(8,128)S(1)} %shard_map.111.kept_ref), channel_id=1, source_target_pairs={{0,16},{16,0},{1,17},{17,1},{2,18},{18,2},{3,19},{19,3},{4,20},{20... | collective-permute-start | bytes 393224 | tf_op jit(solution)/shard_map/ppermute | solution.py:157
  17.2 2.2 %collective-permute-done.3 = f32[128,256]{1,0:T(8,128)S(1)} collective-permute-done((f32[128,256]{1,0:T(8,128)S(1)}, f32[128,256]{1,0:T(8,128)S(1)}, u32[]{:S(2)}, u32[]{:S(2)}) %collective-permute-start.3) | collective-permute-done | bytes 131104 | tf_op jit(solution)/shard_map/ppermute | solution.py:157
  19.4 1.6 %collective-permute-done.2 = f32[128,256]{1,0:T(8,128)S(1)} collective-permute-done((f32[128,256]{1,0:T(8,128)S(1)}, f32[128,256]{1,0:T(8,128)S(1)}, u32[]{:S(2)}, u32[]{:S(2)}) %collective-permute-start.2) | collective-permute-done | bytes 131104 | tf_op jit(solution)/shard_map/ppermute | solution.py:157
  21.1 3.7 %collective-permute-start.7 = (f32[128,256]{1,0:T(8,128)S(1)}, f32[128,256]{1,0:T(8,128)S(1)}, u32[]{:S(2)}, u32[]{:S(2)}) collective-permute-start(f32[128,256]{1,0:T(8,128)S(1)} %multiply_add_fusion.6), channel_id=1, source_target_pairs={{0,12},{1,13},{2,14},{3,15},{4,8},{5,9},{6,10},{7,11},{8,4},{9,5},... | collective-permute-start | bytes 393224 | tf_op jit(solution)/shard_map/ppermute | solution.py:157
  24.9 3.1 %collective-permute-done.7 = f32[128,256]{1,0:T(8,128)S(1)} collective-permute-done((f32[128,256]{1,0:T(8,128)S(1)}, f32[128,256]{1,0:T(8,128)S(1)}, u32[]{:S(2)}, u32[]{:S(2)}) %collective-permute-start.7) | collective-permute-done | bytes 131104 | tf_op jit(solution)/shard_map/ppermute | solution.py:157
  28.2 1.6 %collective-permute-start.8 = (f32[128,256]{1,0:T(8,128)S(1)}, f32[128,256]{1,0:T(8,128)S(1)}, u32[]{:S(2)}, u32[]{:S(2)}) collective-permute-start(f32[128,256]{1,0:T(8,128)S(1)} %multiply_add_fusion.4.entering_ref), channel_id=1, source_target_pairs={{0,16},{16,0},{1,17},{17,1},{2,18},{18,2},{3,19},{19,3},{4,20},{20... | collective-permute-start | bytes 393224 | tf_op jit(solution)/shard_map/ppermute | solution.py:157
  29.8 0.6 shard_map.113.own_ref
  30.8 0.4 shard_map.114.own_side_ref
  31.2 2.9 %collective-permute-done.8.entering_ref = f32[128,256]{1,0:T(8,128)S(1)} collective-permute-done((f32[128,256]{1,0:T(8,128)S(1)}, f32[128,256]{1,0:T(8,128)S(1)}, u32[]{:S(2)}, u32[]{:S(2)}) %collective-permute-start.8) | collective-permute-done | bytes 131104 | tf_op jit(solution)/shard_map/ppermute | solution.py:157
  34.2 1.3 %collective-permute-done.10.came_ref = f32[128,256]{1,0:T(8,128)S(1)} collective-permute-done((f32[128,256]{1,0:T(8,128)S(1)}, f32[128,256]{1,0:T(8,128)S(1)}, u32[]{:S(2)}, u32[]{:S(2)}) %collective-permute-start.10) | collective-permute-done | bytes 131104 | tf_op jit(solution)/shard_map/ppermute | solution.py:157
  35.6 1.0 %shard_map.116 = (f32[256,256]{1,0:T(8,128)S(1)}, f32[128,256]{1,0:T(8,128)S(1)}) custom-call(s32[1]{0:T(128)} %bitcast.6.adjoint_ref, s32[1]{0:T(128)} %bitcast.core_ref, s32[1]{0:T(128)} %bitcast.7.partner_last_ref, f32[256,256]{1,0:T(8,128)S(1)} %shard_map.114.own_side_ref, f32[256,256]{1,0:T(8,128)S(1)} %shard_map.113.own_ref, ...), custom_call_target="tpu_custom_call" | custom-call | tf_op jit(solution)/shard_map/pallas_call | solution.py:145
  36.8 0.4 shard_map.117.kept_ref
  37.2 0.8 %collective-permute-done.11.came_ref = f32[128,256]{1,0:T(8,128)S(1)} collective-permute-done((f32[128,256]{1,0:T(8,128)S(1)}, f32[128,256]{1,0:T(8,128)S(1)}, u32[]{:S(2)}, u32[]{:S(2)}) %collective-permute-start.11) | collective-permute-done | bytes 131104 | tf_op jit(solution)/shard_map/ppermute | solution.py:157
  38.0 1.5 %collective-permute-start.14 = (f32[128,256]{1,0:T(8,128)S(1)}, f32[128,256]{1,0:T(8,128)S(1)}, u32[]{:S(2)}, u32[]{:S(2)}) collective-permute-start(f32[128,256]{1,0:T(8,128)S(1)} %multiply_add_fusion.3), channel_id=1, source_target_pairs={{0,2},{1,5},{2,0},{3,7},{4,6},{5,1},{6,4},{7,3},{8,10},{9,13},{10,... | collective-permute-start | bytes 393224 | tf_op jit(solution)/shard_map/ppermute | solution.py:157
  39.6 1.6 %collective-permute-start.13 = (f32[128,256]{1,0:T(8,128)S(1)}, f32[128,256]{1,0:T(8,128)S(1)}, u32[]{:S(2)}, u32[]{:S(2)}) collective-permute-start(f32[128,256]{1,0:T(8,128)S(1)} %multiply_add_fusion.3), channel_id=1, source_target_pairs={{0,4},{1,3},{2,6},{3,1},{4,0},{5,7},{6,2},{7,5},{8,12},{9,11},{10,... | collective-permute-start | bytes 393224 | tf_op jit(solution)/shard_map/ppermute | solution.py:157
  41.2 0.4 collective-permute-start.12
  41.6 2.3 %collective-permute-done.14 = f32[128,256]{1,0:T(8,128)S(1)} collective-permute-done((f32[128,256]{1,0:T(8,128)S(1)}, f32[128,256]{1,0:T(8,128)S(1)}, u32[]{:S(2)}, u32[]{:S(2)}) %collective-permute-start.14) | collective-permute-done | bytes 131104 | tf_op jit(solution)/shard_map/ppermute | solution.py:157
  43.9 1.7 %collective-permute-done.13 = f32[128,256]{1,0:T(8,128)S(1)} collective-permute-done((f32[128,256]{1,0:T(8,128)S(1)}, f32[128,256]{1,0:T(8,128)S(1)}, u32[]{:S(2)}, u32[]{:S(2)}) %collective-permute-start.13) | collective-permute-done | bytes 131104 | tf_op jit(solution)/shard_map/ppermute | solution.py:157
  45.6 1.7 %collective-permute-done.12 = f32[128,256]{1,0:T(8,128)S(1)} collective-permute-done((f32[128,256]{1,0:T(8,128)S(1)}, f32[128,256]{1,0:T(8,128)S(1)}, u32[]{:S(2)}, u32[]{:S(2)}) %collective-permute-start.12) | collective-permute-done | bytes 131104 | tf_op jit(solution)/shard_map/ppermute | solution.py:157
  47.4 3.7 %collective-permute-start.15 = (f32[128,256]{1,0:T(8,128)S(1)}, f32[128,256]{1,0:T(8,128)S(1)}, u32[]{:S(2)}, u32[]{:S(2)}) collective-permute-start(f32[128,256]{1,0:T(8,128)S(1)} %multiply_add_fusion.2), channel_id=1, source_target_pairs={{0,12},{1,13},{2,14},{3,15},{4,8},{5,9},{6,10},{7,11},{8,4},{9,5},... | collective-permute-start | bytes 393224 | tf_op jit(solution)/shard_map/ppermute | solution.py:157
  51.2 3.2 %collective-permute-done.15 = f32[128,256]{1,0:T(8,128)S(1)} collective-permute-done((f32[128,256]{1,0:T(8,128)S(1)}, f32[128,256]{1,0:T(8,128)S(1)}, u32[]{:S(2)}, u32[]{:S(2)}) %collective-permute-start.15) | collective-permute-done | bytes 131104 | tf_op jit(solution)/shard_map/ppermute | solution.py:157
  54.5 1.3 %collective-permute-done.16.came_ref = f32[128,256]{1,0:T(8,128)S(1)} collective-permute-done((f32[128,256]{1,0:T(8,128)S(1)}, f32[128,256]{1,0:T(8,128)S(1)}, u32[]{:S(2)}, u32[]{:S(2)}) %collective-permute-start.16) | collective-permute-done | bytes 131104 | tf_op jit(solution)/shard_map/ppermute | solution.py:157
  55.9 1.3 %shard_map.119 = f32[256,256]{1,0:T(8,128)} custom-call(s32[1]{0:T(128)} %bitcast.core_ref, s32[1]{0:T(128)} %bitcast.1.last_ref, f32[128,256]{1,0:T(8,128)S(1)} %get-tuple-element.63.kept_ref, f32[128,256]{1,0:T(8,128)S(1)} %collective-permute-done.16.came_ref, f32[256,256]{1,0:T(8,128)S(1)} %shard_map.113.own_ref, bf16[2,256,256]{2,1,0:T(8,128)(2,1)S(1)} %copy-done, ...), custom_call_target="tpu_custom_call" | custom-call | tf_op jit(solution)/shard_map/pallas_call | solution.py:145
  (54 shorter events, 3.3 us)
Async XLA Ops:
  0.0 9.5 %collective-permute-start = (f32[256,256]{1,0:T(8,128)}, f32[256,256]{1,0:T(8,128)S(1)}, u32[]{:S(2)}, u32[]{:S(2)}) collective-permute-start(f32[256,256]{1,0:T(8,128)} %bitcast.17), channel_id=1, source_target_pairs={{0,16},{16,0},{1,17},{17,1},{2,18},{18,2},{3,19},{19,3},{4,20},{20... | collective-permute-start | bytes 786440 | tf_op jit(solution)/shard_map/ppermute | solution.py:157
  3.0 2.0 %copy-start.13 = (f32[256]{0:T(256)S(1)}, f32[256]{0:T(256)}, u32[]{:S(2)}) copy-start(f32[256]{0:T(256)} %constant.48.clone) | copy-start | bytes 3076
  3.0 2.4 %copy-start.1 = (f32[256,256]{1,0:T(8,128)S(1)}, f32[256,256]{1,0:T(8,128)}, u32[]{:S(2)}) copy-start(f32[256,256]{1,0:T(8,128)} %reaction_ref.7) | copy-start | bytes 786436
  3.0 2.4 %copy-start.2 = (f32[1,1,256,256]{3,2,1,0:T(8,128)S(1)}, f32[1,1,256,256]{3,2,1,0:T(8,128)}, u32[]{:S(2)}) copy-start(f32[1,1,256,256]{3,2,1,0:T(8,128)} %param.11) | copy-start | bytes 786436
  5.4 1.0 %copy-start.3 = (f32[1,1,256,256]{3,2,1,0:T(8,128)S(1)}, f32[1,1,256,256]{3,2,1,0:T(8,128)}, u32[]{:S(2)}) copy-start(f32[1,1,256,256]{3,2,1,0:T(8,128)} %param.12) | copy-start | bytes 786436
  6.3 0.9 %copy-start.5 = (f32[256,256]{1,0:T(8,128)S(1)}, f32[256,256]{1,0:T(8,128)}, u32[]{:S(2)}) copy-start(f32[256,256]{1,0:T(8,128)} %diffusion_ref.3) | copy-start | bytes 786436
  7.6 1.8 %copy-start = (bf16[2,256,256]{2,1,0:T(8,128)(2,1)S(1)}, bf16[2,256,256]{2,1,0:T(8,128)(2,1)}, u32[]{:S(2)}) copy-start(bf16[2,256,256]{2,1,0:T(8,128)(2,1)} %constant.47.clone.x_ref.y_ref) | copy-start | bytes 786436
  7.9 16.9 %copy-start.7 = (f32[128,256]{1,0:T(8,128)}, f32[128,256]{1,0:T(8,128)S(1)}, u32[]{:S(2)}) copy-start(f32[128,256]{1,0:T(8,128)S(1)} %get-tuple-element.43) | copy-start | bytes 393220
  7.9 16.9 %copy-start.9 = (f32[128,256]{1,0:T(8,128)}, f32[128,256]{1,0:T(8,128)S(1)}, u32[]{:S(2)}) copy-start(f32[128,256]{1,0:T(8,128)S(1)} %get-tuple-element.42) | copy-start | bytes 393220
  7.9 16.9 %copy-start.11 = (f32[128,256]{1,0:T(8,128)}, f32[128,256]{1,0:T(8,128)S(1)}, u32[]{:S(2)}) copy-start(f32[128,256]{1,0:T(8,128)S(1)} %get-tuple-element.41) | copy-start | bytes 393220
  10.0 1.4 %collective-permute-start.1 = (f32[128,256]{1,0:T(8,128)S(1)}, f32[128,256]{1,0:T(8,128)S(1)}, u32[]{:S(2)}, u32[]{:S(2)}) collective-permute-start(f32[128,256]{1,0:T(8,128)S(1)} %get-tuple-element.39), channel_id=1, source_target_pairs={{0,1},{1,0},{2,3},{3,2},{4,5},{5,4},{6,7},{7,6},{8,9},{9,8},{10,11... | collective-permute-start | bytes 393224 | tf_op jit(solution)/shard_map/ppermute | solution.py:157
  11.4 5.8 %collective-permute-start.4 = (f32[128,256]{1,0:T(8,128)S(1)}, f32[128,256]{1,0:T(8,128)S(1)}, u32[]{:S(2)}, u32[]{:S(2)}) collective-permute-start(f32[128,256]{1,0:T(8,128)S(1)} %multiply_add_fusion.7), channel_id=1, source_target_pairs={{0,2},{1,5},{2,0},{3,7},{4,6},{5,1},{6,4},{7,3},{8,10},{9,13},{10,... | collective-permute-start | bytes 393224 | tf_op jit(solution)/shard_map/ppermute | solution.py:157
  13.2 6.2 %collective-permute-start.3 = (f32[128,256]{1,0:T(8,128)S(1)}, f32[128,256]{1,0:T(8,128)S(1)}, u32[]{:S(2)}, u32[]{:S(2)}) collective-permute-start(f32[128,256]{1,0:T(8,128)S(1)} %multiply_add_fusion.7), channel_id=1, source_target_pairs={{0,4},{1,3},{2,6},{3,1},{4,0},{5,7},{6,2},{7,5},{8,12},{9,11},{10,... | collective-permute-start | bytes 393224 | tf_op jit(solution)/shard_map/ppermute | solution.py:157
  14.8 6.2 %collective-permute-start.2 = (f32[128,256]{1,0:T(8,128)S(1)}, f32[128,256]{1,0:T(8,128)S(1)}, u32[]{:S(2)}, u32[]{:S(2)}) collective-permute-start(f32[128,256]{1,0:T(8,128)S(1)} %multiply_add_fusion.7), channel_id=1, source_target_pairs={{0,6},{1,7},{2,4},{3,5},{4,2},{5,3},{6,0},{7,1},{8,14},{9,15},{10,... | collective-permute-start | bytes 393224 | tf_op jit(solution)/shard_map/ppermute | solution.py:157
  15.0 9.9 %collective-permute-start.5 = (f32[128,256]{1,0:T(8,128)S(1)}, f32[128,256]{1,0:T(8,128)S(1)}, u32[]{:S(2)}, u32[]{:S(2)}) collective-permute-start(f32[128,256]{1,0:T(8,128)S(1)} %shard_map.111.kept_ref), channel_id=1, source_target_pairs={{0,16},{16,0},{1,17},{17,1},{2,18},{18,2},{3,19},{19,3},{4,20},{20... | collective-permute-start | bytes 393224 | tf_op jit(solution)/shard_map/ppermute | solution.py:157
  16.7 8.2 %collective-permute-start.6 = (f32[128,256]{1,0:T(8,128)S(1)}, f32[128,256]{1,0:T(8,128)S(1)}, u32[]{:S(2)}, u32[]{:S(2)}) collective-permute-start(f32[128,256]{1,0:T(8,128)S(1)} %collective-permute-done.1.came_ref), channel_id=1, source_target_pairs={{0,16},{16,0},{1,17},{17,1},{2,18},{18,2},{3,19},{19,3},{4,20},{20... | collective-permute-start | bytes 393224 | tf_op jit(solution)/shard_map/ppermute | solution.py:157
  21.1 6.9 %collective-permute-start.7 = (f32[128,256]{1,0:T(8,128)S(1)}, f32[128,256]{1,0:T(8,128)S(1)}, u32[]{:S(2)}, u32[]{:S(2)}) collective-permute-start(f32[128,256]{1,0:T(8,128)S(1)} %multiply_add_fusion.6), channel_id=1, source_target_pairs={{0,12},{1,13},{2,14},{3,15},{4,8},{5,9},{6,10},{7,11},{8,4},{9,5},... | collective-permute-start | bytes 393224 | tf_op jit(solution)/shard_map/ppermute | solution.py:157
  28.1 1.7 %collective-permute-start.9 = (f32[128,256]{1,0:T(8,128)S(1)}, f32[128,256]{1,0:T(8,128)S(1)}, u32[]{:S(2)}, u32[]{:S(2)}) collective-permute-start(f32[128,256]{1,0:T(8,128)S(1)} %get-tuple-element.54), channel_id=1, source_target_pairs={{0,1},{1,0},{2,3},{3,2},{4,5},{5,4},{6,7},{7,6},{8,9},{9,8},{10,11... | collective-permute-start | bytes 393224 | tf_op jit(solution)/shard_map/ppermute | solution.py:157
  28.2 5.9 %collective-permute-start.8 = (f32[128,256]{1,0:T(8,128)S(1)}, f32[128,256]{1,0:T(8,128)S(1)}, u32[]{:S(2)}, u32[]{:S(2)}) collective-permute-start(f32[128,256]{1,0:T(8,128)S(1)} %multiply_add_fusion.4.entering_ref), channel_id=1, source_target_pairs={{0,16},{16,0},{1,17},{17,1},{2,18},{18,2},{3,19},{19,3},{4,20},{20... | collective-permute-start | bytes 393224 | tf_op jit(solution)/shard_map/ppermute | solution.py:157
  29.8 1.0 %copy-start.4 = (f32[1,1,256,256]{3,2,1,0:T(8,128)S(1)}, f32[1,1,256,256]{3,2,1,0:T(8,128)}, u32[]{:S(2)}) copy-start(f32[1,1,256,256]{3,2,1,0:T(8,128)} %param.12) | copy-start | bytes 786436
  29.8 1.0 %copy-start.6 = (f32[256,256]{1,0:T(8,128)S(1)}, f32[256,256]{1,0:T(8,128)}, u32[]{:S(2)}) copy-start(f32[256,256]{1,0:T(8,128)} %diffusion_ref.3) | copy-start | bytes 786436
  34.2 1.4 %collective-permute-start.10 = (f32[128,256]{1,0:T(8,128)S(1)}, f32[128,256]{1,0:T(8,128)S(1)}, u32[]{:S(2)}, u32[]{:S(2)}) collective-permute-start(f32[128,256]{1,0:T(8,128)S(1)} %get-tuple-element.60), channel_id=1, source_target_pairs={{0,1},{1,0},{2,3},{3,2},{4,5},{5,4},{6,7},{7,6},{8,9},{9,8},{10,11... | collective-permute-start | bytes 393224 | tf_op jit(solution)/shard_map/ppermute | solution.py:157
  36.6 1.4 %collective-permute-start.11 = (f32[128,256]{1,0:T(8,128)S(1)}, f32[128,256]{1,0:T(8,128)S(1)}, u32[]{:S(2)}, u32[]{:S(2)}) collective-permute-start(f32[128,256]{1,0:T(8,128)S(1)} %get-tuple-element.62), channel_id=1, source_target_pairs={{0,1},{1,0},{2,3},{3,2},{4,5},{5,4},{6,7},{7,6},{8,9},{9,8},{10,11... | collective-permute-start | bytes 393224 | tf_op jit(solution)/shard_map/ppermute | solution.py:157
  38.0 13.1 %copy-start.8 = (f32[128,256]{1,0:T(8,128)S(1)}, f32[128,256]{1,0:T(8,128)}, u32[]{:S(2)}) copy-start(f32[128,256]{1,0:T(8,128)} %copy-done.7) | copy-start | bytes 393220
  38.0 13.1 %copy-start.10 = (f32[128,256]{1,0:T(8,128)S(1)}, f32[128,256]{1,0:T(8,128)}, u32[]{:S(2)}) copy-start(f32[128,256]{1,0:T(8,128)} %copy-done.9) | copy-start | bytes 393220
  38.0 13.1 %copy-start.12 = (f32[128,256]{1,0:T(8,128)S(1)}, f32[128,256]{1,0:T(8,128)}, u32[]{:S(2)}) copy-start(f32[128,256]{1,0:T(8,128)} %copy-done.11) | copy-start | bytes 393220
  38.0 5.8 %collective-permute-start.14 = (f32[128,256]{1,0:T(8,128)S(1)}, f32[128,256]{1,0:T(8,128)S(1)}, u32[]{:S(2)}, u32[]{:S(2)}) collective-permute-start(f32[128,256]{1,0:T(8,128)S(1)} %multiply_add_fusion.3), channel_id=1, source_target_pairs={{0,2},{1,5},{2,0},{3,7},{4,6},{5,1},{6,4},{7,3},{8,10},{9,13},{10,... | collective-permute-start | bytes 393224 | tf_op jit(solution)/shard_map/ppermute | solution.py:157
  39.6 6.1 %collective-permute-start.13 = (f32[128,256]{1,0:T(8,128)S(1)}, f32[128,256]{1,0:T(8,128)S(1)}, u32[]{:S(2)}, u32[]{:S(2)}) collective-permute-start(f32[128,256]{1,0:T(8,128)S(1)} %multiply_add_fusion.3), channel_id=1, source_target_pairs={{0,4},{1,3},{2,6},{3,1},{4,0},{5,7},{6,2},{7,5},{8,12},{9,11},{10,... | collective-permute-start | bytes 393224 | tf_op jit(solution)/shard_map/ppermute | solution.py:157
  41.2 6.2 %collective-permute-start.12 = (f32[128,256]{1,0:T(8,128)S(1)}, f32[128,256]{1,0:T(8,128)S(1)}, u32[]{:S(2)}, u32[]{:S(2)}) collective-permute-start(f32[128,256]{1,0:T(8,128)S(1)} %multiply_add_fusion.3), channel_id=1, source_target_pairs={{0,6},{1,7},{2,4},{3,5},{4,2},{5,3},{6,0},{7,1},{8,14},{9,15},{10,... | collective-permute-start | bytes 393224 | tf_op jit(solution)/shard_map/ppermute | solution.py:157
  47.4 6.9 %collective-permute-start.15 = (f32[128,256]{1,0:T(8,128)S(1)}, f32[128,256]{1,0:T(8,128)S(1)}, u32[]{:S(2)}, u32[]{:S(2)}) collective-permute-start(f32[128,256]{1,0:T(8,128)S(1)} %multiply_add_fusion.2), channel_id=1, source_target_pairs={{0,12},{1,13},{2,14},{3,15},{4,8},{5,9},{6,10},{7,11},{8,4},{9,5},... | collective-permute-start | bytes 393224 | tf_op jit(solution)/shard_map/ppermute | solution.py:157
  54.4 1.4 %collective-permute-start.16 = (f32[128,256]{1,0:T(8,128)S(1)}, f32[128,256]{1,0:T(8,128)S(1)}, u32[]{:S(2)}, u32[]{:S(2)}) collective-permute-start(f32[128,256]{1,0:T(8,128)S(1)} %get-tuple-element.64), channel_id=1, source_target_pairs={{0,1},{1,0},{2,3},{3,2},{4,5},{5,4},{6,7},{7,6},{8,9},{9,8},{10,11... | collective-permute-start | bytes 393224 | tf_op jit(solution)/shard_map/ppermute | solution.py:157

commit v11 on v10

--- a/solution.py
+++ b/solution.py
@@ -104,23 +104,23 @@
     send_half(scale, core_ref[0], side, x_ref, y_ref, send_ref)
 
 
-def later_kernel(
-    scale, adjoint_ref, core_ref, partner_last_ref,
-    own_side_ref, own_ref, kept_ref, came_ref, former_ref, reaction_ref, x_ref, y_ref,
-    side_ref, send_ref, *refs,
-):
-    modes = gather_halves(core_ref[0], refs[-1], kept_ref, came_ref)
-    former = jnp.where(partner_last_ref[0] == 1, 1.0, 0.0)
-    sides = []
-    for place in row_halves(own_ref.shape[0]):
-        partner = former * former_ref[place, :] + both_sides(x_ref, modes, parts(y_ref), place)
-        if len(refs) > 1:
-            refs[0][place, :] = partner
-        sides.append(
-            coupled(adjoint_ref[0] == 1, own_side_ref[place, :], own_ref[place, :], partner, reaction_ref[place, :])
-        )
-        side_ref[place, :] = sides[-1]
-    send_half(scale, core_ref[0], jnp.concatenate(sides, 0), x_ref, y_ref, send_ref)
+def later_kernel(scale, adjoint_ref, core_ref, last_ref, other_last_ref, reaction_ref, x_ref, y_ref, *refs):
+    steps_in, out_refs = (refs[:5], refs[5:10]), refs[10:]
+    work_refs = out_refs[-2:]
+    place_out = half_rows(core_ref[0], out_refs[0].shape[0])
+    for number, (side_ref, own_ref, kept_ref, came_ref, former_ref) in enumerate(steps_in):
+        modes = gather_halves(core_ref[0], work_refs[number], kept_ref, came_ref)
+        former = jnp.where((last_ref, other_last_ref)[number][0] == 1, 1.0, 0.0)
+        sides = []
+        for place in row_halves(own_ref.shape[0]):
+            partner = former * former_ref[place, :] + both_sides(x_ref, modes, parts(y_ref), place)
+            if len(out_refs) > 4:
+                out_refs[2 + number][place, :] = partner
+            sides.append(
+                coupled(adjoint_ref[0] == 1, side_ref[place, :], own_ref[place, :], partner, reaction_ref[place, :])
+            )
+        side = split(jnp.concatenate(sides, 0))
+        out_refs[number][...] = both_sides(x_ref, side, parts(y_ref), place_out) * scale
 
 
 def inverse_kernel(core_ref, last_ref, kept_ref, came_ref, own_ref, x_ref, y_ref, out_ref, work_ref):
@@ -139,7 +139,7 @@
     sent_ref[...] = jnp.where(odd, first, second)
 
 
-def call(kernel, scalars, arrays, out_shapes, scratch=(), flops=0):
+def call(kernel, scalars, arrays, out_shapes, scratch=()):
     spec_scalar = pl.BlockSpec(memory_space=pltpu.SMEM)
     spec_array = pl.BlockSpec(memory_space=pltpu.VMEM)
     return pl.pallas_call(
@@ -238,16 +238,17 @@
 
     adjoint, side_of = scalar(group), scalar(core)
     odd, other_odd = scalar(place & 1), scalar(other_place & 1)
-    last, other_last = scalar(place == total - 1), scalar(other_place == total - 1)
+    last = [scalar(one == total - 1) for one in (place, place ^ 1)]
+    other_last = [scalar(one == total - 1) for one in (other_place, other_place ^ 1)]
     eigen_x = lax.dynamic_slice_in_dim(eigenvalues(grid_x), core * half, half, 0)
     rate = 1.0 / (1.0 + spectral_shift + mean_diffusion * (eigen_x[:, None] + eigenvalues(grid_y)[None, :]))
     pair, levels = scan_factors(rate, wrap_factor, place, core, total)
 
-    def own_side(own):
+    def own_side(number):
         (side,) = call(
             own_kernel,
-            (mean_diffusion, spectral_shift, adjoint, last),
-            (own, source, diffusion, reaction),
+            (mean_diffusion, spectral_shift, adjoint, last[number]),
+            (fields_now[number], sources[number], diffusion, reaction),
             [own.shape],
         )
         return side
@@ -255,43 +256,59 @@
     def both_steps(odd, entering, kept, came):
         return call(steps_kernel, (odd,), (entering, kept, came, rate), [kept.shape] * 2)
 
-    partner = [swap(own, "pair", 1)]
-    side = own_side(own)
+    def inverse(number, kept, came):
+        (field,) = call(
+            inverse_kernel,
+            (side_of, last[number]),
+            (kept, came, fields_now[number], *tables),
+            [own.shape],
+            [own.shape],
+        )
+        return field
+
+    partners = [swap(own, "pair", 1)]
+    fields_now, sources = [own], [source]
+    sides = [own_side(0)]
+    if ITERS > 1:
+        fields_now.append(swap(own, "tm", 1))
+        sources.append(swap(source, "tm", 1))
     for iteration in range(ITERS):
         more = iteration + 1 < ITERS
         if iteration == 0:
             side, sent = call(
                 functools.partial(first_kernel, scale),
                 (adjoint, side_of),
-                (side, own, *partner, reaction, *tables),
+                (sides[0], own, partners[0], reaction, *tables),
                 [own.shape, (half, grid_y)],
             )
+            came = swap(sent, "tm", 1)
+            (kept,) = call(functools.partial(keep_kernel, scale), (side_of,), (side, *tables), [(half, grid_y)])
+            if more:
+                partners.append(swap(partners[0], "tm", 1))
         else:
-            side, sent, *partner = call(
+            kept, came, *partners = call(
                 functools.partial(later_kernel, scale),
-                (adjoint, side_of, other_last),
-                (side, own, other_kept, other_came, *partner, reaction, *tables),
-                [own.shape, (half, grid_y)] + [own.shape] * more,
-                [own.shape],
+                (adjoint, side_of, *other_last),
+                (
+                    reaction, *tables,
+                    sides[0], fields_now[0], other_new, swap(other_sent, "tm", 1), partners[0],
+                    sides[1], fields_now[1], other_sent, swap(other_new, "tm", 1), partners[1],
+                ),
+                [(half, grid_y)] * 2 + [own.shape] * (2 * more),
+                [own.shape] * 2,
             )
-        came = swap(sent, "tm", 1)
-        (kept,) = call(functools.partial(keep_kernel, scale), (side_of,), (side, *tables), [(half, grid_y)])
         entering, other_sides = carry_in(kept, came, pair, levels, more)
         new, sent = both_steps(odd, entering, kept, came)
         if more:
             other_entering = swap(entering, "pair", 1)
-        (own,) = call(
-            inverse_kernel,
-            (side_of, last),
-            (new, swap(sent, "tm", 1), own, *tables),
-            [own.shape],
-            [own.shape],
-        )
-        if more:
-            side = own_side(own)
-            other_entering, side = lax.optimization_barrier((other_entering, side))
-            other_kept, other_sent = both_steps(other_odd, other_entering, *other_sides)
-            other_came = swap(other_sent, "tm", 1)
+            own_came, sibling_came = swap(sent, "tm", 1), swap(new, "tm", 1)
+            fields_now = [inverse(0, new, own_came), inverse(1, sent, sibling_came)]
+            sides = [own_side(0), own_side(1)]
+            other_entering, sides = lax.optimization_barrier((other_entering, sides))
+            other_new, other_sent = both_steps(other_odd, other_entering, *other_sides)
+        else:
+            fields_now = [inverse(0, new, swap(sent, "tm", 1))]
+    own = fields_now[0]
     return own[None, None]
 
 

time: 57.4 us -> 60 us (1.045)
  waiting for transfers between devices: 24.7 us -> 18.6 us
  Pallas kernels: 5.1 us -> 8.66 us
  starting transfers between devices: 21.5 us -> 25 us
  local copies, waits for them, and re-layouts: 2.49 us -> 3.87 us
    ppermute x17 -> x21, waiting for transfers between devices: 24.7 us -> 18.6 us  [swap(): lax.ppermute(values, axis, [(i, i ^ masks[i & 1]) for i in range(lax.axis...]
    pallas_call x11 -> x12, Pallas kernels: 5.1 us -> 8.66 us  [call(): pl.pallas_call(kernel, out_shape=[jax.ShapeDtypeStruct(shape, jnp.float32...]
    ppermute x17 -> x21, starting transfers between devices: 21.5 us -> 25 us  [swap(): lax.ppermute(values, axis, [(i, i ^ masks[i & 1]) for i in range(lax.axis...]
    unnamed x28 -> x68, local copies, waits for them, and re-layouts: 2.4 us -> 3.79 us
  transfers between devices with their start and end apart: 17 -> 21, of which waited for: 14 -> 13; matrix products, arithmetic and copies ran while one was open for 2% -> 2% of each run, Pallas kernels for 4% -> 9%
where the time goes in v11:
time: 60 us; the launch traced here: 59.7 us
  starting transfers between devices  25 us (42%)
  waiting for transfers between devices  18.6 us (31%)
  Pallas kernels  8.66 us (14%)
  local copies, waits for them, and re-layouts  3.87 us (6%)
  between operations  2.59 us (4%)
  other arithmetic  1.01 us (2%)
    ppermute x21, starting transfers between devices, swap(): lax.ppermute(values, axis, [(i, i ^ masks[i & 1]) for i in range(lax.axis...  25 us
    ppermute x21, waiting for transfers between devices, swap(): lax.ppermute(values, axis, [(i, i ^ masks[i & 1]) for i in range(lax.axis...  18.6 us
    pallas_call x12, Pallas kernels, call(): pl.pallas_call(kernel, out_shape=[jax.ShapeDtypeStruct(shape, jnp.float32...  8.66 us
    unnamed x68, local copies, waits for them, and re-layouts  3.79 us
  transfers between devices with their start and end apart: 21, of which 13 were waited for; matrix products, arithmetic and copies ran while one was open for 2% of the time, Pallas kernels for 9%

profile of v11, /device:TPU:0, one launch (start us, length us, event | category | flops | bytes accessed | tf_op | source)
XLA Modules:
  0.0 59.7 jit_solution(604114008527241725)
XLA Ops:
  0.0 3.0 %collective-permute-start = (f32[256,256]{1,0:T(8,128)}, f32[256,256]{1,0:T(8,128)S(1)}, u32[]{:S(2)}, u32[]{:S(2)}) collective-permute-start(f32[256,256]{1,0:T(8,128)} %bitcast.19), channel_id=1, source_target_pairs={{0,16},{16,0},{1,17},{17,1},{2,18},{18,2},{3,19},{19,3},{4,20},{20... | collective-permute-start | bytes 786440 | tf_op jit(solution)/shard_map/ppermute | solution.py:157
  5.4 1.0 %copy-done.3 = f32[1,1,256,256]{3,2,1,0:T(8,128)S(1)} copy-done((f32[1,1,256,256]{3,2,1,0:T(8,128)S(1)}, f32[1,1,256,256]{3,2,1,0:T(8,128)}, u32[]{:S(2)}) %copy-start.3) | copy-done | bytes 262168
  6.4 0.9 %copy-done.5 = f32[1,1,256,256]{3,2,1,0:T(8,128)S(1)} copy-done((f32[1,1,256,256]{3,2,1,0:T(8,128)S(1)}, f32[1,1,256,256]{3,2,1,0:T(8,128)}, u32[]{:S(2)}) %copy-start.5) | copy-done | bytes 262168
  8.0 1.5 %collective-permute-done.partner_ref.refs_4_ = f32[256,256]{1,0:T(8,128)S(1)} collective-permute-done((f32[256,256]{1,0:T(8,128)}, f32[256,256]{1,0:T(8,128)S(1)}, u32[]{:S(2)}, u32[]{:S(2)}) %collective-permute-start) | collective-permute-done | bytes 262176 | tf_op jit(solution)/shard_map/ppermute | solution.py:157
  10.7 0.7 %collective-permute-done.1.came_ref = f32[128,256]{1,0:T(8,128)S(1)} collective-permute-done((f32[128,256]{1,0:T(8,128)S(1)}, f32[128,256]{1,0:T(8,128)S(1)}, u32[]{:S(2)}, u32[]{:S(2)}) %collective-permute-start.1) | collective-permute-done | bytes 131104 | tf_op jit(solution)/shard_map/ppermute | solution.py:157
  11.4 1.8 %collective-permute-start.4 = (f32[128,256]{1,0:T(8,128)S(1)}, f32[128,256]{1,0:T(8,128)S(1)}, u32[]{:S(2)}, u32[]{:S(2)}) collective-permute-start(f32[128,256]{1,0:T(8,128)S(1)} %multiply_add_fusion.7), channel_id=1, source_target_pairs={{0,2},{1,5},{2,0},{3,7},{4,6},{5,1},{6,4},{7,3},{8,10},{9,13},{10,... | collective-permute-start | bytes 393224 | tf_op jit(solution)/shard_map/ppermute | solution.py:157
  13.2 1.6 %collective-permute-start.3 = (f32[128,256]{1,0:T(8,128)S(1)}, f32[128,256]{1,0:T(8,128)S(1)}, u32[]{:S(2)}, u32[]{:S(2)}) collective-permute-start(f32[128,256]{1,0:T(8,128)S(1)} %multiply_add_fusion.7), channel_id=1, source_target_pairs={{0,4},{1,3},{2,6},{3,1},{4,0},{5,7},{6,2},{7,5},{8,12},{9,11},{10,... | collective-permute-start | bytes 393224 | tf_op jit(solution)/shard_map/ppermute | solution.py:157
  15.5 1.7 %collective-permute-done.4 = f32[128,256]{1,0:T(8,128)S(1)} collective-permute-done((f32[128,256]{1,0:T(8,128)S(1)}, f32[128,256]{1,0:T(8,128)S(1)}, u32[]{:S(2)}, u32[]{:S(2)}) %collective-permute-start.4) | collective-permute-done | bytes 131104 | tf_op jit(solution)/shard_map/ppermute | solution.py:157
  17.2 2.0 %collective-permute-start.5 = (f32[128,256]{1,0:T(8,128)S(1)}, f32[128,256]{1,0:T(8,128)S(1)}, u32[]{:S(2)}, u32[]{:S(2)}) collective-permute-start(f32[128,256]{1,0:T(8,128)S(1)} %shard_map.111.kept_ref), channel_id=1, source_target_pairs={{0,16},{16,0},{1,17},{17,1},{2,18},{18,2},{3,19},{19,3},{4,20},{20... | collective-permute-start | bytes 393224 | tf_op jit(solution)/shard_map/ppermute | solution.py:157
  19.4 1.5 %collective-permute-start.6 = (f32[128,256]{1,0:T(8,128)S(1)}, f32[128,256]{1,0:T(8,128)S(1)}, u32[]{:S(2)}, u32[]{:S(2)}) collective-permute-start(f32[128,256]{1,0:T(8,128)S(1)} %collective-permute-done.1.came_ref), channel_id=1, source_target_pairs={{0,16},{16,0},{1,17},{17,1},{2,18},{18,2},{3,19},{19,3},{4,20},{20... | collective-permute-start | bytes 393224 | tf_op jit(solution)/shard_map/ppermute | solution.py:157
  21.1 3.7 %collective-permute-start.7 = (f32[128,256]{1,0:T(8,128)S(1)}, f32[128,256]{1,0:T(8,128)S(1)}, u32[]{:S(2)}, u32[]{:S(2)}) collective-permute-start(f32[128,256]{1,0:T(8,128)S(1)} %multiply_add_fusion.6), channel_id=1, source_target_pairs={{0,12},{1,13},{2,14},{3,15},{4,8},{5,9},{6,10},{7,11},{8,4},{9,5},... | collective-permute-start | bytes 393224 | tf_op jit(solution)/shard_map/ppermute | solution.py:157
  24.9 0.6 copy-done.25
  25.5 2.5 %collective-permute-done.7 = f32[128,256]{1,0:T(8,128)S(1)} collective-permute-done((f32[128,256]{1,0:T(8,128)S(1)}, f32[128,256]{1,0:T(8,128)S(1)}, u32[]{:S(2)}, u32[]{:S(2)}) %collective-permute-start.7) | collective-permute-done | bytes 131104 | tf_op jit(solution)/shard_map/ppermute | solution.py:157
  28.1 0.7 %shard_map.112 = (f32[128,256]{1,0:T(8,128)}, f32[128,256]{1,0:T(8,128)S(1)}) custom-call(s32[1]{0:T(128)} %bitcast.2.odd_ref, f32[128,256]{1,0:T(8,128)S(1)} %multiply_add_fusion.4.entering_ref, f32[128,256]{1,0:T(8,128)S(1)} %shard_map.111.kept_ref, f32[128,256]{1,0:T(8,128)S(1)} %collective-permute-done.1.came_ref, f32[128,256]{1,0:T(8,128)S(1)} %get-tuple-element.67.rate_ref), custom_call_target="tpu_custom_call" | custom-call | tf_op jit(solution)/shard_map/pallas_call | solution.py:145
  28.8 0.6 %copy-done.7 = f32[128,256]{1,0:T(8,128)} copy-done((f32[128,256]{1,0:T(8,128)}, f32[128,256]{1,0:T(8,128)S(1)}, u32[]{:S(2)}) %copy-start.7) | copy-done | bytes 131096
  29.4 0.5 collective-permute-start.10
  29.9 1.5 %collective-permute-start.8 = (f32[128,256]{1,0:T(8,128)S(1)}, f32[128,256]{1,0:T(8,128)S(1)}, u32[]{:S(2)}, u32[]{:S(2)}) collective-permute-start(f32[128,256]{1,0:T(8,128)S(1)} %multiply_add_fusion.4.entering_ref), channel_id=1, source_target_pairs={{0,16},{16,0},{1,17},{17,1},{2,18},{18,2},{3,19},{19,3},{4,20},{20... | collective-permute-start | bytes 393224 | tf_op jit(solution)/shard_map/ppermute | solution.py:157
  31.4 1.5 %shard_map.113.own_ref.refs_1_ = f32[256,256]{1,0:T(8,128)S(1)} custom-call(s32[1]{0:T(128)} %bitcast.core_ref, s32[1]{0:T(128)} %bitcast.1.last_ref, f32[128,256]{1,0:T(8,128)} %get-tuple-element.54.kept_ref, f32[128,256]{1,0:T(8,128)S(1)} %collective-permute-done.9.came_ref, f32[256,256]{1,0:T(8,128)S(1)} %bitcast.23, bf16[2,256,256]{2,1,0:T(8,128)(2,1)S(1)} %copy-done, ...), custom_call_target="tpu_custom_call" | custom-call | tf_op jit(solution)/shard_map/pallas_call | solution.py:145
  33.3 0.5 copy-done.8
  33.8 1.5 %shard_map.115.own_ref.refs_6_ = f32[256,256]{1,0:T(8,128)S(1)} custom-call(s32[1]{0:T(128)} %bitcast.core_ref, s32[1]{0:T(128)} %bitcast.11.last_ref, f32[128,256]{1,0:T(8,128)S(1)} %copy-done.8, f32[128,256]{1,0:T(8,128)} %collective-permute-done.10.came_ref, f32[256,256]{1,0:T(8,128)S(1)} %collective-permute-done.11.own_ref, ...), custom_call_target="tpu_custom_call" | custom-call | tf_op jit(solution)/shard_map/pallas_call | solution.py:145
  35.7 0.6 collective-permute-start.14
  36.4 0.9 %collective-permute-done.14.refs_8_ = f32[128,256]{1,0:T(8,128)S(1)} collective-permute-done((f32[128,256]{1,0:T(8,128)S(1)}, f32[128,256]{1,0:T(8,128)S(1)}, u32[]{:S(2)}, u32[]{:S(2)}) %collective-permute-start.14) | collective-permute-done | bytes 131104 | tf_op jit(solution)/shard_map/ppermute | solution.py:157
  37.6 1.6 %shard_map.118 = (f32[128,256]{1,0:T(8,128)S(1)}, f32[128,256]{1,0:T(8,128)S(1)}) custom-call(s32[1]{0:T(128)} %bitcast.6.adjoint_ref, s32[1]{0:T(128)} %bitcast.core_ref, s32[1]{0:T(128)} %bitcast.7.last_ref, s32[1]{0:T(128)} %bitcast.8.other_last_ref, f32[256,256]{1,0:T(8,128)S(1)} %copy-done.1, bf16[2,256,256]{2,1,0:T(8,128)(2,1)S(1)} %copy-done, ...), custom_call_target="tpu_custom_call" | custom-call | tf_op jit(solution)/shard_map/pallas_call | solution.py:145
  39.4 2.7 %collective-permute-start.18 = (f32[128,256]{1,0:T(8,128)S(1)}, f32[128,256]{1,0:T(8,128)S(1)}, u32[]{:S(2)}, u32[]{:S(2)}) collective-permute-start(f32[128,256]{1,0:T(8,128)S(1)} %multiply_add_fusion.3), channel_id=1, source_target_pairs={{0,2},{1,5},{2,0},{3,7},{4,6},{5,1},{6,4},{7,3},{8,10},{9,13},{10,... | collective-permute-start | bytes 393224 | tf_op jit(solution)/shard_map/ppermute | solution.py:157
  42.1 1.3 %collective-permute-start.17 = (f32[128,256]{1,0:T(8,128)S(1)}, f32[128,256]{1,0:T(8,128)S(1)}, u32[]{:S(2)}, u32[]{:S(2)}) collective-permute-start(f32[128,256]{1,0:T(8,128)S(1)} %multiply_add_fusion.3), channel_id=1, source_target_pairs={{0,4},{1,3},{2,6},{3,1},{4,0},{5,7},{6,2},{7,5},{8,12},{9,11},{10,... | collective-permute-start | bytes 393224 | tf_op jit(solution)/shard_map/ppermute | solution.py:157
  43.7 3.4 %collective-permute-done.18 = f32[128,256]{1,0:T(8,128)S(1)} collective-permute-done((f32[128,256]{1,0:T(8,128)S(1)}, f32[128,256]{1,0:T(8,128)S(1)}, u32[]{:S(2)}, u32[]{:S(2)}) %collective-permute-start.18) | collective-permute-done | bytes 131104 | tf_op jit(solution)/shard_map/ppermute | solution.py:157
  47.0 1.1 %collective-permute-done.17 = f32[128,256]{1,0:T(8,128)S(1)} collective-permute-done((f32[128,256]{1,0:T(8,128)S(1)}, f32[128,256]{1,0:T(8,128)S(1)}, u32[]{:S(2)}, u32[]{:S(2)}) %collective-permute-start.17) | collective-permute-done | bytes 131104 | tf_op jit(solution)/shard_map/ppermute | solution.py:157
  48.1 1.8 %collective-permute-done.16 = f32[128,256]{1,0:T(8,128)S(1)} collective-permute-done((f32[128,256]{1,0:T(8,128)S(1)}, f32[128,256]{1,0:T(8,128)S(1)}, u32[]{:S(2)}, u32[]{:S(2)}) %collective-permute-start.16) | collective-permute-done | bytes 131104 | tf_op jit(solution)/shard_map/ppermute | solution.py:157
  50.0 3.8 %collective-permute-start.19 = (f32[128,256]{1,0:T(8,128)S(1)}, f32[128,256]{1,0:T(8,128)S(1)}, u32[]{:S(2)}, u32[]{:S(2)}) collective-permute-start(f32[128,256]{1,0:T(8,128)S(1)} %multiply_add_fusion.2), channel_id=1, source_target_pairs={{0,12},{1,13},{2,14},{3,15},{4,8},{5,9},{6,10},{7,11},{8,4},{9,5},... | collective-permute-start | bytes 393224 | tf_op jit(solution)/shard_map/ppermute | solution.py:157
  53.9 3.0 %collective-permute-done.19 = f32[128,256]{1,0:T(8,128)S(1)} collective-permute-done((f32[128,256]{1,0:T(8,128)S(1)}, f32[128,256]{1,0:T(8,128)S(1)}, u32[]{:S(2)}, u32[]{:S(2)}) %collective-permute-start.19) | collective-permute-done | bytes 131104 | tf_op jit(solution)/shard_map/ppermute | solution.py:157
  57.1 1.3 %collective-permute-done.20.came_ref = f32[128,256]{1,0:T(8,128)S(1)} collective-permute-done((f32[128,256]{1,0:T(8,128)S(1)}, f32[128,256]{1,0:T(8,128)S(1)}, u32[]{:S(2)}, u32[]{:S(2)}) %collective-permute-start.20) | collective-permute-done | bytes 131104 | tf_op jit(solution)/shard_map/ppermute | solution.py:157
  58.4 1.3 %shard_map.120 = f32[256,256]{1,0:T(8,128)} custom-call(s32[1]{0:T(128)} %bitcast.core_ref, s32[1]{0:T(128)} %bitcast.1.last_ref, f32[128,256]{1,0:T(8,128)S(1)} %get-tuple-element.65.kept_ref, f32[128,256]{1,0:T(8,128)S(1)} %collective-permute-done.20.came_ref, f32[256,256]{1,0:T(8,128)S(1)} %shard_map.113.own_ref.refs_1_, ...), custom_call_target="tpu_custom_call" | custom-call | tf_op jit(solution)/shard_map/pallas_call | solution.py:145
  (103 shorter events, 5.2 us)
Async XLA Ops:
  0.0 9.5 %collective-permute-start = (f32[256,256]{1,0:T(8,128)}, f32[256,256]{1,0:T(8,128)S(1)}, u32[]{:S(2)}, u32[]{:S(2)}) collective-permute-start(f32[256,256]{1,0:T(8,128)} %bitcast.19), channel_id=1, source_target_pairs={{0,16},{16,0},{1,17},{17,1},{2,18},{18,2},{3,19},{19,3},{4,20},{20... | collective-permute-start | bytes 786440 | tf_op jit(solution)/shard_map/ppermute | solution.py:157
  5.3 15.7 %copy-start.9 = (f32[128,256]{1,0:T(8,128)}, f32[128,256]{1,0:T(8,128)S(1)}, u32[]{:S(2)}) copy-start(f32[128,256]{1,0:T(8,128)S(1)} %get-tuple-element.48) | copy-start | bytes 393220
  5.3 19.5 %copy-start.23 = (f32[128,256]{1,0:T(8,128)}, f32[128,256]{1,0:T(8,128)S(1)}, u32[]{:S(2)}) copy-start(f32[128,256]{1,0:T(8,128)S(1)} %get-tuple-element.41) | copy-start | bytes 393220
  5.3 22.8 %copy-start.21 = (f32[128,256]{1,0:T(8,128)}, f32[128,256]{1,0:T(8,128)S(1)}, u32[]{:S(2)}) copy-start(f32[128,256]{1,0:T(8,128)S(1)} %get-tuple-element.50) | copy-start | bytes 393220
  8.0 16.8 %copy-start.27 = (f32[128,256]{1,0:T(8,128)}, f32[128,256]{1,0:T(8,128)S(1)}, u32[]{:S(2)}) copy-start(f32[128,256]{1,0:T(8,128)S(1)} %get-tuple-element.44) | copy-start | bytes 393220
  8.0 16.8 %copy-start.29 = (f32[128,256]{1,0:T(8,128)}, f32[128,256]{1,0:T(8,128)S(1)}, u32[]{:S(2)}) copy-start(f32[128,256]{1,0:T(8,128)S(1)} %get-tuple-element.43) | copy-start | bytes 393220
  8.0 16.8 %copy-start.31 = (f32[128,256]{1,0:T(8,128)}, f32[128,256]{1,0:T(8,128)S(1)}, u32[]{:S(2)}) copy-start(f32[128,256]{1,0:T(8,128)S(1)} %get-tuple-element.42) | copy-start | bytes 393220
  10.0 1.4 %collective-permute-start.1 = (f32[128,256]{1,0:T(8,128)S(1)}, f32[128,256]{1,0:T(8,128)S(1)}, u32[]{:S(2)}, u32[]{:S(2)}) collective-permute-start(f32[128,256]{1,0:T(8,128)S(1)} %get-tuple-element.40), channel_id=1, source_target_pairs={{0,1},{1,0},{2,3},{3,2},{4,5},{5,4},{6,7},{7,6},{8,9},{9,8},{10,11... | collective-permute-start | bytes 393224 | tf_op jit(solution)/shard_map/ppermute | solution.py:157
  11.4 5.8 %collective-permute-start.4 = (f32[128,256]{1,0:T(8,128)S(1)}, f32[128,256]{1,0:T(8,128)S(1)}, u32[]{:S(2)}, u32[]{:S(2)}) collective-permute-start(f32[128,256]{1,0:T(8,128)S(1)} %multiply_add_fusion.7), channel_id=1, source_target_pairs={{0,2},{1,5},{2,0},{3,7},{4,6},{5,1},{6,4},{7,3},{8,10},{9,13},{10,... | collective-permute-start | bytes 393224 | tf_op jit(solution)/shard_map/ppermute | solution.py:157
  13.2 6.2 %collective-permute-start.3 = (f32[128,256]{1,0:T(8,128)S(1)}, f32[128,256]{1,0:T(8,128)S(1)}, u32[]{:S(2)}, u32[]{:S(2)}) collective-permute-start(f32[128,256]{1,0:T(8,128)S(1)} %multiply_add_fusion.7), channel_id=1, source_target_pairs={{0,4},{1,3},{2,6},{3,1},{4,0},{5,7},{6,2},{7,5},{8,12},{9,11},{10,... | collective-permute-start | bytes 393224 | tf_op jit(solution)/shard_map/ppermute | solution.py:157
  14.8 6.2 %collective-permute-start.2 = (f32[128,256]{1,0:T(8,128)S(1)}, f32[128,256]{1,0:T(8,128)S(1)}, u32[]{:S(2)}, u32[]{:S(2)}) collective-permute-start(f32[128,256]{1,0:T(8,128)S(1)} %multiply_add_fusion.7), channel_id=1, source_target_pairs={{0,6},{1,7},{2,4},{3,5},{4,2},{5,3},{6,0},{7,1},{8,14},{9,15},{10,... | collective-permute-start | bytes 393224 | tf_op jit(solution)/shard_map/ppermute | solution.py:157
  15.0 18.3 %collective-permute-start.11 = (f32[256,256]{1,0:T(8,128)S(1)}, f32[256,256]{1,0:T(8,128)S(1)}, u32[]{:S(2)}, u32[]{:S(2)}) collective-permute-start(f32[256,256]{1,0:T(8,128)S(1)} %bitcast.22), channel_id=1, source_target_pairs={{0,1},{1,0},{2,3},{3,2},{4,5},{5,4},{6,7},{7,6},{8,9},{9,8},{10,11... | collective-permute-start | bytes 786440 | tf_op jit(solution)/shard_map/ppermute | solution.py:157
  15.0 20.3 %collective-permute-start.12 = (f32[256,256]{1,0:T(8,128)S(1)}, f32[256,256]{1,0:T(8,128)S(1)}, u32[]{:S(2)}, u32[]{:S(2)}) collective-permute-start(f32[256,256]{1,0:T(8,128)S(1)} %bitcast.25), channel_id=1, source_target_pairs={{0,1},{1,0},{2,3},{3,2},{4,5},{5,4},{6,7},{7,6},{8,9},{9,8},{10,11... | collective-permute-start | bytes 786440 | tf_op jit(solution)/shard_map/ppermute | solution.py:157
  17.2 8.3 %collective-permute-start.5 = (f32[128,256]{1,0:T(8,128)S(1)}, f32[128,256]{1,0:T(8,128)S(1)}, u32[]{:S(2)}, u32[]{:S(2)}) collective-permute-start(f32[128,256]{1,0:T(8,128)S(1)} %shard_map.111.kept_ref), channel_id=1, source_target_pairs={{0,16},{16,0},{1,17},{17,1},{2,18},{18,2},{3,19},{19,3},{4,20},{20... | collective-permute-start | bytes 393224 | tf_op jit(solution)/shard_map/ppermute | solution.py:157
  19.4 6.1 %collective-permute-start.6 = (f32[128,256]{1,0:T(8,128)S(1)}, f32[128,256]{1,0:T(8,128)S(1)}, u32[]{:S(2)}, u32[]{:S(2)}) collective-permute-start(f32[128,256]{1,0:T(8,128)S(1)} %collective-permute-done.1.came_ref), channel_id=1, source_target_pairs={{0,16},{16,0},{1,17},{17,1},{2,18},{18,2},{3,19},{19,3},{4,20},{20... | collective-permute-start | bytes 393224 | tf_op jit(solution)/shard_map/ppermute | solution.py:157
  21.1 6.9 %collective-permute-start.7 = (f32[128,256]{1,0:T(8,128)S(1)}, f32[128,256]{1,0:T(8,128)S(1)}, u32[]{:S(2)}, u32[]{:S(2)}) collective-permute-start(f32[128,256]{1,0:T(8,128)S(1)} %multiply_add_fusion.6), channel_id=1, source_target_pairs={{0,12},{1,13},{2,14},{3,15},{4,8},{5,9},{6,10},{7,11},{8,4},{9,5},... | collective-permute-start | bytes 393224 | tf_op jit(solution)/shard_map/ppermute | solution.py:157
  28.8 2.6 %collective-permute-start.9 = (f32[128,256]{1,0:T(8,128)S(1)}, f32[128,256]{1,0:T(8,128)S(1)}, u32[]{:S(2)}, u32[]{:S(2)}) collective-permute-start(f32[128,256]{1,0:T(8,128)S(1)} %get-tuple-element.55.kept_ref), channel_id=1, source_target_pairs={{0,1},{1,0},{2,3},{3,2},{4,5},{5,4},{6,7},{7,6},{8,9},{9,8},{10,11... | collective-permute-start | bytes 393224 | tf_op jit(solution)/shard_map/ppermute | solution.py:157
  29.4 3.9 %collective-permute-start.10 = (f32[128,256]{1,0:T(8,128)}, f32[128,256]{1,0:T(8,128)}, u32[]{:S(2)}, u32[]{:S(2)}) collective-permute-start(f32[128,256]{1,0:T(8,128)} %get-tuple-element.54.kept_ref), channel_id=1, source_target_pairs={{0,1},{1,0},{2,3},{3,2},{4,5},{5,4},{6,7},{7,6},{8,9},{9,8},{10,11... | collective-permute-start | bytes 393224 | tf_op jit(solution)/shard_map/ppermute | solution.py:157
  29.9 5.7 %collective-permute-start.8 = (f32[128,256]{1,0:T(8,128)S(1)}, f32[128,256]{1,0:T(8,128)S(1)}, u32[]{:S(2)}, u32[]{:S(2)}) collective-permute-start(f32[128,256]{1,0:T(8,128)S(1)} %multiply_add_fusion.4.entering_ref), channel_id=1, source_target_pairs={{0,16},{16,0},{1,17},{17,1},{2,18},{18,2},{3,19},{19,3},{4,20},{20... | collective-permute-start | bytes 393224 | tf_op jit(solution)/shard_map/ppermute | solution.py:157
  31.4 5.0 %collective-permute-start.15 = (f32[256,256]{1,0:T(8,128)S(1)}, f32[256,256]{1,0:T(8,128)S(1)}, u32[]{:S(2)}, u32[]{:S(2)}) collective-permute-start(f32[256,256]{1,0:T(8,128)S(1)} %collective-permute-done.partner_ref.refs_4_), channel_id=1, source_target_pairs={{0,1},{1,0},{2,3},{3,2},{4,5},{5,4},{6,7},{7,6},{8,9},{9,8},{10,11... | collective-permute-start | bytes 786440 | tf_op jit(solution)/shard_map/ppermute | solution.py:157
  35.7 1.6 %collective-permute-start.14 = (f32[128,256]{1,0:T(8,128)S(1)}, f32[128,256]{1,0:T(8,128)S(1)}, u32[]{:S(2)}, u32[]{:S(2)}) collective-permute-start(f32[128,256]{1,0:T(8,128)S(1)} %get-tuple-element.60.refs_2_), channel_id=1, source_target_pairs={{0,1},{1,0},{2,3},{3,2},{4,5},{5,4},{6,7},{7,6},{8,9},{9,8},{10,11... | collective-permute-start | bytes 393224 | tf_op jit(solution)/shard_map/ppermute | solution.py:157
  36.3 1.3 %collective-permute-start.13 = (f32[128,256]{1,0:T(8,128)S(1)}, f32[128,256]{1,0:T(8,128)S(1)}, u32[]{:S(2)}, u32[]{:S(2)}) collective-permute-start(f32[128,256]{1,0:T(8,128)S(1)} %get-tuple-element.61.refs_7_), channel_id=1, source_target_pairs={{0,1},{1,0},{2,3},{3,2},{4,5},{5,4},{6,7},{7,6},{8,9},{9,8},{10,11... | collective-permute-start | bytes 393224 | tf_op jit(solution)/shard_map/ppermute | solution.py:157
  39.4 14.4 %copy-start.24 = (f32[128,256]{1,0:T(8,128)S(1)}, f32[128,256]{1,0:T(8,128)}, u32[]{:S(2)}) copy-start(f32[128,256]{1,0:T(8,128)} %copy-done.23) | copy-start | bytes 393220
  39.4 14.4 %copy-start.26 = (f32[128,256]{1,0:T(8,128)S(1)}, f32[128,256]{1,0:T(8,128)}, u32[]{:S(2)}) copy-start(f32[128,256]{1,0:T(8,128)} %copy-done.25) | copy-start | bytes 393220
  39.4 14.4 %copy-start.28 = (f32[128,256]{1,0:T(8,128)S(1)}, f32[128,256]{1,0:T(8,128)}, u32[]{:S(2)}) copy-start(f32[128,256]{1,0:T(8,128)} %copy-done.27) | copy-start | bytes 393220
  39.4 14.4 %copy-start.30 = (f32[128,256]{1,0:T(8,128)S(1)}, f32[128,256]{1,0:T(8,128)}, u32[]{:S(2)}) copy-start(f32[128,256]{1,0:T(8,128)} %copy-done.29) | copy-start | bytes 393220
  39.4 14.4 %copy-start.32 = (f32[128,256]{1,0:T(8,128)S(1)}, f32[128,256]{1,0:T(8,128)}, u32[]{:S(2)}) copy-start(f32[128,256]{1,0:T(8,128)} %copy-done.31) | copy-start | bytes 393220
  39.4 7.6 %collective-permute-start.18 = (f32[128,256]{1,0:T(8,128)S(1)}, f32[128,256]{1,0:T(8,128)S(1)}, u32[]{:S(2)}, u32[]{:S(2)}) collective-permute-start(f32[128,256]{1,0:T(8,128)S(1)} %multiply_add_fusion.3), channel_id=1, source_target_pairs={{0,2},{1,5},{2,0},{3,7},{4,6},{5,1},{6,4},{7,3},{8,10},{9,13},{10,... | collective-permute-start | bytes 393224 | tf_op jit(solution)/shard_map/ppermute | solution.py:157
  42.1 6.0 %collective-permute-start.17 = (f32[128,256]{1,0:T(8,128)S(1)}, f32[128,256]{1,0:T(8,128)S(1)}, u32[]{:S(2)}, u32[]{:S(2)}) collective-permute-start(f32[128,256]{1,0:T(8,128)S(1)} %multiply_add_fusion.3), channel_id=1, source_target_pairs={{0,4},{1,3},{2,6},{3,1},{4,0},{5,7},{6,2},{7,5},{8,12},{9,11},{10,... | collective-permute-start | bytes 393224 | tf_op jit(solution)/shard_map/ppermute | solution.py:157
  43.4 6.5 %collective-permute-start.16 = (f32[128,256]{1,0:T(8,128)S(1)}, f32[128,256]{1,0:T(8,128)S(1)}, u32[]{:S(2)}, u32[]{:S(2)}) collective-permute-start(f32[128,256]{1,0:T(8,128)S(1)} %multiply_add_fusion.3), channel_id=1, source_target_pairs={{0,6},{1,7},{2,4},{3,5},{4,2},{5,3},{6,0},{7,1},{8,14},{9,15},{10,... | collective-permute-start | bytes 393224 | tf_op jit(solution)/shard_map/ppermute | solution.py:157
  50.0 6.9 %collective-permute-start.19 = (f32[128,256]{1,0:T(8,128)S(1)}, f32[128,256]{1,0:T(8,128)S(1)}, u32[]{:S(2)}, u32[]{:S(2)}) collective-permute-start(f32[128,256]{1,0:T(8,128)S(1)} %multiply_add_fusion.2), channel_id=1, source_target_pairs={{0,12},{1,13},{2,14},{3,15},{4,8},{5,9},{6,10},{7,11},{8,4},{9,5},... | collective-permute-start | bytes 393224 | tf_op jit(solution)/shard_map/ppermute | solution.py:157
  57.0 1.4 %collective-permute-start.20 = (f32[128,256]{1,0:T(8,128)S(1)}, f32[128,256]{1,0:T(8,128)S(1)}, u32[]{:S(2)}, u32[]{:S(2)}) collective-permute-start(f32[128,256]{1,0:T(8,128)S(1)} %get-tuple-element.66), channel_id=1, source_target_pairs={{0,1},{1,0},{2,3},{3,2},{4,5},{5,4},{6,7},{7,6},{8,9},{9,8},{10,11... | collective-permute-start | bytes 393224 | tf_op jit(solution)/shard_map/ppermute | solution.py:157
  (23 other events, 115.7 us)

commit v12 on v10

--- a/solution.py
+++ b/solution.py
@@ -207,7 +207,7 @@
 
 
 def carry_in(kept, came, pair, levels, share):
-    others = [swap(kept, "pair", 1), swap(came, "pair", 1)] if share else [None, None]
+    others = jnp.split(swap(jnp.concatenate([kept, came]), "pair", 1), 2) if share else [None, None]
     carry = pair[0] * kept + pair[1] * came
     entering = jnp.zeros_like(carry)
     for masks, join, enter in levels[:-1]:

time: 57.4 us -> 57.3 us (level)
    ppermute x17 -> x16, starting transfers between devices: 21.5 us -> 21.3 us  [swap(): lax.ppermute(values, axis, [(i, i ^ masks[i & 1]) for i in range(lax.axis...]
    ppermute x17 -> x16, waiting for transfers between devices: 24.7 us -> 24.8 us  [swap(): lax.ppermute(values, axis, [(i, i ^ masks[i & 1]) for i in range(lax.axis...]
  transfers between devices with their start and end apart: 17 -> 16, of which waited for: 14 -> 14; matrix products, arithmetic and copies ran while one was open for 2% -> 2% of each run, Pallas kernels for 4% -> 4%
where the time goes in v12:
time: 57.3 us; the launch traced here: 57.1 us
  waiting for transfers between devices  24.8 us (43%)
  starting transfers between devices  21.3 us (37%)
  Pallas kernels  5.1 us (9%)
  local copies, waits for them, and re-layouts  2.51 us (4%)
  between operations  2.37 us (4%)
  other arithmetic  1 us (2%)
    ppermute x16, waiting for transfers between devices, swap(): lax.ppermute(values, axis, [(i, i ^ masks[i & 1]) for i in range(lax.axis...  24.8 us
    ppermute x16, starting transfers between devices, swap(): lax.ppermute(values, axis, [(i, i ^ masks[i & 1]) for i in range(lax.axis...  21.3 us
    pallas_call x11, Pallas kernels, call(): pl.pallas_call(kernel, out_shape=[jax.ShapeDtypeStruct(shape, jnp.float32...  5.1 us
    unnamed x28, local copies, waits for them, and re-layouts  2.4 us
  transfers between devices with their start and end apart: 16, of which 14 were waited for; matrix products, arithmetic and copies ran while one was open for 2% of the time, Pallas kernels for 4%

profile of v12, /device:TPU:0, one launch (start us, length us, event | category | flops | bytes accessed | tf_op | source)
XLA Modules:
  0.0 57.1 jit_solution(15513029168171379499)
XLA Ops:
  0.0 3.0 %collective-permute-start = (f32[256,256]{1,0:T(8,128)}, f32[256,256]{1,0:T(8,128)S(1)}, u32[]{:S(2)}, u32[]{:S(2)}) collective-permute-start(f32[256,256]{1,0:T(8,128)} %bitcast.17), channel_id=1, source_target_pairs={{0,16},{16,0},{1,17},{17,1},{2,18},{18,2},{3,19},{19,3},{4,20},{20... | collective-permute-start | bytes 786440 | tf_op jit(solution)/shard_map/ppermute | solution.py:157
  5.4 0.9 %copy-done.3 = f32[1,1,256,256]{3,2,1,0:T(8,128)S(1)} copy-done((f32[1,1,256,256]{3,2,1,0:T(8,128)S(1)}, f32[1,1,256,256]{3,2,1,0:T(8,128)}, u32[]{:S(2)}) %copy-start.3) | copy-done | bytes 262168
  6.3 0.9 %copy-done.5 = f32[256,256]{1,0:T(8,128)S(1)} copy-done((f32[256,256]{1,0:T(8,128)S(1)}, f32[256,256]{1,0:T(8,128)}, u32[]{:S(2)}) %copy-start.5) | copy-done | bytes 262168
  7.9 1.6 %collective-permute-done.partner_ref.former_ref = f32[256,256]{1,0:T(8,128)S(1)} collective-permute-done((f32[256,256]{1,0:T(8,128)}, f32[256,256]{1,0:T(8,128)S(1)}, u32[]{:S(2)}, u32[]{:S(2)}) %collective-permute-start) | collective-permute-done | bytes 262176 | tf_op jit(solution)/shard_map/ppermute | solution.py:157
  9.5 0.5 shard_map.110
  10.2 0.4 shard_map.111.kept_ref
  10.7 0.7 %collective-permute-done.1.came_ref = f32[128,256]{1,0:T(8,128)S(1)} collective-permute-done((f32[128,256]{1,0:T(8,128)S(1)}, f32[128,256]{1,0:T(8,128)S(1)}, u32[]{:S(2)}, u32[]{:S(2)}) %collective-permute-start.1) | collective-permute-done | bytes 131104 | tf_op jit(solution)/shard_map/ppermute | solution.py:157
  11.4 1.8 %collective-permute-start.4 = (f32[128,256]{1,0:T(8,128)S(1)}, f32[128,256]{1,0:T(8,128)S(1)}, u32[]{:S(2)}, u32[]{:S(2)}) collective-permute-start(f32[128,256]{1,0:T(8,128)S(1)} %multiply_add_fusion.7), channel_id=1, source_target_pairs={{0,2},{1,5},{2,0},{3,7},{4,6},{5,1},{6,4},{7,3},{8,10},{9,13},{10,... | collective-permute-start | bytes 393224 | tf_op jit(solution)/shard_map/ppermute | solution.py:157
  13.2 1.6 %collective-permute-start.3 = (f32[128,256]{1,0:T(8,128)S(1)}, f32[128,256]{1,0:T(8,128)S(1)}, u32[]{:S(2)}, u32[]{:S(2)}) collective-permute-start(f32[128,256]{1,0:T(8,128)S(1)} %multiply_add_fusion.7), channel_id=1, source_target_pairs={{0,4},{1,3},{2,6},{3,1},{4,0},{5,7},{6,2},{7,5},{8,12},{9,11},{10,... | collective-permute-start | bytes 393224 | tf_op jit(solution)/shard_map/ppermute | solution.py:157
  15.0 1.8 %collective-permute-start.5 = (f32[256,256]{1,0:T(8,128)S(1)}, f32[256,256]{1,0:T(8,128)S(1)}, u32[]{:S(2)}, u32[]{:S(2)}) collective-permute-start(f32[256,256]{1,0:T(8,128)S(1)} %pad_maximum_fusion), channel_id=1, source_target_pairs={{0,16},{16,0},{1,17},{17,1},{2,18},{18,2},{3,19},{19,3},{4,20},{20... | collective-permute-start | bytes 786440 | tf_op jit(solution)/shard_map/ppermute | solution.py:157
  16.8 0.4 collective-permute-done.4
  17.2 2.2 %collective-permute-done.3 = f32[128,256]{1,0:T(8,128)S(1)} collective-permute-done((f32[128,256]{1,0:T(8,128)S(1)}, f32[128,256]{1,0:T(8,128)S(1)}, u32[]{:S(2)}, u32[]{:S(2)}) %collective-permute-start.3) | collective-permute-done | bytes 131104 | tf_op jit(solution)/shard_map/ppermute | solution.py:157
  19.4 1.6 %collective-permute-done.2 = f32[128,256]{1,0:T(8,128)S(1)} collective-permute-done((f32[128,256]{1,0:T(8,128)S(1)}, f32[128,256]{1,0:T(8,128)S(1)}, u32[]{:S(2)}, u32[]{:S(2)}) %collective-permute-start.2) | collective-permute-done | bytes 131104 | tf_op jit(solution)/shard_map/ppermute | solution.py:157
  21.1 3.7 %collective-permute-start.6 = (f32[128,256]{1,0:T(8,128)S(1)}, f32[128,256]{1,0:T(8,128)S(1)}, u32[]{:S(2)}, u32[]{:S(2)}) collective-permute-start(f32[128,256]{1,0:T(8,128)S(1)} %multiply_add_fusion.6), channel_id=1, source_target_pairs={{0,12},{1,13},{2,14},{3,15},{4,8},{5,9},{6,10},{7,11},{8,4},{9,5},... | collective-permute-start | bytes 393224 | tf_op jit(solution)/shard_map/ppermute | solution.py:157
  24.9 3.1 %collective-permute-done.6 = f32[128,256]{1,0:T(8,128)S(1)} collective-permute-done((f32[128,256]{1,0:T(8,128)S(1)}, f32[128,256]{1,0:T(8,128)S(1)}, u32[]{:S(2)}, u32[]{:S(2)}) %collective-permute-start.6) | collective-permute-done | bytes 131104 | tf_op jit(solution)/shard_map/ppermute | solution.py:157
  28.2 1.6 %collective-permute-start.7 = (f32[128,256]{1,0:T(8,128)S(1)}, f32[128,256]{1,0:T(8,128)S(1)}, u32[]{:S(2)}, u32[]{:S(2)}) collective-permute-start(f32[128,256]{1,0:T(8,128)S(1)} %multiply_add_fusion.4.entering_ref), channel_id=1, source_target_pairs={{0,16},{16,0},{1,17},{17,1},{2,18},{18,2},{3,19},{19,3},{4,20},{20... | collective-permute-start | bytes 393224 | tf_op jit(solution)/shard_map/ppermute | solution.py:157
  29.8 0.6 shard_map.113.own_ref
  31.2 2.9 %collective-permute-done.7.entering_ref = f32[128,256]{1,0:T(8,128)S(1)} collective-permute-done((f32[128,256]{1,0:T(8,128)S(1)}, f32[128,256]{1,0:T(8,128)S(1)}, u32[]{:S(2)}, u32[]{:S(2)}) %collective-permute-start.7) | collective-permute-done | bytes 131104 | tf_op jit(solution)/shard_map/ppermute | solution.py:157
  34.2 1.3 %collective-permute-done.9.came_ref = f32[128,256]{1,0:T(8,128)S(1)} collective-permute-done((f32[128,256]{1,0:T(8,128)S(1)}, f32[128,256]{1,0:T(8,128)S(1)}, u32[]{:S(2)}, u32[]{:S(2)}) %collective-permute-start.9) | collective-permute-done | bytes 131104 | tf_op jit(solution)/shard_map/ppermute | solution.py:157
  35.6 1.0 %shard_map.116 = (f32[256,256]{1,0:T(8,128)S(1)}, f32[128,256]{1,0:T(8,128)S(1)}) custom-call(s32[1]{0:T(128)} %bitcast.6.adjoint_ref, s32[1]{0:T(128)} %bitcast.core_ref, s32[1]{0:T(128)} %bitcast.7.partner_last_ref, f32[256,256]{1,0:T(8,128)S(1)} %shard_map.114.own_side_ref, f32[256,256]{1,0:T(8,128)S(1)} %shard_map.113.own_ref, ...), custom_call_target="tpu_custom_call" | custom-call | tf_op jit(solution)/shard_map/pallas_call | solution.py:145
  36.8 0.4 shard_map.117.kept_ref
  37.2 0.8 %collective-permute-done.10.came_ref = f32[128,256]{1,0:T(8,128)S(1)} collective-permute-done((f32[128,256]{1,0:T(8,128)S(1)}, f32[128,256]{1,0:T(8,128)S(1)}, u32[]{:S(2)}, u32[]{:S(2)}) %collective-permute-start.10) | collective-permute-done | bytes 131104 | tf_op jit(solution)/shard_map/ppermute | solution.py:157
  38.0 1.5 %collective-permute-start.13 = (f32[128,256]{1,0:T(8,128)S(1)}, f32[128,256]{1,0:T(8,128)S(1)}, u32[]{:S(2)}, u32[]{:S(2)}) collective-permute-start(f32[128,256]{1,0:T(8,128)S(1)} %multiply_add_fusion.3), channel_id=1, source_target_pairs={{0,2},{1,5},{2,0},{3,7},{4,6},{5,1},{6,4},{7,3},{8,10},{9,13},{10,... | collective-permute-start | bytes 393224 | tf_op jit(solution)/shard_map/ppermute | solution.py:157
  39.6 1.6 %collective-permute-start.12 = (f32[128,256]{1,0:T(8,128)S(1)}, f32[128,256]{1,0:T(8,128)S(1)}, u32[]{:S(2)}, u32[]{:S(2)}) collective-permute-start(f32[128,256]{1,0:T(8,128)S(1)} %multiply_add_fusion.3), channel_id=1, source_target_pairs={{0,4},{1,3},{2,6},{3,1},{4,0},{5,7},{6,2},{7,5},{8,12},{9,11},{10,... | collective-permute-start | bytes 393224 | tf_op jit(solution)/shard_map/ppermute | solution.py:157
  41.2 0.4 collective-permute-start.11
  41.6 2.3 %collective-permute-done.13 = f32[128,256]{1,0:T(8,128)S(1)} collective-permute-done((f32[128,256]{1,0:T(8,128)S(1)}, f32[128,256]{1,0:T(8,128)S(1)}, u32[]{:S(2)}, u32[]{:S(2)}) %collective-permute-start.13) | collective-permute-done | bytes 131104 | tf_op jit(solution)/shard_map/ppermute | solution.py:157
  43.9 1.7 %collective-permute-done.12 = f32[128,256]{1,0:T(8,128)S(1)} collective-permute-done((f32[128,256]{1,0:T(8,128)S(1)}, f32[128,256]{1,0:T(8,128)S(1)}, u32[]{:S(2)}, u32[]{:S(2)}) %collective-permute-start.12) | collective-permute-done | bytes 131104 | tf_op jit(solution)/shard_map/ppermute | solution.py:157
  45.6 1.7 %collective-permute-done.11 = f32[128,256]{1,0:T(8,128)S(1)} collective-permute-done((f32[128,256]{1,0:T(8,128)S(1)}, f32[128,256]{1,0:T(8,128)S(1)}, u32[]{:S(2)}, u32[]{:S(2)}) %collective-permute-start.11) | collective-permute-done | bytes 131104 | tf_op jit(solution)/shard_map/ppermute | solution.py:157
  47.4 3.7 %collective-permute-start.14 = (f32[128,256]{1,0:T(8,128)S(1)}, f32[128,256]{1,0:T(8,128)S(1)}, u32[]{:S(2)}, u32[]{:S(2)}) collective-permute-start(f32[128,256]{1,0:T(8,128)S(1)} %multiply_add_fusion.2), channel_id=1, source_target_pairs={{0,12},{1,13},{2,14},{3,15},{4,8},{5,9},{6,10},{7,11},{8,4},{9,5},... | collective-permute-start | bytes 393224 | tf_op jit(solution)/shard_map/ppermute | solution.py:157
  51.2 3.2 %collective-permute-done.14 = f32[128,256]{1,0:T(8,128)S(1)} collective-permute-done((f32[128,256]{1,0:T(8,128)S(1)}, f32[128,256]{1,0:T(8,128)S(1)}, u32[]{:S(2)}, u32[]{:S(2)}) %collective-permute-start.14) | collective-permute-done | bytes 131104 | tf_op jit(solution)/shard_map/ppermute | solution.py:157
  54.5 1.3 %collective-permute-done.15.came_ref = f32[128,256]{1,0:T(8,128)S(1)} collective-permute-done((f32[128,256]{1,0:T(8,128)S(1)}, f32[128,256]{1,0:T(8,128)S(1)}, u32[]{:S(2)}, u32[]{:S(2)}) %collective-permute-start.15) | collective-permute-done | bytes 131104 | tf_op jit(solution)/shard_map/ppermute | solution.py:157
  55.9 1.3 %shard_map.119 = f32[256,256]{1,0:T(8,128)} custom-call(s32[1]{0:T(128)} %bitcast.core_ref, s32[1]{0:T(128)} %bitcast.1.last_ref, f32[128,256]{1,0:T(8,128)S(1)} %get-tuple-element.63.kept_ref, f32[128,256]{1,0:T(8,128)S(1)} %collective-permute-done.15.came_ref, f32[256,256]{1,0:T(8,128)S(1)} %shard_map.113.own_ref, bf16[2,256,256]{2,1,0:T(8,128)(2,1)S(1)} %copy-done, ...), custom_call_target="tpu_custom_call" | custom-call | tf_op jit(solution)/shard_map/pallas_call | solution.py:145
  (54 shorter events, 3.2 us)
Async XLA Ops:
  0.0 9.5 %collective-permute-start = (f32[256,256]{1,0:T(8,128)}, f32[256,256]{1,0:T(8,128)S(1)}, u32[]{:S(2)}, u32[]{:S(2)}) collective-permute-start(f32[256,256]{1,0:T(8,128)} %bitcast.17), channel_id=1, source_target_pairs={{0,16},{16,0},{1,17},{17,1},{2,18},{18,2},{3,19},{19,3},{4,20},{20... | collective-permute-start | bytes 786440 | tf_op jit(solution)/shard_map/ppermute | solution.py:157
  3.0 2.0 %copy-start.13 = (f32[256]{0:T(256)S(1)}, f32[256]{0:T(256)}, u32[]{:S(2)}) copy-start(f32[256]{0:T(256)} %constant.48.clone) | copy-start | bytes 3076
  3.0 2.4 %copy-start.1 = (f32[256,256]{1,0:T(8,128)S(1)}, f32[256,256]{1,0:T(8,128)}, u32[]{:S(2)}) copy-start(f32[256,256]{1,0:T(8,128)} %reaction_ref.7) | copy-start | bytes 786436
  3.0 2.4 %copy-start.2 = (f32[1,1,256,256]{3,2,1,0:T(8,128)S(1)}, f32[1,1,256,256]{3,2,1,0:T(8,128)}, u32[]{:S(2)}) copy-start(f32[1,1,256,256]{3,2,1,0:T(8,128)} %param.11) | copy-start | bytes 786436
  5.4 1.0 %copy-start.3 = (f32[1,1,256,256]{3,2,1,0:T(8,128)S(1)}, f32[1,1,256,256]{3,2,1,0:T(8,128)}, u32[]{:S(2)}) copy-start(f32[1,1,256,256]{3,2,1,0:T(8,128)} %param.12) | copy-start | bytes 786436
  6.3 0.9 %copy-start.5 = (f32[256,256]{1,0:T(8,128)S(1)}, f32[256,256]{1,0:T(8,128)}, u32[]{:S(2)}) copy-start(f32[256,256]{1,0:T(8,128)} %diffusion_ref.3) | copy-start | bytes 786436
  7.6 1.8 %copy-start = (bf16[2,256,256]{2,1,0:T(8,128)(2,1)S(1)}, bf16[2,256,256]{2,1,0:T(8,128)(2,1)}, u32[]{:S(2)}) copy-start(bf16[2,256,256]{2,1,0:T(8,128)(2,1)} %constant.47.clone.x_ref.y_ref) | copy-start | bytes 786436
  7.9 16.9 %copy-start.7 = (f32[128,256]{1,0:T(8,128)}, f32[128,256]{1,0:T(8,128)S(1)}, u32[]{:S(2)}) copy-start(f32[128,256]{1,0:T(8,128)S(1)} %get-tuple-element.43) | copy-start | bytes 393220
  7.9 16.9 %copy-start.9 = (f32[128,256]{1,0:T(8,128)}, f32[128,256]{1,0:T(8,128)S(1)}, u32[]{:S(2)}) copy-start(f32[128,256]{1,0:T(8,128)S(1)} %get-tuple-element.42) | copy-start | bytes 393220
  7.9 16.9 %copy-start.11 = (f32[128,256]{1,0:T(8,128)}, f32[128,256]{1,0:T(8,128)S(1)}, u32[]{:S(2)}) copy-start(f32[128,256]{1,0:T(8,128)S(1)} %get-tuple-element.41) | copy-start | bytes 393220
  10.0 1.4 %collective-permute-start.1 = (f32[128,256]{1,0:T(8,128)S(1)}, f32[128,256]{1,0:T(8,128)S(1)}, u32[]{:S(2)}, u32[]{:S(2)}) collective-permute-start(f32[128,256]{1,0:T(8,128)S(1)} %get-tuple-element.39), channel_id=1, source_target_pairs={{0,1},{1,0},{2,3},{3,2},{4,5},{5,4},{6,7},{7,6},{8,9},{9,8},{10,11... | collective-permute-start | bytes 393224 | tf_op jit(solution)/shard_map/ppermute | solution.py:157
  11.4 5.8 %collective-permute-start.4 = (f32[128,256]{1,0:T(8,128)S(1)}, f32[128,256]{1,0:T(8,128)S(1)}, u32[]{:S(2)}, u32[]{:S(2)}) collective-permute-start(f32[128,256]{1,0:T(8,128)S(1)} %multiply_add_fusion.7), channel_id=1, source_target_pairs={{0,2},{1,5},{2,0},{3,7},{4,6},{5,1},{6,4},{7,3},{8,10},{9,13},{10,... | collective-permute-start | bytes 393224 | tf_op jit(solution)/shard_map/ppermute | solution.py:157
  13.2 6.2 %collective-permute-start.3 = (f32[128,256]{1,0:T(8,128)S(1)}, f32[128,256]{1,0:T(8,128)S(1)}, u32[]{:S(2)}, u32[]{:S(2)}) collective-permute-start(f32[128,256]{1,0:T(8,128)S(1)} %multiply_add_fusion.7), channel_id=1, source_target_pairs={{0,4},{1,3},{2,6},{3,1},{4,0},{5,7},{6,2},{7,5},{8,12},{9,11},{10,... | collective-permute-start | bytes 393224 | tf_op jit(solution)/shard_map/ppermute | solution.py:157
  14.8 6.2 %collective-permute-start.2 = (f32[128,256]{1,0:T(8,128)S(1)}, f32[128,256]{1,0:T(8,128)S(1)}, u32[]{:S(2)}, u32[]{:S(2)}) collective-permute-start(f32[128,256]{1,0:T(8,128)S(1)} %multiply_add_fusion.7), channel_id=1, source_target_pairs={{0,6},{1,7},{2,4},{3,5},{4,2},{5,3},{6,0},{7,1},{8,14},{9,15},{10,... | collective-permute-start | bytes 393224 | tf_op jit(solution)/shard_map/ppermute | solution.py:157
  15.0 9.9 %collective-permute-start.5 = (f32[256,256]{1,0:T(8,128)S(1)}, f32[256,256]{1,0:T(8,128)S(1)}, u32[]{:S(2)}, u32[]{:S(2)}) collective-permute-start(f32[256,256]{1,0:T(8,128)S(1)} %pad_maximum_fusion), channel_id=1, source_target_pairs={{0,16},{16,0},{1,17},{17,1},{2,18},{18,2},{3,19},{19,3},{4,20},{20... | collective-permute-start | bytes 786440 | tf_op jit(solution)/shard_map/ppermute | solution.py:157
  21.1 6.9 %collective-permute-start.6 = (f32[128,256]{1,0:T(8,128)S(1)}, f32[128,256]{1,0:T(8,128)S(1)}, u32[]{:S(2)}, u32[]{:S(2)}) collective-permute-start(f32[128,256]{1,0:T(8,128)S(1)} %multiply_add_fusion.6), channel_id=1, source_target_pairs={{0,12},{1,13},{2,14},{3,15},{4,8},{5,9},{6,10},{7,11},{8,4},{9,5},... | collective-permute-start | bytes 393224 | tf_op jit(solution)/shard_map/ppermute | solution.py:157
  28.1 1.7 %collective-permute-start.8 = (f32[128,256]{1,0:T(8,128)S(1)}, f32[128,256]{1,0:T(8,128)S(1)}, u32[]{:S(2)}, u32[]{:S(2)}) collective-permute-start(f32[128,256]{1,0:T(8,128)S(1)} %get-tuple-element.54), channel_id=1, source_target_pairs={{0,1},{1,0},{2,3},{3,2},{4,5},{5,4},{6,7},{7,6},{8,9},{9,8},{10,11... | collective-permute-start | bytes 393224 | tf_op jit(solution)/shard_map/ppermute | solution.py:157
  28.2 5.9 %collective-permute-start.7 = (f32[128,256]{1,0:T(8,128)S(1)}, f32[128,256]{1,0:T(8,128)S(1)}, u32[]{:S(2)}, u32[]{:S(2)}) collective-permute-start(f32[128,256]{1,0:T(8,128)S(1)} %multiply_add_fusion.4.entering_ref), channel_id=1, source_target_pairs={{0,16},{16,0},{1,17},{17,1},{2,18},{18,2},{3,19},{19,3},{4,20},{20... | collective-permute-start | bytes 393224 | tf_op jit(solution)/shard_map/ppermute | solution.py:157
  29.8 1.0 %copy-start.4 = (f32[1,1,256,256]{3,2,1,0:T(8,128)S(1)}, f32[1,1,256,256]{3,2,1,0:T(8,128)}, u32[]{:S(2)}) copy-start(f32[1,1,256,256]{3,2,1,0:T(8,128)} %param.12) | copy-start | bytes 786436
  29.8 1.0 %copy-start.6 = (f32[256,256]{1,0:T(8,128)S(1)}, f32[256,256]{1,0:T(8,128)}, u32[]{:S(2)}) copy-start(f32[256,256]{1,0:T(8,128)} %diffusion_ref.3) | copy-start | bytes 786436
  34.1 1.4 %collective-permute-start.9 = (f32[128,256]{1,0:T(8,128)S(1)}, f32[128,256]{1,0:T(8,128)S(1)}, u32[]{:S(2)}, u32[]{:S(2)}) collective-permute-start(f32[128,256]{1,0:T(8,128)S(1)} %get-tuple-element.60), channel_id=1, source_target_pairs={{0,1},{1,0},{2,3},{3,2},{4,5},{5,4},{6,7},{7,6},{8,9},{9,8},{10,11... | collective-permute-start | bytes 393224 | tf_op jit(solution)/shard_map/ppermute | solution.py:157
  36.6 1.4 %collective-permute-start.10 = (f32[128,256]{1,0:T(8,128)S(1)}, f32[128,256]{1,0:T(8,128)S(1)}, u32[]{:S(2)}, u32[]{:S(2)}) collective-permute-start(f32[128,256]{1,0:T(8,128)S(1)} %get-tuple-element.62), channel_id=1, source_target_pairs={{0,1},{1,0},{2,3},{3,2},{4,5},{5,4},{6,7},{7,6},{8,9},{9,8},{10,11... | collective-permute-start | bytes 393224 | tf_op jit(solution)/shard_map/ppermute | solution.py:157
  38.0 13.1 %copy-start.8 = (f32[128,256]{1,0:T(8,128)S(1)}, f32[128,256]{1,0:T(8,128)}, u32[]{:S(2)}) copy-start(f32[128,256]{1,0:T(8,128)} %copy-done.7) | copy-start | bytes 393220
  38.0 13.1 %copy-start.10 = (f32[128,256]{1,0:T(8,128)S(1)}, f32[128,256]{1,0:T(8,128)}, u32[]{:S(2)}) copy-start(f32[128,256]{1,0:T(8,128)} %copy-done.9) | copy-start | bytes 393220
  38.0 13.1 %copy-start.12 = (f32[128,256]{1,0:T(8,128)S(1)}, f32[128,256]{1,0:T(8,128)}, u32[]{:S(2)}) copy-start(f32[128,256]{1,0:T(8,128)} %copy-done.11) | copy-start | bytes 393220
  38.0 5.8 %collective-permute-start.13 = (f32[128,256]{1,0:T(8,128)S(1)}, f32[128,256]{1,0:T(8,128)S(1)}, u32[]{:S(2)}, u32[]{:S(2)}) collective-permute-start(f32[128,256]{1,0:T(8,128)S(1)} %multiply_add_fusion.3), channel_id=1, source_target_pairs={{0,2},{1,5},{2,0},{3,7},{4,6},{5,1},{6,4},{7,3},{8,10},{9,13},{10,... | collective-permute-start | bytes 393224 | tf_op jit(solution)/shard_map/ppermute | solution.py:157
  39.6 6.1 %collective-permute-start.12 = (f32[128,256]{1,0:T(8,128)S(1)}, f32[128,256]{1,0:T(8,128)S(1)}, u32[]{:S(2)}, u32[]{:S(2)}) collective-permute-start(f32[128,256]{1,0:T(8,128)S(1)} %multiply_add_fusion.3), channel_id=1, source_target_pairs={{0,4},{1,3},{2,6},{3,1},{4,0},{5,7},{6,2},{7,5},{8,12},{9,11},{10,... | collective-permute-start | bytes 393224 | tf_op jit(solution)/shard_map/ppermute | solution.py:157
  41.2 6.2 %collective-permute-start.11 = (f32[128,256]{1,0:T(8,128)S(1)}, f32[128,256]{1,0:T(8,128)S(1)}, u32[]{:S(2)}, u32[]{:S(2)}) collective-permute-start(f32[128,256]{1,0:T(8,128)S(1)} %multiply_add_fusion.3), channel_id=1, source_target_pairs={{0,6},{1,7},{2,4},{3,5},{4,2},{5,3},{6,0},{7,1},{8,14},{9,15},{10,... | collective-permute-start | bytes 393224 | tf_op jit(solution)/shard_map/ppermute | solution.py:157
  47.4 6.9 %collective-permute-start.14 = (f32[128,256]{1,0:T(8,128)S(1)}, f32[128,256]{1,0:T(8,128)S(1)}, u32[]{:S(2)}, u32[]{:S(2)}) collective-permute-start(f32[128,256]{1,0:T(8,128)S(1)} %multiply_add_fusion.2), channel_id=1, source_target_pairs={{0,12},{1,13},{2,14},{3,15},{4,8},{5,9},{6,10},{7,11},{8,4},{9,5},... | collective-permute-start | bytes 393224 | tf_op jit(solution)/shard_map/ppermute | solution.py:157
  54.4 1.4 %collective-permute-start.15 = (f32[128,256]{1,0:T(8,128)S(1)}, f32[128,256]{1,0:T(8,128)S(1)}, u32[]{:S(2)}, u32[]{:S(2)}) collective-permute-start(f32[128,256]{1,0:T(8,128)S(1)} %get-tuple-element.64), channel_id=1, source_target_pairs={{0,1},{1,0},{2,3},{3,2},{4,5},{5,4},{6,7},{7,6},{8,9},{9,8},{10,11... | collective-permute-start | bytes 393224 | tf_op jit(solution)/shard_map/ppermute | solution.py:157

commit v13 on v10

--- a/solution.py
+++ b/solution.py
@@ -139,7 +139,16 @@
     sent_ref[...] = jnp.where(odd, first, second)
 
 
-def call(kernel, scalars, arrays, out_shapes, scratch=(), flops=0):
+def own_steps_kernel(odd_ref, base_ref, kept_ref, came_ref, rate_ref, *refs):
+    entering_ref, new_ref, sent_ref = refs[-3:]
+    entering = base_ref[...]
+    for factor_ref, piece_ref in zip(refs[:-3:2], refs[1:-3:2]):
+        entering = entering + factor_ref[...] * piece_ref[...]
+    entering_ref[...] = entering
+    steps_kernel(odd_ref, entering_ref, kept_ref, came_ref, rate_ref, new_ref, sent_ref)
+
+
+def call(kernel, scalars, arrays, out_shapes, scratch=()):
     spec_scalar = pl.BlockSpec(memory_space=pltpu.SMEM)
     spec_array = pl.BlockSpec(memory_space=pltpu.VMEM)
     return pl.pallas_call(
@@ -217,8 +226,9 @@
     carry = lax.optimization_barrier(carry)
     masks, _, enter = levels[-1]
     entering, others = lax.optimization_barrier((entering + enter[0] * carry, others))
-    entering = entering + sum(one * swap(carry, "tm", mask) for one, mask in zip(enter[1:], masks))
-    return lax.optimization_barrier((entering, others))
+    last_terms = [(one, swap(carry, "tm", mask)) for one, mask in zip(enter[1:], masks)]
+    last_terms, others = lax.optimization_barrier((last_terms, others))
+    return entering, last_terms, others
 
 
 def on_device(fields, forcing, diffusion, reaction, wrap_factor, mean_diffusion, spectral_shift):
@@ -276,8 +286,11 @@
             )
         came = swap(sent, "tm", 1)
         (kept,) = call(functools.partial(keep_kernel, scale), (side_of,), (side, *tables), [(half, grid_y)])
-        entering, other_sides = carry_in(kept, came, pair, levels, more)
-        new, sent = both_steps(odd, entering, kept, came)
+        base, last_terms, other_sides = carry_in(kept, came, pair, levels, more)
+        terms = [array for term in last_terms for array in term]
+        entering, new, sent = call(
+            own_steps_kernel, (odd,), (base, kept, came, rate, *terms), [kept.shape] * 3
+        )
         if more:
             other_entering = swap(entering, "pair", 1)
         (own,) = call(

time: 57.4 us -> 59.4 us (1.035)
  waiting for transfers between devices: 24.7 us -> 26.3 us
  Pallas kernels: 5.1 us -> 5.79 us
    ppermute x17, waiting for transfers between devices: 24.7 us -> 26.3 us  [swap(): lax.ppermute(values, axis, [(i, i ^ masks[i & 1]) for i in range(lax.axis...]
    pallas_call x11, Pallas kernels: 5.1 us -> 5.79 us  [call(): pl.pallas_call(kernel, out_shape=[jax.ShapeDtypeStruct(shape, jnp.float32...]
    unnamed x28 -> x24, local copies, waits for them, and re-layouts: 2.4 us -> 2.39 us
  transfers between devices with their start and end apart: 17 -> 17, of which waited for: 14 -> 13; matrix products, arithmetic and copies ran while one was open for 2% -> 1% of each run, Pallas kernels for 4% -> 4%
where the time goes in v13:
time: 59.4 us; the launch traced here: 59.2 us
  waiting for transfers between devices  26.3 us (44%)
  starting transfers between devices  21.3 us (36%)
  Pallas kernels  5.79 us (10%)
  local copies, waits for them, and re-layouts  2.48 us (4%)
  between operations  2.32 us (4%)
  other arithmetic  0.94 us (2%)
    ppermute x17, waiting for transfers between devices, swap(): lax.ppermute(values, axis, [(i, i ^ masks[i & 1]) for i in range(lax.axis...  26.3 us
    ppermute x17, starting transfers between devices, swap(): lax.ppermute(values, axis, [(i, i ^ masks[i & 1]) for i in range(lax.axis...  21.3 us
    pallas_call x11, Pallas kernels, call(): pl.pallas_call(kernel, out_shape=[jax.ShapeDtypeStruct(shape, jnp.float32...  5.79 us
    unnamed x24, local copies, waits for them, and re-layouts  2.39 us
  transfers between devices with their start and end apart: 17, of which 13 were waited for; matrix products, arithmetic and copies ran while one was open for 1% of the time, Pallas kernels for 4%

profile of v13, /device:TPU:0, one launch (start us, length us, event | category | flops | bytes accessed | tf_op | source)
XLA Modules:
  0.0 59.2 jit_solution(12394079646552274560)
XLA Ops:
  0.0 3.0 %collective-permute-start = (f32[256,256]{1,0:T(8,128)}, f32[256,256]{1,0:T(8,128)S(1)}, u32[]{:S(2)}, u32[]{:S(2)}) collective-permute-start(f32[256,256]{1,0:T(8,128)} %bitcast.17), channel_id=1, source_target_pairs={{0,16},{16,0},{1,17},{17,1},{2,18},{18,2},{3,19},{19,3},{4,20},{20... | collective-permute-start | bytes 786440 | tf_op jit(solution)/shard_map/ppermute | solution.py:166
  5.4 0.9 %copy-done.3 = f32[1,1,256,256]{3,2,1,0:T(8,128)S(1)} copy-done((f32[1,1,256,256]{3,2,1,0:T(8,128)S(1)}, f32[1,1,256,256]{3,2,1,0:T(8,128)}, u32[]{:S(2)}) %copy-start.3) | copy-done | bytes 262168
  6.3 0.9 %copy-done.5 = f32[256,256]{1,0:T(8,128)S(1)} copy-done((f32[256,256]{1,0:T(8,128)S(1)}, f32[256,256]{1,0:T(8,128)}, u32[]{:S(2)}) %copy-start.5) | copy-done | bytes 262168
  7.9 1.6 %collective-permute-done.partner_ref.former_ref = f32[256,256]{1,0:T(8,128)S(1)} collective-permute-done((f32[256,256]{1,0:T(8,128)}, f32[256,256]{1,0:T(8,128)S(1)}, u32[]{:S(2)}, u32[]{:S(2)}) %collective-permute-start) | collective-permute-done | bytes 262176 | tf_op jit(solution)/shard_map/ppermute | solution.py:166
  9.5 0.5 shard_map.110
  10.2 0.4 shard_map.111.kept_ref
  10.7 0.7 %collective-permute-done.1.came_ref = f32[128,256]{1,0:T(8,128)S(1)} collective-permute-done((f32[128,256]{1,0:T(8,128)S(1)}, f32[128,256]{1,0:T(8,128)S(1)}, u32[]{:S(2)}, u32[]{:S(2)}) %collective-permute-start.1) | collective-permute-done | bytes 131104 | tf_op jit(solution)/shard_map/ppermute | solution.py:166
  11.4 2.8 %collective-permute-start.2 = (f32[128,256]{1,0:T(8,128)S(1)}, f32[128,256]{1,0:T(8,128)S(1)}, u32[]{:S(2)}, u32[]{:S(2)}) collective-permute-start(f32[128,256]{1,0:T(8,128)S(1)} %multiply_add_fusion.5), channel_id=1, source_target_pairs={{0,6},{1,7},{2,4},{3,5},{4,2},{5,3},{6,0},{7,1},{8,14},{9,15},{10,... | collective-permute-start | bytes 393224 | tf_op jit(solution)/shard_map/ppermute | solution.py:166
  14.2 0.4 collective-permute-start.3
  15.0 1.7 %collective-permute-start.5 = (f32[128,256]{1,0:T(8,128)S(1)}, f32[128,256]{1,0:T(8,128)S(1)}, u32[]{:S(2)}, u32[]{:S(2)}) collective-permute-start(f32[128,256]{1,0:T(8,128)S(1)} %shard_map.111.kept_ref), channel_id=1, source_target_pairs={{0,16},{16,0},{1,17},{17,1},{2,18},{18,2},{3,19},{19,3},{4,20},{20... | collective-permute-start | bytes 393224 | tf_op jit(solution)/shard_map/ppermute | solution.py:166
  17.0 1.1 %collective-permute-done.2 = f32[128,256]{1,0:T(8,128)S(1)} collective-permute-done((f32[128,256]{1,0:T(8,128)S(1)}, f32[128,256]{1,0:T(8,128)S(1)}, u32[]{:S(2)}, u32[]{:S(2)}) %collective-permute-start.2) | collective-permute-done | bytes 131104 | tf_op jit(solution)/shard_map/ppermute | solution.py:166
  18.2 2.9 %collective-permute-done.3 = f32[128,256]{1,0:T(8,128)S(1)} collective-permute-done((f32[128,256]{1,0:T(8,128)S(1)}, f32[128,256]{1,0:T(8,128)S(1)}, u32[]{:S(2)}, u32[]{:S(2)}) %collective-permute-start.3) | collective-permute-done | bytes 131104 | tf_op jit(solution)/shard_map/ppermute | solution.py:166
  21.1 3.7 %collective-permute-start.7 = (f32[128,256]{1,0:T(8,128)S(1)}, f32[128,256]{1,0:T(8,128)S(1)}, u32[]{:S(2)}, u32[]{:S(2)}) collective-permute-start(f32[128,256]{1,0:T(8,128)S(1)} %multiply_add_fusion.4), channel_id=1, source_target_pairs={{0,12},{1,13},{2,14},{3,15},{4,8},{5,9},{6,10},{7,11},{8,4},{9,5},... | collective-permute-start | bytes 393224 | tf_op jit(solution)/shard_map/ppermute | solution.py:166
  25.0 3.3 %collective-permute-done.7.refs_1_ = f32[128,256]{1,0:T(8,128)S(1)} collective-permute-done((f32[128,256]{1,0:T(8,128)S(1)}, f32[128,256]{1,0:T(8,128)S(1)}, u32[]{:S(2)}, u32[]{:S(2)}) %collective-permute-start.7) | collective-permute-done | bytes 131104 | tf_op jit(solution)/shard_map/ppermute | solution.py:166
  28.4 1.8 %collective-permute-start.8 = (f32[128,256]{1,0:T(8,128)S(1)}, f32[128,256]{1,0:T(8,128)S(1)}, u32[]{:S(2)}, u32[]{:S(2)}) collective-permute-start(f32[128,256]{1,0:T(8,128)S(1)} %get-tuple-element.58), channel_id=1, source_target_pairs={{0,16},{16,0},{1,17},{17,1},{2,18},{18,2},{3,19},{19,3},{4,20},{20... | collective-permute-start | bytes 393224 | tf_op jit(solution)/shard_map/ppermute | solution.py:166
  30.2 0.6 shard_map.113.own_ref
  31.2 0.4 shard_map.114.own_side_ref
  31.6 2.7 %collective-permute-done.8.entering_ref = f32[128,256]{1,0:T(8,128)S(1)} collective-permute-done((f32[128,256]{1,0:T(8,128)S(1)}, f32[128,256]{1,0:T(8,128)S(1)}, u32[]{:S(2)}, u32[]{:S(2)}) %collective-permute-start.8) | collective-permute-done | bytes 131104 | tf_op jit(solution)/shard_map/ppermute | solution.py:166
  34.4 1.3 %collective-permute-done.10.came_ref = f32[128,256]{1,0:T(8,128)S(1)} collective-permute-done((f32[128,256]{1,0:T(8,128)S(1)}, f32[128,256]{1,0:T(8,128)S(1)}, u32[]{:S(2)}, u32[]{:S(2)}) %collective-permute-start.10) | collective-permute-done | bytes 131104 | tf_op jit(solution)/shard_map/ppermute | solution.py:166
  35.8 1.0 %shard_map.116 = (f32[256,256]{1,0:T(8,128)S(1)}, f32[128,256]{1,0:T(8,128)S(1)}) custom-call(s32[1]{0:T(128)} %bitcast.6.adjoint_ref, s32[1]{0:T(128)} %bitcast.core_ref, s32[1]{0:T(128)} %bitcast.7.partner_last_ref, f32[256,256]{1,0:T(8,128)S(1)} %shard_map.114.own_side_ref, f32[256,256]{1,0:T(8,128)S(1)} %shard_map.113.own_ref, ...), custom_call_target="tpu_custom_call" | custom-call | tf_op jit(solution)/shard_map/pallas_call | solution.py:154
  37.0 0.4 shard_map.117.kept_ref
  37.4 0.8 %collective-permute-done.11.came_ref = f32[128,256]{1,0:T(8,128)S(1)} collective-permute-done((f32[128,256]{1,0:T(8,128)S(1)}, f32[128,256]{1,0:T(8,128)S(1)}, u32[]{:S(2)}, u32[]{:S(2)}) %collective-permute-start.11) | collective-permute-done | bytes 131104 | tf_op jit(solution)/shard_map/ppermute | solution.py:166
  38.2 3.6 %collective-permute-start.12 = (f32[128,256]{1,0:T(8,128)S(1)}, f32[128,256]{1,0:T(8,128)S(1)}, u32[]{:S(2)}, u32[]{:S(2)}) collective-permute-start(f32[128,256]{1,0:T(8,128)S(1)} %multiply_add_fusion.2), channel_id=1, source_target_pairs={{0,6},{1,7},{2,4},{3,5},{4,2},{5,3},{6,0},{7,1},{8,14},{9,15},{10,... | collective-permute-start | bytes 393224 | tf_op jit(solution)/shard_map/ppermute | solution.py:166
  41.8 0.6 %collective-permute-start.14 = (f32[128,256]{1,0:T(8,128)S(1)}, f32[128,256]{1,0:T(8,128)S(1)}, u32[]{:S(2)}, u32[]{:S(2)}) collective-permute-start(f32[128,256]{1,0:T(8,128)S(1)} %multiply_add_fusion.2), channel_id=1, source_target_pairs={{0,2},{1,5},{2,0},{3,7},{4,6},{5,1},{6,4},{7,3},{8,10},{9,13},{10,... | collective-permute-start | bytes 393224 | tf_op jit(solution)/shard_map/ppermute | solution.py:166
  42.4 3.3 %collective-permute-done.12 = f32[128,256]{1,0:T(8,128)S(1)} collective-permute-done((f32[128,256]{1,0:T(8,128)S(1)}, f32[128,256]{1,0:T(8,128)S(1)}, u32[]{:S(2)}, u32[]{:S(2)}) %collective-permute-start.12) | collective-permute-done | bytes 131104 | tf_op jit(solution)/shard_map/ppermute | solution.py:166
  45.7 2.1 %collective-permute-done.13 = f32[128,256]{1,0:T(8,128)S(1)} collective-permute-done((f32[128,256]{1,0:T(8,128)S(1)}, f32[128,256]{1,0:T(8,128)S(1)}, u32[]{:S(2)}, u32[]{:S(2)}) %collective-permute-start.13) | collective-permute-done | bytes 131104 | tf_op jit(solution)/shard_map/ppermute | solution.py:166
  47.8 0.6 collective-permute-done.14
  48.5 2.7 %collective-permute-start.15 = (f32[128,256]{1,0:T(8,128)S(1)}, f32[128,256]{1,0:T(8,128)S(1)}, u32[]{:S(2)}, u32[]{:S(2)}) collective-permute-start(f32[128,256]{1,0:T(8,128)S(1)} %multiply_add_fusion.1), channel_id=1, source_target_pairs={{0,12},{1,13},{2,14},{3,15},{4,8},{5,9},{6,10},{7,11},{8,4},{9,5},... | collective-permute-start | bytes 393224 | tf_op jit(solution)/shard_map/ppermute | solution.py:166
  51.3 4.6 %collective-permute-done.15.refs_1_ = f32[128,256]{1,0:T(8,128)S(1)} collective-permute-done((f32[128,256]{1,0:T(8,128)S(1)}, f32[128,256]{1,0:T(8,128)S(1)}, u32[]{:S(2)}, u32[]{:S(2)}) %collective-permute-start.15) | collective-permute-done | bytes 131104 | tf_op jit(solution)/shard_map/ppermute | solution.py:166
  55.9 0.7 %shard_map.118 = (f32[128,256]{1,0:T(8,128)}, f32[128,256]{1,0:T(8,128)S(1)}, f32[128,256]{1,0:T(8,128)S(1)}) custom-call(s32[1]{0:T(128)} %bitcast.2.odd_ref, f32[128,256]{1,0:T(8,128)S(1)} %multiply_add_fusion.base_ref, f32[128,256]{1,0:T(8,128)S(1)} %shard_map.117.kept_ref, f32[128,256]{1,0:T(8,128)S(1)} %collective-permute-done.11.came_ref, ...), custom_call_target="tpu_custom_call" | custom-call | tf_op jit(solution)/shard_map/pallas_call | solution.py:154
  56.6 1.3 %collective-permute-done.16.came_ref = f32[128,256]{1,0:T(8,128)S(1)} collective-permute-done((f32[128,256]{1,0:T(8,128)S(1)}, f32[128,256]{1,0:T(8,128)S(1)}, u32[]{:S(2)}, u32[]{:S(2)}) %collective-permute-start.16) | collective-permute-done | bytes 131104 | tf_op jit(solution)/shard_map/ppermute | solution.py:166
  57.9 1.3 %shard_map.119 = f32[256,256]{1,0:T(8,128)} custom-call(s32[1]{0:T(128)} %bitcast.core_ref, s32[1]{0:T(128)} %bitcast.1.last_ref, f32[128,256]{1,0:T(8,128)S(1)} %get-tuple-element.71.kept_ref, f32[128,256]{1,0:T(8,128)S(1)} %collective-permute-done.16.came_ref, f32[256,256]{1,0:T(8,128)S(1)} %shard_map.113.own_ref, bf16[2,256,256]{2,1,0:T(8,128)(2,1)S(1)} %copy-done, ...), custom_call_target="tpu_custom_call" | custom-call | tf_op jit(solution)/shard_map/pallas_call | solution.py:154
  (48 shorter events, 3.1 us)
Async XLA Ops:
  0.0 9.5 %collective-permute-start = (f32[256,256]{1,0:T(8,128)}, f32[256,256]{1,0:T(8,128)S(1)}, u32[]{:S(2)}, u32[]{:S(2)}) collective-permute-start(f32[256,256]{1,0:T(8,128)} %bitcast.17), channel_id=1, source_target_pairs={{0,16},{16,0},{1,17},{17,1},{2,18},{18,2},{3,19},{19,3},{4,20},{20... | collective-permute-start | bytes 786440 | tf_op jit(solution)/shard_map/ppermute | solution.py:166
  3.0 2.0 %copy-start.11 = (f32[256]{0:T(256)S(1)}, f32[256]{0:T(256)}, u32[]{:S(2)}) copy-start(f32[256]{0:T(256)} %constant.48.clone) | copy-start | bytes 3076
  3.0 2.4 %copy-start.1 = (f32[256,256]{1,0:T(8,128)S(1)}, f32[256,256]{1,0:T(8,128)}, u32[]{:S(2)}) copy-start(f32[256,256]{1,0:T(8,128)} %reaction_ref.7) | copy-start | bytes 786436
  3.0 2.4 %copy-start.2 = (f32[1,1,256,256]{3,2,1,0:T(8,128)S(1)}, f32[1,1,256,256]{3,2,1,0:T(8,128)}, u32[]{:S(2)}) copy-start(f32[1,1,256,256]{3,2,1,0:T(8,128)} %param.11) | copy-start | bytes 786436
  5.4 1.0 %copy-start.3 = (f32[1,1,256,256]{3,2,1,0:T(8,128)S(1)}, f32[1,1,256,256]{3,2,1,0:T(8,128)}, u32[]{:S(2)}) copy-start(f32[1,1,256,256]{3,2,1,0:T(8,128)} %param.12) | copy-start | bytes 786436
  6.3 0.9 %copy-start.5 = (f32[256,256]{1,0:T(8,128)S(1)}, f32[256,256]{1,0:T(8,128)}, u32[]{:S(2)}) copy-start(f32[256,256]{1,0:T(8,128)} %diffusion_ref.3) | copy-start | bytes 786436
  7.6 1.8 %copy-start = (bf16[2,256,256]{2,1,0:T(8,128)(2,1)S(1)}, bf16[2,256,256]{2,1,0:T(8,128)(2,1)}, u32[]{:S(2)}) copy-start(bf16[2,256,256]{2,1,0:T(8,128)(2,1)} %constant.47.clone.x_ref.y_ref) | copy-start | bytes 786436
  7.9 16.9 %copy-start.7 = (f32[128,256]{1,0:T(8,128)}, f32[128,256]{1,0:T(8,128)S(1)}, u32[]{:S(2)}) copy-start(f32[128,256]{1,0:T(8,128)S(1)} %get-tuple-element.46) | copy-start | bytes 393220
  7.9 16.9 %copy-start.9 = (f32[128,256]{1,0:T(8,128)}, f32[128,256]{1,0:T(8,128)S(1)}, u32[]{:S(2)}) copy-start(f32[128,256]{1,0:T(8,128)S(1)} %get-tuple-element.45) | copy-start | bytes 393220
  10.0 1.4 %collective-permute-start.1 = (f32[128,256]{1,0:T(8,128)S(1)}, f32[128,256]{1,0:T(8,128)S(1)}, u32[]{:S(2)}, u32[]{:S(2)}) collective-permute-start(f32[128,256]{1,0:T(8,128)S(1)} %get-tuple-element.43), channel_id=1, source_target_pairs={{0,1},{1,0},{2,3},{3,2},{4,5},{5,4},{6,7},{7,6},{8,9},{9,8},{10,11... | collective-permute-start | bytes 393224 | tf_op jit(solution)/shard_map/ppermute | solution.py:166
  11.4 6.7 %collective-permute-start.2 = (f32[128,256]{1,0:T(8,128)S(1)}, f32[128,256]{1,0:T(8,128)S(1)}, u32[]{:S(2)}, u32[]{:S(2)}) collective-permute-start(f32[128,256]{1,0:T(8,128)S(1)} %multiply_add_fusion.5), channel_id=1, source_target_pairs={{0,6},{1,7},{2,4},{3,5},{4,2},{5,3},{6,0},{7,1},{8,14},{9,15},{10,... | collective-permute-start | bytes 393224 | tf_op jit(solution)/shard_map/ppermute | solution.py:166
  14.2 6.8 %collective-permute-start.3 = (f32[128,256]{1,0:T(8,128)S(1)}, f32[128,256]{1,0:T(8,128)S(1)}, u32[]{:S(2)}, u32[]{:S(2)}) collective-permute-start(f32[128,256]{1,0:T(8,128)S(1)} %multiply_add_fusion.5), channel_id=1, source_target_pairs={{0,4},{1,3},{2,6},{3,1},{4,0},{5,7},{6,2},{7,5},{8,12},{9,11},{10,... | collective-permute-start | bytes 393224 | tf_op jit(solution)/shard_map/ppermute | solution.py:166
  14.7 6.4 %collective-permute-start.4 = (f32[128,256]{1,0:T(8,128)S(1)}, f32[128,256]{1,0:T(8,128)S(1)}, u32[]{:S(2)}, u32[]{:S(2)}) collective-permute-start(f32[128,256]{1,0:T(8,128)S(1)} %multiply_add_fusion.5), channel_id=1, source_target_pairs={{0,2},{1,5},{2,0},{3,7},{4,6},{5,1},{6,4},{7,3},{8,10},{9,13},{10,... | collective-permute-start | bytes 393224 | tf_op jit(solution)/shard_map/ppermute | solution.py:166
  15.0 9.9 %collective-permute-start.5 = (f32[128,256]{1,0:T(8,128)S(1)}, f32[128,256]{1,0:T(8,128)S(1)}, u32[]{:S(2)}, u32[]{:S(2)}) collective-permute-start(f32[128,256]{1,0:T(8,128)S(1)} %shard_map.111.kept_ref), channel_id=1, source_target_pairs={{0,16},{16,0},{1,17},{17,1},{2,18},{18,2},{3,19},{19,3},{4,20},{20... | collective-permute-start | bytes 393224 | tf_op jit(solution)/shard_map/ppermute | solution.py:166
  16.7 8.2 %collective-permute-start.6 = (f32[128,256]{1,0:T(8,128)S(1)}, f32[128,256]{1,0:T(8,128)S(1)}, u32[]{:S(2)}, u32[]{:S(2)}) collective-permute-start(f32[128,256]{1,0:T(8,128)S(1)} %collective-permute-done.1.came_ref), channel_id=1, source_target_pairs={{0,16},{16,0},{1,17},{17,1},{2,18},{18,2},{3,19},{19,3},{4,20},{20... | collective-permute-start | bytes 393224 | tf_op jit(solution)/shard_map/ppermute | solution.py:166
  21.1 7.1 %collective-permute-start.7 = (f32[128,256]{1,0:T(8,128)S(1)}, f32[128,256]{1,0:T(8,128)S(1)}, u32[]{:S(2)}, u32[]{:S(2)}) collective-permute-start(f32[128,256]{1,0:T(8,128)S(1)} %multiply_add_fusion.4), channel_id=1, source_target_pairs={{0,12},{1,13},{2,14},{3,15},{4,8},{5,9},{6,10},{7,11},{8,4},{9,5},... | collective-permute-start | bytes 393224 | tf_op jit(solution)/shard_map/ppermute | solution.py:166
  28.3 1.9 %collective-permute-start.9 = (f32[128,256]{1,0:T(8,128)S(1)}, f32[128,256]{1,0:T(8,128)S(1)}, u32[]{:S(2)}, u32[]{:S(2)}) collective-permute-start(f32[128,256]{1,0:T(8,128)S(1)} %get-tuple-element.60), channel_id=1, source_target_pairs={{0,1},{1,0},{2,3},{3,2},{4,5},{5,4},{6,7},{7,6},{8,9},{9,8},{10,11... | collective-permute-start | bytes 393224 | tf_op jit(solution)/shard_map/ppermute | solution.py:166
  28.4 5.9 %collective-permute-start.8 = (f32[128,256]{1,0:T(8,128)S(1)}, f32[128,256]{1,0:T(8,128)S(1)}, u32[]{:S(2)}, u32[]{:S(2)}) collective-permute-start(f32[128,256]{1,0:T(8,128)S(1)} %get-tuple-element.58), channel_id=1, source_target_pairs={{0,16},{16,0},{1,17},{17,1},{2,18},{18,2},{3,19},{19,3},{4,20},{20... | collective-permute-start | bytes 393224 | tf_op jit(solution)/shard_map/ppermute | solution.py:166
  30.2 1.0 %copy-start.4 = (f32[1,1,256,256]{3,2,1,0:T(8,128)S(1)}, f32[1,1,256,256]{3,2,1,0:T(8,128)}, u32[]{:S(2)}) copy-start(f32[1,1,256,256]{3,2,1,0:T(8,128)} %param.12) | copy-start | bytes 786436
  30.2 1.0 %copy-start.6 = (f32[256,256]{1,0:T(8,128)S(1)}, f32[256,256]{1,0:T(8,128)}, u32[]{:S(2)}) copy-start(f32[256,256]{1,0:T(8,128)} %diffusion_ref.3) | copy-start | bytes 786436
  34.3 1.4 %collective-permute-start.10 = (f32[128,256]{1,0:T(8,128)S(1)}, f32[128,256]{1,0:T(8,128)S(1)}, u32[]{:S(2)}, u32[]{:S(2)}) collective-permute-start(f32[128,256]{1,0:T(8,128)S(1)} %get-tuple-element.66), channel_id=1, source_target_pairs={{0,1},{1,0},{2,3},{3,2},{4,5},{5,4},{6,7},{7,6},{8,9},{9,8},{10,11... | collective-permute-start | bytes 393224 | tf_op jit(solution)/shard_map/ppermute | solution.py:166
  36.8 1.4 %collective-permute-start.11 = (f32[128,256]{1,0:T(8,128)S(1)}, f32[128,256]{1,0:T(8,128)S(1)}, u32[]{:S(2)}, u32[]{:S(2)}) collective-permute-start(f32[128,256]{1,0:T(8,128)S(1)} %get-tuple-element.68), channel_id=1, source_target_pairs={{0,1},{1,0},{2,3},{3,2},{4,5},{5,4},{6,7},{7,6},{8,9},{9,8},{10,11... | collective-permute-start | bytes 393224 | tf_op jit(solution)/shard_map/ppermute | solution.py:166
  38.2 13.0 %copy-start.8 = (f32[128,256]{1,0:T(8,128)S(1)}, f32[128,256]{1,0:T(8,128)}, u32[]{:S(2)}) copy-start(f32[128,256]{1,0:T(8,128)} %copy-done.7) | copy-start | bytes 393220
  38.2 13.0 %copy-start.10 = (f32[128,256]{1,0:T(8,128)S(1)}, f32[128,256]{1,0:T(8,128)}, u32[]{:S(2)}) copy-start(f32[128,256]{1,0:T(8,128)} %copy-done.9) | copy-start | bytes 393220
  38.2 7.5 %collective-permute-start.12 = (f32[128,256]{1,0:T(8,128)S(1)}, f32[128,256]{1,0:T(8,128)S(1)}, u32[]{:S(2)}, u32[]{:S(2)}) collective-permute-start(f32[128,256]{1,0:T(8,128)S(1)} %multiply_add_fusion.2), channel_id=1, source_target_pairs={{0,6},{1,7},{2,4},{3,5},{4,2},{5,3},{6,0},{7,1},{8,14},{9,15},{10,... | collective-permute-start | bytes 393224 | tf_op jit(solution)/shard_map/ppermute | solution.py:166
  41.8 6.0 %collective-permute-start.13 = (f32[128,256]{1,0:T(8,128)S(1)}, f32[128,256]{1,0:T(8,128)S(1)}, u32[]{:S(2)}, u32[]{:S(2)}) collective-permute-start(f32[128,256]{1,0:T(8,128)S(1)} %multiply_add_fusion.2), channel_id=1, source_target_pairs={{0,4},{1,3},{2,6},{3,1},{4,0},{5,7},{6,2},{7,5},{8,12},{9,11},{10,... | collective-permute-start | bytes 393224 | tf_op jit(solution)/shard_map/ppermute | solution.py:166
  41.8 6.6 %collective-permute-start.14 = (f32[128,256]{1,0:T(8,128)S(1)}, f32[128,256]{1,0:T(8,128)S(1)}, u32[]{:S(2)}, u32[]{:S(2)}) collective-permute-start(f32[128,256]{1,0:T(8,128)S(1)} %multiply_add_fusion.2), channel_id=1, source_target_pairs={{0,2},{1,5},{2,0},{3,7},{4,6},{5,1},{6,4},{7,3},{8,10},{9,13},{10,... | collective-permute-start | bytes 393224 | tf_op jit(solution)/shard_map/ppermute | solution.py:166
  48.5 7.4 %collective-permute-start.15 = (f32[128,256]{1,0:T(8,128)S(1)}, f32[128,256]{1,0:T(8,128)S(1)}, u32[]{:S(2)}, u32[]{:S(2)}) collective-permute-start(f32[128,256]{1,0:T(8,128)S(1)} %multiply_add_fusion.1), channel_id=1, source_target_pairs={{0,12},{1,13},{2,14},{3,15},{4,8},{5,9},{6,10},{7,11},{8,4},{9,5},... | collective-permute-start | bytes 393224 | tf_op jit(solution)/shard_map/ppermute | solution.py:166
  56.6 1.3 %collective-permute-start.16 = (f32[128,256]{1,0:T(8,128)S(1)}, f32[128,256]{1,0:T(8,128)S(1)}, u32[]{:S(2)}, u32[]{:S(2)}) collective-permute-start(f32[128,256]{1,0:T(8,128)S(1)} %get-tuple-element.72), channel_id=1, source_target_pairs={{0,1},{1,0},{2,3},{3,2},{4,5},{5,4},{6,7},{7,6},{8,9},{9,8},{10,11... | collective-permute-start | bytes 393224 | tf_op jit(solution)/shard_map/ppermute | solution.py:166

commit v14 on v10

--- a/solution.py
+++ b/solution.py
@@ -130,6 +130,20 @@
         out_ref[place, :] = former * own_ref[place, :] + both_sides(x_ref, modes, parts(y_ref), place)
 
 
+def final_kernel(
+    core_ref, last_ref, kept_ref, came_ref, own_ref, x_ref, y_ref, out_ref, work_ref, field_ref, semaphores
+):
+    modes = gather_halves(core_ref[0], work_ref, kept_ref, came_ref)
+    former = jnp.where(last_ref[0] == 1, 1.0, 0.0)
+    copies = []
+    for number, place in enumerate(row_halves(work_ref.shape[0])):
+        field_ref[place, :] = former * own_ref[place, :] + both_sides(x_ref, modes, parts(y_ref), place)
+        copies.append(pltpu.make_async_copy(field_ref.at[place], out_ref.at[place], semaphores.at[number]))
+        copies[-1].start()
+    for copy in copies:
+        copy.wait()
+
+
 def steps_kernel(odd_ref, entering_ref, kept_ref, came_ref, rate_ref, new_ref, sent_ref):
     odd = odd_ref[0] == 1
     kept, came, rate = kept_ref[...], came_ref[...], rate_ref[...]
@@ -139,15 +153,16 @@
     sent_ref[...] = jnp.where(odd, first, second)
 
 
-def call(kernel, scalars, arrays, out_shapes, scratch=(), flops=0):
+def call(kernel, scalars, arrays, out_shapes, scratch=(), copies=0):
     spec_scalar = pl.BlockSpec(memory_space=pltpu.SMEM)
     spec_array = pl.BlockSpec(memory_space=pltpu.VMEM)
     return pl.pallas_call(
         kernel,
         out_shape=[jax.ShapeDtypeStruct(shape, jnp.float32) for shape in out_shapes],
         in_specs=[spec_scalar] * len(scalars) + [spec_array] * len(arrays),
-        out_specs=[spec_array] * len(out_shapes),
-        scratch_shapes=[pltpu.VMEM(shape, jnp.float32) for shape in scratch],
+        out_specs=[pl.BlockSpec(memory_space=pl.ANY) if copies else spec_array] * len(out_shapes),
+        scratch_shapes=[pltpu.VMEM(shape, jnp.float32) for shape in scratch]
+        + [pltpu.SemaphoreType.DMA((copies,))] * (copies > 0),
         compiler_params=pltpu.CompilerParams(vmem_limit_bytes=16 * 1024 * 1024),
     )(*scalars, *arrays)
 
@@ -281,11 +296,12 @@
         if more:
             other_entering = swap(entering, "pair", 1)
         (own,) = call(
-            inverse_kernel,
+            inverse_kernel if more else final_kernel,
             (side_of, last),
             (new, swap(sent, "tm", 1), own, *tables),
             [own.shape],
-            [own.shape],
+            [own.shape] * (1 if more else 2),
+            0 if more else 2,
         )
         if more:
             side = own_side(own)

time: 57.4 us -> 57.3 us (level)
  no operation moved by 1% of the time
where the time goes in v14:
time: 57.3 us; the launch traced here: 57.1 us
  waiting for transfers between devices  24.7 us (43%)
  starting transfers between devices  21.5 us (38%)
  Pallas kernels  5.06 us (9%)
  local copies, waits for them, and re-layouts  2.49 us (4%)
  between operations  2.37 us (4%)
  other arithmetic  0.99 us (2%)
    ppermute x17, waiting for transfers between devices, swap(): lax.ppermute(values, axis, [(i, i ^ masks[i & 1]) for i in range(lax.axis...  24.7 us
    ppermute x17, starting transfers between devices, swap(): lax.ppermute(values, axis, [(i, i ^ masks[i & 1]) for i in range(lax.axis...  21.5 us
    pallas_call x11, Pallas kernels, call(): pl.pallas_call(kernel, out_shape=[jax.ShapeDtypeStruct(shape, jnp.float32...  5.06 us
    unnamed x28, local copies, waits for them, and re-layouts  2.4 us
  transfers between devices with their start and end apart: 17, of which 14 were waited for; matrix products, arithmetic and copies ran while one was open for 2% of the time, Pallas kernels for 4%

profile of v14, /device:TPU:0, one launch (start us, length us, event | category | flops | bytes accessed | tf_op | source)
XLA Modules:
  0.0 57.1 jit_solution(13000352519637940113)
XLA Ops:
  0.0 3.0 %collective-permute-start = (f32[256,256]{1,0:T(8,128)}, f32[256,256]{1,0:T(8,128)S(1)}, u32[]{:S(2)}, u32[]{:S(2)}) collective-permute-start(f32[256,256]{1,0:T(8,128)} %bitcast.17), channel_id=1, source_target_pairs={{0,16},{16,0},{1,17},{17,1},{2,18},{18,2},{3,19},{19,3},{4,20},{20... | collective-permute-start | bytes 786440 | tf_op jit(solution)/shard_map/ppermute | solution.py:172
  5.4 0.9 %copy-done.3 = f32[1,1,256,256]{3,2,1,0:T(8,128)S(1)} copy-done((f32[1,1,256,256]{3,2,1,0:T(8,128)S(1)}, f32[1,1,256,256]{3,2,1,0:T(8,128)}, u32[]{:S(2)}) %copy-start.3) | copy-done | bytes 262168
  6.3 0.9 %copy-done.5 = f32[256,256]{1,0:T(8,128)S(1)} copy-done((f32[256,256]{1,0:T(8,128)S(1)}, f32[256,256]{1,0:T(8,128)}, u32[]{:S(2)}) %copy-start.5) | copy-done | bytes 262168
  7.9 1.6 %collective-permute-done.partner_ref.former_ref = f32[256,256]{1,0:T(8,128)S(1)} collective-permute-done((f32[256,256]{1,0:T(8,128)}, f32[256,256]{1,0:T(8,128)S(1)}, u32[]{:S(2)}, u32[]{:S(2)}) %collective-permute-start) | collective-permute-done | bytes 262176 | tf_op jit(solution)/shard_map/ppermute | solution.py:172
  9.5 0.5 shard_map.110
  10.2 0.4 shard_map.111.kept_ref
  10.7 0.7 %collective-permute-done.1.came_ref = f32[128,256]{1,0:T(8,128)S(1)} collective-permute-done((f32[128,256]{1,0:T(8,128)S(1)}, f32[128,256]{1,0:T(8,128)S(1)}, u32[]{:S(2)}, u32[]{:S(2)}) %collective-permute-start.1) | collective-permute-done | bytes 131104 | tf_op jit(solution)/shard_map/ppermute | solution.py:172
  11.4 1.8 %collective-permute-start.4 = (f32[128,256]{1,0:T(8,128)S(1)}, f32[128,256]{1,0:T(8,128)S(1)}, u32[]{:S(2)}, u32[]{:S(2)}) collective-permute-start(f32[128,256]{1,0:T(8,128)S(1)} %multiply_add_fusion.7), channel_id=1, source_target_pairs={{0,2},{1,5},{2,0},{3,7},{4,6},{5,1},{6,4},{7,3},{8,10},{9,13},{10,... | collective-permute-start | bytes 393224 | tf_op jit(solution)/shard_map/ppermute | solution.py:172
  13.2 1.6 %collective-permute-start.3 = (f32[128,256]{1,0:T(8,128)S(1)}, f32[128,256]{1,0:T(8,128)S(1)}, u32[]{:S(2)}, u32[]{:S(2)}) collective-permute-start(f32[128,256]{1,0:T(8,128)S(1)} %multiply_add_fusion.7), channel_id=1, source_target_pairs={{0,4},{1,3},{2,6},{3,1},{4,0},{5,7},{6,2},{7,5},{8,12},{9,11},{10,... | collective-permute-start | bytes 393224 | tf_op jit(solution)/shard_map/ppermute | solution.py:172
  15.0 1.7 %collective-permute-start.5 = (f32[128,256]{1,0:T(8,128)S(1)}, f32[128,256]{1,0:T(8,128)S(1)}, u32[]{:S(2)}, u32[]{:S(2)}) collective-permute-start(f32[128,256]{1,0:T(8,128)S(1)} %shard_map.111.kept_ref), channel_id=1, source_target_pairs={{0,16},{16,0},{1,17},{17,1},{2,18},{18,2},{3,19},{19,3},{4,20},{20... | collective-permute-start | bytes 393224 | tf_op jit(solution)/shard_map/ppermute | solution.py:172
  17.2 2.2 %collective-permute-done.3 = f32[128,256]{1,0:T(8,128)S(1)} collective-permute-done((f32[128,256]{1,0:T(8,128)S(1)}, f32[128,256]{1,0:T(8,128)S(1)}, u32[]{:S(2)}, u32[]{:S(2)}) %collective-permute-start.3) | collective-permute-done | bytes 131104 | tf_op jit(solution)/shard_map/ppermute | solution.py:172
  19.4 1.6 %collective-permute-done.2 = f32[128,256]{1,0:T(8,128)S(1)} collective-permute-done((f32[128,256]{1,0:T(8,128)S(1)}, f32[128,256]{1,0:T(8,128)S(1)}, u32[]{:S(2)}, u32[]{:S(2)}) %collective-permute-start.2) | collective-permute-done | bytes 131104 | tf_op jit(solution)/shard_map/ppermute | solution.py:172
  21.1 3.7 %collective-permute-start.7 = (f32[128,256]{1,0:T(8,128)S(1)}, f32[128,256]{1,0:T(8,128)S(1)}, u32[]{:S(2)}, u32[]{:S(2)}) collective-permute-start(f32[128,256]{1,0:T(8,128)S(1)} %multiply_add_fusion.6), channel_id=1, source_target_pairs={{0,12},{1,13},{2,14},{3,15},{4,8},{5,9},{6,10},{7,11},{8,4},{9,5},... | collective-permute-start | bytes 393224 | tf_op jit(solution)/shard_map/ppermute | solution.py:172
  24.9 3.1 %collective-permute-done.7 = f32[128,256]{1,0:T(8,128)S(1)} collective-permute-done((f32[128,256]{1,0:T(8,128)S(1)}, f32[128,256]{1,0:T(8,128)S(1)}, u32[]{:S(2)}, u32[]{:S(2)}) %collective-permute-start.7) | collective-permute-done | bytes 131104 | tf_op jit(solution)/shard_map/ppermute | solution.py:172
  28.2 1.6 %collective-permute-start.8 = (f32[128,256]{1,0:T(8,128)S(1)}, f32[128,256]{1,0:T(8,128)S(1)}, u32[]{:S(2)}, u32[]{:S(2)}) collective-permute-start(f32[128,256]{1,0:T(8,128)S(1)} %multiply_add_fusion.4.entering_ref), channel_id=1, source_target_pairs={{0,16},{16,0},{1,17},{17,1},{2,18},{18,2},{3,19},{19,3},{4,20},{20... | collective-permute-start | bytes 393224 | tf_op jit(solution)/shard_map/ppermute | solution.py:172
  29.8 0.6 shard_map.113.own_ref
  30.8 0.4 shard_map.114.own_side_ref
  31.2 2.9 %collective-permute-done.8.entering_ref = f32[128,256]{1,0:T(8,128)S(1)} collective-permute-done((f32[128,256]{1,0:T(8,128)S(1)}, f32[128,256]{1,0:T(8,128)S(1)}, u32[]{:S(2)}, u32[]{:S(2)}) %collective-permute-start.8) | collective-permute-done | bytes 131104 | tf_op jit(solution)/shard_map/ppermute | solution.py:172
  34.2 1.3 %collective-permute-done.10.came_ref = f32[128,256]{1,0:T(8,128)S(1)} collective-permute-done((f32[128,256]{1,0:T(8,128)S(1)}, f32[128,256]{1,0:T(8,128)S(1)}, u32[]{:S(2)}, u32[]{:S(2)}) %collective-permute-start.10) | collective-permute-done | bytes 131104 | tf_op jit(solution)/shard_map/ppermute | solution.py:172
  35.6 1.0 %shard_map.116 = (f32[256,256]{1,0:T(8,128)S(1)}, f32[128,256]{1,0:T(8,128)S(1)}) custom-call(s32[1]{0:T(128)} %bitcast.6.adjoint_ref, s32[1]{0:T(128)} %bitcast.core_ref, s32[1]{0:T(128)} %bitcast.7.partner_last_ref, f32[256,256]{1,0:T(8,128)S(1)} %shard_map.114.own_side_ref, f32[256,256]{1,0:T(8,128)S(1)} %shard_map.113.own_ref, ...), custom_call_target="tpu_custom_call" | custom-call | tf_op jit(solution)/shard_map/pallas_call | solution.py:159
  36.8 0.4 shard_map.117.kept_ref
  37.2 0.8 %collective-permute-done.11.came_ref = f32[128,256]{1,0:T(8,128)S(1)} collective-permute-done((f32[128,256]{1,0:T(8,128)S(1)}, f32[128,256]{1,0:T(8,128)S(1)}, u32[]{:S(2)}, u32[]{:S(2)}) %collective-permute-start.11) | collective-permute-done | bytes 131104 | tf_op jit(solution)/shard_map/ppermute | solution.py:172
  38.0 1.5 %collective-permute-start.14 = (f32[128,256]{1,0:T(8,128)S(1)}, f32[128,256]{1,0:T(8,128)S(1)}, u32[]{:S(2)}, u32[]{:S(2)}) collective-permute-start(f32[128,256]{1,0:T(8,128)S(1)} %multiply_add_fusion.3), channel_id=1, source_target_pairs={{0,2},{1,5},{2,0},{3,7},{4,6},{5,1},{6,4},{7,3},{8,10},{9,13},{10,... | collective-permute-start | bytes 393224 | tf_op jit(solution)/shard_map/ppermute | solution.py:172
  39.6 1.6 %collective-permute-start.13 = (f32[128,256]{1,0:T(8,128)S(1)}, f32[128,256]{1,0:T(8,128)S(1)}, u32[]{:S(2)}, u32[]{:S(2)}) collective-permute-start(f32[128,256]{1,0:T(8,128)S(1)} %multiply_add_fusion.3), channel_id=1, source_target_pairs={{0,4},{1,3},{2,6},{3,1},{4,0},{5,7},{6,2},{7,5},{8,12},{9,11},{10,... | collective-permute-start | bytes 393224 | tf_op jit(solution)/shard_map/ppermute | solution.py:172
  41.2 0.4 collective-permute-start.12
  41.6 2.3 %collective-permute-done.14 = f32[128,256]{1,0:T(8,128)S(1)} collective-permute-done((f32[128,256]{1,0:T(8,128)S(1)}, f32[128,256]{1,0:T(8,128)S(1)}, u32[]{:S(2)}, u32[]{:S(2)}) %collective-permute-start.14) | collective-permute-done | bytes 131104 | tf_op jit(solution)/shard_map/ppermute | solution.py:172
  43.9 1.7 %collective-permute-done.13 = f32[128,256]{1,0:T(8,128)S(1)} collective-permute-done((f32[128,256]{1,0:T(8,128)S(1)}, f32[128,256]{1,0:T(8,128)S(1)}, u32[]{:S(2)}, u32[]{:S(2)}) %collective-permute-start.13) | collective-permute-done | bytes 131104 | tf_op jit(solution)/shard_map/ppermute | solution.py:172
  45.6 1.7 %collective-permute-done.12 = f32[128,256]{1,0:T(8,128)S(1)} collective-permute-done((f32[128,256]{1,0:T(8,128)S(1)}, f32[128,256]{1,0:T(8,128)S(1)}, u32[]{:S(2)}, u32[]{:S(2)}) %collective-permute-start.12) | collective-permute-done | bytes 131104 | tf_op jit(solution)/shard_map/ppermute | solution.py:172
  47.4 3.7 %collective-permute-start.15 = (f32[128,256]{1,0:T(8,128)S(1)}, f32[128,256]{1,0:T(8,128)S(1)}, u32[]{:S(2)}, u32[]{:S(2)}) collective-permute-start(f32[128,256]{1,0:T(8,128)S(1)} %multiply_add_fusion.2), channel_id=1, source_target_pairs={{0,12},{1,13},{2,14},{3,15},{4,8},{5,9},{6,10},{7,11},{8,4},{9,5},... | collective-permute-start | bytes 393224 | tf_op jit(solution)/shard_map/ppermute | solution.py:172
  51.2 3.2 %collective-permute-done.15 = f32[128,256]{1,0:T(8,128)S(1)} collective-permute-done((f32[128,256]{1,0:T(8,128)S(1)}, f32[128,256]{1,0:T(8,128)S(1)}, u32[]{:S(2)}, u32[]{:S(2)}) %collective-permute-start.15) | collective-permute-done | bytes 131104 | tf_op jit(solution)/shard_map/ppermute | solution.py:172
  54.5 1.3 %collective-permute-done.16.came_ref = f32[128,256]{1,0:T(8,128)S(1)} collective-permute-done((f32[128,256]{1,0:T(8,128)S(1)}, f32[128,256]{1,0:T(8,128)S(1)}, u32[]{:S(2)}, u32[]{:S(2)}) %collective-permute-start.16) | collective-permute-done | bytes 131104 | tf_op jit(solution)/shard_map/ppermute | solution.py:172
  55.9 1.2 %shard_map.119 = f32[256,256]{1,0:T(8,128)} custom-call(s32[1]{0:T(128)} %bitcast.core_ref, s32[1]{0:T(128)} %bitcast.1.last_ref, f32[128,256]{1,0:T(8,128)S(1)} %get-tuple-element.63.kept_ref, f32[128,256]{1,0:T(8,128)S(1)} %collective-permute-done.16.came_ref, f32[256,256]{1,0:T(8,128)S(1)} %shard_map.113.own_ref, bf16[2,256,256]{2,1,0:T(8,128)(2,1)S(1)} %copy-done, ...), custom_call_target="tpu_custom_call" | custom-call | tf_op jit(solution)/shard_map/pallas_call | solution.py:159
  (54 shorter events, 3.3 us)
Async XLA Ops:
  0.0 9.5 %collective-permute-start = (f32[256,256]{1,0:T(8,128)}, f32[256,256]{1,0:T(8,128)S(1)}, u32[]{:S(2)}, u32[]{:S(2)}) collective-permute-start(f32[256,256]{1,0:T(8,128)} %bitcast.17), channel_id=1, source_target_pairs={{0,16},{16,0},{1,17},{17,1},{2,18},{18,2},{3,19},{19,3},{4,20},{20... | collective-permute-start | bytes 786440 | tf_op jit(solution)/shard_map/ppermute | solution.py:172
  3.0 2.0 %copy-start.13 = (f32[256]{0:T(256)S(1)}, f32[256]{0:T(256)}, u32[]{:S(2)}) copy-start(f32[256]{0:T(256)} %constant.48.clone) | copy-start | bytes 3076
  3.0 2.4 %copy-start.1 = (f32[256,256]{1,0:T(8,128)S(1)}, f32[256,256]{1,0:T(8,128)}, u32[]{:S(2)}) copy-start(f32[256,256]{1,0:T(8,128)} %reaction_ref.7) | copy-start | bytes 786436
  3.0 2.4 %copy-start.2 = (f32[1,1,256,256]{3,2,1,0:T(8,128)S(1)}, f32[1,1,256,256]{3,2,1,0:T(8,128)}, u32[]{:S(2)}) copy-start(f32[1,1,256,256]{3,2,1,0:T(8,128)} %param.11) | copy-start | bytes 786436
  5.4 1.0 %copy-start.3 = (f32[1,1,256,256]{3,2,1,0:T(8,128)S(1)}, f32[1,1,256,256]{3,2,1,0:T(8,128)}, u32[]{:S(2)}) copy-start(f32[1,1,256,256]{3,2,1,0:T(8,128)} %param.12) | copy-start | bytes 786436
  6.3 0.9 %copy-start.5 = (f32[256,256]{1,0:T(8,128)S(1)}, f32[256,256]{1,0:T(8,128)}, u32[]{:S(2)}) copy-start(f32[256,256]{1,0:T(8,128)} %diffusion_ref.3) | copy-start | bytes 786436
  7.6 1.8 %copy-start = (bf16[2,256,256]{2,1,0:T(8,128)(2,1)S(1)}, bf16[2,256,256]{2,1,0:T(8,128)(2,1)}, u32[]{:S(2)}) copy-start(bf16[2,256,256]{2,1,0:T(8,128)(2,1)} %constant.47.clone.x_ref.y_ref) | copy-start | bytes 786436
  7.9 16.9 %copy-start.7 = (f32[128,256]{1,0:T(8,128)}, f32[128,256]{1,0:T(8,128)S(1)}, u32[]{:S(2)}) copy-start(f32[128,256]{1,0:T(8,128)S(1)} %get-tuple-element.43) | copy-start | bytes 393220
  7.9 16.9 %copy-start.9 = (f32[128,256]{1,0:T(8,128)}, f32[128,256]{1,0:T(8,128)S(1)}, u32[]{:S(2)}) copy-start(f32[128,256]{1,0:T(8,128)S(1)} %get-tuple-element.42) | copy-start | bytes 393220
  7.9 16.9 %copy-start.11 = (f32[128,256]{1,0:T(8,128)}, f32[128,256]{1,0:T(8,128)S(1)}, u32[]{:S(2)}) copy-start(f32[128,256]{1,0:T(8,128)S(1)} %get-tuple-element.41) | copy-start | bytes 393220
  10.0 1.4 %collective-permute-start.1 = (f32[128,256]{1,0:T(8,128)S(1)}, f32[128,256]{1,0:T(8,128)S(1)}, u32[]{:S(2)}, u32[]{:S(2)}) collective-permute-start(f32[128,256]{1,0:T(8,128)S(1)} %get-tuple-element.39), channel_id=1, source_target_pairs={{0,1},{1,0},{2,3},{3,2},{4,5},{5,4},{6,7},{7,6},{8,9},{9,8},{10,11... | collective-permute-start | bytes 393224 | tf_op jit(solution)/shard_map/ppermute | solution.py:172
  11.4 5.8 %collective-permute-start.4 = (f32[128,256]{1,0:T(8,128)S(1)}, f32[128,256]{1,0:T(8,128)S(1)}, u32[]{:S(2)}, u32[]{:S(2)}) collective-permute-start(f32[128,256]{1,0:T(8,128)S(1)} %multiply_add_fusion.7), channel_id=1, source_target_pairs={{0,2},{1,5},{2,0},{3,7},{4,6},{5,1},{6,4},{7,3},{8,10},{9,13},{10,... | collective-permute-start | bytes 393224 | tf_op jit(solution)/shard_map/ppermute | solution.py:172
  13.2 6.2 %collective-permute-start.3 = (f32[128,256]{1,0:T(8,128)S(1)}, f32[128,256]{1,0:T(8,128)S(1)}, u32[]{:S(2)}, u32[]{:S(2)}) collective-permute-start(f32[128,256]{1,0:T(8,128)S(1)} %multiply_add_fusion.7), channel_id=1, source_target_pairs={{0,4},{1,3},{2,6},{3,1},{4,0},{5,7},{6,2},{7,5},{8,12},{9,11},{10,... | collective-permute-start | bytes 393224 | tf_op jit(solution)/shard_map/ppermute | solution.py:172
  14.8 6.2 %collective-permute-start.2 = (f32[128,256]{1,0:T(8,128)S(1)}, f32[128,256]{1,0:T(8,128)S(1)}, u32[]{:S(2)}, u32[]{:S(2)}) collective-permute-start(f32[128,256]{1,0:T(8,128)S(1)} %multiply_add_fusion.7), channel_id=1, source_target_pairs={{0,6},{1,7},{2,4},{3,5},{4,2},{5,3},{6,0},{7,1},{8,14},{9,15},{10,... | collective-permute-start | bytes 393224 | tf_op jit(solution)/shard_map/ppermute | solution.py:172
  15.0 9.9 %collective-permute-start.5 = (f32[128,256]{1,0:T(8,128)S(1)}, f32[128,256]{1,0:T(8,128)S(1)}, u32[]{:S(2)}, u32[]{:S(2)}) collective-permute-start(f32[128,256]{1,0:T(8,128)S(1)} %shard_map.111.kept_ref), channel_id=1, source_target_pairs={{0,16},{16,0},{1,17},{17,1},{2,18},{18,2},{3,19},{19,3},{4,20},{20... | collective-permute-start | bytes 393224 | tf_op jit(solution)/shard_map/ppermute | solution.py:172
  16.7 8.2 %collective-permute-start.6 = (f32[128,256]{1,0:T(8,128)S(1)}, f32[128,256]{1,0:T(8,128)S(1)}, u32[]{:S(2)}, u32[]{:S(2)}) collective-permute-start(f32[128,256]{1,0:T(8,128)S(1)} %collective-permute-done.1.came_ref), channel_id=1, source_target_pairs={{0,16},{16,0},{1,17},{17,1},{2,18},{18,2},{3,19},{19,3},{4,20},{20... | collective-permute-start | bytes 393224 | tf_op jit(solution)/shard_map/ppermute | solution.py:172
  21.1 6.9 %collective-permute-start.7 = (f32[128,256]{1,0:T(8,128)S(1)}, f32[128,256]{1,0:T(8,128)S(1)}, u32[]{:S(2)}, u32[]{:S(2)}) collective-permute-start(f32[128,256]{1,0:T(8,128)S(1)} %multiply_add_fusion.6), channel_id=1, source_target_pairs={{0,12},{1,13},{2,14},{3,15},{4,8},{5,9},{6,10},{7,11},{8,4},{9,5},... | collective-permute-start | bytes 393224 | tf_op jit(solution)/shard_map/ppermute | solution.py:172
  28.1 1.7 %collective-permute-start.9 = (f32[128,256]{1,0:T(8,128)S(1)}, f32[128,256]{1,0:T(8,128)S(1)}, u32[]{:S(2)}, u32[]{:S(2)}) collective-permute-start(f32[128,256]{1,0:T(8,128)S(1)} %get-tuple-element.54), channel_id=1, source_target_pairs={{0,1},{1,0},{2,3},{3,2},{4,5},{5,4},{6,7},{7,6},{8,9},{9,8},{10,11... | collective-permute-start | bytes 393224 | tf_op jit(solution)/shard_map/ppermute | solution.py:172
  28.2 5.9 %collective-permute-start.8 = (f32[128,256]{1,0:T(8,128)S(1)}, f32[128,256]{1,0:T(8,128)S(1)}, u32[]{:S(2)}, u32[]{:S(2)}) collective-permute-start(f32[128,256]{1,0:T(8,128)S(1)} %multiply_add_fusion.4.entering_ref), channel_id=1, source_target_pairs={{0,16},{16,0},{1,17},{17,1},{2,18},{18,2},{3,19},{19,3},{4,20},{20... | collective-permute-start | bytes 393224 | tf_op jit(solution)/shard_map/ppermute | solution.py:172
  29.8 1.0 %copy-start.4 = (f32[1,1,256,256]{3,2,1,0:T(8,128)S(1)}, f32[1,1,256,256]{3,2,1,0:T(8,128)}, u32[]{:S(2)}) copy-start(f32[1,1,256,256]{3,2,1,0:T(8,128)} %param.12) | copy-start | bytes 786436
  29.8 1.0 %copy-start.6 = (f32[256,256]{1,0:T(8,128)S(1)}, f32[256,256]{1,0:T(8,128)}, u32[]{:S(2)}) copy-start(f32[256,256]{1,0:T(8,128)} %diffusion_ref.3) | copy-start | bytes 786436
  34.2 1.4 %collective-permute-start.10 = (f32[128,256]{1,0:T(8,128)S(1)}, f32[128,256]{1,0:T(8,128)S(1)}, u32[]{:S(2)}, u32[]{:S(2)}) collective-permute-start(f32[128,256]{1,0:T(8,128)S(1)} %get-tuple-element.60), channel_id=1, source_target_pairs={{0,1},{1,0},{2,3},{3,2},{4,5},{5,4},{6,7},{7,6},{8,9},{9,8},{10,11... | collective-permute-start | bytes 393224 | tf_op jit(solution)/shard_map/ppermute | solution.py:172
  36.6 1.4 %collective-permute-start.11 = (f32[128,256]{1,0:T(8,128)S(1)}, f32[128,256]{1,0:T(8,128)S(1)}, u32[]{:S(2)}, u32[]{:S(2)}) collective-permute-start(f32[128,256]{1,0:T(8,128)S(1)} %get-tuple-element.62), channel_id=1, source_target_pairs={{0,1},{1,0},{2,3},{3,2},{4,5},{5,4},{6,7},{7,6},{8,9},{9,8},{10,11... | collective-permute-start | bytes 393224 | tf_op jit(solution)/shard_map/ppermute | solution.py:172
  38.0 13.1 %copy-start.8 = (f32[128,256]{1,0:T(8,128)S(1)}, f32[128,256]{1,0:T(8,128)}, u32[]{:S(2)}) copy-start(f32[128,256]{1,0:T(8,128)} %copy-done.7) | copy-start | bytes 393220
  38.0 13.1 %copy-start.10 = (f32[128,256]{1,0:T(8,128)S(1)}, f32[128,256]{1,0:T(8,128)}, u32[]{:S(2)}) copy-start(f32[128,256]{1,0:T(8,128)} %copy-done.9) | copy-start | bytes 393220
  38.0 13.1 %copy-start.12 = (f32[128,256]{1,0:T(8,128)S(1)}, f32[128,256]{1,0:T(8,128)}, u32[]{:S(2)}) copy-start(f32[128,256]{1,0:T(8,128)} %copy-done.11) | copy-start | bytes 393220
  38.0 5.8 %collective-permute-start.14 = (f32[128,256]{1,0:T(8,128)S(1)}, f32[128,256]{1,0:T(8,128)S(1)}, u32[]{:S(2)}, u32[]{:S(2)}) collective-permute-start(f32[128,256]{1,0:T(8,128)S(1)} %multiply_add_fusion.3), channel_id=1, source_target_pairs={{0,2},{1,5},{2,0},{3,7},{4,6},{5,1},{6,4},{7,3},{8,10},{9,13},{10,... | collective-permute-start | bytes 393224 | tf_op jit(solution)/shard_map/ppermute | solution.py:172
  39.6 6.1 %collective-permute-start.13 = (f32[128,256]{1,0:T(8,128)S(1)}, f32[128,256]{1,0:T(8,128)S(1)}, u32[]{:S(2)}, u32[]{:S(2)}) collective-permute-start(f32[128,256]{1,0:T(8,128)S(1)} %multiply_add_fusion.3), channel_id=1, source_target_pairs={{0,4},{1,3},{2,6},{3,1},{4,0},{5,7},{6,2},{7,5},{8,12},{9,11},{10,... | collective-permute-start | bytes 393224 | tf_op jit(solution)/shard_map/ppermute | solution.py:172
  41.2 6.2 %collective-permute-start.12 = (f32[128,256]{1,0:T(8,128)S(1)}, f32[128,256]{1,0:T(8,128)S(1)}, u32[]{:S(2)}, u32[]{:S(2)}) collective-permute-start(f32[128,256]{1,0:T(8,128)S(1)} %multiply_add_fusion.3), channel_id=1, source_target_pairs={{0,6},{1,7},{2,4},{3,5},{4,2},{5,3},{6,0},{7,1},{8,14},{9,15},{10,... | collective-permute-start | bytes 393224 | tf_op jit(solution)/shard_map/ppermute | solution.py:172
  47.4 6.9 %collective-permute-start.15 = (f32[128,256]{1,0:T(8,128)S(1)}, f32[128,256]{1,0:T(8,128)S(1)}, u32[]{:S(2)}, u32[]{:S(2)}) collective-permute-start(f32[128,256]{1,0:T(8,128)S(1)} %multiply_add_fusion.2), channel_id=1, source_target_pairs={{0,12},{1,13},{2,14},{3,15},{4,8},{5,9},{6,10},{7,11},{8,4},{9,5},... | collective-permute-start | bytes 393224 | tf_op jit(solution)/shard_map/ppermute | solution.py:172
  54.4 1.4 %collective-permute-start.16 = (f32[128,256]{1,0:T(8,128)S(1)}, f32[128,256]{1,0:T(8,128)S(1)}, u32[]{:S(2)}, u32[]{:S(2)}) collective-permute-start(f32[128,256]{1,0:T(8,128)S(1)} %get-tuple-element.64), channel_id=1, source_target_pairs={{0,1},{1,0},{2,3},{3,2},{4,5},{5,4},{6,7},{7,6},{8,9},{9,8},{10,11... | collective-permute-start | bytes 393224 | tf_op jit(solution)/shard_map/ppermute | solution.py:172
